TPU v7x, 32 devices: a whole 2x2x4 slice. The times are simulated.
32 devices in a mesh: px: 4 (over x, core), py: 8 (over z, y).
Axes of the slice: x: 2, y: 2, z: 4, core: 2. Of those that a mesh axis runs over, the one named last changes fastest.
Arguments:
- potential: float32 [128, 128, 256], P('px', 'py'), may hold values from -2.4 to 2.4
- owner: int32 [4, 8, 256, 1], P('px', 'py'), may hold values from 0 to 31; in each aligned block of 256 rows (0 to 255, 256 to 511, ..., all dimensions but the last counted through in order) at most 16 rows name the same one
- window: int32 [4, 8, 256], P('px', 'py'), may hold values from 0 to 255
Outputs:
- displacement: float32 [3, 128, 128, 256], P(None, 'px', 'py')
- density: float32 [128, 128, 256], P('px', 'py')
Inputs may be any that keep to these rules, and one draw needn't show every extreme that they name: Among the 256 blocks of one tile (i, j), no owner is named more than 16 times, and the bound 16 is reached.
All inputs are finite; a program needn't handle non-finite values.
Results may differ from a plain program's by a relative error of at most 0.0003.
Values sent between devices are 32-bit elements; how exact they have to be, the bound alone decides.
No kernel may reach another device: no remote copies, remote signals or barrier semaphores. Data moves between devices by JAX's collectives and lax.ppermute only.
A program may use at most 128 MiB of HBM per device.

v0:
```python
import math

import jax
import jax.numpy as jnp
from jax import lax
from jax.sharding import PartitionSpec as P

SECOND_ORDER = 3.0 / 7.0
HIGHEST = lax.Precision.HIGHEST


def with_halo(x, sides, width):
    for axis, dim in sides:
        size, length = (lax.axis_size(axis), x.shape[dim])
        up = [(i, (i + 1) % size) for i in range(size)]
        down = [(j, i) for i, j in up]
        last = lax.slice_in_dim(x, length - width, length, axis=dim)
        leading = lax.slice_in_dim(x, 0, width, axis=dim)
        before = lax.ppermute(last, axis, up)
        after = lax.ppermute(leading, axis, down)
        x = jnp.concatenate([before, x, after], axis=dim)
    return x


def spline_weight(offset):
    magnitude = jnp.abs(offset)
    inner = (4.0 - 6.0 * magnitude * magnitude + 3.0 * magnitude * magnitude * magnitude) / 6.0
    reach = jnp.maximum(2.0 - magnitude, 0.0)
    outer = reach * reach * reach / 6.0
    return jnp.where(magnitude < 1.0, inner, outer)


def deposit_blocks(shifts):
    count = shifts.shape[0]
    within = jnp.arange(512)
    offsets = jnp.stack([within // 64, within // 8 % 8, within % 8]).astype(jnp.float32)
    places = 2.0 + offsets[None] + shifts
    cells = jnp.arange(12).astype(jnp.float32)
    weights = spline_weight(cells[None, None, :, None] - places[:, :, None, :])
    planar = (weights[:, 0, :, None, :] * weights[:, 1, None, :, :]).reshape(count, 144, 512)
    windows = jnp.einsum("sqp,swp->sqw", planar, weights[:, 2], precision=HIGHEST)
    return windows.reshape(count, 1728)


def grouped_deposit(shifts):
    total = shifts.shape[0]
    group = math.gcd(64, total)
    outputs = lax.map(deposit_blocks, shifts.reshape(total // group, group, 3, 512))
    return outputs.reshape(total, 1728)


def neighbors(field):
    return with_halo(field, (("px", 0), ("py", 1)), 1)


def differences(padded, center):
    along_x = (padded[2:, 1:-1] - padded[:-2, 1:-1]) * 0.5
    along_y = (padded[1:-1, 2:] - padded[1:-1, :-2]) * 0.5
    along_z = (jnp.roll(center, -1, 2) - jnp.roll(center, 1, 2)) * 0.5
    return (along_x, along_y, along_z)


def hartley_table(length):
    modes = jnp.arange(length)
    product = modes[:, None] * modes[None, :] % length
    angle = product.astype(jnp.float32) * (2.0 * math.pi / length)
    return jnp.cos(angle) + jnp.sin(angle)


def laplace_modes(modes, length):
    return 2.0 * jnp.cos(modes.astype(jnp.float32) * (2.0 * math.pi / length)) - 2.0


def spread_cells(blocked):
    count = blocked.shape[0]
    rest = blocked.shape[2:]
    head = blocked[:, :8]
    tail = jnp.concatenate([blocked[:, 8:], jnp.zeros((count, 4) + rest, blocked.dtype)], 1)
    empty_row = jnp.zeros((1, 8) + rest, blocked.dtype)
    joined = jnp.concatenate([head, empty_row], 0) + jnp.concatenate([empty_row, tail], 0)
    return joined.reshape((8 * (count + 1),) + rest)[: 8 * count + 4]


def fold_rims(halo_field):
    length = halo_field.shape[0] - 8
    core = halo_field[4 : length + 4]
    lower = jnp.pad(halo_field[:2], ((0, length - 2), (0, 0), (0, 0)))
    upper = jnp.pad(halo_field[length + 6 :], ((length - 2, 0), (0, 0), (0, 0)))
    return core + lower + upper


def per_device(potential, owner, window):
    rows_x, rows_y, cells_z = potential.shape
    tiles_x = lax.axis_size("px")
    tiles_y = lax.axis_size("py")
    tile_count = tiles_x * tiles_y
    grid_x = rows_x * tiles_x
    grid_y = rows_y * tiles_y
    plane_count = cells_z // tile_count
    padded = neighbors(potential)
    ahead_x = padded[2:, 1:-1]
    behind_x = padded[:-2, 1:-1]
    ahead_y = padded[1:-1, 2:]
    behind_y = padded[1:-1, :-2]
    ahead_z = jnp.roll(potential, -1, 2)
    behind_z = jnp.roll(potential, 1, 2)
    curve_xx = ahead_x - 2.0 * potential + behind_x
    curve_yy = ahead_y - 2.0 * potential + behind_y
    curve_zz = ahead_z - 2.0 * potential + behind_z
    curve_xy = (padded[2:, 2:] - padded[2:, :-2] - padded[:-2, 2:] + padded[:-2, :-2]) * 0.25
    curve_xz = (
        jnp.roll(ahead_x, -1, 2)
        - jnp.roll(ahead_x, 1, 2)
        - jnp.roll(behind_x, -1, 2)
        + jnp.roll(behind_x, 1, 2)
    ) * 0.25
    curve_yz = (
        jnp.roll(ahead_y, -1, 2)
        - jnp.roll(ahead_y, 1, 2)
        - jnp.roll(behind_y, -1, 2)
        + jnp.roll(behind_y, 1, 2)
    ) * 0.25
    source = (
        curve_xx * curve_yy
        + curve_xx * curve_zz
        + curve_yy * curve_zz
        - curve_xy * curve_xy
        - curve_xz * curve_xz
        - curve_yz * curve_yz
    )
    split_z = hartley_table(cells_z).reshape(cells_z, tiles_x, tiles_y, plane_count)
    spectrum = jnp.einsum("xyz,zabq->qabxy", source, split_z, precision=HIGHEST)
    slabs = lax.all_to_all(
        lax.all_to_all(spectrum, "px", split_axis=1, concat_axis=3, tiled=True),
        "py",
        split_axis=2,
        concat_axis=4,
        tiled=True,
    ).reshape(plane_count, grid_x, grid_y)
    table_x = hartley_table(grid_x)
    table_y = hartley_table(grid_y)
    along_x = jnp.einsum("qxy,xk->qky", slabs, table_x, precision=HIGHEST)
    modes = jnp.einsum("qky,yl->qkl", along_x, table_y, precision=HIGHEST)
    modes_z = lax.axis_index(("px", "py")) * plane_count + jnp.arange(plane_count)
    modes_x = jnp.arange(grid_x)
    modes_y = jnp.arange(grid_y)
    eigen = (
        laplace_modes(modes_x, grid_x)[None, :, None]
        + laplace_modes(modes_y, grid_y)[None, None, :]
        + laplace_modes(modes_z, cells_z)[:, None, None]
    )
    anchor = (
        (modes_z == 0)[:, None, None]
        & (modes_x == 0)[None, :, None]
        & (modes_y == 0)[None, None, :]
    )
    scale = 1.0 / (grid_x * grid_y * cells_z)
    inverse = jnp.where(anchor, 0.0, scale / jnp.where(anchor, -1.0, eigen))
    solved = modes * inverse
    back_x = jnp.einsum("qkl,kx->qxl", solved, table_x, precision=HIGHEST)
    back_plane = jnp.einsum("qxl,ly->qxy", back_x, table_y, precision=HIGHEST)
    returned = lax.all_to_all(
        lax.all_to_all(
            back_plane.reshape(plane_count, 1, 1, grid_x, grid_y),
            "px",
            split_axis=3,
            concat_axis=1,
            tiled=True,
        ),
        "py",
        split_axis=4,
        concat_axis=2,
        tiled=True,
    )
    second = jnp.einsum("qabxy,zabq->xyz", returned, split_z, precision=HIGHEST)
    first_grad = differences(padded, potential)
    second_grad = differences(neighbors(second), second)
    displacement = jnp.stack(
        [-first_grad[component] - SECOND_ORDER * second_grad[component] for component in range(3)]
    )
    shift = jnp.clip(displacement, -1.0, 1.0)
    blocks_x = rows_x // 8
    blocks_y = rows_y // 8
    blocks_z = cells_z // 8
    block_count = blocks_x * blocks_y * blocks_z
    blocks = (
        shift.reshape(3, blocks_x, 8, blocks_y, 8, blocks_z, 8)
        .transpose(1, 3, 5, 0, 2, 4, 6)
        .reshape(block_count, 3, 512)
    )
    targets = owner.reshape(block_count)
    places = window.reshape(block_count)
    capacity = max(2, 2 * block_count // tile_count)
    chosen = (targets[:, None] == jnp.arange(tile_count)[None, :]).astype(jnp.int32)
    before = jnp.cumsum(chosen, 0) - chosen
    ranks = jnp.sum(before * chosen, 1)
    slots = targets * capacity + ranks
    labels = (
        jnp.full((tile_count * capacity,), float(block_count), jnp.float32)
        .at[slots]
        .set(places.astype(jnp.float32))
        .reshape(tile_count, capacity)
    )
    own_windows = grouped_deposit(blocks)
    outgoing = (
        jnp.zeros((tile_count * capacity, 1728), jnp.float32)
        .at[slots]
        .set(own_windows)
        .reshape(tile_count, capacity, 1728)
    )
    arrived, arrived_labels = (
        lax.all_to_all(outgoing, ("px", "py"), split_axis=0, concat_axis=0, tiled=True),
        lax.all_to_all(labels, ("px", "py"), split_axis=0, concat_axis=0, tiled=True),
    )
    contributions = arrived.reshape(tile_count * capacity, 1728)
    segment_ids = arrived_labels.reshape(tile_count * capacity).astype(jnp.int32)
    gathered = jax.ops.segment_sum(contributions, segment_ids, num_segments=block_count + 1)[
        :block_count
    ]
    cubes = gathered.reshape(blocks_x, blocks_y, blocks_z, 12, 12, 12).transpose(0, 3, 1, 4, 2, 5)
    spread_x = spread_cells(cubes)
    spread_y = spread_cells(jnp.moveaxis(spread_x, 0, -1))
    spread_z = spread_cells(jnp.moveaxis(spread_y, 0, -1))
    tile = jnp.moveaxis(spread_z, 0, -1)
    wrapped = (
        tile[:, :, 2 : cells_z + 2]
        + jnp.pad(tile[:, :, cells_z + 2 :], ((0, 0), (0, 0), (0, cells_z - 2)))
        + jnp.pad(tile[:, :, :2], ((0, 0), (0, 0), (cells_z - 2, 0)))
    )
    rimmed = with_halo(wrapped, (("px", 0), ("py", 1)), 2)
    folded = fold_rims(rimmed)
    density = jnp.swapaxes(fold_rims(jnp.swapaxes(folded, 0, 1)), 0, 1)
    return (displacement, density)


def solution(mesh):
    return jax.shard_map(
        per_device,
        mesh=mesh,
        in_specs=(P("px", "py", None), P("px", "py", None, None), P("px", "py", None)),
        out_specs=(P(None, "px", "py", None), P("px", "py", None)),
        check_vma=False,
    )
```

profile of v0, /device:TPU:0, one launch (start us, length us, event | category | flops | bytes accessed | tf_op | source)
XLA Modules:
  0.0 590.9 jit_solution(12623799569676033952)
XLA Ops:
  3.8 2.4 fusion.132
  7.0 5.4 collective-permute-start.2
  14.0 5.0 collective-permute-done.3
  19.8 2.1 fusion.36
  22.0 4.4 fusion.135
  26.3 2.2 reshape.601
  28.5 11.9 %all_to_all.77 = f32[4,1,32768]{2,1,0:T(1,128)} all-to-all(f32[4,1,32768]{2,1,0:T(1,128)S(1)} %reshape.601), channel_id=1, replica_groups=mesh['px'=4,'py'=8] {'px'}, dimensions={0} | all-to-all | bytes 1048576 | tf_op jit(solution)/shard_map/all_to_all | solution.py:134
  41.0 3.0 reduce.6
  43.9 2.1 reshape.602
  47.8 2.7 copy.153
  50.5 3.1 reshape.586
  53.5 3.7 all-to-all-start.1
  57.5 14.0 %all-to-all-done.1 = f32[8,1,8,128,16]{3,4,0,1,2:T(8,128)S(1)} async-done(((f32[8,1,8,128,16]{3,4,0,1,2:T(8,128)}), f32[8,1,8,128,16]{3,4,0,1,2:T(8,128)S(1)}, u32[]{:S(2)}, u32[]{:S(2)}) %all-to-all-start.1) | async-done | bytes 524320 | tf_op jit(solution)/shard_map/all_to_all | solution.py:133
  75.4 11.2 %all_to_all.78 = f32[8,1,1,128,128]{4,0,2,1,3:T(8,128)S(1)} all-to-all(f32[8,1,1,128,128]{4,0,2,1,3:T(8,128)S(1)} %copy.111), channel_id=1, replica_groups=mesh['px'=4,'py'=8] {'px'}, dimensions={3} | all-to-all | bytes 1048576 | tf_op jit(solution)/shard_map/all_to_all | solution.py:163
  86.6 2.9 copy.112
  89.5 3.5 reshape.603
  93.0 3.6 all-to-all-start.3
  103.8 7.0 %all-to-all-done.3 = f32[8,1,16384]{2,1,0:T(1,128)S(1)} async-done(((f32[8,1,16384]{2,1,0:T(1,128)}), f32[8,1,16384]{2,1,0:T(1,128)S(1)}, u32[]{:S(2)}, u32[]{:S(2)}) %all-to-all-start.3) | async-done | bytes 524320 | tf_op jit(solution)/shard_map/all_to_all | solution.py:162
  110.9 3.6 all-to-all-start.4
  116.3 2.5 reshape.604
  118.7 4.7 copy.156
  123.5 9.8 %fusion.17 = f32[32,16,256]{2,1,0:T(8,128)S(1)} fusion(f32[8,4,1,32,8,16]{5,0,4,3,1,2:T(8,128)} %copy.156, s32[4,8,8]{2,1,0:T(8,128)S(1)} %copy-done.11), kind=kOutput, calls=%fused_computation.78 | convolution fusion | flops 403636224 | bytes 1049600 | tf_op jit(solution)/shard_map/qabxy,zabq->xyz/dot_general | solution.py:175
  141.4 4.4 collective-permute-start.6
  147.9 6.4 %sub.189 = f32[1,4,8,2,8,32,8]{6,5,4,3,2,1,0:T(8,128)} reshape(f32[1,32,16,256]{3,2,1,0:T(8,128)S(1)} %fusion.66) | data formatting | bytes 1048576 | tf_op jit(solution)/shard_map/sub | solution.py:179
  154.3 6.3 %copy.127 = f32[1,4,8,2,8,32,8]{5,6,4,3,2,1,0:T(8,128)} copy(f32[1,4,8,2,8,32,8]{6,5,4,3,2,1,0:T(8,128)} %sub.189) | data formatting | bytes 1048576 | tf_op jit(solution)/shard_map/sub | solution.py:179
  161.9 6.2 %stack.25 = f32[1,4,8,2,8,32,8]{6,5,4,3,2,1,0:T(8,128)} reshape(f32[32,16,256]{2,1,0:T(8,128)S(1)} %get-tuple-element.104) | data formatting | bytes 1048576 | tf_op jit(solution)/shard_map/stack | solution.py:178
  168.1 6.3 %copy.125 = f32[1,4,8,2,8,32,8]{5,6,4,3,2,1,0:T(8,128)} copy(f32[1,4,8,2,8,32,8]{6,5,4,3,2,1,0:T(8,128)} %stack.25) | data formatting | bytes 1048576 | tf_op jit(solution)/shard_map/stack | solution.py:178
  174.4 6.2 %stack.26 = f32[1,4,8,2,8,32,8]{6,5,4,3,2,1,0:T(8,128)} reshape(f32[32,16,256]{2,1,0:T(8,128)S(1)} %get-tuple-element.105) | data formatting | bytes 1048576 | tf_op jit(solution)/shard_map/stack | solution.py:178
  180.6 6.3 %copy.126 = f32[1,4,8,2,8,32,8]{5,6,4,3,2,1,0:T(8,128)} copy(f32[1,4,8,2,8,32,8]{6,5,4,3,2,1,0:T(8,128)} %stack.26) | data formatting | bytes 1048576 | tf_op jit(solution)/shard_map/stack | solution.py:178
  186.9 3.6 fusion.10
  190.5 8.7 %copy.128 = f32[4,2,32,3,8,8,8]{2,1,6,5,4,3,0:T(2,128)} copy(f32[4,2,32,3,8,8,8]{2,6,5,1,4,0,3:T(8,128)S(1)} %fusion.10) | data formatting | bytes 3145728 | tf_op jit(solution)/shard_map/transpose | solution.py:188
  199.2 5.8 reshape_reshape.3
  207.1 196.8 %while.13 = (s32[]{:T(128)}, f32[4,64,1728]{2,1,0:T(8,128)}, f32[4,64,3,512]{3,1,2,0:T(8,128)}, s32[]{:T(128)}) while((s32[]{:T(128)}, f32[4,64,1728]{2,1,0:T(8,128)}, f32[4,64,3,512]{3,1,2,0:T(8,128)}, s32[]{:T(128)}) %tuple.72), condition=%wide.region_5.6_spmd, body=%wide.region_4.5_spmd.sunk | while | flops 704370176 | bytes 65495704 | solution.py:48
  208.6 3.5 fusion.150
  214.5 8.9 %broadcast_multiply_fusion.2 = f32[64,12,12,512]{3,0,2,1:T(8,128)} fusion(f32[64,12,512]{2,0,1:T(8,128)S(1)} %copy.190, f32[64,12,512]{2,0,1:T(8,128)S(1)} %copy.191), kind=kLoop, calls=%fused_computation.8.clone.1 | loop fusion | flops 4718592 | bytes 22020096 | tf_op jit(solution)/shard_map/while/body/eval_jaxpr/mul | solution.py:40
  223.3 31.0 %fusion.151 = f32[64,144,12]{1,2,0:T(8,128)S(1)} fusion(f32[64,144,512]{2,0,1:T(8,128)} %bitcast.158, f32[64,3,12,512]{3,2,0,1:T(8,128)S(1)} %fusion.150), kind=kOutput, calls=%fused_computation.3.clone.1 | convolution fusion | flops 679477248 | bytes 21413888 | tf_op jit(solution)/shard_map/while/body/eval_jaxpr/sqp,swp->sqw/dot_general | solution.py:41
  257.6 3.5 fusion.150
  263.5 8.9 %broadcast_multiply_fusion.2 = f32[64,12,12,512]{3,0,2,1:T(8,128)} fusion(f32[64,12,512]{2,0,1:T(8,128)S(1)} %copy.190, f32[64,12,512]{2,0,1:T(8,128)S(1)} %copy.191), kind=kLoop, calls=%fused_computation.8.clone.1 | loop fusion | flops 4718592 | bytes 22020096 | tf_op jit(solution)/shard_map/while/body/eval_jaxpr/mul | solution.py:40
  272.4 31.0 %fusion.151 = f32[64,144,12]{1,2,0:T(8,128)S(1)} fusion(f32[64,144,512]{2,0,1:T(8,128)} %bitcast.158, f32[64,3,12,512]{3,2,0,1:T(8,128)S(1)} %fusion.150), kind=kOutput, calls=%fused_computation.3.clone.1 | convolution fusion | flops 679477248 | bytes 21413888 | tf_op jit(solution)/shard_map/while/body/eval_jaxpr/sqp,swp->sqw/dot_general | solution.py:41
  306.7 3.5 fusion.150
  312.6 8.9 %broadcast_multiply_fusion.2 = f32[64,12,12,512]{3,0,2,1:T(8,128)} fusion(f32[64,12,512]{2,0,1:T(8,128)S(1)} %copy.190, f32[64,12,512]{2,0,1:T(8,128)S(1)} %copy.191), kind=kLoop, calls=%fused_computation.8.clone.1 | loop fusion | flops 4718592 | bytes 22020096 | tf_op jit(solution)/shard_map/while/body/eval_jaxpr/mul | solution.py:40
  321.5 31.0 %fusion.151 = f32[64,144,12]{1,2,0:T(8,128)S(1)} fusion(f32[64,144,512]{2,0,1:T(8,128)} %bitcast.158, f32[64,3,12,512]{3,2,0,1:T(8,128)S(1)} %fusion.150), kind=kOutput, calls=%fused_computation.3.clone.1 | convolution fusion | flops 679477248 | bytes 21413888 | tf_op jit(solution)/shard_map/while/body/eval_jaxpr/sqp,swp->sqw/dot_general | solution.py:41
  355.7 3.5 fusion.150
  361.6 8.9 %broadcast_multiply_fusion.2 = f32[64,12,12,512]{3,0,2,1:T(8,128)} fusion(f32[64,12,512]{2,0,1:T(8,128)S(1)} %copy.190, f32[64,12,512]{2,0,1:T(8,128)S(1)} %copy.191), kind=kLoop, calls=%fused_computation.8.clone.1 | loop fusion | flops 4718592 | bytes 22020096 | tf_op jit(solution)/shard_map/while/body/eval_jaxpr/mul | solution.py:40
  370.5 31.0 %fusion.151 = f32[64,144,12]{1,2,0:T(8,128)S(1)} fusion(f32[64,144,512]{2,0,1:T(8,128)} %bitcast.158, f32[64,3,12,512]{3,2,0,1:T(8,128)S(1)} %fusion.150), kind=kOutput, calls=%fused_computation.3.clone.1 | convolution fusion | flops 679477248 | bytes 21413888 | tf_op jit(solution)/shard_map/while/body/eval_jaxpr/sqp,swp->sqw/dot_general | solution.py:41
  403.9 4.6 scatter_custom_fusion.1
  408.5 5.3 all-to-all-start.5
  414.7 83.6 %all-to-all-done.5 = f32[32,16,1728]{2,1,0:T(8,128)} async-done(((f32[32,16,1728]{2,1,0:T(8,128)}), f32[32,16,1728]{2,1,0:T(8,128)}, u32[]{:S(2)}, u32[]{:S(2)}) %all-to-all-start.5) | async-done | bytes 3538976 | tf_op jit(solution)/shard_map/all_to_all | solution.py:212
  498.3 8.2 %scatter_custom_fusion.2 = f32[257,1728]{1,0:T(8,128)S(1)} fusion(s32[512]{0:T(512)S(1)} %reshape.573, f32[512,1728]{1,0:T(8,128)} %bitcast.50, f32[]{:T(128)} %constant.230.clone.1), kind=kCustom, calls=%fused_computation.84 | custom fusion | flops 884736 | bytes 1776896 | tf_op jit(solution)/shard_map/scatter-add | solution.py:217
  509.7 7.3 %reshape.551 = f32[4,2,32,12,12,12]{2,1,0,5,4,3:T(2,128)} reshape(f32[256,1728]{0,1:T(8,128)S(1)} %copy.131) | data formatting | bytes 3538944 | tf_op jit(solution)/shard_map/reshape | solution.py:220
  517.0 6.4 %slice.386 = f32[4,8,2,12,32,12]{4,2,0,5,3,1:T(2,128)} slice(f32[4,12,2,12,32,12]{4,2,0,5,3,1:T(2,128)} %bitcast.159), slice={[0:4], [0:8], [0:2], [0:12], [0:32], [0:12]} | slice | bytes 2359296 | tf_op jit(solution)/shard_map/slice | solution.py:77
  523.4 4.0 slice.387
  527.4 6.3 %pad_add_fusion.1 = f32[5,8,2,12,32,12]{4,2,0,5,3,1:T(2,128)S(1)} fusion(f32[4,4,2,12,32,12]{4,2,0,5,3,1:T(2,128)} %slice.387, f32[4,8,2,12,32,12]{4,2,0,5,3,1:T(2,128)} %slice.386), kind=kLoop, calls=%fused_computation.40 | loop fusion | flops 368640 | bytes 3244032 | tf_op jit(solution)/shard_map/add | solution.py:80
  533.7 3.4 copy.183
  538.4 2.6 slice.391
  541.0 6.6 %copy.160 = f32[20,32,12,36]{3,2,1,0:T(8,128)} copy(f32[20,32,12,36]{1,3,2,0:T(8,128)} %slice.391) | data formatting | bytes 2211840
  552.5 3.2 fusion.124
  555.8 2.5 copy.134
  558.3 2.5 copy.135
  562.6 2.3 copy.136
  564.9 2.3 copy.137
  567.2 4.1 pad_maximum_fusion
  573.6 4.7 collective-permute-start.11
  581.5 4.4 collective-permute-done.10
  (175 shorter events, 79.4 us)
Async XLA Ops:
  0.6 5.5 copy-start
  1.4 4.9 collective-permute-start.1
  1.9 4.7 collective-permute-start
  6.3 15.6 %copy-start.10 = (s32[4,8,8]{2,1,0:T(8,128)}, s32[4,8,8]{2,1,0:T(8,128)S(1)}, u32[]{:S(2)}) copy-start(s32[4,8,8]{2,1,0:T(8,128)S(1)} %multiply_add_fusion.1) | copy-start | bytes 3076
  7.0 7.0 %collective-permute-start.2 = (f32[34,1,256]{2,1,0:T(1,128)S(1)}, f32[34,1,256]{2,1,0:T(1,128)S(1)}, u32[]{:S(2)}, u32[]{:S(2)}) collective-permute-start(f32[34,1,256]{2,1,0:T(1,128)S(1)} %get-tuple-element.112), channel_id=1, source_target_pairs={{1,0},{2,1},{3,2},{4,3},{5,4},{6,5},{7,6},{0,7},{9,8},{10,9},{11,1... | collective-permute-start | bytes 104456 | tf_op jit(solution)/shard_map/ppermute | solution.py:20
  12.4 6.6 %collective-permute-start.3 = (f32[34,1,256]{2,1,0:T(1,128)S(1)}, f32[34,1,256]{2,1,0:T(1,128)S(1)}, u32[]{:S(2)}, u32[]{:S(2)}) collective-permute-start(f32[34,1,256]{2,1,0:T(1,128)S(1)} %get-tuple-element.113), channel_id=1, source_target_pairs={{0,1},{1,2},{2,3},{3,4},{4,5},{5,6},{6,7},{7,0},{8,9},{9,10},{10,1... | collective-permute-start | bytes 104456 | tf_op jit(solution)/shard_map/ppermute | solution.py:19
  53.5 18.0 %all-to-all-start.1 = ((f32[8,1,8,128,16]{3,4,0,1,2:T(8,128)}), f32[8,1,8,128,16]{3,4,0,1,2:T(8,128)S(1)}, u32[]{:S(2)}, u32[]{:S(2)}) async-start(f32[8,1,8,128,16]{3,4,0,1,2:T(8,128)} %reshape.586), calls=%async_computation.1 | async-start | bytes 1048576 | tf_op jit(solution)/shard_map/all_to_all | solution.py:133
  93.0 17.9 %all-to-all-start.3 = ((f32[8,1,16384]{2,1,0:T(1,128)}), f32[8,1,16384]{2,1,0:T(1,128)S(1)}, u32[]{:S(2)}, u32[]{:S(2)}) async-start(f32[8,1,16384]{2,1,0:T(1,128)} %reshape.603), calls=%async_computation.3 | async-start | bytes 1048576 | tf_op jit(solution)/shard_map/all_to_all | solution.py:162
  101.7 9.1 %copy-start.12 = (s32[256,1]{0,1:T(1,128)}, s32[256,1]{0,1:T(1,128)S(1)}, u32[]{:S(2)}) copy-start(s32[256,1]{0,1:T(1,128)S(1)} %compare_select_fusion.2) | copy-start | bytes 3076
  110.9 297.6 %all-to-all-start.4 = ((f32[32,1,16]{2,1,0:T(1,128)}), f32[32,1,16]{2,1,0:T(1,128)}, u32[]{:S(2)}, u32[]{:S(2)}) async-start(f32[32,1,16]{2,1,0:T(1,128)} %bitcast.46), calls=%async_computation.4 | async-start | bytes 32768 | tf_op jit(solution)/shard_map/all_to_all | solution.py:213
  118.7 4.7 copy-start.11
  135.0 3.8 collective-permute-start.4
  136.5 3.5 collective-permute-start.5
  141.4 19.2 %collective-permute-start.6 = (f32[34,1,256]{2,1,0:T(1,128)}, f32[34,1,256]{2,1,0:T(1,128)}, u32[]{:S(2)}, u32[]{:S(2)}) collective-permute-start(f32[34,1,256]{2,1,0:T(1,128)} %get-tuple-element.106), channel_id=1, source_target_pairs={{1,0},{2,1},{3,2},{4,3},{5,4},{6,5},{7,6},{0,7},{9,8},{10,9},{11,1... | collective-permute-start | bytes 104456 | tf_op jit(solution)/shard_map/ppermute | solution.py:20
  145.8 14.8 %collective-permute-start.7 = (f32[34,1,256]{2,1,0:T(1,128)}, f32[34,1,256]{2,1,0:T(1,128)}, u32[]{:S(2)}, u32[]{:S(2)}) collective-permute-start(f32[34,1,256]{2,1,0:T(1,128)} %get-tuple-element.107), channel_id=1, source_target_pairs={{0,1},{1,2},{2,3},{3,4},{4,5},{5,6},{6,7},{7,0},{8,9},{9,10},{10,1... | collective-permute-start | bytes 104456 | tf_op jit(solution)/shard_map/ppermute | solution.py:19
  147.9 6.4 %copy-start.4 = (f32[1,32,16,256]{3,2,1,0:T(8,128)}, f32[1,32,16,256]{3,2,1,0:T(8,128)S(1)}, u32[]{:S(2)}) copy-start(f32[1,32,16,256]{3,2,1,0:T(8,128)S(1)} %fusion.66) | copy-start | bytes 1572868
  161.9 6.2 %copy-start.6 = (f32[32,16,256]{2,1,0:T(8,128)}, f32[32,16,256]{2,1,0:T(8,128)S(1)}, u32[]{:S(2)}) copy-start(f32[32,16,256]{2,1,0:T(8,128)S(1)} %get-tuple-element.104) | copy-start | bytes 1572868
  161.9 12.5 %copy-start.8 = (f32[32,16,256]{2,1,0:T(8,128)}, f32[32,16,256]{2,1,0:T(8,128)S(1)}, u32[]{:S(2)}) copy-start(f32[32,16,256]{2,1,0:T(8,128)S(1)} %get-tuple-element.105) | copy-start | bytes 1572868
  408.5 89.8 %all-to-all-start.5 = ((f32[32,16,1728]{2,1,0:T(8,128)}), f32[32,16,1728]{2,1,0:T(8,128)}, u32[]{:S(2)}, u32[]{:S(2)}) async-start(f32[32,16,1728]{2,1,0:T(8,128)} %bitcast.165), calls=%async_computation.5 | async-start | bytes 7340032 | tf_op jit(solution)/shard_map/all_to_all | solution.py:212
  558.3 4.3 collective-permute-start.8
  560.8 4.1 collective-permute-start.9
  567.2 11.1 %copy-start.5 = (f32[1,32,16,256]{3,2,1,0:T(8,128)S(1)}, f32[1,32,16,256]{3,2,1,0:T(8,128)}, u32[]{:S(2)}) copy-start(f32[1,32,16,256]{3,2,1,0:T(8,128)} %copy-done.4) | copy-start | bytes 1572868
  567.2 11.1 %copy-start.7 = (f32[32,16,256]{2,1,0:T(8,128)S(1)}, f32[32,16,256]{2,1,0:T(8,128)}, u32[]{:S(2)}) copy-start(f32[32,16,256]{2,1,0:T(8,128)} %copy-done.6) | copy-start | bytes 1572868
  567.2 11.1 %copy-start.9 = (f32[32,16,256]{2,1,0:T(8,128)S(1)}, f32[32,16,256]{2,1,0:T(8,128)}, u32[]{:S(2)}) copy-start(f32[32,16,256]{2,1,0:T(8,128)} %copy-done.8) | copy-start | bytes 1572868
  571.3 1.5 copy-start.1
  573.5 6.0 %copy-start.2 = (f32[40,20,256]{0,2,1:T(8,128)S(1)}, f32[40,20,256]{0,2,1:T(8,128)}, u32[]{:S(2)}) copy-start(f32[40,20,256]{0,2,1:T(8,128)} %copy-done.1) | copy-start | bytes 2457604
  573.6 12.3 %collective-permute-start.10 = (f32[40,2,256]{0,2,1:T(8,128)}, f32[40,2,256]{0,2,1:T(8,128)S(1)}, u32[]{:S(2)}, u32[]{:S(2)}) collective-permute-start(f32[40,2,256]{0,2,1:T(8,128)} %get-tuple-element.96), channel_id=1, source_target_pairs={{0,1},{1,2},{2,3},{3,4},{4,5},{5,6},{6,7},{7,0},{8,9},{9,10},{10,1... | collective-permute-start | bytes 245768 | tf_op jit(solution)/shard_map/ppermute | solution.py:19
  573.6 14.2 %collective-permute-start.11 = (f32[40,2,256]{0,2,1:T(8,128)S(1)}, f32[40,2,256]{0,2,1:T(8,128)S(1)}, u32[]{:S(2)}, u32[]{:S(2)}) collective-permute-start(f32[40,2,256]{0,2,1:T(8,128)S(1)} %get-tuple-element.97), channel_id=1, source_target_pairs={{1,0},{2,1},{3,2},{4,3},{5,4},{6,5},{7,6},{0,7},{9,8},{10,9},{11,1... | collective-permute-start | bytes 245768 | tf_op jit(solution)/shard_map/ppermute | solution.py:20
  579.5 9.7 %copy-start.14 = (pred[32]{0:T(512)(128)(4,1)S(1)}, pred[32]{0:T(512)(128)(4,1)}, u32[]{:S(2)}) copy-start(pred[32]{0:T(512)(128)(4,1)} %constant.239.clone.1) | copy-start | bytes 100
  581.4 7.8 %copy-start.3 = (f32[40,20,256]{2,1,0:T(8,128)S(1)}, f32[40,20,256]{2,1,0:T(8,128)}, u32[]{:S(2)}) copy-start(f32[40,20,256]{2,1,0:T(8,128)} %copy.139) | copy-start | bytes 2457604
  587.9 1.6 copy-start.13
where the time goes:
time: 601 us; the launch traced here: 591 us
  local copies, waits for them, and re-layouts  171 us (28%)
  matrix products  142 us (24%)
  waiting for transfers between devices  118 us (20%)
  other arithmetic  97.8 us (16%)
  starting transfers between devices  36.4 us (6%)
  blocking collectives  23.2 us (4%)
    dot_general x4, matrix products, deposit_blocks(): jnp.einsum('sqp,swp->sqw', planar, weights[:, 2], precision=HIGHEST)  124 us
    all_to_all x1, waiting for transfers between devices, per_device(): lax.all_to_all(outgoing, ('px', 'py'), split_axis=0, concat_axis=0, tiled...  83.6 us
    mul x4, other arithmetic, deposit_blocks(): weights[:, 0, :, None, :] * weights[:, 1, None, :, :]  35.5 us
    another operation x4, local copies, waits for them, and re-layouts, per_device(): jnp.stack([-first_grad[component] - SECOND_ORDER * second_grad[component]...  25 us
    ppermute x6, starting transfers between devices, with_halo(): after = lax.ppermute(leading, axis, down)  19.7 us
    unnamed x36, local copies, waits for them, and re-layouts  18.4 us
    select_n x4, other arithmetic, spline_weight(): return jnp.where(magnitude < 1.0, inner, outer)  14 us
    all_to_all x1, waiting for transfers between devices, per_device(): lax.all_to_all(lax.all_to_all(spectrum, 'px', split_axis=1, concat_axis=3...  14 us
  transfers between devices with their start and end apart: 16, of which 8 were waited for; matrix products, arithmetic and copies ran while one was open for 52% of the time, Pallas kernels for 0%

commit v1 on v0

v1 whole, which is shorter than its diff:
```python
import functools
import math

import jax
import jax.numpy as jnp
import numpy as np
from jax import lax
from jax.experimental import pallas as pl
from jax.experimental.pallas import tpu as pltpu
from jax.sharding import PartitionSpec as P

SECOND_ORDER = 3.0 / 7.0
F32 = jnp.float32
BF16 = jnp.bfloat16
LANES = 128
ROWS = 896
VMEM = pl.BlockSpec(memory_space=pltpu.VMEM)
SMEM = pl.BlockSpec(memory_space=pltpu.SMEM)
NN = (((1,), (0,)), ((), ()))
NT = (((1,), (1,)), ((), ()))
TN = (((0,), (0,)), ((), ()))


def split(x, pieces):
    out = []
    for piece in range(pieces):
        part = x.astype(BF16)
        out.append(part)
        if piece < pieces - 1:
            x = x - part.astype(F32)
    return out


def dot(a, b, dims=NN):
    return lax.dot_general(a, b, dims, preferred_element_type=F32)


def dot3(a, b, dims=NN):
    return dot(a[0], b[0], dims) + (dot(a[0], b[1], dims) + dot(a[1], b[0], dims))


def swap_groups(rows, group):
    rows = list(rows)
    count = len(rows)
    axis = rows[0].ndim - 1
    lane = lax.broadcasted_iota(jnp.int32, rows[0].shape, axis) // group
    step = 1
    while step < count:
        low = (lane & step) == 0
        for k in range(count):
            if k & step:
                continue
            a, b = rows[k], rows[k + step]
            rows[k] = jnp.where(low, a, pltpu.roll(b, step * group, axis))
            rows[k + step] = jnp.where(low, pltpu.roll(a, LANES - step * group, axis), b)
        step *= 2
    return rows


def table_of(length):
    modes = np.arange(length)
    angle = (modes[:, None] * modes[None, :] % length) * (2.0 * math.pi / length)
    return (np.cos(angle) + np.sin(angle)).astype(np.float32)


def pieces_of(table):
    high = table.astype(jnp.bfloat16)
    low = (table - high.astype(np.float32)).astype(jnp.bfloat16)
    return np.asarray(high), np.asarray(low)


def laplace_of(length):
    return (2.0 * np.cos(np.arange(length) * (2.0 * math.pi / length)) - 2.0).astype(np.float32)


def call(body, outs, scratch, vmem, flops, moved):
    return pl.pallas_call(
        body,
        out_shape=outs,
        scratch_shapes=scratch,
        compiler_params=pltpu.CompilerParams(vmem_limit_bytes=vmem << 20),
        cost_estimate=pl.CostEstimate(flops=flops, bytes_accessed=moved, transcendentals=0),
    )


def shape(*dims, dtype=F32):
    return jax.ShapeDtypeStruct(dims, dtype)


def send(x, dx, dy):
    size_x, size_y = lax.axis_size("px"), lax.axis_size("py")
    pairs = []
    for i in range(size_x):
        for j in range(size_y):
            pairs.append((i * size_y + j, ((i + dx) % size_x) * size_y + (j + dy) % size_y))
    return lax.ppermute(x, ("px", "py"), pairs)


def slot_kernel(half, owner_col, owner_row, window_row, slot_out, label_out):
    count = owner_row.shape[1]
    later = lax.broadcasted_iota(jnp.int32, (count, count), 0) < lax.broadcasted_iota(
        jnp.int32, (count, count), 1
    )
    same = (owner_col[...] == owner_row[...]) & later
    rank = jnp.sum(same.astype(F32), axis=0, keepdims=True).astype(jnp.int32)
    second = rank >= half
    place = owner_row[...] * half + jnp.where(second, rank - half, rank)
    slot_out[...] = jnp.where(second, place + count, place)
    named = jnp.broadcast_to((window_row[...] + 1).astype(BF16), (8, count))
    where_row = slot_out[...]
    for part in range(2):
        rows = lax.broadcasted_iota(jnp.int32, (count, count), 0) + part * count
        chosen = (where_row == rows).astype(BF16)
        label_out[part : part + 1, :] = dot(named, chosen, NT)[0:1, :].astype(jnp.int32) - 1


def pad_tile(pad, core, x_faces, y_faces):
    rows_x, rows_y, _ = core.shape
    pad[1 : rows_x + 1, 8 : rows_y + 8, :] = core[...]
    pad[0, 8 : rows_y + 8, :] = x_faces[0]
    pad[rows_x + 1, 8 : rows_y + 8, :] = x_faces[1]
    for x in range(rows_x):
        pad[x + 1, 7:8, :] = y_faces[0, x : x + 1, :]
        pad[x + 1, rows_y + 8 : rows_y + 9, :] = y_faces[1, x : x + 1, :]


def source_kernel(core, x_faces, y_faces, corners, high, low, spectrum, pad, source):
    rows_x, rows_y, cells_z = core.shape
    pad_tile(pad, core, x_faces, y_faces)
    for side in range(2):
        edge = side * (rows_x + 1)
        pad[edge, 7:8, :] = corners[2 * side : 2 * side + 1, :]
        pad[edge, rows_y + 8 : rows_y + 9, :] = corners[2 * side + 1 : 2 * side + 2, :]

    def ahead(value):
        return pltpu.roll(value, cells_z - 1, 1)

    def behind(value):
        return pltpu.roll(value, 1, 1)

    @pl.loop(0, rows_x)
    def _(x):
        def at(dx, dy):
            return pad[x + 1 + dx, 8 + dy : 8 + dy + rows_y, :]

        here = at(0, 0)
        ahead_x, behind_x, ahead_y, behind_y = at(1, 0), at(-1, 0), at(0, 1), at(0, -1)
        xx = ahead_x - 2.0 * here + behind_x
        yy = ahead_y - 2.0 * here + behind_y
        zz = ahead(here) - 2.0 * here + behind(here)
        xy = (at(1, 1) - at(1, -1) - at(-1, 1) + at(-1, -1)) * 0.25
        across_x, across_y = ahead_x - behind_x, ahead_y - behind_y
        xz = (ahead(across_x) - behind(across_x)) * 0.25
        yz = (ahead(across_y) - behind(across_y)) * 0.25
        value = xx * yy + xx * zz + yy * zz - xy * xy - xz * xz - yz * yz
        source[pl.ds(pl.multiple_of(x * rows_y, rows_y), rows_y), :] = value

    spectrum[...] = dot3((high[...], low[...]), split(source[...], 2), NT)


def solve_kernel(
    tiles_x, tiles_y, rows_x, rows_y, scale,
    first, lap_z, slab, lap_xy, hx_high, hx_low, hy_high, hy_low, hf_high, hf_low,
    out, planes, faces,
):
    grid_x, grid_y = tiles_x * rows_x, tiles_y * rows_y
    count = slab.shape[1]
    per = LANES // rows_y
    for i in range(tiles_x):
        for part in range(rows_x // per):
            lanes = slice(part * LANES, (part + 1) * LANES)
            for wide in range(tiles_y // per):
                rows = [slab[i * tiles_y + wide * per + j, :, lanes] for j in range(per)]
                for t, row in enumerate(swap_groups(rows, rows_y)):
                    x = i * rows_x + part * per + t
                    planes[x * count : (x + 1) * count, wide * LANES : (wide + 1) * LANES] = row
    hx = (hx_high[...], hx_low[...])
    hy = (hy_high[...], hy_low[...])
    hf = (hf_high[...], hf_low[...])
    planes[...] = dot3(split(planes[...], 2), hy)
    for q in range(count):
        rows = pl.ds(q, grid_x, stride=count)
        modes = dot3(hx, split(planes[rows, :], 2))
        eigen = lap_xy[...] + lap_z[first[0] + q]
        anchor = eigen == 0.0
        solved = jnp.where(anchor, 0.0, scale / jnp.where(anchor, -1.0, eigen)) * modes
        back = dot3(hx, split(solved, 2))
        planes[rows, :] = back
        faces[pl.ds(q, 2 * tiles_y, stride=count), :] = dot3(hf, split(back, 2), NT)
    planes[...] = dot3(split(planes[...], 2), hy)

    lane = lax.broadcasted_iota(jnp.int32, (count, LANES), 1)
    for i in range(tiles_x):
        for wide in range(tiles_y // per):
            cols = slice(wide * LANES, (wide + 1) * LANES)

            def row_of(x):
                x = x % grid_x
                return planes[x * count : (x + 1) * count, cols]

            for part in range(rows_x // per):
                lanes = slice(part * LANES, (part + 1) * LANES)
                rows = [row_of(i * rows_x + part * per + t) for t in range(per)]
                for j, row in enumerate(swap_groups(rows, rows_y)):
                    out[i * tiles_y + wide * per + j, :, lanes] = row
            before, after = row_of(i * rows_x - 1), row_of((i + 1) * rows_x)
            for k in range(per):
                j = wide * per + k
                shift = (LANES - k * rows_y) % LANES
                line = pltpu.roll(before, shift, 1) if shift else before
                moved = pltpu.roll(after, (shift + rows_y) % LANES, 1)
                line = jnp.where(lane < rows_y, line, moved)
                for side in range(2):
                    at = (side * tiles_y + j) * count
                    face = faces[at : at + count, :]
                    start = 2 * rows_y + side * rows_x
                    move = (start - i * rows_x) % LANES
                    face = pltpu.roll(face, move, 1) if move else face
                    line = jnp.where(lane < start, line, face)
                out[i * tiles_y + j, :, rows_x * rows_y : rows_x * rows_y + LANES] = line


def solve_plain(slab, rows_x, rows_y, cells_z, tiles_x, tiles_y, scale):
    high = lax.Precision.HIGHEST
    grid_x, grid_y = tiles_x * rows_x, tiles_y * rows_y
    count = slab.shape[1]
    hx, hy = jnp.asarray(table_of(grid_x)), jnp.asarray(table_of(grid_y))
    planes = slab.reshape(tiles_x, tiles_y, count, rows_x, rows_y).transpose(2, 0, 3, 1, 4)
    planes = planes.reshape(count, grid_x, grid_y)
    modes = jnp.einsum("qxy,xk,yl->qkl", planes, hx, hy, precision=high)
    first = lax.axis_index(("px", "py")) * count
    lap_z = lax.dynamic_slice_in_dim(jnp.asarray(laplace_of(cells_z)), first, count)
    eigen = (
        jnp.asarray(laplace_of(grid_x))[None, :, None]
        + jnp.asarray(laplace_of(grid_y))[None, None, :]
        + lap_z[:, None, None]
    )
    anchor = eigen == 0.0
    solved = jnp.where(anchor, 0.0, scale / jnp.where(anchor, -1.0, eigen)) * modes
    back = jnp.einsum("qkl,xk,yl->qxy", solved, hx, hy, precision=high)
    tiles = back.reshape(count, tiles_x, rows_x, tiles_y, rows_y).transpose(1, 3, 0, 2, 4)
    starts_x, starts_y = np.arange(tiles_x) * rows_x, np.arange(tiles_y) * rows_y
    faces = []
    for edge in (-1, rows_x):
        line = back[:, (starts_x + edge) % grid_x].reshape(count, tiles_x, tiles_y, rows_y)
        faces.append(line.transpose(1, 2, 0, 3))
    for edge in (-1, rows_y):
        line = back[:, :, (starts_y + edge) % grid_y].reshape(count, tiles_x, rows_x, tiles_y)
        faces.append(line.transpose(1, 3, 0, 2))
    used = rows_x * rows_y + 2 * (rows_x + rows_y)
    faces.append(jnp.zeros((tiles_x, tiles_y, count, -used % LANES), F32))
    parts = [tiles.reshape(tiles_x, tiles_y, count, rows_x * rows_y)] + faces
    return jnp.concatenate(parts, -1).reshape(tiles_x * tiles_y, count, -1)


def block_kernel(
    core, x_faces, y_faces, spectrum, high, low, slots,
    displacement, first_half, second_half,
    pad, cells, spread, values,
):
    rows_x, rows_y, cells_z = core.shape
    inner = rows_x * rows_y
    blocks_x, blocks_y, blocks_z = rows_x // 8, rows_y // 8, cells_z // 8
    per = LANES // blocks_z
    cells[...] = dot3(split(spectrum[...], 2), (high[...], low[...]), TN)
    cells[0:inner, :] = cells[0:inner, :] + core[...].reshape(inner, cells_z)
    start = inner
    for faces in (x_faces, y_faces):
        for side in range(2):
            rows = slice(start, start + faces.shape[1])
            cells[rows, :] = cells[rows, :] + faces[side]
            start += faces.shape[1]
    x_edge = [inner, inner + rows_y]
    y_edge = [inner + 2 * rows_y, inner + 2 * rows_y + rows_x]

    for x in range(rows_x):
        pad[x, 8 : rows_y + 8, :] = cells[x * rows_y : (x + 1) * rows_y, :]
        pad[x, 7:8, :] = cells[y_edge[0] + x : y_edge[0] + x + 1, :]
        pad[x, rows_y + 8 : rows_y + 9, :] = cells[y_edge[1] + x : y_edge[1] + x + 1, :]

    def line(x):
        if x < 0:
            return cells[x_edge[0] : x_edge[0] + rows_y, :]
        if x >= rows_x:
            return cells[x_edge[1] : x_edge[1] + rows_y, :]
        return cells[x * rows_y : (x + 1) * rows_y, :]

    for x in range(rows_x):
        here = line(x)
        displacement[0, x] = (line(x - 1) - line(x + 1)) * 0.5
        displacement[1, x] = (pad[x, 7 : rows_y + 7, :] - pad[x, 9 : rows_y + 9, :]) * 0.5
        displacement[2, x] = (pltpu.roll(here, 1, 1) - pltpu.roll(here, cells_z - 1, 1)) * 0.5

    width = spread.shape[0] * LANES
    col = lax.broadcasted_iota(jnp.int32, (cells_z, width), 1)
    wanted = (8 * (col % blocks_z) + col // blocks_z + cells_z - 1) % cells_z
    choose = (wanted == lax.broadcasted_iota(jnp.int32, (cells_z, width), 0)).astype(BF16)
    pieces = split(cells[...], 3)
    moved = dot(pieces[0], choose) + dot(pieces[1], choose) + dot(pieces[2], choose)
    for quad in range(spread.shape[0]):
        spread[quad] = moved[:, quad * LANES : (quad + 1) * LANES]

    def put(row, tiles):
        for quad in range(width // LANES):
            every = [tiles(b // blocks_y, b % blocks_y, quad) for b in range(blocks_x * blocks_y)]
            for block in range(0, len(every), per):
                for k, item in enumerate(swap_groups(every[block : block + per], blocks_z)):
                    where = row(quad * per + k - 1)
                    if where is not None:
                        start = block * blocks_z
                        values[where : where + 8, start : start + LANES] = item

    def x_tile(a):
        def tile(bx, by, quad):
            x = 8 * bx + a
            top = x_edge[0] if x < 0 else x_edge[1] if x >= rows_x else x * rows_y
            return spread[quad, top + 8 * by : top + 8 * by + 8, :]

        return tile

    for a in range(-1, 9):
        def row(e, a=a):
            if 0 <= e < 8:
                return ((a + 1) * 8 + e) * 8
            if e in (-1, 8) and 0 <= a < 8:
                return 640 + (64 if e == 8 else 0) + a * 8
            return None

        put(row, x_tile(a))
    for side, edge in enumerate((-1, 8)):
        def tile(bx, by, quad, edge=edge):
            y = 8 * by + edge
            if y < 0 or y >= rows_y:
                top = y_edge[0 if y < 0 else 1] + 8 * bx
                return spread[quad, top : top + 8, :]
            return spread[quad, pl.ds(8 * bx * rows_y + y, 8, stride=rows_y), :]

        put(lambda e, side=side: 768 + side * 64 + e * 8 if 0 <= e < 8 else None, tile)

    count = slots.shape[1]
    pieces = split(values[...], 3)
    for part, out in enumerate((first_half, second_half)):
        rows = lax.broadcasted_iota(jnp.int32, (count, count), 0) + part * count
        chosen = (slots[...] == rows).astype(BF16)
        out[...] = dot(chosen, pieces[0], NT) + dot(chosen, pieces[1], NT) + dot(chosen, pieces[2], NT)


def spline(shift):
    g = jnp.abs(shift)
    h = 1.0 - g
    gg, hh = g * g, h * h
    near = (2.0 / 3.0) - gg + 0.5 * gg * g
    ahead = (2.0 / 3.0) - hh + 0.5 * hh * h
    back = hh * h * (1.0 / 6.0)
    far = gg * g * (1.0 / 6.0)
    up = shift >= 0.0
    zero = jnp.zeros_like(far)
    return (
        jnp.where(up, zero, far),
        jnp.where(up, back, ahead),
        near,
        jnp.where(up, ahead, back),
        jnp.where(up, far, zero),
    )


def deposit_kernel(blocks_x, blocks_y, blocks_z, last, blocks, labels, *refs):
    if last:
        before, core, x_rims, y_rims, corners, turned, weights, high, low, grouped, tile = refs
    else:
        core, turned, weights, high, low, grouped, tile = refs
    slots = blocks.shape[0]
    cells_z = 8 * blocks_z
    per = LANES // blocks_z
    windows = blocks_x * blocks_y * blocks_z
    sub = lax.broadcasted_iota(jnp.int32, (8, LANES), 0)
    for g in range(slots // LANES):
        turned[g] = jnp.transpose(blocks[g * LANES : (g + 1) * LANES, :])

    @pl.loop(0, slots // LANES)
    def _(g):
        def rows(start):
            return turned[g, pl.ds(pl.multiple_of(start, 8), 8), :]

        @pl.loop(0, 8)
        def _(a):
            for e in range(8):
                here = rows((a + 1) * 64 + e * 8)
                x_diff = rows(a * 64 + e * 8) - rows((a + 2) * 64 + e * 8)
                z_low = rows((a + 1) * 64 + e * 8 - 8) if e > 0 else rows(640 + a * 8)
                z_top = rows((a + 1) * 64 + e * 8 + 8) if e < 7 else rows(704 + a * 8)
                y_low = jnp.where(
                    sub == 0, turned[g, pl.ds(768 + e * 8 + a, 1), :], pltpu.roll(here, 1, 0)
                )
                y_top = jnp.where(
                    sub == 7, turned[g, pl.ds(832 + e * 8 + a, 1), :], pltpu.roll(here, 7, 0)
                )
                for axis, diff in enumerate((x_diff, y_low - y_top, z_low - z_top)):
                    for k, weight in enumerate(spline(jnp.clip(diff * 0.5, -1.0, 1.0))):
                        weights[axis * 5 + k, a * 8 + e] = weight

        lanes = pl.ds(pl.multiple_of(g * LANES, LANES), LANES)

        def cell_row(s, depths):
            sums = {}
            for a in range(8):
                for k in depths:
                    at = a * 8 + (s - k)
                    w_z = weights[10 + k, at]
                    w_y = [weights[5 + j, at] for j in range(5)]
                    for i in range(5):
                        plane = weights[i, at] * w_z
                        for j in range(5):
                            key = (a + i, j)
                            term = plane * w_y[j]
                            sums[key] = sums[key] + term if key in sums else term
                for u in [a] if a < 7 else range(7, 12):
                    head = sums[u, 0]
                    tail = jnp.zeros_like(head)
                    for j in range(1, 5):
                        moved = pltpu.roll(sums[u, j], j, 0)
                        head = head + jnp.where(sub >= j, moved, 0.0)
                        tail = tail + jnp.where(sub < j, moved, 0.0)
                    both = jnp.concatenate([head, tail], 0)
                    top, rest = split(both, 2)
                    out = pl.ds(pl.multiple_of((s * 12 + u) * 16, 16), 16)
                    high[out, lanes] = top
                    low[out, lanes] = rest

        for s in (0, 1, 2, 3, 8, 9, 10, 11):
            cell_row(s, [k for k in range(5) if 0 <= s - k < 8])

        @pl.loop(4, 8)
        def _(s):
            cell_row(s, range(5))

    named = (labels[...] == lax.broadcasted_iota(jnp.int32, (windows, slots), 0)).astype(BF16)
    area = 12 * 16

    @pl.loop(0, 12 // per)
    def _(quad):
        part = []
        for k in range(per):
            rows = pl.ds(pl.multiple_of((quad * per + k) * area, 16), area)
            part.append(dot(high[rows, :], named, NT) + dot(low[rows, :], named, NT))
        for wide in range(windows // LANES):
            lanes = slice(wide * LANES, (wide + 1) * LANES)
            for t, item in enumerate(swap_groups([p[:, lanes] for p in part], blocks_z)):
                grouped[wide * per + t, quad] = item

    depth = 12 * blocks_z
    row = lax.broadcasted_iota(jnp.int32, (depth, cells_z), 0)
    wanted = (8 * (row % blocks_z) + row // blocks_z + cells_z - 2) % cells_z
    place = (wanted == lax.broadcasted_iota(jnp.int32, (depth, cells_z), 1)).astype(BF16)
    tile[...] = before[...] if last else jnp.zeros_like(tile)

    @pl.loop(0, blocks_x)
    def _(bx):
        for by in range(blocks_y):
            total = None
            for quad in range(12 // per):
                piece = place[quad * LANES : (quad + 1) * LANES, :]
                for item in split(grouped[bx * blocks_y + by, quad], 2):
                    term = dot(item, piece)
                    total = term if total is None else total + term
            rows = pl.ds(bx * 8, 12)
            cols = slice(by * 8, by * 8 + 16)
            tile[rows, cols, :] = tile[rows, cols, :] + total.reshape(12, 16, cells_z)

    if not last:
        core[...] = tile[...]
        return
    rows_x, rows_y = 8 * blocks_x, 8 * blocks_y
    core[...] = tile[2 : rows_x + 2, 2 : rows_y + 2, :]
    for side in range(2):
        x = side * (rows_x + 2)
        y = side * (rows_y + 2)
        x_rims[side] = tile[x : x + 2, 2 : rows_y + 2, :]
        y_rims[side] = tile[2 : rows_x + 2, y : y + 2, :]
        for other in range(2):
            y = other * (rows_y + 2)
            corners[side * 2 + other] = tile[x : x + 2, y : y + 2, :]


def rim_kernel(core, x_low, x_top, y_low, y_top, c_low_low, c_low_top, c_top_low, c_top_top, out):
    rows_x, rows_y, _ = core.shape
    out[...] = core[...]
    xs, ys = (slice(0, 2), slice(rows_x - 2, rows_x)), (slice(0, 2), slice(rows_y - 2, rows_y))
    for part, face in zip(xs, (x_low, x_top)):
        out[part] = out[part] + face[...]
    for part, face in zip(ys, (y_low, y_top)):
        out[:, part, :] = out[:, part, :] + face[...]
    for x, y, face in (
        (0, 0, c_low_low), (0, 1, c_low_top), (1, 0, c_top_low), (1, 1, c_top_top),
    ):
        out[xs[x], ys[y], :] = out[xs[x], ys[y], :] + face[...]


def per_device(potential, owner, window):
    rows_x, rows_y, cells_z = potential.shape
    tiles_x, tiles_y = lax.axis_size("px"), lax.axis_size("py")
    tiles = tiles_x * tiles_y
    grid_x, grid_y = rows_x * tiles_x, rows_y * tiles_y
    planes = cells_z // tiles
    inner = rows_x * rows_y
    used = inner + -(-2 * (rows_x + rows_y) // LANES) * LANES
    blocks_x, blocks_y, blocks_z = rows_x // 8, rows_y // 8, cells_z // 8
    blocks = blocks_x * blocks_y * blocks_z
    half = max(2, 2 * blocks // tiles) // 2
    both = ("px", "py")

    def exchange(x):
        return lax.all_to_all(x, both, split_axis=0, concat_axis=0, tiled=True)

    slots, labels = call(
        functools.partial(slot_kernel, half),
        (shape(1, blocks, dtype=jnp.int32), shape(2, blocks, dtype=jnp.int32)),
        [], 16, 4 * blocks**3, 8 * blocks,
    )(owner.reshape(blocks, 1), owner.reshape(1, blocks), window.reshape(1, blocks))
    arrived_labels = exchange(labels.reshape(2, tiles, half).transpose(1, 0, 2).reshape(tiles, 2 * half))
    arrived_labels = arrived_labels.reshape(tiles, 2, half).transpose(1, 0, 2).reshape(2, 1, blocks)

    last_x, last_y = rows_x - 1, rows_y - 1
    x_faces = jnp.stack([send(potential[last_x], 1, 0), send(potential[0], -1, 0)])
    y_faces = jnp.stack([send(potential[:, last_y], 0, 1), send(potential[:, 0], 0, -1)])
    corners = jnp.stack(
        [
            send(potential[last_x, last_y], 1, 1), send(potential[last_x, 0], 1, -1),
            send(potential[0, last_y], -1, 1), send(potential[0, 0], -1, -1),
        ]
    )

    z_high, z_low = pieces_of(table_of(cells_z))
    spectrum = call(
        source_kernel, shape(cells_z, inner),
        [pltpu.VMEM((rows_x + 2, rows_y + 16, cells_z), F32), pltpu.VMEM((inner, cells_z), F32)],
        24, 6 * inner * cells_z**2, 2 << 20,
    )(potential, x_faces, y_faces, corners, z_high, z_low)
    slab = exchange(spectrum).reshape(tiles, planes, inner)

    scale = SECOND_ORDER / (grid_x * grid_y * cells_z)
    if planes % 8 == 0 and tiles_y % (LANES // rows_y) == 0 and grid_x == LANES:
        first = (lax.axis_index(both) * planes).astype(jnp.int32).reshape(1)
        x_table, y_table = table_of(grid_x), table_of(grid_y)
        starts = np.arange(tiles_y) * rows_y
        edge = np.concatenate([(starts - 1) % grid_y, (starts + rows_y) % grid_y])
        lap_xy = laplace_of(grid_x)[:, None] + laplace_of(grid_y)[None, :]
        tables = pieces_of(x_table) + pieces_of(y_table) + pieces_of(y_table[edge])
        body = functools.partial(solve_kernel, tiles_x, tiles_y, rows_x, rows_y, scale)
        specs = [SMEM, SMEM] + [VMEM] * 8
        returned = pl.pallas_call(
            body,
            out_shape=shape(tiles, planes, used),
            in_specs=specs,
            out_specs=VMEM,
            scratch_shapes=[
                pltpu.VMEM((grid_x * planes, grid_y), F32),
                pltpu.VMEM((2 * tiles_y * planes, grid_x), F32),
            ],
            compiler_params=pltpu.CompilerParams(vmem_limit_bytes=24 << 20),
            cost_estimate=pl.CostEstimate(
                flops=24 * planes * grid_x**2 * grid_y, bytes_accessed=2 << 20, transcendentals=0
            ),
        )(first, laplace_of(cells_z), slab, lap_xy, *tables)
    else:
        returned = solve_plain(slab, rows_x, rows_y, cells_z, tiles_x, tiles_y, scale)
    modes = exchange(returned.reshape(cells_z, used))

    pad = pltpu.VMEM((rows_x, rows_y + 16, cells_z), F32)
    width = -(-10 * blocks_z // LANES) * LANES
    displacement, *sent = call(
        block_kernel,
        (shape(3, rows_x, rows_y, cells_z), shape(blocks, ROWS), shape(blocks, ROWS)),
        [pad, pltpu.VMEM((used, cells_z), F32), pltpu.VMEM((width // LANES, used, LANES), F32), pltpu.VMEM((ROWS, blocks), F32)],
        40, 20 * used * cells_z**2, 6 << 20,
    )(potential, x_faces, y_faces, modes, z_high, z_low, slots)

    arrived = [exchange(part) for part in sent]
    tile_shape = (rows_x + 4, rows_y + 8, cells_z)
    scratch = [
        pltpu.VMEM((blocks // LANES, ROWS, LANES), F32),
        pltpu.VMEM((15, 64, 8, LANES), F32),
        pltpu.VMEM((12 * 12 * 16, blocks), BF16),
        pltpu.VMEM((12 * 12 * 16, blocks), BF16),
        pltpu.VMEM((blocks_x * blocks_y, 12 * blocks_z // LANES, 12 * 16, LANES), F32),
        pltpu.VMEM(tile_shape, F32),
    ]
    sizes = (blocks_x, blocks_y, blocks_z)
    cost = (300 * blocks * 512, 4 << 20)
    tile = call(
        functools.partial(deposit_kernel, *sizes, False), shape(*tile_shape), scratch, 40, *cost
    )(arrived[0], arrived_labels[0])
    core, x_rims, y_rims, edges = call(
        functools.partial(deposit_kernel, *sizes, True),
        (
            shape(rows_x, rows_y, cells_z), shape(2, 2, rows_y, cells_z),
            shape(2, rows_x, 2, cells_z), shape(4, 2, 2, cells_z),
        ),
        scratch, 40, *cost,
    )(arrived[1], arrived_labels[1], tile)

    density = call(rim_kernel, shape(rows_x, rows_y, cells_z), [], 16, inner * cells_z, 2 << 20)(
        core,
        send(x_rims[1], 1, 0), send(x_rims[0], -1, 0),
        send(y_rims[1], 0, 1), send(y_rims[0], 0, -1),
        send(edges[3], 1, 1), send(edges[2], 1, -1), send(edges[1], -1, 1), send(edges[0], -1, -1),
    )
    return (displacement, density)


def solution(mesh):
    return jax.shard_map(
        per_device,
        mesh=mesh,
        in_specs=(P("px", "py", None), P("px", "py", None, None), P("px", "py", None)),
        out_specs=(P(None, "px", "py", None), P("px", "py", None)),
        check_vma=False,
    )
```

time: 601 us -> 180 us (0.30); the launches traced: 591 us -> 179 us
  local copies, waits for them, and re-layouts: 171 us -> 6.95 us
  matrix products: 142 us -> 0 us
  other arithmetic: 97.8 us -> 0.02 us
  waiting for transfers between devices: 118 us -> 70.3 us
  Pallas kernels: 0 us -> 39 us
    dot_general x10 -> x0, matrix products: 142 us -> none  [the longest x4 124 us: deposit_blocks(): jnp.einsum('sqp,swp->sqw', planar, weights[:, 2], precision=HIGHEST)]
    all_to_all x4, waiting for transfers between devices: 105 us -> 49.3 us  [exchange(): return lax.all_to_all(x, both, split_axis=0, concat_axis=0, tiled=True)]
    pallas_call x0 -> x7, Pallas kernels: none -> 39 us  [the longest x1 12 us: per_device(): call(functools.partial(deposit_kernel, *sizes, True), (shape(rows_x, rows...]
    mul x5 -> x0, other arithmetic: 35.5 us -> none  [the longest x4 35.5 us: deposit_blocks(): weights[:, 0, :, None, :] * weights[:, 1, None, :, :]]
    slice x29 -> x5, local copies, waits for them, and re-layouts: 35 us -> 2.02 us  [the longest x1 1.08 us: per_device(): potential[:, last_y]]
    another operation x7 -> x0, local copies, waits for them, and re-layouts: 31 us -> none  [the longest x4 25 us: per_device(): jnp.stack([-first_grad[component] - SECOND_ORDER * second_grad[component]...]
    all_to_all x8 -> x2, local copies, waits for them, and re-layouts: 16.4 us -> 0.76 us  [exchange(): return lax.all_to_all(x, both, split_axis=0, concat_axis=0, tiled=True)]
    unnamed x36 -> x30, local copies, waits for them, and re-layouts: 18.4 us -> 2.93 us
  transfers between devices with their start and end apart: 16 -> 20, of which waited for: 8 -> 10; matrix products, arithmetic and copies ran while one was open for 52% -> 2% of each run, Pallas kernels for 0% -> 9%
where the time goes in v1:
time: 180 us; the launch traced here: 179 us
  waiting for transfers between devices  70.3 us (39%)
  Pallas kernels  39 us (22%)
  starting transfers between devices  34.5 us (19%)
  blocking collectives  27.4 us (15%)
  local copies, waits for them, and re-layouts  6.95 us (4%)
    all_to_all x4, waiting for transfers between devices, exchange(): return lax.all_to_all(x, both, split_axis=0, concat_axis=0, tiled=True)  49.3 us
    all_to_all x1, blocking collectives, exchange(): return lax.all_to_all(x, both, split_axis=0, concat_axis=0, tiled=True)  27.4 us
    ppermute x16, starting transfers between devices, send(): return lax.ppermute(x, ('px', 'py'), pairs)  23.9 us
    ppermute x16, waiting for transfers between devices, send(): return lax.ppermute(x, ('px', 'py'), pairs)  21 us
    pallas_call x1, Pallas kernels, per_device(): call(functools.partial(deposit_kernel, *sizes, True), (shape(rows_x, rows...  12 us
    pallas_call x1, Pallas kernels, per_device(): call(functools.partial(deposit_kernel, *sizes, False), shape(*tile_shape)...  12 us
    all_to_all x4, starting transfers between devices, exchange(): return lax.all_to_all(x, both, split_axis=0, concat_axis=0, tiled=True)  10.6 us
    pallas_call x1, Pallas kernels, per_device(): pl.pallas_call(body, out_shape=shape(tiles, planes, used), in_specs=specs...  5.32 us
  transfers between devices with their start and end apart: 20, of which 10 were waited for; matrix products, arithmetic and copies ran while one was open for 2% of the time, Pallas kernels for 9%

profile of v1, /device:TPU:0, one launch (start us, length us, event | category | flops | bytes accessed | tf_op | source)
XLA Modules:
  0.0 179.1 jit_solution(8118718617970873089)
XLA Ops:
  0.6 0.0 copy-start.11
  0.6 0.0 copy-start.12
  0.7 0.0 copy-start.9
  0.7 0.0 copy-start.10
  0.7 0.0 copy-start.8
  0.7 0.0 copy-start.13
  0.7 0.8 fusion
  1.5 3.3 %collective-permute-start.6 = (f32[256]{0:T(256)S(1)}, f32[256]{0:T(256)S(1)}, u32[]{:S(2)}, u32[]{:S(2)}) collective-permute-start(f32[256]{0:T(256)S(1)} %bitcast.76), channel_id=1, source_target_pairs={{0,25},{1,26},{2,27},{3,28},{4,29},{5,30},{6,31},{7,24},{8,1},{9,2... | collective-permute-start | bytes 3080 | tf_op jit(solution)/shard_map/ppermute | solution.py:96
  4.8 0.9 collective-permute-start.4
  5.7 3.5 %collective-permute-start.5 = (f32[256]{0:T(256)S(1)}, f32[256]{0:T(256)S(1)}, u32[]{:S(2)}, u32[]{:S(2)}) collective-permute-start(f32[256]{0:T(256)S(1)} %bitcast.73), channel_id=1, source_target_pairs={{0,15},{1,8},{2,9},{3,10},{4,11},{5,12},{6,13},{7,14},{8,23},{9,16... | collective-permute-start | bytes 3080 | tf_op jit(solution)/shard_map/ppermute | solution.py:96
  9.2 1.3 collective-permute-start.7
  10.5 0.7 slice_bitcast_fusion.5
  11.3 0.0 collective-permute-start
  11.3 1.1 fusion.1
  12.4 0.0 collective-permute-done.6
  12.4 1.8 %collective-permute-start.1 = (f32[16,256]{1,0:T(8,128)S(1)}, f32[16,256]{1,0:T(8,128)S(1)}, u32[]{:S(2)}, u32[]{:S(2)}) collective-permute-start(f32[16,256]{1,0:T(8,128)S(1)} %get-tuple-element.27), channel_id=1, source_target_pairs={{0,24},{1,25},{2,26},{3,27},{4,28},{5,29},{6,30},{7,31},{8,0},{9,1... | collective-permute-start | bytes 49160 | tf_op jit(solution)/shard_map/ppermute | solution.py:96
  14.2 0.0 collective-permute-done.4
  14.2 2.3 %collective-permute-start.3 = (f32[32,256]{1,0:T(8,128)S(1)}, f32[32,256]{1,0:T(8,128)S(1)}, u32[]{:S(2)}, u32[]{:S(2)}) collective-permute-start(f32[32,256]{1,0:T(8,128)S(1)} %bitcast.64), channel_id=1, source_target_pairs={{0,7},{1,0},{2,1},{3,2},{4,3},{5,4},{6,5},{7,6},{8,15},{9,8},{10,9... | collective-permute-start | bytes 98312 | tf_op jit(solution)/shard_map/ppermute | solution.py:96
  16.5 1.6 collective-permute-done.3
  18.1 5.0 %collective-permute-done.2 = f32[32,256]{1,0:T(8,128)S(1)} collective-permute-done((f32[32,256]{1,0:T(8,128)S(1)}, f32[32,256]{1,0:T(8,128)S(1)}, u32[]{:S(2)}, u32[]{:S(2)}) %collective-permute-start.2) | collective-permute-done | bytes 32800 | tf_op jit(solution)/shard_map/ppermute | solution.py:96
  23.1 1.0 copy-done
  24.1 0.9 copy-done.2
  25.0 0.9 copy-done.4
  25.9 4.4 %shard_map.140 = f32[256,512]{1,0:T(8,128)} custom-call(f32[32,16,256]{2,1,0:T(8,128)S(1)} %copy-done, f32[2,16,256]{2,1,0:T(8,128)S(1)} %pad_maximum_fusion.1.x_faces, f32[2,32,256]{2,1,0:T(8,128)S(1)} %pad_maximum_fusion.y_faces, f32[4,256]{1,0:T(4,128)S(1)} %pad_maximum_fusion.2.corners, bf16[256,256]{1,0:T(8,128)(2,1)S(1)} %copy-done.4, ...), custom_call_target="tpu_custom_call" | custom-call | flops 201326592 | bytes 2097152 | tf_op jit(solution)/shard_map/pallas_call | solution.py:534
  30.3 2.6 %all-to-all-start = ((f32[32,8,512]{2,1,0:T(8,128)}), f32[32,8,512]{2,1,0:T(8,128)S(1)}, u32[]{:S(2)}, u32[]{:S(2)}) async-start(f32[32,8,512]{2,1,0:T(8,128)} %bitcast.17), calls=%async_computation | async-start | bytes 1048576 | tf_op jit(solution)/shard_map/all_to_all | solution.py:513
  32.9 0.0 copy-start.6
  32.9 0.0 copy-start.7
  33.0 16.3 %all-to-all-done.slab = f32[32,8,512]{2,1,0:T(8,128)S(1)} async-done(((f32[32,8,512]{2,1,0:T(8,128)}), f32[32,8,512]{2,1,0:T(8,128)S(1)}, u32[]{:S(2)}, u32[]{:S(2)}) %all-to-all-start) | async-done | bytes 524320 | tf_op jit(solution)/shard_map/all_to_all | solution.py:513
  49.3 0.0 copy-start.1
  49.3 0.0 copy-start.3
  49.3 0.0 copy-start.5
  49.4 5.3 %shard_map.141 = f32[32,8,640]{2,1,0:T(8,128)} custom-call(s32[1]{0:T(128)} %bitcast.8.first, f32[256]{0:T(256)S(1)} %copy-done.13, f32[32,8,512]{2,1,0:T(8,128)S(1)} %all-to-all-done.slab, f32[128,128]{1,0:T(8,128)S(1)} %copy-done.8, bf16[128,128]{1,0:T(8,128)(2,1)S(1)} %copy-done.10, bf16[128,128]{1,0:T(8,128)(2,1)S(1)} %copy-done.9, ...), custom_call_target="tpu_custom_call" | custom-call | flops 402653184 | bytes 2097152 | tf_op jit(solution)/shard_map/pallas_call | solution.py:551
  54.7 2.6 %all-to-all-start.1 = ((f32[32,8,640]{2,1,0:T(8,128)}), f32[32,8,640]{2,1,0:T(8,128)S(1)}, u32[]{:S(2)}, u32[]{:S(2)}) async-start(f32[32,8,640]{2,1,0:T(8,128)} %shard_map.141), calls=%async_computation.1 | async-start | bytes 1310720 | tf_op jit(solution)/shard_map/all_to_all | solution.py:513
  57.3 0.1 copy.25.owner_col
  57.5 0.3 shard_map.142
  57.8 0.1 reshape.48
  57.9 0.1 copy.26
  57.9 0.7 copy.27
  58.6 17.8 %all-to-all-done.1 = f32[32,8,640]{2,1,0:T(8,128)S(1)} async-done(((f32[32,8,640]{2,1,0:T(8,128)}), f32[32,8,640]{2,1,0:T(8,128)S(1)}, u32[]{:S(2)}, u32[]{:S(2)}) %all-to-all-start.1) | async-done | bytes 655392 | tf_op jit(solution)/shard_map/all_to_all | solution.py:513
  76.5 2.5 %all-to-all-start.3 = ((s32[32,1,16]{2,1,0:T(1,128)}), s32[32,1,16]{2,1,0:T(1,128)S(1)}, u32[]{:S(2)}, u32[]{:S(2)}) async-start(s32[32,1,16]{2,1,0:T(1,128)} %copy.27), calls=%async_computation.3 | async-start | bytes 32768 | tf_op jit(solution)/shard_map/all_to_all | solution.py:513
  79.0 4.0 %shard_map.143 = (f32[3,32,16,256]{3,2,1,0:T(8,128)}, f32[256,896]{1,0:T(8,128)S(1)}, f32[256,896]{1,0:T(8,128)}) custom-call(f32[32,16,256]{2,1,0:T(8,128)S(1)} %copy-done.1, f32[2,16,256]{2,1,0:T(8,128)S(1)} %pad_maximum_fusion.1.x_faces, f32[2,32,256]{2,1,0:T(8,128)S(1)} %pad_maximum_fusion.y_faces, f32[256,640]{1,0:T(8,128)S(1)} %bitcast.56, ...), custom_call_target="tpu_custom_call" | custom-call | flops 838860800 | bytes 6291456 | tf_op jit(solution)/shard_map/pallas_call | solution.py:571
  83.1 3.0 %all-to-all-done.3 = s32[32,1,16]{2,1,0:T(1,128)S(1)} async-done(((s32[32,1,16]{2,1,0:T(1,128)}), s32[32,1,16]{2,1,0:T(1,128)S(1)}, u32[]{:S(2)}, u32[]{:S(2)}) %all-to-all-start.3) | async-done | bytes 2080 | tf_op jit(solution)/shard_map/all_to_all | solution.py:513
  86.1 27.4 %all_to_all.48 = f32[32,8,896]{2,1,0:T(8,128)S(1)} all-to-all(f32[32,8,896]{2,1,0:T(8,128)S(1)} %bitcast.55), channel_id=1, replica_groups=mesh['px'=4,'py'=8] {'px','py'}, dimensions={0} | all-to-all | bytes 1835008 | tf_op jit(solution)/shard_map/all_to_all | solution.py:513
  113.5 2.8 %all-to-all-start.2 = ((f32[32,8,896]{2,1,0:T(8,128)}), f32[32,8,896]{2,1,0:T(8,128)S(1)}, u32[]{:S(2)}, u32[]{:S(2)}) async-start(f32[32,8,896]{2,1,0:T(8,128)} %bitcast.22), calls=%async_computation.2 | async-start | bytes 1835008 | tf_op jit(solution)/shard_map/all_to_all | solution.py:513
  116.3 0.1 copy.28
  116.4 0.1 copy.30
  116.5 0.1 squeeze.63.labels
  116.6 0.1 copy.29
  116.6 0.1 squeeze.62.labels
  116.7 12.0 %shard_map.144.refs_0_ = f32[36,24,256]{2,1,0:T(8,128)S(1)} custom-call(f32[256,896]{1,0:T(8,128)S(1)} %bitcast.54, s32[1,256]{1,0:T(1,128)S(1)} %squeeze.63.labels), custom_call_target="tpu_custom_call" | custom-call | flops 39321600 | bytes 4194304 | tf_op jit(solution)/shard_map/pallas_call | solution.py:590
  128.7 12.2 %all-to-all-done.2 = f32[32,8,896]{2,1,0:T(8,128)S(1)} async-done(((f32[32,8,896]{2,1,0:T(8,128)}), f32[32,8,896]{2,1,0:T(8,128)S(1)}, u32[]{:S(2)}, u32[]{:S(2)}) %all-to-all-start.2) | async-done | bytes 917536 | tf_op jit(solution)/shard_map/all_to_all | solution.py:513
  140.9 12.0 %shard_map.145 = (f32[32,16,256]{2,1,0:T(8,128)S(1)}, f32[2,2,16,256]{3,2,1,0:T(8,128)S(1)}, f32[2,32,2,256]{3,2,1,0:T(2,128)S(1)}, f32[4,2,2,256]{3,2,1,0:T(2,128)S(1)}) custom-call(f32[256,896]{1,0:T(8,128)S(1)} %bitcast.53, s32[1,256]{1,0:T(1,128)S(1)} %squeeze.62.labels, f32[36,24,256]{2,1,0:T(8,128)S(1)} %shard_map.144.refs_0_), custom_call_target="tpu_custom_call" | custom-call | flops 39321600 | bytes 4194304 | tf_op jit(solution)/shard_map/pallas_call | solution.py:593
  153.0 0.5 collective-permute-start.9
  153.5 0.0 collective-permute-start.8
  153.5 1.4 collective-permute-start.11
  155.0 0.6 collective-permute-start.10
  155.6 4.3 %collective-permute-start.15 = (f32[2,2,256]{2,1,0:T(2,128)S(1)}, f32[2,2,256]{2,1,0:T(2,128)S(1)}, u32[]{:S(2)}, u32[]{:S(2)}) collective-permute-start(f32[2,2,256]{2,1,0:T(2,128)S(1)} %get-tuple-element.32), channel_id=1, source_target_pairs={{0,31},{1,24},{2,25},{3,26},{4,27},{5,28},{6,29},{7,30},{8,7},{9,0... | collective-permute-start | bytes 12296 | tf_op jit(solution)/shard_map/ppermute | solution.py:96
  159.9 1.3 collective-permute-done.15.c_top_top
  161.2 1.2 collective-permute-start.14
  162.4 5.1 %collective-permute-done.14.c_top_low = f32[2,2,256]{2,1,0:T(2,128)S(1)} collective-permute-done((f32[2,2,256]{2,1,0:T(2,128)S(1)}, f32[2,2,256]{2,1,0:T(2,128)S(1)}, u32[]{:S(2)}, u32[]{:S(2)}) %collective-permute-start.14) | collective-permute-done | bytes 4128 | tf_op jit(solution)/shard_map/ppermute | solution.py:96
  167.6 2.6 %collective-permute-start.13 = (f32[2,2,256]{2,1,0:T(2,128)S(1)}, f32[2,2,256]{2,1,0:T(2,128)S(1)}, u32[]{:S(2)}, u32[]{:S(2)}) collective-permute-start(f32[2,2,256]{2,1,0:T(2,128)S(1)} %get-tuple-element.34), channel_id=1, source_target_pairs={{0,15},{1,8},{2,9},{3,10},{4,11},{5,12},{6,13},{7,14},{8,23},{9,16... | collective-permute-start | bytes 12296 | tf_op jit(solution)/shard_map/ppermute | solution.py:96
  170.2 1.3 collective-permute-done.13.c_low_top
  171.5 6.6 %collective-permute-done.12.c_low_low = f32[2,2,256]{2,1,0:T(2,128)S(1)} collective-permute-done((f32[2,2,256]{2,1,0:T(2,128)S(1)}, f32[2,2,256]{2,1,0:T(2,128)S(1)}, u32[]{:S(2)}, u32[]{:S(2)}) %collective-permute-start.12) | collective-permute-done | bytes 4128 | tf_op jit(solution)/shard_map/ppermute | solution.py:96
  178.2 0.9 shard_map.146
  (33 shorter events, 0.1 us)
Async XLA Ops:
  0.6 48.7 %copy-start.11 = (bf16[16,128]{1,0:T(8,128)(2,1)S(1)}, bf16[16,128]{1,0:T(8,128)(2,1)}, u32[]{:S(2)}) copy-start(bf16[16,128]{1,0:T(8,128)(2,1)} %constant.33.clone.hf_low) | copy-start | bytes 12292
  0.6 48.6 %copy-start.12 = (bf16[16,128]{1,0:T(8,128)(2,1)S(1)}, bf16[16,128]{1,0:T(8,128)(2,1)}, u32[]{:S(2)}) copy-start(bf16[16,128]{1,0:T(8,128)(2,1)} %constant.32.clone.hf_high) | copy-start | bytes 12292
  0.7 48.6 %copy-start.9 = (bf16[128,128]{1,0:T(8,128)(2,1)S(1)}, bf16[128,128]{1,0:T(8,128)(2,1)}, u32[]{:S(2)}) copy-start(bf16[128,128]{1,0:T(8,128)(2,1)} %constant.31.clone.hx_low.hy_low) | copy-start | bytes 98308
  0.7 48.6 %copy-start.10 = (bf16[128,128]{1,0:T(8,128)(2,1)S(1)}, bf16[128,128]{1,0:T(8,128)(2,1)}, u32[]{:S(2)}) copy-start(bf16[128,128]{1,0:T(8,128)(2,1)} %constant.30.clone.hx_high.hy_high) | copy-start | bytes 98308
  0.7 48.6 %copy-start.8 = (f32[128,128]{1,0:T(8,128)S(1)}, f32[128,128]{1,0:T(8,128)}, u32[]{:S(2)}) copy-start(f32[128,128]{1,0:T(8,128)} %constant.29.clone.lap_xy) | copy-start | bytes 196612
  0.7 48.6 %copy-start.13 = (f32[256]{0:T(256)S(1)}, f32[256]{0:T(256)}, u32[]{:S(2)}) copy-start(f32[256]{0:T(256)} %constant.28.clone.lap_z) | copy-start | bytes 3076
  1.5 10.9 %collective-permute-start.6 = (f32[256]{0:T(256)S(1)}, f32[256]{0:T(256)S(1)}, u32[]{:S(2)}, u32[]{:S(2)}) collective-permute-start(f32[256]{0:T(256)S(1)} %bitcast.76), channel_id=1, source_target_pairs={{0,25},{1,26},{2,27},{3,28},{4,29},{5,30},{6,31},{7,24},{8,1},{9,2... | collective-permute-start | bytes 3080 | tf_op jit(solution)/shard_map/ppermute | solution.py:96
  4.8 9.3 %collective-permute-start.4 = (f32[256]{0:T(256)S(1)}, f32[256]{0:T(256)S(1)}, u32[]{:S(2)}, u32[]{:S(2)}) collective-permute-start(f32[256]{0:T(256)S(1)} %bitcast.75), channel_id=1, source_target_pairs={{0,9},{1,10},{2,11},{3,12},{4,13},{5,14},{6,15},{7,8},{8,17},{9,18... | collective-permute-start | bytes 3080 | tf_op jit(solution)/shard_map/ppermute | solution.py:96
  5.7 10.7 %collective-permute-start.5 = (f32[256]{0:T(256)S(1)}, f32[256]{0:T(256)S(1)}, u32[]{:S(2)}, u32[]{:S(2)}) collective-permute-start(f32[256]{0:T(256)S(1)} %bitcast.73), channel_id=1, source_target_pairs={{0,15},{1,8},{2,9},{3,10},{4,11},{5,12},{6,13},{7,14},{8,23},{9,16... | collective-permute-start | bytes 3080 | tf_op jit(solution)/shard_map/ppermute | solution.py:96
  9.2 7.2 %collective-permute-start.7 = (f32[256]{0:T(256)S(1)}, f32[256]{0:T(256)S(1)}, u32[]{:S(2)}, u32[]{:S(2)}) collective-permute-start(f32[256]{0:T(256)S(1)} %bitcast.70), channel_id=1, source_target_pairs={{0,31},{1,24},{2,25},{3,26},{4,27},{5,28},{6,29},{7,30},{8,7},{9,0... | collective-permute-start | bytes 3080 | tf_op jit(solution)/shard_map/ppermute | solution.py:96
  11.3 5.2 %collective-permute-start = (f32[16,256]{1,0:T(8,128)S(1)}, f32[16,256]{1,0:T(8,128)S(1)}, u32[]{:S(2)}, u32[]{:S(2)}) collective-permute-start(f32[16,256]{1,0:T(8,128)S(1)} %get-tuple-element.26), channel_id=1, source_target_pairs={{0,8},{1,9},{2,10},{3,11},{4,12},{5,13},{6,14},{7,15},{8,16},{9,17... | collective-permute-start | bytes 49160 | tf_op jit(solution)/shard_map/ppermute | solution.py:96
  12.4 4.1 %collective-permute-start.1 = (f32[16,256]{1,0:T(8,128)S(1)}, f32[16,256]{1,0:T(8,128)S(1)}, u32[]{:S(2)}, u32[]{:S(2)}) collective-permute-start(f32[16,256]{1,0:T(8,128)S(1)} %get-tuple-element.27), channel_id=1, source_target_pairs={{0,24},{1,25},{2,26},{3,27},{4,28},{5,29},{6,30},{7,31},{8,0},{9,1... | collective-permute-start | bytes 49160 | tf_op jit(solution)/shard_map/ppermute | solution.py:96
  14.2 3.9 %collective-permute-start.3 = (f32[32,256]{1,0:T(8,128)S(1)}, f32[32,256]{1,0:T(8,128)S(1)}, u32[]{:S(2)}, u32[]{:S(2)}) collective-permute-start(f32[32,256]{1,0:T(8,128)S(1)} %bitcast.64), channel_id=1, source_target_pairs={{0,7},{1,0},{2,1},{3,2},{4,3},{5,4},{6,5},{7,6},{8,15},{9,8},{10,9... | collective-permute-start | bytes 98312 | tf_op jit(solution)/shard_map/ppermute | solution.py:96
  16.4 6.6 %collective-permute-start.2 = (f32[32,256]{1,0:T(8,128)S(1)}, f32[32,256]{1,0:T(8,128)S(1)}, u32[]{:S(2)}, u32[]{:S(2)}) collective-permute-start(f32[32,256]{1,0:T(8,128)S(1)} %bitcast.63), channel_id=1, source_target_pairs={{0,1},{1,2},{2,3},{3,4},{4,5},{5,6},{6,7},{7,0},{8,9},{9,10},{10,1... | collective-permute-start | bytes 98312 | tf_op jit(solution)/shard_map/ppermute | solution.py:96
  23.1 1.0 copy-start
  24.1 0.9 copy-start.2
  25.0 0.9 copy-start.4
  30.3 19.0 %all-to-all-start = ((f32[32,8,512]{2,1,0:T(8,128)}), f32[32,8,512]{2,1,0:T(8,128)S(1)}, u32[]{:S(2)}, u32[]{:S(2)}) async-start(f32[32,8,512]{2,1,0:T(8,128)} %bitcast.17), calls=%async_computation | async-start | bytes 1048576 | tf_op jit(solution)/shard_map/all_to_all | solution.py:513
  32.9 24.4 %copy-start.6 = (s32[1,1,256,1]{2,3,1,0:T(1,128)S(1)}, s32[1,1,256,1]{2,3,1,0:T(1,128)}, u32[]{:S(2)}) copy-start(s32[1,1,256,1]{2,3,1,0:T(1,128)} %param.14) | copy-start | bytes 3076
  32.9 24.5 %copy-start.7 = (s32[1,1,256]{2,1,0:T(1,128)S(1)}, s32[1,1,256]{2,1,0:T(1,128)}, u32[]{:S(2)}) copy-start(s32[1,1,256]{2,1,0:T(1,128)} %param.15) | copy-start | bytes 3076
  49.3 29.7 %copy-start.1 = (f32[32,16,256]{2,1,0:T(8,128)S(1)}, f32[32,16,256]{2,1,0:T(8,128)}, u32[]{:S(2)}) copy-start(f32[32,16,256]{2,1,0:T(8,128)} %core.3) | copy-start | bytes 1572868
  49.3 29.7 %copy-start.3 = (bf16[256,256]{1,0:T(8,128)(2,1)S(1)}, bf16[256,256]{1,0:T(8,128)(2,1)}, u32[]{:S(2)}) copy-start(bf16[256,256]{1,0:T(8,128)(2,1)} %constant.27.clone.low) | copy-start | bytes 393220
  49.3 29.7 %copy-start.5 = (bf16[256,256]{1,0:T(8,128)(2,1)S(1)}, bf16[256,256]{1,0:T(8,128)(2,1)}, u32[]{:S(2)}) copy-start(bf16[256,256]{1,0:T(8,128)(2,1)} %constant.26.clone.high) | copy-start | bytes 393220
  54.7 21.8 %all-to-all-start.1 = ((f32[32,8,640]{2,1,0:T(8,128)}), f32[32,8,640]{2,1,0:T(8,128)S(1)}, u32[]{:S(2)}, u32[]{:S(2)}) async-start(f32[32,8,640]{2,1,0:T(8,128)} %shard_map.141), calls=%async_computation.1 | async-start | bytes 1310720 | tf_op jit(solution)/shard_map/all_to_all | solution.py:513
  76.5 9.6 %all-to-all-start.3 = ((s32[32,1,16]{2,1,0:T(1,128)}), s32[32,1,16]{2,1,0:T(1,128)S(1)}, u32[]{:S(2)}, u32[]{:S(2)}) async-start(s32[32,1,16]{2,1,0:T(1,128)} %copy.27), calls=%async_computation.3 | async-start | bytes 32768 | tf_op jit(solution)/shard_map/all_to_all | solution.py:513
  113.5 27.4 %all-to-all-start.2 = ((f32[32,8,896]{2,1,0:T(8,128)}), f32[32,8,896]{2,1,0:T(8,128)S(1)}, u32[]{:S(2)}, u32[]{:S(2)}) async-start(f32[32,8,896]{2,1,0:T(8,128)} %bitcast.22), calls=%async_computation.2 | async-start | bytes 1835008 | tf_op jit(solution)/shard_map/all_to_all | solution.py:513
  153.0 25.2 %collective-permute-start.9 = (f32[2,16,256]{2,1,0:T(8,128)S(1)}, f32[2,16,256]{2,1,0:T(8,128)S(1)}, u32[]{:S(2)}, u32[]{:S(2)}) collective-permute-start(f32[2,16,256]{2,1,0:T(8,128)S(1)} %get-tuple-element.30), channel_id=1, source_target_pairs={{0,24},{1,25},{2,26},{3,27},{4,28},{5,29},{6,30},{7,31},{8,0},{9,1... | collective-permute-start | bytes 98312 | tf_op jit(solution)/shard_map/ppermute | solution.py:96
  153.5 24.7 %collective-permute-start.8 = (f32[2,16,256]{2,1,0:T(8,128)S(1)}, f32[2,16,256]{2,1,0:T(8,128)S(1)}, u32[]{:S(2)}, u32[]{:S(2)}) collective-permute-start(f32[2,16,256]{2,1,0:T(8,128)S(1)} %get-tuple-element.31), channel_id=1, source_target_pairs={{0,8},{1,9},{2,10},{3,11},{4,12},{5,13},{6,14},{7,15},{8,16},{9,17... | collective-permute-start | bytes 98312 | tf_op jit(solution)/shard_map/ppermute | solution.py:96
  153.5 24.6 %collective-permute-start.11 = (f32[32,2,256]{2,1,0:T(2,128)S(1)}, f32[32,2,256]{2,1,0:T(2,128)S(1)}, u32[]{:S(2)}, u32[]{:S(2)}) collective-permute-start(f32[32,2,256]{2,1,0:T(2,128)S(1)} %get-tuple-element.28), channel_id=1, source_target_pairs={{0,7},{1,0},{2,1},{3,2},{4,3},{5,4},{6,5},{7,6},{8,15},{9,8},{10,9... | collective-permute-start | bytes 196616 | tf_op jit(solution)/shard_map/ppermute | solution.py:96
  155.0 23.2 %collective-permute-start.10 = (f32[32,2,256]{2,1,0:T(2,128)S(1)}, f32[32,2,256]{2,1,0:T(2,128)S(1)}, u32[]{:S(2)}, u32[]{:S(2)}) collective-permute-start(f32[32,2,256]{2,1,0:T(2,128)S(1)} %get-tuple-element.29), channel_id=1, source_target_pairs={{0,1},{1,2},{2,3},{3,4},{4,5},{5,6},{6,7},{7,0},{8,9},{9,10},{10,1... | collective-permute-start | bytes 196616 | tf_op jit(solution)/shard_map/ppermute | solution.py:96
  155.6 5.6 %collective-permute-start.15 = (f32[2,2,256]{2,1,0:T(2,128)S(1)}, f32[2,2,256]{2,1,0:T(2,128)S(1)}, u32[]{:S(2)}, u32[]{:S(2)}) collective-permute-start(f32[2,2,256]{2,1,0:T(2,128)S(1)} %get-tuple-element.32), channel_id=1, source_target_pairs={{0,31},{1,24},{2,25},{3,26},{4,27},{5,28},{6,29},{7,30},{8,7},{9,0... | collective-permute-start | bytes 12296 | tf_op jit(solution)/shard_map/ppermute | solution.py:96
  161.2 6.3 %collective-permute-start.14 = (f32[2,2,256]{2,1,0:T(2,128)S(1)}, f32[2,2,256]{2,1,0:T(2,128)S(1)}, u32[]{:S(2)}, u32[]{:S(2)}) collective-permute-start(f32[2,2,256]{2,1,0:T(2,128)S(1)} %get-tuple-element.33), channel_id=1, source_target_pairs={{0,25},{1,26},{2,27},{3,28},{4,29},{5,30},{6,31},{7,24},{8,1},{9,2... | collective-permute-start | bytes 12296 | tf_op jit(solution)/shard_map/ppermute | solution.py:96
  167.6 4.0 %collective-permute-start.13 = (f32[2,2,256]{2,1,0:T(2,128)S(1)}, f32[2,2,256]{2,1,0:T(2,128)S(1)}, u32[]{:S(2)}, u32[]{:S(2)}) collective-permute-start(f32[2,2,256]{2,1,0:T(2,128)S(1)} %get-tuple-element.34), channel_id=1, source_target_pairs={{0,15},{1,8},{2,9},{3,10},{4,11},{5,12},{6,13},{7,14},{8,23},{9,16... | collective-permute-start | bytes 12296 | tf_op jit(solution)/shard_map/ppermute | solution.py:96
  171.5 6.6 %collective-permute-start.12 = (f32[2,2,256]{2,1,0:T(2,128)S(1)}, f32[2,2,256]{2,1,0:T(2,128)S(1)}, u32[]{:S(2)}, u32[]{:S(2)}) collective-permute-start(f32[2,2,256]{2,1,0:T(2,128)S(1)} %get-tuple-element.35), channel_id=1, source_target_pairs={{0,9},{1,10},{2,11},{3,12},{4,13},{5,14},{6,15},{7,8},{8,17},{9,18... | collective-permute-start | bytes 12296 | tf_op jit(solution)/shard_map/ppermute | solution.py:96

commit v2 on v1

--- a/solution.py
+++ b/solution.py
@@ -87,31 +87,27 @@
     return jax.ShapeDtypeStruct(dims, dtype)
 
 
-def send(x, dx, dy):
-    size_x, size_y = lax.axis_size("px"), lax.axis_size("py")
-    pairs = []
-    for i in range(size_x):
-        for j in range(size_y):
-            pairs.append((i * size_y + j, ((i + dx) % size_x) * size_y + (j + dy) % size_y))
-    return lax.ppermute(x, ("px", "py"), pairs)
-
-
-def slot_kernel(half, owner_col, owner_row, window_row, slot_out, label_out):
+def send(x, axis, step):
+    size = lax.axis_size(axis)
+    return lax.ppermute(x, axis, [(i, (i + step) % size) for i in range(size)])
+
+
+def slot_kernel(half, start, owner_col, owner_row, window_row, slot_out, label_out):
     count = owner_row.shape[1]
+    tiles = label_out.shape[0]
     later = lax.broadcasted_iota(jnp.int32, (count, count), 0) < lax.broadcasted_iota(
         jnp.int32, (count, count), 1
     )
-    same = (owner_col[...] == owner_row[...]) & later
+    owners = owner_row[...]
+    same = (owner_col[...] == owners) & later
     rank = jnp.sum(same.astype(F32), axis=0, keepdims=True).astype(jnp.int32)
     second = rank >= half
-    place = owner_row[...] * half + jnp.where(second, rank - half, rank)
+    place = owners * half + jnp.where(second, rank - half, rank)
     slot_out[...] = jnp.where(second, place + count, place)
-    named = jnp.broadcast_to((window_row[...] + 1).astype(BF16), (8, count))
-    where_row = slot_out[...]
-    for part in range(2):
-        rows = lax.broadcasted_iota(jnp.int32, (count, count), 0) + part * count
-        chosen = (where_row == rows).astype(BF16)
-        label_out[part : part + 1, :] = dot(named, chosen, NT)[0:1, :].astype(jnp.int32) - 1
+    tile = lax.broadcasted_iota(jnp.int32, (tiles, count), 0)
+    named = jnp.where(tile == owners, window_row[...] + 1, 0).astype(F32).astype(BF16)
+    lane = lax.broadcasted_iota(jnp.int32, (LANES, count), 0)
+    label_out[...] = dot(named, (lane == rank + start).astype(BF16), NT) - 1.0
 
 
 def pad_tile(pad, core, x_faces, y_faces):
@@ -120,17 +116,17 @@
     pad[0, 8 : rows_y + 8, :] = x_faces[0]
     pad[rows_x + 1, 8 : rows_y + 8, :] = x_faces[1]
     for x in range(rows_x):
-        pad[x + 1, 7:8, :] = y_faces[0, x : x + 1, :]
-        pad[x + 1, rows_y + 8 : rows_y + 9, :] = y_faces[1, x : x + 1, :]
-
-
-def source_kernel(core, x_faces, y_faces, corners, high, low, spectrum, pad, source):
+        pad[x + 1, 7:8, :] = y_faces[0, x + 1 : x + 2, :]
+        pad[x + 1, rows_y + 8 : rows_y + 9, :] = y_faces[1, x + 1 : x + 2, :]
+
+
+def source_kernel(core, x_faces, y_faces, high, low, spectrum, pad, source):
     rows_x, rows_y, cells_z = core.shape
     pad_tile(pad, core, x_faces, y_faces)
     for side in range(2):
         edge = side * (rows_x + 1)
-        pad[edge, 7:8, :] = corners[2 * side : 2 * side + 1, :]
-        pad[edge, rows_y + 8 : rows_y + 9, :] = corners[2 * side + 1 : 2 * side + 2, :]
+        pad[edge, 7:8, :] = y_faces[0, edge : edge + 1, :]
+        pad[edge, rows_y + 8 : rows_y + 9, :] = y_faces[1, edge : edge + 1, :]
 
     def ahead(value):
         return pltpu.roll(value, cells_z - 1, 1)
@@ -160,7 +156,7 @@
 
 def solve_kernel(
     tiles_x, tiles_y, rows_x, rows_y, scale,
-    first, lap_z, slab, lap_xy, hx_high, hx_low, hy_high, hy_low, hf_high, hf_low,
+    first, lap_z, slab, labels, lap_xy, hx_high, hx_low, hy_high, hy_low, hf_high, hf_low,
     out, planes, faces,
 ):
     grid_x, grid_y = tiles_x * rows_x, tiles_y * rows_y
@@ -217,10 +213,12 @@
                     move = (start - i * rows_x) % LANES
                     face = pltpu.roll(face, move, 1) if move else face
                     line = jnp.where(lane < start, line, face)
+                at = i * tiles_y + j
+                line = jnp.where(lane < 2 * (rows_x + rows_y), line, labels[at : at + 1, :])
                 out[i * tiles_y + j, :, rows_x * rows_y : rows_x * rows_y + LANES] = line
 
 
-def solve_plain(slab, rows_x, rows_y, cells_z, tiles_x, tiles_y, scale):
+def solve_plain(slab, labels, rows_x, rows_y, cells_z, tiles_x, tiles_y, scale):
     high = lax.Precision.HIGHEST
     grid_x, grid_y = tiles_x * rows_x, tiles_y * rows_y
     count = slab.shape[1]
@@ -247,15 +245,15 @@
     for edge in (-1, rows_y):
         line = back[:, :, (starts_y + edge) % grid_y].reshape(count, tiles_x, rows_x, tiles_y)
         faces.append(line.transpose(1, 3, 0, 2))
-    used = rows_x * rows_y + 2 * (rows_x + rows_y)
-    faces.append(jnp.zeros((tiles_x, tiles_y, count, -used % LANES), F32))
+    tail = labels[:, 2 * (rows_x + rows_y) :].reshape(tiles_x, tiles_y, 1, -1)
+    faces.append(jnp.broadcast_to(tail, (tiles_x, tiles_y, count, tail.shape[-1])))
     parts = [tiles.reshape(tiles_x, tiles_y, count, rows_x * rows_y)] + faces
     return jnp.concatenate(parts, -1).reshape(tiles_x * tiles_y, count, -1)
 
 
 def block_kernel(
-    core, x_faces, y_faces, spectrum, high, low, slots,
-    displacement, first_half, second_half,
+    planes, half, core, x_faces, y_faces, spectrum, high, low, slots,
+    displacement, first_half, second_half, labels,
     pad, cells, spread, values,
 ):
     rows_x, rows_y, cells_z = core.shape
@@ -265,11 +263,12 @@
     cells[...] = dot3(split(spectrum[...], 2), (high[...], low[...]), TN)
     cells[0:inner, :] = cells[0:inner, :] + core[...].reshape(inner, cells_z)
     start = inner
-    for faces in (x_faces, y_faces):
+    for faces, skip in ((x_faces, 0), (y_faces, 1)):
         for side in range(2):
-            rows = slice(start, start + faces.shape[1])
-            cells[rows, :] = cells[rows, :] + faces[side]
-            start += faces.shape[1]
+            length = faces.shape[1] - 2 * skip
+            rows = slice(start, start + length)
+            cells[rows, :] = cells[rows, :] + faces[side, skip : skip + length, :]
+            start += length
     x_edge = [inner, inner + rows_y]
     y_edge = [inner + 2 * rows_y, inner + 2 * rows_y + rows_x]
 
@@ -338,6 +337,17 @@
         put(lambda e, side=side: 768 + side * 64 + e * 8 if 0 <= e < 8 else None, tile)
 
     count = slots.shape[1]
+    named = spectrum[:, inner : inner + LANES].astype(BF16)
+    row = lax.broadcasted_iota(jnp.int32, (cells_z, count), 0)
+    slot = lax.broadcasted_iota(jnp.int32, (cells_z, count), 1)
+    source = (row % planes == 0) & (row // planes == slot // half)
+    by_lane = dot(named, source.astype(BF16), TN)
+    lane = lax.broadcasted_iota(jnp.int32, (LANES, count), 0) - 2 * (rows_x + rows_y)
+    place = lax.broadcasted_iota(jnp.int32, (LANES, count), 1) % half
+    for part in range(2):
+        label = jnp.sum(jnp.where(lane == place + part * half, by_lane, 0.0), axis=0, keepdims=True)
+        labels[part] = label.astype(jnp.int32)
+
     pieces = split(values[...], 3)
     for part, out in enumerate((first_half, second_half)):
         rows = lax.broadcasted_iota(jnp.int32, (count, count), 0) + part * count
@@ -366,7 +376,7 @@
 
 def deposit_kernel(blocks_x, blocks_y, blocks_z, last, blocks, labels, *refs):
     if last:
-        before, core, x_rims, y_rims, corners, turned, weights, high, low, grouped, tile = refs
+        before, core, x_rims, y_rims, turned, weights, high, low, grouped, tile = refs
     else:
         core, turned, weights, high, low, grouped, tile = refs
     slots = blocks.shape[0]
@@ -476,24 +486,25 @@
         x = side * (rows_x + 2)
         y = side * (rows_y + 2)
         x_rims[side] = tile[x : x + 2, 2 : rows_y + 2, :]
-        y_rims[side] = tile[2 : rows_x + 2, y : y + 2, :]
-        for other in range(2):
-            y = other * (rows_y + 2)
-            corners[side * 2 + other] = tile[x : x + 2, y : y + 2, :]
-
-
-def rim_kernel(core, x_low, x_top, y_low, y_top, c_low_low, c_low_top, c_top_low, c_top_top, out):
+        y_rims[side] = tile[:, y : y + 2, :]
+
+
+def corner_kernel(x_rims, y_low, y_top, out):
+    rows_x, rows_y = y_low.shape[0] - 4, x_rims.shape[2]
+    for side in range(2):
+        x = side * (rows_x + 2)
+        out[side] = x_rims[side]
+        out[side, :, 0:2, :] = out[side, :, 0:2, :] + y_low[x : x + 2]
+        out[side, :, rows_y - 2 :, :] = out[side, :, rows_y - 2 :, :] + y_top[x : x + 2]
+
+
+def rim_kernel(core, y_low, y_top, x_low, x_top, out):
     rows_x, rows_y, _ = core.shape
     out[...] = core[...]
-    xs, ys = (slice(0, 2), slice(rows_x - 2, rows_x)), (slice(0, 2), slice(rows_y - 2, rows_y))
-    for part, face in zip(xs, (x_low, x_top)):
+    for part, face in ((slice(0, 2), y_low), (slice(rows_y - 2, rows_y), y_top)):
+        out[:, part, :] = out[:, part, :] + face[2 : rows_x + 2]
+    for part, face in ((slice(0, 2), x_low), (slice(rows_x - 2, rows_x), x_top)):
         out[part] = out[part] + face[...]
-    for part, face in zip(ys, (y_low, y_top)):
-        out[:, part, :] = out[:, part, :] + face[...]
-    for x, y, face in (
-        (0, 0, c_low_low), (0, 1, c_low_top), (1, 0, c_top_low), (1, 1, c_top_top),
-    ):
-        out[xs[x], ys[y], :] = out[xs[x], ys[y], :] + face[...]
 
 
 def per_device(potential, owner, window):
@@ -513,29 +524,25 @@
         return lax.all_to_all(x, both, split_axis=0, concat_axis=0, tiled=True)
 
     slots, labels = call(
-        functools.partial(slot_kernel, half),
-        (shape(1, blocks, dtype=jnp.int32), shape(2, blocks, dtype=jnp.int32)),
-        [], 16, 4 * blocks**3, 8 * blocks,
+        functools.partial(slot_kernel, half, 2 * (rows_x + rows_y)),
+        (shape(1, blocks, dtype=jnp.int32), shape(tiles, LANES)),
+        [], 16, 2 * tiles * LANES * blocks, 8 * blocks,
     )(owner.reshape(blocks, 1), owner.reshape(1, blocks), window.reshape(1, blocks))
-    arrived_labels = exchange(labels.reshape(2, tiles, half).transpose(1, 0, 2).reshape(tiles, 2 * half))
-    arrived_labels = arrived_labels.reshape(tiles, 2, half).transpose(1, 0, 2).reshape(2, 1, blocks)
 
     last_x, last_y = rows_x - 1, rows_y - 1
-    x_faces = jnp.stack([send(potential[last_x], 1, 0), send(potential[0], -1, 0)])
-    y_faces = jnp.stack([send(potential[:, last_y], 0, 1), send(potential[:, 0], 0, -1)])
-    corners = jnp.stack(
-        [
-            send(potential[last_x, last_y], 1, 1), send(potential[last_x, 0], 1, -1),
-            send(potential[0, last_y], -1, 1), send(potential[0, 0], -1, -1),
-        ]
-    )
+    x_faces = jnp.stack([send(potential[last_x], "px", 1), send(potential[0], "px", -1)])
+    y_lines = [
+        jnp.concatenate([x_faces[0, y : y + 1], potential[:, y], x_faces[1, y : y + 1]])
+        for y in (last_y, 0)
+    ]
+    y_faces = jnp.stack([send(y_lines[0], "py", 1), send(y_lines[1], "py", -1)])
 
     z_high, z_low = pieces_of(table_of(cells_z))
     spectrum = call(
         source_kernel, shape(cells_z, inner),
         [pltpu.VMEM((rows_x + 2, rows_y + 16, cells_z), F32), pltpu.VMEM((inner, cells_z), F32)],
         24, 6 * inner * cells_z**2, 2 << 20,
-    )(potential, x_faces, y_faces, corners, z_high, z_low)
+    )(potential, x_faces, y_faces, z_high, z_low)
     slab = exchange(spectrum).reshape(tiles, planes, inner)
 
     scale = SECOND_ORDER / (grid_x * grid_y * cells_z)
@@ -547,7 +554,7 @@
         lap_xy = laplace_of(grid_x)[:, None] + laplace_of(grid_y)[None, :]
         tables = pieces_of(x_table) + pieces_of(y_table) + pieces_of(y_table[edge])
         body = functools.partial(solve_kernel, tiles_x, tiles_y, rows_x, rows_y, scale)
-        specs = [SMEM, SMEM] + [VMEM] * 8
+        specs = [SMEM, SMEM] + [VMEM] * 9
         returned = pl.pallas_call(
             body,
             out_shape=shape(tiles, planes, used),
@@ -561,16 +568,19 @@
             cost_estimate=pl.CostEstimate(
                 flops=24 * planes * grid_x**2 * grid_y, bytes_accessed=2 << 20, transcendentals=0
             ),
-        )(first, laplace_of(cells_z), slab, lap_xy, *tables)
+        )(first, laplace_of(cells_z), slab, labels, lap_xy, *tables)
     else:
-        returned = solve_plain(slab, rows_x, rows_y, cells_z, tiles_x, tiles_y, scale)
+        returned = solve_plain(slab, labels, rows_x, rows_y, cells_z, tiles_x, tiles_y, scale)
     modes = exchange(returned.reshape(cells_z, used))
 
     pad = pltpu.VMEM((rows_x, rows_y + 16, cells_z), F32)
     width = -(-10 * blocks_z // LANES) * LANES
-    displacement, *sent = call(
-        block_kernel,
-        (shape(3, rows_x, rows_y, cells_z), shape(blocks, ROWS), shape(blocks, ROWS)),
+    displacement, *sent, arrived_labels = call(
+        functools.partial(block_kernel, planes, half),
+        (
+            shape(3, rows_x, rows_y, cells_z), shape(blocks, ROWS), shape(blocks, ROWS),
+            shape(2, 1, blocks, dtype=jnp.int32),
+        ),
         [pad, pltpu.VMEM((used, cells_z), F32), pltpu.VMEM((width // LANES, used, LANES), F32), pltpu.VMEM((ROWS, blocks), F32)],
         40, 20 * used * cells_z**2, 6 << 20,
     )(potential, x_faces, y_faces, modes, z_high, z_low, slots)
@@ -590,20 +600,22 @@
     tile = call(
         functools.partial(deposit_kernel, *sizes, False), shape(*tile_shape), scratch, 40, *cost
     )(arrived[0], arrived_labels[0])
-    core, x_rims, y_rims, edges = call(
+    core, x_rims, y_rims = call(
         functools.partial(deposit_kernel, *sizes, True),
         (
             shape(rows_x, rows_y, cells_z), shape(2, 2, rows_y, cells_z),
-            shape(2, rows_x, 2, cells_z), shape(4, 2, 2, cells_z),
+            shape(2, rows_x + 4, 2, cells_z),
         ),
         scratch, 40, *cost,
     )(arrived[1], arrived_labels[1], tile)
 
+    y_sides = send(y_rims[1], "py", 1), send(y_rims[0], "py", -1)
+    x_rims = call(corner_kernel, shape(*x_rims.shape), [], 16, 8 * rows_y * cells_z, 1 << 17)(
+        x_rims, *y_sides
+    )
+    x_sides = send(x_rims[1], "px", 1), send(x_rims[0], "px", -1)
     density = call(rim_kernel, shape(rows_x, rows_y, cells_z), [], 16, inner * cells_z, 2 << 20)(
-        core,
-        send(x_rims[1], 1, 0), send(x_rims[0], -1, 0),
-        send(y_rims[1], 0, 1), send(y_rims[0], 0, -1),
-        send(edges[3], 1, 1), send(edges[2], 1, -1), send(edges[1], -1, 1), send(edges[0], -1, -1),
+        core, *y_sides, *x_sides
     )
     return (displacement, density)
 

time: 180 us -> 153 us (0.85)
  waiting for transfers between devices: 70.3 us -> 44.9 us
  blocking collectives: 27.4 us -> 48 us
  starting transfers between devices: 34.5 us -> 15.9 us
  local copies, waits for them, and re-layouts: 6.95 us -> 4.89 us
    all_to_all x4 -> x2, waiting for transfers between devices: 49.3 us -> 28.5 us  [exchange(): return lax.all_to_all(x, both, split_axis=0, concat_axis=0, tiled=True)]
    all_to_all x1 -> x2, blocking collectives: 27.4 us -> 48 us  [exchange(): return lax.all_to_all(x, both, split_axis=0, concat_axis=0, tiled=True)]
    ppermute x16 -> x8, starting transfers between devices: 23.9 us -> 10.5 us  [send(): return lax.ppermute(x, axis, [(i, (i + step) % size) for i in range(size)])]
    all_to_all x4 -> x2, starting transfers between devices: 10.6 us -> 5.42 us  [exchange(): return lax.all_to_all(x, both, split_axis=0, concat_axis=0, tiled=True)]
    ppermute x16 -> x8, waiting for transfers between devices: 21 us -> 16.4 us  [send(): return lax.ppermute(x, axis, [(i, (i + step) % size) for i in range(size)])]
    pallas_call x2 -> x3, Pallas kernels: 4.33 us -> 4.3 us  [the longest x1 4.04 us: per_device(): call(functools.partial(block_kernel, planes, half), (shape(3, rows_x, row...]
  transfers between devices with their start and end apart: 20 -> 10, of which waited for: 10 -> 10; matrix products, arithmetic and copies ran while one was open for 2% -> 1% of each run, Pallas kernels for 9% -> 8%
where the time goes in v2:
time: 153 us
  blocking collectives  48 us (31%)
  waiting for transfers between devices  44.9 us (29%)
  Pallas kernels  38.1 us (25%)
  starting transfers between devices  15.9 us (10%)
  local copies, waits for them, and re-layouts  4.89 us (3%)
    all_to_all x2, blocking collectives, exchange(): return lax.all_to_all(x, both, split_axis=0, concat_axis=0, tiled=True)  48 us
    all_to_all x2, waiting for transfers between devices, exchange(): return lax.all_to_all(x, both, split_axis=0, concat_axis=0, tiled=True)  28.5 us
    ppermute x8, waiting for transfers between devices, send(): return lax.ppermute(x, axis, [(i, (i + step) % size) for i in range(size)])  16.4 us
    pallas_call x1, Pallas kernels, per_device(): call(functools.partial(deposit_kernel, *sizes, True), (shape(rows_x, rows...  12 us
    pallas_call x1, Pallas kernels, per_device(): call(functools.partial(deposit_kernel, *sizes, False), shape(*tile_shape)...  12 us
    ppermute x8, starting transfers between devices, send(): return lax.ppermute(x, axis, [(i, (i + step) % size) for i in range(size)])  10.5 us
    all_to_all x2, starting transfers between devices, exchange(): return lax.all_to_all(x, both, split_axis=0, concat_axis=0, tiled=True)  5.42 us
    pallas_call x1, Pallas kernels, per_device(): pl.pallas_call(body, out_shape=shape(tiles, planes, used), in_specs=specs...  4.49 us
  transfers between devices with their start and end apart: 10, of which 10 were waited for; matrix products, arithmetic and copies ran while one was open for 1% of the time, Pallas kernels for 8%

profile of v2, /device:TPU:0, one launch (start us, length us, event | category | flops | bytes accessed | tf_op | source)
XLA Modules:
  0.0 152.7 jit_solution(8426857819258086526)
XLA Ops:
  0.6 0.7 slice_bitcast_fusion.5
  1.4 0.5 collective-permute-start
  1.8 0.0 copy-start.6
  1.8 2.0 %collective-permute-start.1 = (f32[16,256]{1,0:T(8,128)S(1)}, f32[16,256]{1,0:T(8,128)S(1)}, u32[]{:S(2)}, u32[]{:S(2)}) collective-permute-start(f32[16,256]{1,0:T(8,128)S(1)} %get-tuple-element.23), channel_id=1, source_target_pairs={{0,24},{8,0},{16,8},{24,16},{1,25},{9,1},{17,9},{25,17},{2,26},{10... | collective-permute-start | bytes 49160 | tf_op jit(solution)/shard_map/ppermute | solution.py:92
  3.8 1.1 fusion
  4.9 0.0 copy-start.7
  4.9 0.3 collective-permute-done
  5.2 0.1 collective-permute-done.1
  5.2 0.0 copy-start.8
  5.3 0.0 copy-start.9
  5.3 0.0 copy-start.10
  5.3 0.0 copy-start.11
  5.3 0.0 copy-start.12
  5.3 0.0 copy-start.13
  5.3 5.4 %collective-permute-start.3 = (f32[34,256]{1,0:T(8,128)S(1)}, f32[34,256]{1,0:T(8,128)S(1)}, u32[]{:S(2)}, u32[]{:S(2)}) collective-permute-start(f32[34,256]{1,0:T(8,128)S(1)} %pad_maximum_fusion.2), channel_id=1, source_target_pairs={{0,7},{1,0},{2,1},{3,2},{4,3},{5,4},{6,5},{7,6},{8,15},{9,8},{10,9... | collective-permute-start | bytes 104456 | tf_op jit(solution)/shard_map/ppermute | solution.py:92
  10.7 0.1 collective-permute-start.2
  10.8 1.6 %collective-permute-done.3 = f32[34,256]{1,0:T(8,128)S(1)} collective-permute-done((f32[34,256]{1,0:T(8,128)S(1)}, f32[34,256]{1,0:T(8,128)S(1)}, u32[]{:S(2)}, u32[]{:S(2)}) %collective-permute-start.3) | collective-permute-done | bytes 34848 | tf_op jit(solution)/shard_map/ppermute | solution.py:92
  12.4 5.2 %collective-permute-done.2 = f32[34,256]{1,0:T(8,128)S(1)} collective-permute-done((f32[34,256]{1,0:T(8,128)S(1)}, f32[34,256]{1,0:T(8,128)S(1)}, u32[]{:S(2)}, u32[]{:S(2)}) %collective-permute-start.2) | collective-permute-done | bytes 34848 | tf_op jit(solution)/shard_map/ppermute | solution.py:92
  17.6 0.0 copy-start
  17.6 1.0 copy-done
  18.6 0.0 copy-start.2
  18.6 0.9 copy-done.2
  19.5 0.0 copy-start.4
  19.5 0.9 copy-done.4
  20.4 4.4 %shard_map.140 = f32[256,512]{1,0:T(8,128)} custom-call(f32[32,16,256]{2,1,0:T(8,128)S(1)} %copy-done, f32[2,16,256]{2,1,0:T(8,128)S(1)} %pad_maximum_fusion.3.x_faces, f32[2,34,256]{2,1,0:T(8,128)S(1)} %pad_maximum_fusion.y_faces, bf16[256,256]{1,0:T(8,128)(2,1)S(1)} %copy-done.4, bf16[256,256]{1,0:T(8,128)(2,1)S(1)} %copy-done.2), custom_call_target="tpu_custom_call" | custom-call | flops 201326592 | bytes 2097152 | tf_op jit(solution)/shard_map/pallas_call | solution.py:541
  24.8 2.6 %all-to-all-start = ((f32[32,8,512]{2,1,0:T(8,128)}), f32[32,8,512]{2,1,0:T(8,128)S(1)}, u32[]{:S(2)}, u32[]{:S(2)}) async-start(f32[32,8,512]{2,1,0:T(8,128)} %bitcast.13), calls=%async_computation | async-start | bytes 1048576 | tf_op jit(solution)/shard_map/all_to_all | solution.py:524
  27.5 0.0 copy-start.1
  27.5 0.0 copy-start.3
  27.5 0.0 copy-start.5
  27.5 0.0 copy-done.6
  27.5 0.1 copy.19.owner_col
  27.6 0.0 copy-done.7
  27.7 0.2 shard_map.141
  27.9 15.9 %all-to-all-done.slab = f32[32,8,512]{2,1,0:T(8,128)S(1)} async-done(((f32[32,8,512]{2,1,0:T(8,128)}), f32[32,8,512]{2,1,0:T(8,128)S(1)}, u32[]{:S(2)}, u32[]{:S(2)}) %all-to-all-start) | async-done | bytes 524320 | tf_op jit(solution)/shard_map/all_to_all | solution.py:524
  43.8 0.0 copy-done.8
  43.8 0.0 copy-done.9
  43.8 0.0 copy-done.10
  43.8 0.0 copy-done.11
  43.8 0.0 copy-done.12
  43.8 0.0 copy-done.13
  43.8 4.5 %shard_map.142 = f32[32,8,640]{2,1,0:T(8,128)S(1)} custom-call(s32[1]{0:T(128)} %bitcast.12.first, f32[256]{0:T(256)S(1)} %copy-done.13, f32[32,8,512]{2,1,0:T(8,128)S(1)} %all-to-all-done.slab, f32[32,128]{1,0:T(8,128)S(1)} %get-tuple-element.11.labels, f32[128,128]{1,0:T(8,128)S(1)} %copy-done.8, bf16[128,128]{1,0:T(8,128)(2,1)S(1)} %copy-done.10, ...), custom_call_target="tpu_custom_call" | custom-call | flops 402653184 | bytes 2097152 | tf_op jit(solution)/shard_map/pallas_call | solution.py:558
  48.3 21.1 %all_to_all.39 = f32[32,8,640]{2,1,0:T(8,128)S(1)} all-to-all(f32[32,8,640]{2,1,0:T(8,128)S(1)} %shard_map.142), channel_id=1, replica_groups=mesh['px'=4,'py'=8] {'px','py'}, dimensions={0} | all-to-all | bytes 1310720 | tf_op jit(solution)/shard_map/all_to_all | solution.py:524
  69.5 0.0 copy-done.1
  69.5 0.0 copy-done.3
  69.5 0.0 copy-done.5
  69.5 4.0 %shard_map.143 = (f32[3,32,16,256]{3,2,1,0:T(8,128)}, f32[256,896]{1,0:T(8,128)S(1)}, f32[256,896]{1,0:T(8,128)}, s32[2,1,256]{2,1,0:T(1,128)S(1)}) custom-call(f32[32,16,256]{2,1,0:T(8,128)S(1)} %copy-done.1, f32[2,16,256]{2,1,0:T(8,128)S(1)} %pad_maximum_fusion.3.x_faces, f32[2,34,256]{2,1,0:T(8,128)S(1)} %pad_maximum_fusion.y_faces, ...), custom_call_target="tpu_custom_call" | custom-call | flops 838860800 | bytes 6291456 | tf_op jit(solution)/shard_map/pallas_call | solution.py:578
  73.5 26.9 %all_to_all.40 = f32[32,8,896]{2,1,0:T(8,128)S(1)} all-to-all(f32[32,8,896]{2,1,0:T(8,128)S(1)} %bitcast.46), channel_id=1, replica_groups=mesh['px'=4,'py'=8] {'px','py'}, dimensions={0} | all-to-all | bytes 1835008 | tf_op jit(solution)/shard_map/all_to_all | solution.py:524
  100.4 2.8 %all-to-all-start.2 = ((f32[32,8,896]{2,1,0:T(8,128)}), f32[32,8,896]{2,1,0:T(8,128)S(1)}, u32[]{:S(2)}, u32[]{:S(2)}) async-start(f32[32,8,896]{2,1,0:T(8,128)} %bitcast.18), calls=%async_computation.2 | async-start | bytes 1835008 | tf_op jit(solution)/shard_map/all_to_all | solution.py:524
  103.2 12.0 %shard_map.144.refs_0_ = f32[36,24,256]{2,1,0:T(8,128)S(1)} custom-call(f32[256,896]{1,0:T(8,128)S(1)} %bitcast.45, s32[1,256]{1,0:T(1,128)S(1)} %get-tuple-element.32.labels), custom_call_target="tpu_custom_call" | custom-call | flops 39321600 | bytes 4194304 | tf_op jit(solution)/shard_map/pallas_call | solution.py:600
  115.2 12.6 %all-to-all-done.2 = f32[32,8,896]{2,1,0:T(8,128)S(1)} async-done(((f32[32,8,896]{2,1,0:T(8,128)}), f32[32,8,896]{2,1,0:T(8,128)S(1)}, u32[]{:S(2)}, u32[]{:S(2)}) %all-to-all-start.2) | async-done | bytes 917536 | tf_op jit(solution)/shard_map/all_to_all | solution.py:524
  127.8 12.0 %shard_map.145 = (f32[32,16,256]{2,1,0:T(8,128)S(1)}, f32[2,2,16,256]{3,2,1,0:T(8,128)S(1)}, f32[2,36,2,256]{3,2,1,0:T(2,128)S(1)}) custom-call(f32[256,896]{1,0:T(8,128)S(1)} %bitcast.44, s32[1,256]{1,0:T(1,128)S(1)} %get-tuple-element.33.labels, f32[36,24,256]{2,1,0:T(8,128)S(1)} %shard_map.144.refs_0_), custom_call_target="tpu_custom_call" | custom-call | flops 39321600 | bytes 4194304 | tf_op jit(solution)/shard_map/pallas_call | solution.py:603
  139.8 1.4 collective-permute-start.5
  141.3 0.6 collective-permute-start.4
  141.9 2.3 %collective-permute-done.5.y_top = f32[36,2,256]{2,1,0:T(2,128)S(1)} collective-permute-done((f32[36,2,256]{2,1,0:T(2,128)S(1)}, f32[36,2,256]{2,1,0:T(2,128)S(1)}, u32[]{:S(2)}, u32[]{:S(2)}) %collective-permute-start.5) | collective-permute-done | bytes 73760 | tf_op jit(solution)/shard_map/ppermute | solution.py:92
  144.3 4.1 %collective-permute-done.4.y_low = f32[36,2,256]{2,1,0:T(2,128)S(1)} collective-permute-done((f32[36,2,256]{2,1,0:T(2,128)S(1)}, f32[36,2,256]{2,1,0:T(2,128)S(1)}, u32[]{:S(2)}, u32[]{:S(2)}) %collective-permute-start.4) | collective-permute-done | bytes 73760 | tf_op jit(solution)/shard_map/ppermute | solution.py:92
  148.4 0.1 collective-permute-start.7
  148.4 0.5 collective-permute-start.6
  148.9 1.2 collective-permute-done.7.x_top
  150.1 1.7 %collective-permute-done.6.x_low = f32[2,16,256]{2,1,0:T(8,128)S(1)} collective-permute-done((f32[2,16,256]{2,1,0:T(8,128)S(1)}, f32[2,16,256]{2,1,0:T(8,128)S(1)}, u32[]{:S(2)}, u32[]{:S(2)}) %collective-permute-start.6) | collective-permute-done | bytes 32800 | tf_op jit(solution)/shard_map/ppermute | solution.py:92
  151.8 0.9 shard_map.147
  (12 shorter events, 0.1 us)
Async XLA Ops:
  1.4 3.8 %collective-permute-start = (f32[16,256]{1,0:T(8,128)S(1)}, f32[16,256]{1,0:T(8,128)S(1)}, u32[]{:S(2)}, u32[]{:S(2)}) collective-permute-start(f32[16,256]{1,0:T(8,128)S(1)} %get-tuple-element.22), channel_id=1, source_target_pairs={{0,8},{8,16},{16,24},{24,0},{1,9},{9,17},{17,25},{25,1},{2,10},{10... | collective-permute-start | bytes 49160 | tf_op jit(solution)/shard_map/ppermute | solution.py:92
  1.8 25.7 %copy-start.6 = (s32[1,1,256,1]{2,3,1,0:T(1,128)S(1)}, s32[1,1,256,1]{2,3,1,0:T(1,128)}, u32[]{:S(2)}) copy-start(s32[1,1,256,1]{2,3,1,0:T(1,128)} %param.14) | copy-start | bytes 3076
  1.8 3.4 %collective-permute-start.1 = (f32[16,256]{1,0:T(8,128)S(1)}, f32[16,256]{1,0:T(8,128)S(1)}, u32[]{:S(2)}, u32[]{:S(2)}) collective-permute-start(f32[16,256]{1,0:T(8,128)S(1)} %get-tuple-element.23), channel_id=1, source_target_pairs={{0,24},{8,0},{16,8},{24,16},{1,25},{9,1},{17,9},{25,17},{2,26},{10... | collective-permute-start | bytes 49160 | tf_op jit(solution)/shard_map/ppermute | solution.py:92
  4.9 22.8 %copy-start.7 = (s32[1,1,256]{2,1,0:T(1,128)S(1)}, s32[1,1,256]{2,1,0:T(1,128)}, u32[]{:S(2)}) copy-start(s32[1,1,256]{2,1,0:T(1,128)} %param.15) | copy-start | bytes 3076
  5.2 38.6 %copy-start.8 = (f32[128,128]{1,0:T(8,128)S(1)}, f32[128,128]{1,0:T(8,128)}, u32[]{:S(2)}) copy-start(f32[128,128]{1,0:T(8,128)} %constant.29.clone.lap_xy) | copy-start | bytes 196612
  5.3 38.6 %copy-start.9 = (bf16[128,128]{1,0:T(8,128)(2,1)S(1)}, bf16[128,128]{1,0:T(8,128)(2,1)}, u32[]{:S(2)}) copy-start(bf16[128,128]{1,0:T(8,128)(2,1)} %constant.31.clone.hx_low.hy_low) | copy-start | bytes 98308
  5.3 38.6 %copy-start.10 = (bf16[128,128]{1,0:T(8,128)(2,1)S(1)}, bf16[128,128]{1,0:T(8,128)(2,1)}, u32[]{:S(2)}) copy-start(bf16[128,128]{1,0:T(8,128)(2,1)} %constant.30.clone.hx_high.hy_high) | copy-start | bytes 98308
  5.3 38.6 %copy-start.11 = (bf16[16,128]{1,0:T(8,128)(2,1)S(1)}, bf16[16,128]{1,0:T(8,128)(2,1)}, u32[]{:S(2)}) copy-start(bf16[16,128]{1,0:T(8,128)(2,1)} %constant.33.clone.hf_low) | copy-start | bytes 12292
  5.3 38.6 %copy-start.12 = (bf16[16,128]{1,0:T(8,128)(2,1)S(1)}, bf16[16,128]{1,0:T(8,128)(2,1)}, u32[]{:S(2)}) copy-start(bf16[16,128]{1,0:T(8,128)(2,1)} %constant.32.clone.hf_high) | copy-start | bytes 12292
  5.3 38.6 %copy-start.13 = (f32[256]{0:T(256)S(1)}, f32[256]{0:T(256)}, u32[]{:S(2)}) copy-start(f32[256]{0:T(256)} %constant.28.clone.lap_z) | copy-start | bytes 3076
  5.3 7.1 %collective-permute-start.3 = (f32[34,256]{1,0:T(8,128)S(1)}, f32[34,256]{1,0:T(8,128)S(1)}, u32[]{:S(2)}, u32[]{:S(2)}) collective-permute-start(f32[34,256]{1,0:T(8,128)S(1)} %pad_maximum_fusion.2), channel_id=1, source_target_pairs={{0,7},{1,0},{2,1},{3,2},{4,3},{5,4},{6,5},{7,6},{8,15},{9,8},{10,9... | collective-permute-start | bytes 104456 | tf_op jit(solution)/shard_map/ppermute | solution.py:92
  10.7 6.9 %collective-permute-start.2 = (f32[34,256]{1,0:T(8,128)S(1)}, f32[34,256]{1,0:T(8,128)S(1)}, u32[]{:S(2)}, u32[]{:S(2)}) collective-permute-start(f32[34,256]{1,0:T(8,128)S(1)} %pad_maximum_fusion.1), channel_id=1, source_target_pairs={{0,1},{1,2},{2,3},{3,4},{4,5},{5,6},{6,7},{7,0},{8,9},{9,10},{10,1... | collective-permute-start | bytes 104456 | tf_op jit(solution)/shard_map/ppermute | solution.py:92
  17.6 1.0 copy-start
  18.6 0.9 copy-start.2
  19.5 0.9 copy-start.4
  24.8 19.0 %all-to-all-start = ((f32[32,8,512]{2,1,0:T(8,128)}), f32[32,8,512]{2,1,0:T(8,128)S(1)}, u32[]{:S(2)}, u32[]{:S(2)}) async-start(f32[32,8,512]{2,1,0:T(8,128)} %bitcast.13), calls=%async_computation | async-start | bytes 1048576 | tf_op jit(solution)/shard_map/all_to_all | solution.py:524
  27.5 42.0 %copy-start.1 = (f32[32,16,256]{2,1,0:T(8,128)S(1)}, f32[32,16,256]{2,1,0:T(8,128)}, u32[]{:S(2)}) copy-start(f32[32,16,256]{2,1,0:T(8,128)} %core.3) | copy-start | bytes 1572868
  27.5 42.0 %copy-start.3 = (bf16[256,256]{1,0:T(8,128)(2,1)S(1)}, bf16[256,256]{1,0:T(8,128)(2,1)}, u32[]{:S(2)}) copy-start(bf16[256,256]{1,0:T(8,128)(2,1)} %constant.27.clone.low) | copy-start | bytes 393220
  27.5 42.0 %copy-start.5 = (bf16[256,256]{1,0:T(8,128)(2,1)S(1)}, bf16[256,256]{1,0:T(8,128)(2,1)}, u32[]{:S(2)}) copy-start(bf16[256,256]{1,0:T(8,128)(2,1)} %constant.26.clone.high) | copy-start | bytes 393220
  100.4 27.4 %all-to-all-start.2 = ((f32[32,8,896]{2,1,0:T(8,128)}), f32[32,8,896]{2,1,0:T(8,128)S(1)}, u32[]{:S(2)}, u32[]{:S(2)}) async-start(f32[32,8,896]{2,1,0:T(8,128)} %bitcast.18), calls=%async_computation.2 | async-start | bytes 1835008 | tf_op jit(solution)/shard_map/all_to_all | solution.py:524
  139.8 4.4 %collective-permute-start.5 = (f32[36,2,256]{2,1,0:T(2,128)S(1)}, f32[36,2,256]{2,1,0:T(2,128)S(1)}, u32[]{:S(2)}, u32[]{:S(2)}) collective-permute-start(f32[36,2,256]{2,1,0:T(2,128)S(1)} %get-tuple-element.24), channel_id=1, source_target_pairs={{0,7},{1,0},{2,1},{3,2},{4,3},{5,4},{6,5},{7,6},{8,15},{9,8},{10,9... | collective-permute-start | bytes 221192 | tf_op jit(solution)/shard_map/ppermute | solution.py:92
  141.3 7.0 %collective-permute-start.4 = (f32[36,2,256]{2,1,0:T(2,128)S(1)}, f32[36,2,256]{2,1,0:T(2,128)S(1)}, u32[]{:S(2)}, u32[]{:S(2)}) collective-permute-start(f32[36,2,256]{2,1,0:T(2,128)S(1)} %get-tuple-element.25), channel_id=1, source_target_pairs={{0,1},{1,2},{2,3},{3,4},{4,5},{5,6},{6,7},{7,0},{8,9},{9,10},{10,1... | collective-permute-start | bytes 221192 | tf_op jit(solution)/shard_map/ppermute | solution.py:92
  148.4 1.8 %collective-permute-start.7 = (f32[2,16,256]{2,1,0:T(8,128)S(1)}, f32[2,16,256]{2,1,0:T(8,128)S(1)}, u32[]{:S(2)}, u32[]{:S(2)}) collective-permute-start(f32[2,16,256]{2,1,0:T(8,128)S(1)} %get-tuple-element.26), channel_id=1, source_target_pairs={{0,24},{8,0},{16,8},{24,16},{1,25},{9,1},{17,9},{25,17},{2,26},{10... | collective-permute-start | bytes 98312 | tf_op jit(solution)/shard_map/ppermute | solution.py:92
  148.4 3.4 %collective-permute-start.6 = (f32[2,16,256]{2,1,0:T(8,128)S(1)}, f32[2,16,256]{2,1,0:T(8,128)S(1)}, u32[]{:S(2)}, u32[]{:S(2)}) collective-permute-start(f32[2,16,256]{2,1,0:T(8,128)S(1)} %get-tuple-element.27), channel_id=1, source_target_pairs={{0,8},{8,16},{16,24},{24,0},{1,9},{9,17},{17,25},{25,1},{2,10},{10... | collective-permute-start | bytes 98312 | tf_op jit(solution)/shard_map/ppermute | solution.py:92

commit v3 on v2

--- a/solution.py
+++ b/solution.py
@@ -110,54 +110,73 @@
     label_out[...] = dot(named, (lane == rank + start).astype(BF16), NT) - 1.0
 
 
-def pad_tile(pad, core, x_faces, y_faces):
-    rows_x, rows_y, _ = core.shape
-    pad[1 : rows_x + 1, 8 : rows_y + 8, :] = core[...]
-    pad[0, 8 : rows_y + 8, :] = x_faces[0]
-    pad[rows_x + 1, 8 : rows_y + 8, :] = x_faces[1]
-    for x in range(rows_x):
-        pad[x + 1, 7:8, :] = y_faces[0, x + 1 : x + 2, :]
-        pad[x + 1, rows_y + 8 : rows_y + 9, :] = y_faces[1, x + 1 : x + 2, :]
-
-
-def source_kernel(core, x_faces, y_faces, high, low, spectrum, pad, source):
-    rows_x, rows_y, cells_z = core.shape
-    pad_tile(pad, core, x_faces, y_faces)
-    for side in range(2):
-        edge = side * (rows_x + 1)
-        pad[edge, 7:8, :] = y_faces[0, edge : edge + 1, :]
-        pad[edge, rows_y + 8 : rows_y + 9, :] = y_faces[1, edge : edge + 1, :]
-
+def source_of(at, cells_z):
     def ahead(value):
         return pltpu.roll(value, cells_z - 1, 1)
 
     def behind(value):
         return pltpu.roll(value, 1, 1)
 
-    @pl.loop(0, rows_x)
+    here = at(0, 0)
+    ahead_x, behind_x, ahead_y, behind_y = at(1, 0), at(-1, 0), at(0, 1), at(0, -1)
+    xx = ahead_x - 2.0 * here + behind_x
+    yy = ahead_y - 2.0 * here + behind_y
+    zz = ahead(here) - 2.0 * here + behind(here)
+    xy = (at(1, 1) - at(1, -1) - at(-1, 1) + at(-1, -1)) * 0.25
+    across_x, across_y = ahead_x - behind_x, ahead_y - behind_y
+    xz = (ahead(across_x) - behind(across_x)) * 0.25
+    yz = (ahead(across_y) - behind(across_y)) * 0.25
+    return xx * yy + xx * zz + yy * zz - xy * xy - xz * xz - yz * yz
+
+
+def source_kernel(core, y_faces, high, low, pad):
+    rows_x, rows_y, cells_z = core.shape
+    pad[:, 8 : rows_y + 8, :] = core[...]
+    for x in range(rows_x):
+        pad[x, 7:8, :] = y_faces[0, x : x + 1, :]
+        pad[x, rows_y + 8 : rows_y + 9, :] = y_faces[1, x : x + 1, :]
+
+    @pl.loop(1, rows_x - 1)
     def _(x):
         def at(dx, dy):
-            return pad[x + 1 + dx, 8 + dy : 8 + dy + rows_y, :]
-
-        here = at(0, 0)
-        ahead_x, behind_x, ahead_y, behind_y = at(1, 0), at(-1, 0), at(0, 1), at(0, -1)
-        xx = ahead_x - 2.0 * here + behind_x
-        yy = ahead_y - 2.0 * here + behind_y
-        zz = ahead(here) - 2.0 * here + behind(here)
-        xy = (at(1, 1) - at(1, -1) - at(-1, 1) + at(-1, -1)) * 0.25
-        across_x, across_y = ahead_x - behind_x, ahead_y - behind_y
-        xz = (ahead(across_x) - behind(across_x)) * 0.25
-        yz = (ahead(across_y) - behind(across_y)) * 0.25
-        value = xx * yy + xx * zz + yy * zz - xy * xy - xz * xz - yz * yz
-        source[pl.ds(pl.multiple_of(x * rows_y, rows_y), rows_y), :] = value
-
-    spectrum[...] = dot3((high[...], low[...]), split(source[...], 2), NT)
+            return pad[x + dx, 8 + dy : 8 + dy + rows_y, :]
+
+        rows = pl.ds(pl.multiple_of(x * rows_y, rows_y), rows_y)
+        high[rows, :], low[rows, :] = split(source_of(at, cells_z), 2)
+
+    for x in (0, rows_x - 1):
+        rows = slice(x * rows_y, (x + 1) * rows_y)
+        high[rows, :] = jnp.zeros((rows_y, cells_z), BF16)
+        low[rows, :] = jnp.zeros((rows_y, cells_z), BF16)
+
+
+def spectrum_kernel(core, y_faces, x_faces, inner_high, inner_low, high, low, spectrum, pad, source_high, source_low):
+    rows_x, rows_y, cells_z = core.shape
+    source_high[...] = inner_high[...]
+    source_low[...] = inner_low[...]
+    for side in range(2):
+        edge = side * (rows_x - 1)
+        for line in range(3):
+            x = edge + line - 1
+            if 0 <= x < rows_x:
+                pad[line, 8 : rows_y + 8, :] = core[x]
+                pad[line, 7:8, :] = y_faces[0, x : x + 1, :]
+                pad[line, rows_y + 8 : rows_y + 9, :] = y_faces[1, x : x + 1, :]
+            else:
+                pad[line, 7 : rows_y + 9, :] = x_faces[side]
+
+        def at(dx, dy):
+            return pad[1 + dx, 8 + dy : 8 + dy + rows_y, :]
+
+        rows = slice(edge * rows_y, (edge + 1) * rows_y)
+        source_high[rows, :], source_low[rows, :] = split(source_of(at, cells_z), 2)
+    spectrum[...] = dot3((high[...], low[...]), (source_high[...], source_low[...]), NT)
 
 
 def solve_kernel(
     tiles_x, tiles_y, rows_x, rows_y, scale,
     first, lap_z, slab, labels, lap_xy, hx_high, hx_low, hy_high, hy_low, hf_high, hf_low,
-    out, planes, faces,
+    out, planes, solved_planes, faces,
 ):
     grid_x, grid_y = tiles_x * rows_x, tiles_y * rows_y
     count = slab.shape[1]
@@ -181,9 +200,9 @@
         anchor = eigen == 0.0
         solved = jnp.where(anchor, 0.0, scale / jnp.where(anchor, -1.0, eigen)) * modes
         back = dot3(hx, split(solved, 2))
-        planes[rows, :] = back
+        solved_planes[rows, :] = back
         faces[pl.ds(q, 2 * tiles_y, stride=count), :] = dot3(hf, split(back, 2), NT)
-    planes[...] = dot3(split(planes[...], 2), hy)
+    planes[...] = dot3(split(solved_planes[...], 2), hy)
 
     lane = lax.broadcasted_iota(jnp.int32, (count, LANES), 1)
     for i in range(tiles_x):
@@ -251,19 +270,13 @@
     return jnp.concatenate(parts, -1).reshape(tiles_x * tiles_y, count, -1)
 
 
-def block_kernel(
-    planes, half, core, x_faces, y_faces, spectrum, high, low, slots,
-    displacement, first_half, second_half, labels,
-    pad, cells, spread, values,
-):
+def combine(core, x_faces, y_faces, spectrum, high, low, cells):
     rows_x, rows_y, cells_z = core.shape
     inner = rows_x * rows_y
-    blocks_x, blocks_y, blocks_z = rows_x // 8, rows_y // 8, cells_z // 8
-    per = LANES // blocks_z
     cells[...] = dot3(split(spectrum[...], 2), (high[...], low[...]), TN)
     cells[0:inner, :] = cells[0:inner, :] + core[...].reshape(inner, cells_z)
     start = inner
-    for faces, skip in ((x_faces, 0), (y_faces, 1)):
+    for faces, skip in ((x_faces, 1), (y_faces, 0)):
         for side in range(2):
             length = faces.shape[1] - 2 * skip
             rows = slice(start, start + length)
@@ -271,7 +284,12 @@
             start += length
     x_edge = [inner, inner + rows_y]
     y_edge = [inner + 2 * rows_y, inner + 2 * rows_y + rows_x]
-
+    return x_edge, y_edge
+
+
+def displacement_kernel(core, x_faces, y_faces, spectrum, high, low, displacement, pad, cells):
+    rows_x, rows_y, cells_z = core.shape
+    x_edge, y_edge = combine(core, x_faces, y_faces, spectrum, high, low, cells)
     for x in range(rows_x):
         pad[x, 8 : rows_y + 8, :] = cells[x * rows_y : (x + 1) * rows_y, :]
         pad[x, 7:8, :] = cells[y_edge[0] + x : y_edge[0] + x + 1, :]
@@ -289,6 +307,18 @@
         displacement[0, x] = (line(x - 1) - line(x + 1)) * 0.5
         displacement[1, x] = (pad[x, 7 : rows_y + 7, :] - pad[x, 9 : rows_y + 9, :]) * 0.5
         displacement[2, x] = (pltpu.roll(here, 1, 1) - pltpu.roll(here, cells_z - 1, 1)) * 0.5
+
+
+def block_kernel(
+    planes, half, core, x_faces, y_faces, spectrum, high, low, slots,
+    first_half, second_half, labels,
+    cells, spread, values,
+):
+    rows_x, rows_y, cells_z = core.shape
+    inner = rows_x * rows_y
+    blocks_x, blocks_y, blocks_z = rows_x // 8, rows_y // 8, cells_z // 8
+    per = LANES // blocks_z
+    x_edge, y_edge = combine(core, x_faces, y_faces, spectrum, high, low, cells)
 
     width = spread.shape[0] * LANES
     col = lax.broadcasted_iota(jnp.int32, (cells_z, width), 1)
@@ -376,9 +406,9 @@
 
 def deposit_kernel(blocks_x, blocks_y, blocks_z, last, blocks, labels, *refs):
     if last:
-        before, core, x_rims, y_rims, turned, weights, high, low, grouped, tile = refs
+        before, core, x_rims, y_rims, turned, weights, pieces, grouped, tile = refs
     else:
-        core, turned, weights, high, low, grouped, tile = refs
+        core, turned, weights, pieces, grouped, tile = refs
     slots = blocks.shape[0]
     cells_z = 8 * blocks_z
     per = LANES // blocks_z
@@ -409,7 +439,8 @@
                     for k, weight in enumerate(spline(jnp.clip(diff * 0.5, -1.0, 1.0))):
                         weights[axis * 5 + k, a * 8 + e] = weight
 
-        lanes = pl.ds(pl.multiple_of(g * LANES, LANES), LANES)
+        top_lanes = pl.ds(pl.multiple_of(g * LANES, LANES), LANES)
+        rest_lanes = pl.ds(pl.multiple_of(slots + g * LANES, LANES), LANES)
 
         def cell_row(s, depths):
             sums = {}
@@ -434,8 +465,8 @@
                     both = jnp.concatenate([head, tail], 0)
                     top, rest = split(both, 2)
                     out = pl.ds(pl.multiple_of((s * 12 + u) * 16, 16), 16)
-                    high[out, lanes] = top
-                    low[out, lanes] = rest
+                    pieces[out, top_lanes] = top
+                    pieces[out, rest_lanes] = rest
 
         for s in (0, 1, 2, 3, 8, 9, 10, 11):
             cell_row(s, [k for k in range(5) if 0 <= s - k < 8])
@@ -444,38 +475,36 @@
         def _(s):
             cell_row(s, range(5))
 
-    named = (labels[...] == lax.broadcasted_iota(jnp.int32, (windows, slots), 0)).astype(BF16)
+    named = (labels[...] == lax.broadcasted_iota(jnp.int32, (windows, slots), 0)).astype(F32)
+    named = jnp.transpose(named).astype(BF16)
     area = 12 * 16
+    named = jnp.concatenate([named, named], 0)
 
     @pl.loop(0, 12 // per)
     def _(quad):
-        part = []
-        for k in range(per):
-            rows = pl.ds(pl.multiple_of((quad * per + k) * area, 16), area)
-            part.append(dot(high[rows, :], named, NT) + dot(low[rows, :], named, NT))
+        rows = pl.ds(pl.multiple_of(quad * per * area, 16), per * area)
+        summed = dot(pieces[rows, :], named)
         for wide in range(windows // LANES):
             lanes = slice(wide * LANES, (wide + 1) * LANES)
-            for t, item in enumerate(swap_groups([p[:, lanes] for p in part], blocks_z)):
-                grouped[wide * per + t, quad] = item
+            part = [summed[k * area : (k + 1) * area, lanes] for k in range(per)]
+            for t, item in enumerate(swap_groups(part, blocks_z)):
+                rows = slice((wide * per + t) * area, (wide * per + t + 1) * area)
+                grouped[0, quad, rows, :], grouped[1, quad, rows, :] = split(item, 2)
 
     depth = 12 * blocks_z
     row = lax.broadcasted_iota(jnp.int32, (depth, cells_z), 0)
     wanted = (8 * (row % blocks_z) + row // blocks_z + cells_z - 2) % cells_z
     place = (wanted == lax.broadcasted_iota(jnp.int32, (depth, cells_z), 1)).astype(BF16)
     tile[...] = before[...] if last else jnp.zeros_like(tile)
-
-    @pl.loop(0, blocks_x)
-    def _(bx):
+    quads = depth // LANES
+    left = jnp.concatenate([grouped[piece, quad] for piece in range(2) for quad in range(quads)], 1)
+    total = dot(left, jnp.concatenate([place, place], 0))
+    for bx in range(blocks_x):
         for by in range(blocks_y):
-            total = None
-            for quad in range(12 // per):
-                piece = place[quad * LANES : (quad + 1) * LANES, :]
-                for item in split(grouped[bx * blocks_y + by, quad], 2):
-                    term = dot(item, piece)
-                    total = term if total is None else total + term
-            rows = pl.ds(bx * 8, 12)
+            at = (bx * blocks_y + by) * area
+            rows = slice(bx * 8, bx * 8 + 12)
             cols = slice(by * 8, by * 8 + 16)
-            tile[rows, cols, :] = tile[rows, cols, :] + total.reshape(12, 16, cells_z)
+            tile[rows, cols, :] = tile[rows, cols, :] + total[at : at + area].reshape(12, 16, cells_z)
 
     if not last:
         core[...] = tile[...]
@@ -526,23 +555,28 @@
     slots, labels = call(
         functools.partial(slot_kernel, half, 2 * (rows_x + rows_y)),
         (shape(1, blocks, dtype=jnp.int32), shape(tiles, LANES)),
-        [], 16, 2 * tiles * LANES * blocks, 8 * blocks,
+        [], 8, 2 * tiles * LANES * blocks, 8 * blocks,
     )(owner.reshape(blocks, 1), owner.reshape(1, blocks), window.reshape(1, blocks))
 
     last_x, last_y = rows_x - 1, rows_y - 1
-    x_faces = jnp.stack([send(potential[last_x], "px", 1), send(potential[0], "px", -1)])
-    y_lines = [
-        jnp.concatenate([x_faces[0, y : y + 1], potential[:, y], x_faces[1, y : y + 1]])
-        for y in (last_y, 0)
+    y_faces = jnp.stack([send(potential[:, last_y], "py", 1), send(potential[:, 0], "py", -1)])
+    x_lines = [
+        jnp.concatenate([y_faces[0, x : x + 1], potential[x], y_faces[1, x : x + 1]])
+        for x in (last_x, 0)
     ]
-    y_faces = jnp.stack([send(y_lines[0], "py", 1), send(y_lines[1], "py", -1)])
+    x_faces = jnp.stack([send(x_lines[0], "px", 1), send(x_lines[1], "px", -1)])
 
     z_high, z_low = pieces_of(table_of(cells_z))
+    halves = shape(inner, cells_z, dtype=BF16)
+    source = call(
+        source_kernel, (halves, halves), [pltpu.VMEM((rows_x, rows_y + 16, cells_z), F32)],
+        8, 60 * inner * cells_z, 2 << 20,
+    )(potential, y_faces)
     spectrum = call(
-        source_kernel, shape(cells_z, inner),
-        [pltpu.VMEM((rows_x + 2, rows_y + 16, cells_z), F32), pltpu.VMEM((inner, cells_z), F32)],
-        24, 6 * inner * cells_z**2, 2 << 20,
-    )(potential, x_faces, y_faces, z_high, z_low)
+        spectrum_kernel, shape(cells_z, inner),
+        [pltpu.VMEM((3, rows_y + 16, cells_z), F32)] + [pltpu.VMEM((inner, cells_z), BF16)] * 2,
+        12, 6 * inner * cells_z**2, 2 << 20,
+    )(potential, y_faces, x_faces, *source, z_high, z_low)
     slab = exchange(spectrum).reshape(tiles, planes, inner)
 
     scale = SECOND_ORDER / (grid_x * grid_y * cells_z)
@@ -562,9 +596,10 @@
             out_specs=VMEM,
             scratch_shapes=[
                 pltpu.VMEM((grid_x * planes, grid_y), F32),
+                pltpu.VMEM((grid_x * planes, grid_y), F32),
                 pltpu.VMEM((2 * tiles_y * planes, grid_x), F32),
             ],
-            compiler_params=pltpu.CompilerParams(vmem_limit_bytes=24 << 20),
+            compiler_params=pltpu.CompilerParams(vmem_limit_bytes=16 << 20),
             cost_estimate=pl.CostEstimate(
                 flops=24 * planes * grid_x**2 * grid_y, bytes_accessed=2 << 20, transcendentals=0
             ),
@@ -573,32 +608,36 @@
         returned = solve_plain(slab, labels, rows_x, rows_y, cells_z, tiles_x, tiles_y, scale)
     modes = exchange(returned.reshape(cells_z, used))
 
-    pad = pltpu.VMEM((rows_x, rows_y + 16, cells_z), F32)
     width = -(-10 * blocks_z // LANES) * LANES
-    displacement, *sent, arrived_labels = call(
+    cells = pltpu.VMEM((used, cells_z), F32)
+    tile_args = (potential, x_faces, y_faces, modes, z_high, z_low)
+    *sent, arrived_labels = call(
         functools.partial(block_kernel, planes, half),
-        (
-            shape(3, rows_x, rows_y, cells_z), shape(blocks, ROWS), shape(blocks, ROWS),
-            shape(2, 1, blocks, dtype=jnp.int32),
-        ),
-        [pad, pltpu.VMEM((used, cells_z), F32), pltpu.VMEM((width // LANES, used, LANES), F32), pltpu.VMEM((ROWS, blocks), F32)],
-        40, 20 * used * cells_z**2, 6 << 20,
-    )(potential, x_faces, y_faces, modes, z_high, z_low, slots)
-
-    arrived = [exchange(part) for part in sent]
+        (shape(blocks, ROWS), shape(blocks, ROWS), shape(2, 1, blocks, dtype=jnp.int32)),
+        [cells, pltpu.VMEM((width // LANES, used, LANES), F32), pltpu.VMEM((ROWS, blocks), F32)],
+        24, 20 * used * cells_z**2, 6 << 20,
+    )(*tile_args, slots)
+    displacement = call(
+        displacement_kernel, shape(3, rows_x, rows_y, cells_z),
+        [pltpu.VMEM((rows_x, rows_y + 16, cells_z), F32), cells],
+        16, 6 * used * cells_z**2, 4 << 20,
+    )(*tile_args)
+
+    first = exchange(sent[0])
+    later, displacement = lax.optimization_barrier((sent[1], displacement))
+    arrived = first, exchange(later)
     tile_shape = (rows_x + 4, rows_y + 8, cells_z)
     scratch = [
         pltpu.VMEM((blocks // LANES, ROWS, LANES), F32),
         pltpu.VMEM((15, 64, 8, LANES), F32),
-        pltpu.VMEM((12 * 12 * 16, blocks), BF16),
-        pltpu.VMEM((12 * 12 * 16, blocks), BF16),
-        pltpu.VMEM((blocks_x * blocks_y, 12 * blocks_z // LANES, 12 * 16, LANES), F32),
+        pltpu.VMEM((12 * 12 * 16, 2 * blocks), BF16),
+        pltpu.VMEM((2, 12 * blocks_z // LANES, blocks_x * blocks_y * 12 * 16, LANES), BF16),
         pltpu.VMEM(tile_shape, F32),
     ]
     sizes = (blocks_x, blocks_y, blocks_z)
     cost = (300 * blocks * 512, 4 << 20)
     tile = call(
-        functools.partial(deposit_kernel, *sizes, False), shape(*tile_shape), scratch, 40, *cost
+        functools.partial(deposit_kernel, *sizes, False), shape(*tile_shape), scratch, 32, *cost
     )(arrived[0], arrived_labels[0])
     core, x_rims, y_rims = call(
         functools.partial(deposit_kernel, *sizes, True),
@@ -606,15 +645,15 @@
             shape(rows_x, rows_y, cells_z), shape(2, 2, rows_y, cells_z),
             shape(2, rows_x + 4, 2, cells_z),
         ),
-        scratch, 40, *cost,
+        scratch, 32, *cost,
     )(arrived[1], arrived_labels[1], tile)
 
     y_sides = send(y_rims[1], "py", 1), send(y_rims[0], "py", -1)
-    x_rims = call(corner_kernel, shape(*x_rims.shape), [], 16, 8 * rows_y * cells_z, 1 << 17)(
+    x_rims = call(corner_kernel, shape(*x_rims.shape), [], 4, 8 * rows_y * cells_z, 1 << 17)(
         x_rims, *y_sides
     )
     x_sides = send(x_rims[1], "px", 1), send(x_rims[0], "px", -1)
-    density = call(rim_kernel, shape(rows_x, rows_y, cells_z), [], 16, inner * cells_z, 2 << 20)(
+    density = call(rim_kernel, shape(rows_x, rows_y, cells_z), [], 8, inner * cells_z, 2 << 20)(
         core, *y_sides, *x_sides
     )
     return (displacement, density)

time: 153 us -> 149 us (0.974)
  blocking collectives: 48 us -> 21.2 us
  waiting for transfers between devices: 44.9 us -> 57.9 us
  starting transfers between devices: 15.9 us -> 26.1 us
    all_to_all x2 -> x1, blocking collectives: 48 us -> 21.2 us  [exchange(): return lax.all_to_all(x, both, split_axis=0, concat_axis=0, tiled=True)]
    all_to_all x2 -> x3, waiting for transfers between devices: 28.5 us -> 52.9 us  [exchange(): return lax.all_to_all(x, both, split_axis=0, concat_axis=0, tiled=True)]
    ppermute x8, waiting for transfers between devices: 16.4 us -> 5.01 us  [send(): return lax.ppermute(x, axis, [(i, (i + step) % size) for i in range(size)])]
    all_to_all x2 -> x3, starting transfers between devices: 5.42 us -> 11.6 us  [exchange(): return lax.all_to_all(x, both, split_axis=0, concat_axis=0, tiled=True)]
    ppermute x8, starting transfers between devices: 10.5 us -> 14.5 us  [send(): return lax.ppermute(x, axis, [(i, (i + step) % size) for i in range(size)])]
    pallas_call x4 -> x6, Pallas kernels: 9.36 us -> 11.2 us  [the longest x1 3.94 us: per_device(): call(functools.partial(block_kernel, planes, half), (shape(blocks, ROWS),...]
    pallas_call x1, Pallas kernels: 12 us -> 10.4 us  [per_device(): call(functools.partial(deposit_kernel, *sizes, False), shape(*tile_shape)...]
  transfers between devices with their start and end apart: 10 -> 11, of which waited for: 10 -> 6; matrix products, arithmetic and copies ran while one was open for 1% -> 1% of each run, Pallas kernels for 8% -> 11%
where the time goes in v3:
time: 149 us; the launch traced here: 148 us
  waiting for transfers between devices  57.9 us (39%)
  Pallas kernels  36.9 us (25%)
  starting transfers between devices  26.1 us (18%)
  blocking collectives  21.2 us (14%)
  local copies, waits for them, and re-layouts  4.95 us (3%)
    all_to_all x3, waiting for transfers between devices, exchange(): return lax.all_to_all(x, both, split_axis=0, concat_axis=0, tiled=True)  52.9 us
    all_to_all x1, blocking collectives, exchange(): return lax.all_to_all(x, both, split_axis=0, concat_axis=0, tiled=True)  21.2 us
    ppermute x8, starting transfers between devices, send(): return lax.ppermute(x, axis, [(i, (i + step) % size) for i in range(size)])  14.5 us
    all_to_all x3, starting transfers between devices, exchange(): return lax.all_to_all(x, both, split_axis=0, concat_axis=0, tiled=True)  11.6 us
    pallas_call x1, Pallas kernels, per_device(): call(functools.partial(deposit_kernel, *sizes, True), (shape(rows_x, rows...  10.5 us
    pallas_call x1, Pallas kernels, per_device(): call(functools.partial(deposit_kernel, *sizes, False), shape(*tile_shape)...  10.4 us
    ppermute x8, waiting for transfers between devices, send(): return lax.ppermute(x, axis, [(i, (i + step) % size) for i in range(size)])  5.01 us
    pallas_call x1, Pallas kernels, per_device(): pl.pallas_call(body, out_shape=shape(tiles, planes, used), in_specs=specs...  4.51 us
  transfers between devices with their start and end apart: 11, of which 6 were waited for; matrix products, arithmetic and copies ran while one was open for 1% of the time, Pallas kernels for 11%

profile of v3, /device:TPU:0, one launch (start us, length us, event | category | flops | bytes accessed | tf_op | source)
XLA Modules:
  0.0 148.1 jit_solution(15716641633616164879)
XLA Ops:
  0.6 0.0 copy-start.1
  0.6 1.1 fusion
  1.8 3.0 %collective-permute-start = (f32[32,256]{1,0:T(8,128)S(1)}, f32[32,256]{1,0:T(8,128)S(1)}, u32[]{:S(2)}, u32[]{:S(2)}) collective-permute-start(f32[32,256]{1,0:T(8,128)S(1)} %bitcast.55), channel_id=1, source_target_pairs={{0,1},{1,2},{2,3},{3,4},{4,5},{5,6},{6,7},{7,0},{8,9},{9,10},{10,1... | collective-permute-start | bytes 98312 | tf_op jit(solution)/shard_map/ppermute | solution.py:92
  4.8 3.1 %collective-permute-start.1 = (f32[32,256]{1,0:T(8,128)S(1)}, f32[32,256]{1,0:T(8,128)S(1)}, u32[]{:S(2)}, u32[]{:S(2)}) collective-permute-start(f32[32,256]{1,0:T(8,128)S(1)} %bitcast.56), channel_id=1, source_target_pairs={{0,7},{1,0},{2,1},{3,2},{4,3},{5,4},{6,5},{7,6},{8,15},{9,8},{10,9... | collective-permute-start | bytes 98312 | tf_op jit(solution)/shard_map/ppermute | solution.py:92
  7.9 0.7 slice_bitcast_fusion.5
  8.7 1.1 collective-permute-done
  9.7 0.0 collective-permute-done.1
  9.8 0.1 collective-permute-start.2
  9.9 1.7 %collective-permute-start.3 = (f32[18,256]{1,0:T(8,128)S(1)}, f32[18,256]{1,0:T(8,128)S(1)}, u32[]{:S(2)}, u32[]{:S(2)}) collective-permute-start(f32[18,256]{1,0:T(8,128)S(1)} %pad_maximum_fusion.3), channel_id=1, source_target_pairs={{0,24},{8,0},{16,8},{24,16},{1,25},{9,1},{17,9},{25,17},{2,26},{10... | collective-permute-start | bytes 55304 | tf_op jit(solution)/shard_map/ppermute | solution.py:92
  11.6 0.0 copy-start
  11.6 1.0 copy-done
  12.6 3.1 %shard_map.140 = (bf16[512,256]{1,0:T(8,128)(2,1)S(1)}, bf16[512,256]{1,0:T(8,128)(2,1)S(1)}) custom-call(f32[32,16,256]{2,1,0:T(8,128)S(1)} %copy-done, f32[2,32,256]{2,1,0:T(8,128)S(1)} %pad_maximum_fusion.y_faces), custom_call_target="tpu_custom_call" | custom-call | flops 7864320 | bytes 2097152 | tf_op jit(solution)/shard_map/pallas_call | solution.py:571
  15.7 0.0 copy-start.6
  15.8 0.0 collective-permute-done.2
  15.8 0.0 collective-permute-done.3
  15.8 0.0 copy-done.1
  15.8 0.0 copy-start.2
  15.8 0.9 copy-done.2
  16.7 0.0 copy-start.4
  16.7 0.9 copy-done.4
  17.6 0.0 copy-start.7
  17.6 0.0 copy-start.8
  17.6 0.0 copy-start.9
  17.6 0.0 copy-start.10
  17.6 0.0 copy-start.11
  17.6 0.0 copy-start.12
  17.6 0.0 copy-start.13
  17.7 1.3 shard_map.141
  19.0 6.2 %all-to-all-start = ((f32[32,8,512]{2,1,0:T(8,128)}), f32[32,8,512]{2,1,0:T(8,128)S(1)}, u32[]{:S(2)}, u32[]{:S(2)}) async-start(f32[32,8,512]{2,1,0:T(8,128)} %bitcast.13), calls=%async_computation | async-start | bytes 1048576 | tf_op jit(solution)/shard_map/all_to_all | solution.py:553
  25.1 0.0 copy-start.3
  25.1 0.0 copy-start.5
  25.2 0.0 copy-done.6
  25.2 0.1 copy.19.owner_col
  25.3 0.0 copy-done.7
  25.3 0.2 shard_map.142
  25.6 15.9 %all-to-all-done.slab = f32[32,8,512]{2,1,0:T(8,128)S(1)} async-done(((f32[32,8,512]{2,1,0:T(8,128)}), f32[32,8,512]{2,1,0:T(8,128)S(1)}, u32[]{:S(2)}, u32[]{:S(2)}) %all-to-all-start) | async-done | bytes 524320 | tf_op jit(solution)/shard_map/all_to_all | solution.py:553
  41.5 0.0 copy-done.8
  41.5 0.0 copy-done.9
  41.5 0.0 copy-done.10
  41.5 0.0 copy-done.11
  41.5 0.0 copy-done.12
  41.5 0.0 copy-done.13
  41.5 4.5 %shard_map.143 = f32[32,8,640]{2,1,0:T(8,128)S(1)} custom-call(s32[1]{0:T(128)} %bitcast.12.first, f32[256]{0:T(256)S(1)} %copy-done.13, f32[32,8,512]{2,1,0:T(8,128)S(1)} %all-to-all-done.slab, f32[32,128]{1,0:T(8,128)S(1)} %get-tuple-element.16.labels, f32[128,128]{1,0:T(8,128)S(1)} %copy-done.8, bf16[128,128]{1,0:T(8,128)(2,1)S(1)} %copy-done.9, ...), custom_call_target="tpu_custom_call" | custom-call | flops 402653184 | bytes 2097152 | tf_op jit(solution)/shard_map/pallas_call | solution.py:592
  46.0 21.2 %all_to_all.39 = f32[32,8,640]{2,1,0:T(8,128)S(1)} all-to-all(f32[32,8,640]{2,1,0:T(8,128)S(1)} %shard_map.143), channel_id=1, replica_groups=mesh['px'=4,'py'=8] {'px','py'}, dimensions={0} | all-to-all | bytes 1310720 | tf_op jit(solution)/shard_map/all_to_all | solution.py:553
  67.3 0.0 copy-done.3
  67.3 0.0 copy-done.5
  67.3 3.9 %shard_map.144 = (f32[256,896]{1,0:T(8,128)}, f32[256,896]{1,0:T(8,128)}, s32[2,1,256]{2,1,0:T(1,128)S(1)}) custom-call(f32[32,16,256]{2,1,0:T(8,128)S(1)} %copy-done.1, f32[2,18,256]{2,1,0:T(8,128)S(1)} %pad_maximum_fusion.1.x_faces, f32[2,32,256]{2,1,0:T(8,128)S(1)} %pad_maximum_fusion.y_faces, f32[256,640]{1,0:T(8,128)S(1)} %bitcast.46, ...), custom_call_target="tpu_custom_call" | custom-call | flops 838860800 | bytes 6291456 | tf_op jit(solution)/shard_map/pallas_call | solution.py:614
  71.2 2.6 %all-to-all-start.3 = ((f32[32,8,896]{2,1,0:T(8,128)}), f32[32,8,896]{2,1,0:T(8,128)S(1)}, u32[]{:S(2)}, u32[]{:S(2)}) async-start(f32[32,8,896]{2,1,0:T(8,128)} %bitcast.21), calls=%async_computation.3 | async-start | bytes 1835008 | tf_op jit(solution)/shard_map/all_to_all | solution.py:553
  73.9 2.0 %shard_map.145 = f32[3,32,16,256]{3,2,1,0:T(8,128)} custom-call(f32[32,16,256]{2,1,0:T(8,128)S(1)} %copy-done.1, f32[2,18,256]{2,1,0:T(8,128)S(1)} %pad_maximum_fusion.1.x_faces, f32[2,32,256]{2,1,0:T(8,128)S(1)} %pad_maximum_fusion.y_faces, f32[256,640]{1,0:T(8,128)S(1)} %bitcast.47, bf16[256,256]{1,0:T(8,128)(2,1)S(1)} %copy-done.3, ...), custom_call_target="tpu_custom_call" | custom-call | flops 251658240 | bytes 4194304 | tf_op jit(solution)/shard_map/pallas_call | solution.py:620
  75.8 22.8 %all-to-all-done.3 = f32[32,8,896]{2,1,0:T(8,128)S(1)} async-done(((f32[32,8,896]{2,1,0:T(8,128)}), f32[32,8,896]{2,1,0:T(8,128)S(1)}, u32[]{:S(2)}, u32[]{:S(2)}) %all-to-all-start.3) | async-done | bytes 917536 | tf_op jit(solution)/shard_map/all_to_all | solution.py:553
  98.6 2.8 %all-to-all-start.2 = ((f32[32,8,896]{2,1,0:T(8,128)}), f32[32,8,896]{2,1,0:T(8,128)S(1)}, u32[]{:S(2)}, u32[]{:S(2)}) async-start(f32[32,8,896]{2,1,0:T(8,128)} %bitcast.18), calls=%async_computation.2 | async-start | bytes 1835008 | tf_op jit(solution)/shard_map/all_to_all | solution.py:553
  101.5 10.4 %shard_map.146.refs_0_ = f32[36,24,256]{2,1,0:T(8,128)S(1)} custom-call(f32[256,896]{1,0:T(8,128)S(1)} %bitcast.44, s32[1,256]{1,0:T(1,128)S(1)} %get-tuple-element.38.labels), custom_call_target="tpu_custom_call" | custom-call | flops 39321600 | bytes 4194304 | tf_op jit(solution)/shard_map/pallas_call | solution.py:639
  111.9 14.2 %all-to-all-done.2 = f32[32,8,896]{2,1,0:T(8,128)S(1)} async-done(((f32[32,8,896]{2,1,0:T(8,128)}), f32[32,8,896]{2,1,0:T(8,128)S(1)}, u32[]{:S(2)}, u32[]{:S(2)}) %all-to-all-start.2) | async-done | bytes 917536 | tf_op jit(solution)/shard_map/all_to_all | solution.py:553
  126.1 10.5 %shard_map.147 = (f32[32,16,256]{2,1,0:T(8,128)S(1)}, f32[2,2,16,256]{3,2,1,0:T(8,128)S(1)}, f32[2,36,2,256]{3,2,1,0:T(2,128)S(1)}) custom-call(f32[256,896]{1,0:T(8,128)S(1)} %bitcast.45, s32[1,256]{1,0:T(1,128)S(1)} %get-tuple-element.39.labels, f32[36,24,256]{2,1,0:T(8,128)S(1)} %shard_map.146.refs_0_), custom_call_target="tpu_custom_call" | custom-call | flops 39321600 | bytes 4194304 | tf_op jit(solution)/shard_map/pallas_call | solution.py:642
  136.6 0.7 collective-permute-start.4
  137.4 4.0 %collective-permute-start.5 = (f32[36,2,256]{2,1,0:T(2,128)S(1)}, f32[36,2,256]{2,1,0:T(2,128)S(1)}, u32[]{:S(2)}, u32[]{:S(2)}) collective-permute-start(f32[36,2,256]{2,1,0:T(2,128)S(1)} %get-tuple-element.30), channel_id=1, source_target_pairs={{0,7},{1,0},{2,1},{3,2},{4,3},{5,4},{6,5},{7,6},{8,15},{9,8},{10,9... | collective-permute-start | bytes 221192 | tf_op jit(solution)/shard_map/ppermute | solution.py:92
  141.4 2.3 %collective-permute-done.4.y_low = f32[36,2,256]{2,1,0:T(2,128)S(1)} collective-permute-done((f32[36,2,256]{2,1,0:T(2,128)S(1)}, f32[36,2,256]{2,1,0:T(2,128)S(1)}, u32[]{:S(2)}, u32[]{:S(2)}) %collective-permute-start.4) | collective-permute-done | bytes 73760 | tf_op jit(solution)/shard_map/ppermute | solution.py:92
  143.7 0.0 collective-permute-done.5.y_top
  143.8 0.1 collective-permute-start.6
  143.8 1.7 %collective-permute-start.7 = (f32[2,16,256]{2,1,0:T(8,128)S(1)}, f32[2,16,256]{2,1,0:T(8,128)S(1)}, u32[]{:S(2)}, u32[]{:S(2)}) collective-permute-start(f32[2,16,256]{2,1,0:T(8,128)S(1)} %get-tuple-element.32), channel_id=1, source_target_pairs={{0,24},{8,0},{16,8},{24,16},{1,25},{9,1},{17,9},{25,17},{2,26},{10... | collective-permute-start | bytes 98312 | tf_op jit(solution)/shard_map/ppermute | solution.py:92
  145.6 1.6 %collective-permute-done.6.x_low = f32[2,16,256]{2,1,0:T(8,128)S(1)} collective-permute-done((f32[2,16,256]{2,1,0:T(8,128)S(1)}, f32[2,16,256]{2,1,0:T(8,128)S(1)}, u32[]{:S(2)}, u32[]{:S(2)}) %collective-permute-start.6) | collective-permute-done | bytes 32800 | tf_op jit(solution)/shard_map/ppermute | solution.py:92
  147.2 0.0 collective-permute-done.7.x_top
  147.2 0.9 shard_map.149
  (12 shorter events, 0.1 us)
Async XLA Ops:
  0.6 15.2 %copy-start.1 = (f32[32,16,256]{2,1,0:T(8,128)S(1)}, f32[32,16,256]{2,1,0:T(8,128)}, u32[]{:S(2)}) copy-start(f32[32,16,256]{2,1,0:T(8,128)} %core.7) | copy-start | bytes 1572868
  1.8 8.0 %collective-permute-start = (f32[32,256]{1,0:T(8,128)S(1)}, f32[32,256]{1,0:T(8,128)S(1)}, u32[]{:S(2)}, u32[]{:S(2)}) collective-permute-start(f32[32,256]{1,0:T(8,128)S(1)} %bitcast.55), channel_id=1, source_target_pairs={{0,1},{1,2},{2,3},{3,4},{4,5},{5,6},{6,7},{7,0},{8,9},{9,10},{10,1... | collective-permute-start | bytes 98312 | tf_op jit(solution)/shard_map/ppermute | solution.py:92
  4.8 4.9 %collective-permute-start.1 = (f32[32,256]{1,0:T(8,128)S(1)}, f32[32,256]{1,0:T(8,128)S(1)}, u32[]{:S(2)}, u32[]{:S(2)}) collective-permute-start(f32[32,256]{1,0:T(8,128)S(1)} %bitcast.56), channel_id=1, source_target_pairs={{0,7},{1,0},{2,1},{3,2},{4,3},{5,4},{6,5},{7,6},{8,15},{9,8},{10,9... | collective-permute-start | bytes 98312 | tf_op jit(solution)/shard_map/ppermute | solution.py:92
  9.8 6.0 %collective-permute-start.2 = (f32[18,256]{1,0:T(8,128)S(1)}, f32[18,256]{1,0:T(8,128)S(1)}, u32[]{:S(2)}, u32[]{:S(2)}) collective-permute-start(f32[18,256]{1,0:T(8,128)S(1)} %pad_maximum_fusion.2), channel_id=1, source_target_pairs={{0,8},{8,16},{16,24},{24,0},{1,9},{9,17},{17,25},{25,1},{2,10},{10... | collective-permute-start | bytes 55304 | tf_op jit(solution)/shard_map/ppermute | solution.py:92
  9.9 5.9 %collective-permute-start.3 = (f32[18,256]{1,0:T(8,128)S(1)}, f32[18,256]{1,0:T(8,128)S(1)}, u32[]{:S(2)}, u32[]{:S(2)}) collective-permute-start(f32[18,256]{1,0:T(8,128)S(1)} %pad_maximum_fusion.3), channel_id=1, source_target_pairs={{0,24},{8,0},{16,8},{24,16},{1,25},{9,1},{17,9},{25,17},{2,26},{10... | collective-permute-start | bytes 55304 | tf_op jit(solution)/shard_map/ppermute | solution.py:92
  11.6 1.0 copy-start
  15.7 9.4 %copy-start.6 = (s32[1,1,256,1]{2,3,1,0:T(1,128)S(1)}, s32[1,1,256,1]{2,3,1,0:T(1,128)}, u32[]{:S(2)}) copy-start(s32[1,1,256,1]{2,3,1,0:T(1,128)} %param.14) | copy-start | bytes 3076
  15.8 0.9 copy-start.2
  16.7 0.9 copy-start.4
  17.6 7.7 %copy-start.7 = (s32[1,1,256]{2,1,0:T(1,128)S(1)}, s32[1,1,256]{2,1,0:T(1,128)}, u32[]{:S(2)}) copy-start(s32[1,1,256]{2,1,0:T(1,128)} %param.15) | copy-start | bytes 3076
  17.6 23.9 %copy-start.8 = (f32[128,128]{1,0:T(8,128)S(1)}, f32[128,128]{1,0:T(8,128)}, u32[]{:S(2)}) copy-start(f32[128,128]{1,0:T(8,128)} %constant.29.clone.lap_xy) | copy-start | bytes 196612
  17.6 23.9 %copy-start.9 = (bf16[128,128]{1,0:T(8,128)(2,1)S(1)}, bf16[128,128]{1,0:T(8,128)(2,1)}, u32[]{:S(2)}) copy-start(bf16[128,128]{1,0:T(8,128)(2,1)} %constant.30.clone.hx_high.hy_high) | copy-start | bytes 98308
  17.6 23.9 %copy-start.10 = (bf16[128,128]{1,0:T(8,128)(2,1)S(1)}, bf16[128,128]{1,0:T(8,128)(2,1)}, u32[]{:S(2)}) copy-start(bf16[128,128]{1,0:T(8,128)(2,1)} %constant.31.clone.hx_low.hy_low) | copy-start | bytes 98308
  17.6 23.9 %copy-start.11 = (bf16[16,128]{1,0:T(8,128)(2,1)S(1)}, bf16[16,128]{1,0:T(8,128)(2,1)}, u32[]{:S(2)}) copy-start(bf16[16,128]{1,0:T(8,128)(2,1)} %constant.32.clone.hf_high) | copy-start | bytes 12292
  17.6 23.9 %copy-start.12 = (bf16[16,128]{1,0:T(8,128)(2,1)S(1)}, bf16[16,128]{1,0:T(8,128)(2,1)}, u32[]{:S(2)}) copy-start(bf16[16,128]{1,0:T(8,128)(2,1)} %constant.33.clone.hf_low) | copy-start | bytes 12292
  17.6 23.9 %copy-start.13 = (f32[256]{0:T(256)S(1)}, f32[256]{0:T(256)}, u32[]{:S(2)}) copy-start(f32[256]{0:T(256)} %constant.28.clone.lap_z) | copy-start | bytes 3076
  19.0 22.5 %all-to-all-start = ((f32[32,8,512]{2,1,0:T(8,128)}), f32[32,8,512]{2,1,0:T(8,128)S(1)}, u32[]{:S(2)}, u32[]{:S(2)}) async-start(f32[32,8,512]{2,1,0:T(8,128)} %bitcast.13), calls=%async_computation | async-start | bytes 1048576 | tf_op jit(solution)/shard_map/all_to_all | solution.py:553
  25.1 42.2 %copy-start.3 = (bf16[256,256]{1,0:T(8,128)(2,1)S(1)}, bf16[256,256]{1,0:T(8,128)(2,1)}, u32[]{:S(2)}) copy-start(bf16[256,256]{1,0:T(8,128)(2,1)} %constant.26.clone.high) | copy-start | bytes 393220
  25.1 42.1 %copy-start.5 = (bf16[256,256]{1,0:T(8,128)(2,1)S(1)}, bf16[256,256]{1,0:T(8,128)(2,1)}, u32[]{:S(2)}) copy-start(bf16[256,256]{1,0:T(8,128)(2,1)} %constant.27.clone.low) | copy-start | bytes 393220
  71.2 27.4 %all-to-all-start.3 = ((f32[32,8,896]{2,1,0:T(8,128)}), f32[32,8,896]{2,1,0:T(8,128)S(1)}, u32[]{:S(2)}, u32[]{:S(2)}) async-start(f32[32,8,896]{2,1,0:T(8,128)} %bitcast.21), calls=%async_computation.3 | async-start | bytes 1835008 | tf_op jit(solution)/shard_map/all_to_all | solution.py:553
  98.6 27.4 %all-to-all-start.2 = ((f32[32,8,896]{2,1,0:T(8,128)}), f32[32,8,896]{2,1,0:T(8,128)S(1)}, u32[]{:S(2)}, u32[]{:S(2)}) async-start(f32[32,8,896]{2,1,0:T(8,128)} %bitcast.18), calls=%async_computation.2 | async-start | bytes 1835008 | tf_op jit(solution)/shard_map/all_to_all | solution.py:553
  136.6 7.1 %collective-permute-start.4 = (f32[36,2,256]{2,1,0:T(2,128)S(1)}, f32[36,2,256]{2,1,0:T(2,128)S(1)}, u32[]{:S(2)}, u32[]{:S(2)}) collective-permute-start(f32[36,2,256]{2,1,0:T(2,128)S(1)} %get-tuple-element.31), channel_id=1, source_target_pairs={{0,1},{1,2},{2,3},{3,4},{4,5},{5,6},{6,7},{7,0},{8,9},{9,10},{10,1... | collective-permute-start | bytes 221192 | tf_op jit(solution)/shard_map/ppermute | solution.py:92
  137.4 6.4 %collective-permute-start.5 = (f32[36,2,256]{2,1,0:T(2,128)S(1)}, f32[36,2,256]{2,1,0:T(2,128)S(1)}, u32[]{:S(2)}, u32[]{:S(2)}) collective-permute-start(f32[36,2,256]{2,1,0:T(2,128)S(1)} %get-tuple-element.30), channel_id=1, source_target_pairs={{0,7},{1,0},{2,1},{3,2},{4,3},{5,4},{6,5},{7,6},{8,15},{9,8},{10,9... | collective-permute-start | bytes 221192 | tf_op jit(solution)/shard_map/ppermute | solution.py:92
  143.8 3.4 %collective-permute-start.6 = (f32[2,16,256]{2,1,0:T(8,128)S(1)}, f32[2,16,256]{2,1,0:T(8,128)S(1)}, u32[]{:S(2)}, u32[]{:S(2)}) collective-permute-start(f32[2,16,256]{2,1,0:T(8,128)S(1)} %get-tuple-element.33), channel_id=1, source_target_pairs={{0,8},{8,16},{16,24},{24,0},{1,9},{9,17},{17,25},{25,1},{2,10},{10... | collective-permute-start | bytes 98312 | tf_op jit(solution)/shard_map/ppermute | solution.py:92
  143.8 3.3 %collective-permute-start.7 = (f32[2,16,256]{2,1,0:T(8,128)S(1)}, f32[2,16,256]{2,1,0:T(8,128)S(1)}, u32[]{:S(2)}, u32[]{:S(2)}) collective-permute-start(f32[2,16,256]{2,1,0:T(8,128)S(1)} %get-tuple-element.32), channel_id=1, source_target_pairs={{0,24},{8,0},{16,8},{24,16},{1,25},{9,1},{17,9},{25,17},{2,26},{10... | collective-permute-start | bytes 98312 | tf_op jit(solution)/shard_map/ppermute | solution.py:92

commit v4 on v3

--- a/solution.py
+++ b/solution.py
@@ -16,6 +16,7 @@
 ROWS = 896
 VMEM = pl.BlockSpec(memory_space=pltpu.VMEM)
 SMEM = pl.BlockSpec(memory_space=pltpu.SMEM)
+FAR = pl.BlockSpec(memory_space=pltpu.HBM)
 NN = (((1,), (0,)), ((), ()))
 NT = (((1,), (1,)), ((), ()))
 TN = (((0,), (0,)), ((), ()))
@@ -69,6 +70,14 @@
     return np.asarray(high), np.asarray(low)
 
 
+def seeds_of(length, step):
+    along = np.arange(length)
+    coarse = (np.arange(length // step)[:, None] * step * along[None, :] % length) * (2.0 * math.pi / length)
+    fine = (np.arange(step)[:, None] * along[None, :] % length) * (2.0 * math.pi / length)
+    rows = [np.cos(coarse), np.sin(coarse), np.cos(fine) + np.sin(fine), np.cos(fine) - np.sin(fine)]
+    return np.concatenate(rows).astype(np.float32)
+
+
 def laplace_of(length):
     return (2.0 * np.cos(np.arange(length) * (2.0 * math.pi / length)) - 2.0).astype(np.float32)
 
@@ -129,14 +138,31 @@
     return xx * yy + xx * zz + yy * zz - xy * xy - xz * xz - yz * yz
 
 
-def source_kernel(core, y_faces, high, low, pad):
+def prepare_kernel(potential, core, y_last, y_first, sem):
+    copy = pltpu.make_async_copy(potential, core, sem)
+    copy.start()
+    copy.wait()
+    rows_x, rows_y, _ = core.shape
+    for x in range(rows_x):
+        y_last[x : x + 1, :] = core[x, rows_y - 1 : rows_y, :]
+        y_first[x : x + 1, :] = core[x, 0:1, :]
+
+
+def source_kernel(step, core, y_faces, seeds, high, low, table_high, table_low, pad):
+    coarse = seeds.shape[1] // step
+    fine = seeds[2 * coarse : 2 * coarse + step, :]
+    turned = seeds[2 * coarse + step : 2 * coarse + 2 * step, :]
+    for k in range(coarse):
+        rows = slice(k * step, (k + 1) * step)
+        value = seeds[k : k + 1, :] * fine + seeds[coarse + k : coarse + k + 1, :] * turned
+        table_high[rows, :], table_low[rows, :] = split(value, 2)
     rows_x, rows_y, cells_z = core.shape
     pad[:, 8 : rows_y + 8, :] = core[...]
     for x in range(rows_x):
         pad[x, 7:8, :] = y_faces[0, x : x + 1, :]
         pad[x, rows_y + 8 : rows_y + 9, :] = y_faces[1, x : x + 1, :]
 
-    @pl.loop(1, rows_x - 1)
+    @pl.loop(1, rows_x - 1, unroll=3)
     def _(x):
         def at(dx, dy):
             return pad[x + dx, 8 + dy : 8 + dy + rows_y, :]
@@ -181,28 +207,54 @@
     grid_x, grid_y = tiles_x * rows_x, tiles_y * rows_y
     count = slab.shape[1]
     per = LANES // rows_y
+    chunk = rows_x * count
+
+    def stacked(pieces):
+        high, low = pieces
+        zero = jnp.zeros_like(high)
+        return jnp.concatenate(
+            [jnp.concatenate([high, low], 1), jnp.concatenate([high, zero], 1)], 0
+        )
+
+    def joined(value):
+        width = value.shape[1] // 2
+        return value[:, :width] + value[:, width:]
+
+    along_y = stacked((hy_high[...], hy_low[...]))
+    along_x = jnp.concatenate([hx_high[...], hx_low[...]], 1)
+    high, low = hf_high[...], hf_low[...]
+    along_f = jnp.concatenate(
+        [jnp.concatenate([high, high], 1), jnp.concatenate([low, jnp.zeros_like(low)], 1)], 0
+    )
+
+    def times_y(value):
+        return joined(dot(jnp.concatenate(split(value, 2), 1), along_y))
+
     for i in range(tiles_x):
         for part in range(rows_x // per):
             lanes = slice(part * LANES, (part + 1) * LANES)
+            lines = [[] for _ in range(per)]
             for wide in range(tiles_y // per):
                 rows = [slab[i * tiles_y + wide * per + j, :, lanes] for j in range(per)]
                 for t, row in enumerate(swap_groups(rows, rows_y)):
-                    x = i * rows_x + part * per + t
-                    planes[x * count : (x + 1) * count, wide * LANES : (wide + 1) * LANES] = row
-    hx = (hx_high[...], hx_low[...])
-    hy = (hy_high[...], hy_low[...])
-    hf = (hf_high[...], hf_low[...])
-    planes[...] = dot3(split(planes[...], 2), hy)
+                    lines[t].append(row)
+            x = (i * rows_x + part * per) * count
+            block = jnp.concatenate([jnp.concatenate(line, 1) for line in lines], 0)
+            planes[x : x + per * count, :] = times_y(block)
     for q in range(count):
         rows = pl.ds(q, grid_x, stride=count)
-        modes = dot3(hx, split(planes[rows, :], 2))
+        modes = joined(dot(along_x, stacked(split(planes[rows, :], 2))))
         eigen = lap_xy[...] + lap_z[first[0] + q]
         anchor = eigen == 0.0
         solved = jnp.where(anchor, 0.0, scale / jnp.where(anchor, -1.0, eigen)) * modes
-        back = dot3(hx, split(solved, 2))
+        back = joined(dot(along_x, stacked(split(solved, 2))))
         solved_planes[rows, :] = back
-        faces[pl.ds(q, 2 * tiles_y, stride=count), :] = dot3(hf, split(back, 2), NT)
-    planes[...] = dot3(split(solved_planes[...], 2), hy)
+        pieces = jnp.concatenate(split(back, 2), 1)
+        value = dot(along_f, pieces, NT)
+        faces[pl.ds(q, 2 * tiles_y, stride=count), :] = value[: 2 * tiles_y] + value[2 * tiles_y :]
+    for i in range(tiles_x):
+        rows = slice(i * chunk, (i + 1) * chunk)
+        planes[rows, :] = times_y(solved_planes[rows, :])
 
     lane = lax.broadcasted_iota(jnp.int32, (count, LANES), 1)
     for i in range(tiles_x):
@@ -311,8 +363,8 @@
 
 def block_kernel(
     planes, half, core, x_faces, y_faces, spectrum, high, low, slots,
-    first_half, second_half, labels,
-    cells, spread, values,
+    out, values, labels,
+    cells, spread,
 ):
     rows_x, rows_y, cells_z = core.shape
     inner = rows_x * rows_y
@@ -378,11 +430,15 @@
         label = jnp.sum(jnp.where(lane == place + part * half, by_lane, 0.0), axis=0, keepdims=True)
         labels[part] = label.astype(jnp.int32)
 
+    fill_slots(0, values, slots, out)
+
+
+def fill_slots(part, values, slots, out):
+    count = slots.shape[1]
     pieces = split(values[...], 3)
-    for part, out in enumerate((first_half, second_half)):
-        rows = lax.broadcasted_iota(jnp.int32, (count, count), 0) + part * count
-        chosen = (slots[...] == rows).astype(BF16)
-        out[...] = dot(chosen, pieces[0], NT) + dot(chosen, pieces[1], NT) + dot(chosen, pieces[2], NT)
+    number = lax.broadcasted_iota(jnp.int32, (count, count), 0) + part * count
+    chosen = (slots[...] == number).astype(BF16)
+    out[...] = dot(chosen, pieces[0], NT) + dot(chosen, pieces[1], NT) + dot(chosen, pieces[2], NT)
 
 
 def spline(shift):
@@ -437,7 +493,8 @@
                 )
                 for axis, diff in enumerate((x_diff, y_low - y_top, z_low - z_top)):
                     for k, weight in enumerate(spline(jnp.clip(diff * 0.5, -1.0, 1.0))):
-                        weights[axis * 5 + k, a * 8 + e] = weight
+                        if (axis, k) != (1, 2):
+                            weights[axis * 5 + k, a * 8 + e] = weight
 
         top_lanes = pl.ds(pl.multiple_of(g * LANES, LANES), LANES)
         rest_lanes = pl.ds(pl.multiple_of(slots + g * LANES, LANES), LANES)
@@ -448,22 +505,21 @@
                 for k in depths:
                     at = a * 8 + (s - k)
                     w_z = weights[10 + k, at]
-                    w_y = [weights[5 + j, at] for j in range(5)]
+                    w_y = [weights[5 + j, at] if j != 2 else None for j in range(5)]
                     for i in range(5):
                         plane = weights[i, at] * w_z
                         for j in range(5):
                             key = (a + i, j)
-                            term = plane * w_y[j]
+                            term = plane * w_y[j] if j != 2 else plane
                             sums[key] = sums[key] + term if key in sums else term
                 for u in [a] if a < 7 else range(7, 12):
-                    head = sums[u, 0]
-                    tail = jnp.zeros_like(head)
-                    for j in range(1, 5):
-                        moved = pltpu.roll(sums[u, j], j, 0)
-                        head = head + jnp.where(sub >= j, moved, 0.0)
-                        tail = tail + jnp.where(sub < j, moved, 0.0)
-                    both = jnp.concatenate([head, tail], 0)
-                    top, rest = split(both, 2)
+                    rows = [sums[u, j] for j in range(5)]
+                    rows[2] = rows[2] - ((rows[0] + rows[1]) + (rows[3] + rows[4]))
+                    moved = [pltpu.roll(rows[j], j, 0) for j in range(1, 5)]
+                    every = rows[0] + ((moved[0] + moved[1]) + (moved[2] + moved[3]))
+                    past = [jnp.where(sub < j + 1, moved[j], 0.0) for j in range(4)]
+                    tail = (past[0] + past[1]) + (past[2] + past[3])
+                    top, rest = split(jnp.concatenate([every - tail, tail], 0), 2)
                     out = pl.ds(pl.multiple_of((s * 12 + u) * 16, 16), 16)
                     pieces[out, top_lanes] = top
                     pieces[out, rest_lanes] = rest
@@ -558,25 +614,37 @@
         [], 8, 2 * tiles * LANES * blocks, 8 * blocks,
     )(owner.reshape(blocks, 1), owner.reshape(1, blocks), window.reshape(1, blocks))
 
-    last_x, last_y = rows_x - 1, rows_y - 1
-    y_faces = jnp.stack([send(potential[:, last_y], "py", 1), send(potential[:, 0], "py", -1)])
+    line = shape(rows_x, cells_z)
+    core, y_last, y_first = pl.pallas_call(
+        prepare_kernel,
+        out_shape=(shape(rows_x, rows_y, cells_z), line, line),
+        in_specs=[FAR],
+        out_specs=[VMEM] * 3,
+        scratch_shapes=[pltpu.SemaphoreType.DMA],
+        compiler_params=pltpu.CompilerParams(vmem_limit_bytes=8 << 20),
+        cost_estimate=pl.CostEstimate(flops=0, bytes_accessed=2 << 20, transcendentals=0),
+    )(potential)
+    last_x = rows_x - 1
+    y_faces = jnp.stack([send(y_last, "py", 1), send(y_first, "py", -1)])
     x_lines = [
-        jnp.concatenate([y_faces[0, x : x + 1], potential[x], y_faces[1, x : x + 1]])
+        jnp.concatenate([y_faces[0, x : x + 1], core[x], y_faces[1, x : x + 1]])
         for x in (last_x, 0)
     ]
     x_faces = jnp.stack([send(x_lines[0], "px", 1), send(x_lines[1], "px", -1)])
 
-    z_high, z_low = pieces_of(table_of(cells_z))
     halves = shape(inner, cells_z, dtype=BF16)
-    source = call(
-        source_kernel, (halves, halves), [pltpu.VMEM((rows_x, rows_y + 16, cells_z), F32)],
+    table = shape(cells_z, cells_z, dtype=BF16)
+    step = 16
+    *source, z_high, z_low = call(
+        functools.partial(source_kernel, step), (halves, halves, table, table),
+        [pltpu.VMEM((rows_x, rows_y + 16, cells_z), F32)],
         8, 60 * inner * cells_z, 2 << 20,
-    )(potential, y_faces)
+    )(core, y_faces, seeds_of(cells_z, step))
     spectrum = call(
         spectrum_kernel, shape(cells_z, inner),
         [pltpu.VMEM((3, rows_y + 16, cells_z), F32)] + [pltpu.VMEM((inner, cells_z), BF16)] * 2,
         12, 6 * inner * cells_z**2, 2 << 20,
-    )(potential, y_faces, x_faces, *source, z_high, z_low)
+    )(core, y_faces, x_faces, *source, z_high, z_low)
     slab = exchange(spectrum).reshape(tiles, planes, inner)
 
     scale = SECOND_ORDER / (grid_x * grid_y * cells_z)
@@ -610,21 +678,23 @@
 
     width = -(-10 * blocks_z // LANES) * LANES
     cells = pltpu.VMEM((used, cells_z), F32)
-    tile_args = (potential, x_faces, y_faces, modes, z_high, z_low)
-    *sent, arrived_labels = call(
+    tile_args = (core, x_faces, y_faces, modes, z_high, z_low)
+    half_out = shape(blocks, ROWS)
+    sent, values, arrived_labels = call(
         functools.partial(block_kernel, planes, half),
-        (shape(blocks, ROWS), shape(blocks, ROWS), shape(2, 1, blocks, dtype=jnp.int32)),
-        [cells, pltpu.VMEM((width // LANES, used, LANES), F32), pltpu.VMEM((ROWS, blocks), F32)],
-        24, 20 * used * cells_z**2, 6 << 20,
+        (half_out, shape(ROWS, blocks), shape(2, 1, blocks, dtype=jnp.int32)),
+        [cells, pltpu.VMEM((width // LANES, used, LANES), F32)],
+        40, 20 * used * cells_z**2, 6 << 20,
     )(*tile_args, slots)
+    first = exchange(sent)
+    later = call(functools.partial(fill_slots, 1), half_out, [], 16, 6 * ROWS * blocks**2, 4 << 20)(values, slots)
     displacement = call(
         displacement_kernel, shape(3, rows_x, rows_y, cells_z),
         [pltpu.VMEM((rows_x, rows_y + 16, cells_z), F32), cells],
         16, 6 * used * cells_z**2, 4 << 20,
     )(*tile_args)
 
-    first = exchange(sent[0])
-    later, displacement = lax.optimization_barrier((sent[1], displacement))
+    later, displacement = lax.optimization_barrier((later, displacement))
     arrived = first, exchange(later)
     tile_shape = (rows_x + 4, rows_y + 8, cells_z)
     scratch = [
@@ -639,7 +709,7 @@
     tile = call(
         functools.partial(deposit_kernel, *sizes, False), shape(*tile_shape), scratch, 32, *cost
     )(arrived[0], arrived_labels[0])
-    core, x_rims, y_rims = call(
+    middle, x_rims, y_rims = call(
         functools.partial(deposit_kernel, *sizes, True),
         (
             shape(rows_x, rows_y, cells_z), shape(2, 2, rows_y, cells_z),
@@ -654,7 +724,7 @@
     )
     x_sides = send(x_rims[1], "px", 1), send(x_rims[0], "px", -1)
     density = call(rim_kernel, shape(rows_x, rows_y, cells_z), [], 8, inner * cells_z, 2 << 20)(
-        core, *y_sides, *x_sides
+        middle, *y_sides, *x_sides
     )
     return (displacement, density)
 

time: 149 us -> 144 us (0.966)
  Pallas kernels: 36.9 us -> 34.1 us
  local copies, waits for them, and re-layouts: 4.95 us -> 3.04 us
    pallas_call x2 -> x4, Pallas kernels: 7.05 us -> 5.95 us  [the longest x1 2.67 us: per_device(): call(functools.partial(block_kernel, planes, half), (half_out, shape(ROWS...]
  transfers between devices with their start and end apart: 11 -> 11, of which waited for: 6 -> 6; matrix products, arithmetic and copies ran while one was open for 1% -> 0% of each run, Pallas kernels for 11% -> 11%
where the time goes in v4:
time: 144 us; the launch traced here: 143 us
  waiting for transfers between devices  57.6 us (40%)
  Pallas kernels  34.1 us (24%)
  starting transfers between devices  26.1 us (18%)
  blocking collectives  21.2 us (15%)
  local copies, waits for them, and re-layouts  3.04 us (2%)
    all_to_all x3, waiting for transfers between devices, exchange(): return lax.all_to_all(x, both, split_axis=0, concat_axis=0, tiled=True)  51.9 us
    all_to_all x1, blocking collectives, exchange(): return lax.all_to_all(x, both, split_axis=0, concat_axis=0, tiled=True)  21.2 us
    ppermute x8, starting transfers between devices, send(): return lax.ppermute(x, axis, [(i, (i + step) % size) for i in range(size)])  14.5 us
    all_to_all x3, starting transfers between devices, exchange(): return lax.all_to_all(x, both, split_axis=0, concat_axis=0, tiled=True)  11.6 us
    pallas_call x1, Pallas kernels, per_device(): call(functools.partial(deposit_kernel, *sizes, True), (shape(rows_x, rows...  9.98 us
    pallas_call x1, Pallas kernels, per_device(): call(functools.partial(deposit_kernel, *sizes, False), shape(*tile_shape)...  9.87 us
    ppermute x8, waiting for transfers between devices, send(): return lax.ppermute(x, axis, [(i, (i + step) % size) for i in range(size)])  5.76 us
    pallas_call x1, Pallas kernels, per_device(): pl.pallas_call(body, out_shape=shape(tiles, planes, used), in_specs=specs...  3.87 us
  transfers between devices with their start and end apart: 11, of which 6 were waited for; matrix products, arithmetic and copies ran while one was open for 0% of the time, Pallas kernels for 11%

profile of v4, /device:TPU:0, one launch (start us, length us, event | category | flops | bytes accessed | tf_op | source)
XLA Modules:
  0.0 143.0 jit_solution(3154153152686074789)
XLA Ops:
  0.6 0.0 copy-start.1
  0.6 1.0 copy-done.1
  1.7 0.1 shard_map.131
  1.8 3.0 %collective-permute-start = (f32[32,256]{1,0:T(8,128)S(1)}, f32[32,256]{1,0:T(8,128)S(1)}, u32[]{:S(2)}, u32[]{:S(2)}) collective-permute-start(f32[32,256]{1,0:T(8,128)S(1)} %get-tuple-element.20), channel_id=1, source_target_pairs={{0,1},{1,2},{2,3},{3,4},{4,5},{5,6},{6,7},{7,0},{8,9},{9,10},{10,1... | collective-permute-start | bytes 98312 | tf_op jit(solution)/shard_map/ppermute | solution.py:101
  4.8 3.1 %collective-permute-start.1 = (f32[32,256]{1,0:T(8,128)S(1)}, f32[32,256]{1,0:T(8,128)S(1)}, u32[]{:S(2)}, u32[]{:S(2)}) collective-permute-start(f32[32,256]{1,0:T(8,128)S(1)} %get-tuple-element.21), channel_id=1, source_target_pairs={{0,7},{1,0},{2,1},{3,2},{4,3},{5,4},{6,5},{7,6},{8,15},{9,8},{10,9... | collective-permute-start | bytes 98312 | tf_op jit(solution)/shard_map/ppermute | solution.py:101
  7.9 1.8 %collective-permute-done = f32[32,256]{1,0:T(8,128)S(1)} collective-permute-done((f32[32,256]{1,0:T(8,128)S(1)}, f32[32,256]{1,0:T(8,128)S(1)}, u32[]{:S(2)}, u32[]{:S(2)}) %collective-permute-start) | collective-permute-done | bytes 32800 | tf_op jit(solution)/shard_map/ppermute | solution.py:101
  9.7 0.0 collective-permute-done.1
  9.7 0.1 collective-permute-start.2
  9.8 1.7 %collective-permute-start.3 = (f32[18,256]{1,0:T(8,128)S(1)}, f32[18,256]{1,0:T(8,128)S(1)}, u32[]{:S(2)}, u32[]{:S(2)}) collective-permute-start(f32[18,256]{1,0:T(8,128)S(1)} %pad_maximum_fusion.3), channel_id=1, source_target_pairs={{0,24},{8,0},{16,8},{24,16},{1,25},{9,1},{17,9},{25,17},{2,26},{10... | collective-permute-start | bytes 55304 | tf_op jit(solution)/shard_map/ppermute | solution.py:101
  11.6 0.0 copy-start.2
  11.6 0.8 copy-done.2
  12.4 1.6 %shard_map.132 = (bf16[512,256]{1,0:T(8,128)(2,1)S(1)}, bf16[512,256]{1,0:T(8,128)(2,1)S(1)}, bf16[256,256]{1,0:T(8,128)(2,1)S(1)}, bf16[256,256]{1,0:T(8,128)(2,1)S(1)}) custom-call(f32[32,16,256]{2,1,0:T(8,128)S(1)} %get-tuple-element.19.core, f32[2,32,256]{2,1,0:T(8,128)S(1)} %pad_maximum_fusion.y_faces, f32[64,256]{1,0:T(8,128)S(1)} %copy-done.2), custom_call_target="tpu_custom_call" | custom-call | flops 7864320 | bytes 2097152 | tf_op jit(solution)/shard_map/pallas_call | solution.py:638
  14.0 0.0 copy-start.3
  14.0 0.0 collective-permute-done.2
  14.0 0.0 collective-permute-done.3
  14.1 0.0 copy-start.4
  14.1 0.0 copy-start.5
  14.1 0.0 copy-start.6
  14.1 0.0 copy-start.7
  14.1 0.0 copy-start.8
  14.1 0.0 copy-start.9
  14.1 0.0 copy-start.10
  14.2 1.3 shard_map.133
  15.4 6.2 %all-to-all-start = ((f32[32,8,512]{2,1,0:T(8,128)}), f32[32,8,512]{2,1,0:T(8,128)S(1)}, u32[]{:S(2)}, u32[]{:S(2)}) async-start(f32[32,8,512]{2,1,0:T(8,128)} %bitcast.11), calls=%async_computation | async-start | bytes 1048576 | tf_op jit(solution)/shard_map/all_to_all | solution.py:609
  21.6 0.0 copy-done.3
  21.6 0.1 copy.14.owner_col
  21.8 0.0 copy-done.4
  21.8 0.2 shard_map.134
  22.0 15.9 %all-to-all-done.slab = f32[32,8,512]{2,1,0:T(8,128)S(1)} async-done(((f32[32,8,512]{2,1,0:T(8,128)}), f32[32,8,512]{2,1,0:T(8,128)S(1)}, u32[]{:S(2)}, u32[]{:S(2)}) %all-to-all-start) | async-done | bytes 524320 | tf_op jit(solution)/shard_map/all_to_all | solution.py:609
  38.0 0.0 copy-done.5
  38.0 0.0 copy-done.6
  38.0 0.0 copy-done.7
  38.0 0.0 copy-done.8
  38.0 0.0 copy-done.9
  38.0 0.0 copy-done.10
  38.0 3.9 %shard_map.135 = f32[32,8,640]{2,1,0:T(8,128)S(1)} custom-call(s32[1]{0:T(128)} %bitcast.10.first, f32[256]{0:T(256)S(1)} %copy-done.10, f32[32,8,512]{2,1,0:T(8,128)S(1)} %all-to-all-done.slab, f32[32,128]{1,0:T(8,128)S(1)} %get-tuple-element.26.labels, f32[128,128]{1,0:T(8,128)S(1)} %copy-done.5, bf16[128,128]{1,0:T(8,128)(2,1)S(1)} %copy-done.6, ...), custom_call_target="tpu_custom_call" | custom-call | flops 402653184 | bytes 2097152 | tf_op jit(solution)/shard_map/pallas_call | solution.py:660
  41.9 21.2 %all_to_all.39 = f32[32,8,640]{2,1,0:T(8,128)S(1)} all-to-all(f32[32,8,640]{2,1,0:T(8,128)S(1)} %shard_map.135), channel_id=1, replica_groups=mesh['px'=4,'py'=8] {'px','py'}, dimensions={0} | all-to-all | bytes 1310720 | tf_op jit(solution)/shard_map/all_to_all | solution.py:609
  63.1 2.7 %shard_map.136 = (f32[256,896]{1,0:T(8,128)S(1)}, f32[896,256]{1,0:T(8,128)S(1)}, s32[2,1,256]{2,1,0:T(1,128)S(1)}) custom-call(f32[32,16,256]{2,1,0:T(8,128)S(1)} %get-tuple-element.19.core, f32[2,18,256]{2,1,0:T(8,128)S(1)} %pad_maximum_fusion.1.x_faces, f32[2,32,256]{2,1,0:T(8,128)S(1)} %pad_maximum_fusion.y_faces, f32[256,640]{1,0:T(8,128)S(1)} %bitcast.40, ...), custom_call_target="tpu_custom_call" | custom-call | flops 838860800 | bytes 6291456 | tf_op jit(solution)/shard_map/pallas_call | solution.py:683
  65.8 0.0 copy-start
  65.8 0.9 copy-done
  66.8 2.6 %all-to-all-start.3 = ((f32[32,8,896]{2,1,0:T(8,128)}), f32[32,8,896]{2,1,0:T(8,128)S(1)}, u32[]{:S(2)}, u32[]{:S(2)}) async-start(f32[32,8,896]{2,1,0:T(8,128)} %bitcast.42), calls=%async_computation.3 | async-start | bytes 1835008 | tf_op jit(solution)/shard_map/all_to_all | solution.py:609
  69.4 2.0 %shard_map.138 = f32[3,32,16,256]{3,2,1,0:T(8,128)} custom-call(f32[32,16,256]{2,1,0:T(8,128)S(1)} %get-tuple-element.19.core, f32[2,18,256]{2,1,0:T(8,128)S(1)} %pad_maximum_fusion.1.x_faces, f32[2,32,256]{2,1,0:T(8,128)S(1)} %pad_maximum_fusion.y_faces, f32[256,640]{1,0:T(8,128)S(1)} %bitcast.41, bf16[256,256]{1,0:T(8,128)(2,1)S(1)} %get-tuple-element.24.high, ...), custom_call_target="tpu_custom_call" | custom-call | flops 251658240 | bytes 4194304 | tf_op jit(solution)/shard_map/pallas_call | solution.py:691
  71.4 1.6 %shard_map.137 = f32[256,896]{1,0:T(8,128)} custom-call(f32[896,256]{1,0:T(8,128)S(1)} %get-tuple-element.28.values, s32[1,256]{1,0:T(1,128)S(1)} %get-tuple-element.27.slots), custom_call_target="tpu_custom_call" | custom-call | flops 352321536 | bytes 4194304 | tf_op jit(solution)/shard_map/pallas_call | solution.py:690
  72.9 21.2 %all-to-all-done.3 = f32[32,8,896]{2,1,0:T(8,128)S(1)} async-done(((f32[32,8,896]{2,1,0:T(8,128)}), f32[32,8,896]{2,1,0:T(8,128)S(1)}, u32[]{:S(2)}, u32[]{:S(2)}) %all-to-all-start.3) | async-done | bytes 917536 | tf_op jit(solution)/shard_map/all_to_all | solution.py:609
  94.2 2.8 %all-to-all-start.2 = ((f32[32,8,896]{2,1,0:T(8,128)}), f32[32,8,896]{2,1,0:T(8,128)S(1)}, u32[]{:S(2)}, u32[]{:S(2)}) async-start(f32[32,8,896]{2,1,0:T(8,128)} %bitcast.16), calls=%async_computation.2 | async-start | bytes 1835008 | tf_op jit(solution)/shard_map/all_to_all | solution.py:609
  97.0 9.9 %shard_map.139.refs_0_ = f32[36,24,256]{2,1,0:T(8,128)S(1)} custom-call(f32[256,896]{1,0:T(8,128)S(1)} %bitcast.38, s32[1,256]{1,0:T(1,128)S(1)} %get-tuple-element.46.labels), custom_call_target="tpu_custom_call" | custom-call | flops 39321600 | bytes 4194304 | tf_op jit(solution)/shard_map/pallas_call | solution.py:709
  106.9 14.7 %all-to-all-done.2 = f32[32,8,896]{2,1,0:T(8,128)S(1)} async-done(((f32[32,8,896]{2,1,0:T(8,128)}), f32[32,8,896]{2,1,0:T(8,128)S(1)}, u32[]{:S(2)}, u32[]{:S(2)}) %all-to-all-start.2) | async-done | bytes 917536 | tf_op jit(solution)/shard_map/all_to_all | solution.py:609
  121.6 10.0 %shard_map.140 = (f32[32,16,256]{2,1,0:T(8,128)S(1)}, f32[2,2,16,256]{3,2,1,0:T(8,128)S(1)}, f32[2,36,2,256]{3,2,1,0:T(2,128)S(1)}) custom-call(f32[256,896]{1,0:T(8,128)S(1)} %bitcast.39, s32[1,256]{1,0:T(1,128)S(1)} %get-tuple-element.47.labels, f32[36,24,256]{2,1,0:T(8,128)S(1)} %shard_map.139.refs_0_), custom_call_target="tpu_custom_call" | custom-call | flops 39321600 | bytes 4194304 | tf_op jit(solution)/shard_map/pallas_call | solution.py:712
  131.6 0.8 collective-permute-start.4
  132.4 4.0 %collective-permute-start.5 = (f32[36,2,256]{2,1,0:T(2,128)S(1)}, f32[36,2,256]{2,1,0:T(2,128)S(1)}, u32[]{:S(2)}, u32[]{:S(2)}) collective-permute-start(f32[36,2,256]{2,1,0:T(2,128)S(1)} %get-tuple-element.38), channel_id=1, source_target_pairs={{0,7},{1,0},{2,1},{3,2},{4,3},{5,4},{6,5},{7,6},{8,15},{9,8},{10,9... | collective-permute-start | bytes 221192 | tf_op jit(solution)/shard_map/ppermute | solution.py:101
  136.4 2.3 %collective-permute-done.4.y_low = f32[36,2,256]{2,1,0:T(2,128)S(1)} collective-permute-done((f32[36,2,256]{2,1,0:T(2,128)S(1)}, f32[36,2,256]{2,1,0:T(2,128)S(1)}, u32[]{:S(2)}, u32[]{:S(2)}) %collective-permute-start.4) | collective-permute-done | bytes 73760 | tf_op jit(solution)/shard_map/ppermute | solution.py:101
  138.7 0.0 collective-permute-done.5.y_top
  138.7 0.1 collective-permute-start.6
  138.8 1.7 %collective-permute-start.7 = (f32[2,16,256]{2,1,0:T(8,128)S(1)}, f32[2,16,256]{2,1,0:T(8,128)S(1)}, u32[]{:S(2)}, u32[]{:S(2)}) collective-permute-start(f32[2,16,256]{2,1,0:T(8,128)S(1)} %get-tuple-element.40), channel_id=1, source_target_pairs={{0,24},{8,0},{16,8},{24,16},{1,25},{9,1},{17,9},{25,17},{2,26},{10... | collective-permute-start | bytes 98312 | tf_op jit(solution)/shard_map/ppermute | solution.py:101
  140.5 1.6 %collective-permute-done.6.x_low = f32[2,16,256]{2,1,0:T(8,128)S(1)} collective-permute-done((f32[2,16,256]{2,1,0:T(8,128)S(1)}, f32[2,16,256]{2,1,0:T(8,128)S(1)}, u32[]{:S(2)}, u32[]{:S(2)}) %collective-permute-start.6) | collective-permute-done | bytes 32800 | tf_op jit(solution)/shard_map/ppermute | solution.py:101
  142.1 0.0 collective-permute-done.7.x_top
  142.1 0.9 shard_map.142
  (11 shorter events, 0.1 us)
Async XLA Ops:
  0.6 1.0 copy-start.1
  1.8 8.0 %collective-permute-start = (f32[32,256]{1,0:T(8,128)S(1)}, f32[32,256]{1,0:T(8,128)S(1)}, u32[]{:S(2)}, u32[]{:S(2)}) collective-permute-start(f32[32,256]{1,0:T(8,128)S(1)} %get-tuple-element.20), channel_id=1, source_target_pairs={{0,1},{1,2},{2,3},{3,4},{4,5},{5,6},{6,7},{7,0},{8,9},{9,10},{10,1... | collective-permute-start | bytes 98312 | tf_op jit(solution)/shard_map/ppermute | solution.py:101
  4.8 4.9 %collective-permute-start.1 = (f32[32,256]{1,0:T(8,128)S(1)}, f32[32,256]{1,0:T(8,128)S(1)}, u32[]{:S(2)}, u32[]{:S(2)}) collective-permute-start(f32[32,256]{1,0:T(8,128)S(1)} %get-tuple-element.21), channel_id=1, source_target_pairs={{0,7},{1,0},{2,1},{3,2},{4,3},{5,4},{6,5},{7,6},{8,15},{9,8},{10,9... | collective-permute-start | bytes 98312 | tf_op jit(solution)/shard_map/ppermute | solution.py:101
  9.7 4.3 %collective-permute-start.2 = (f32[18,256]{1,0:T(8,128)S(1)}, f32[18,256]{1,0:T(8,128)S(1)}, u32[]{:S(2)}, u32[]{:S(2)}) collective-permute-start(f32[18,256]{1,0:T(8,128)S(1)} %pad_maximum_fusion.2), channel_id=1, source_target_pairs={{0,8},{8,16},{16,24},{24,0},{1,9},{9,17},{17,25},{25,1},{2,10},{10... | collective-permute-start | bytes 55304 | tf_op jit(solution)/shard_map/ppermute | solution.py:101
  9.8 4.2 %collective-permute-start.3 = (f32[18,256]{1,0:T(8,128)S(1)}, f32[18,256]{1,0:T(8,128)S(1)}, u32[]{:S(2)}, u32[]{:S(2)}) collective-permute-start(f32[18,256]{1,0:T(8,128)S(1)} %pad_maximum_fusion.3), channel_id=1, source_target_pairs={{0,24},{8,0},{16,8},{24,16},{1,25},{9,1},{17,9},{25,17},{2,26},{10... | collective-permute-start | bytes 55304 | tf_op jit(solution)/shard_map/ppermute | solution.py:101
  11.6 0.8 copy-start.2
  14.0 7.6 %copy-start.3 = (s32[1,1,256,1]{2,3,1,0:T(1,128)S(1)}, s32[1,1,256,1]{2,3,1,0:T(1,128)}, u32[]{:S(2)}) copy-start(s32[1,1,256,1]{2,3,1,0:T(1,128)} %param.13) | copy-start | bytes 3076
  14.1 7.7 %copy-start.4 = (s32[1,1,256]{2,1,0:T(1,128)S(1)}, s32[1,1,256]{2,1,0:T(1,128)}, u32[]{:S(2)}) copy-start(s32[1,1,256]{2,1,0:T(1,128)} %param.14) | copy-start | bytes 3076
  14.1 23.9 %copy-start.5 = (f32[128,128]{1,0:T(8,128)S(1)}, f32[128,128]{1,0:T(8,128)}, u32[]{:S(2)}) copy-start(f32[128,128]{1,0:T(8,128)} %constant.26.clone.lap_xy) | copy-start | bytes 196612
  14.1 23.9 %copy-start.6 = (bf16[128,128]{1,0:T(8,128)(2,1)S(1)}, bf16[128,128]{1,0:T(8,128)(2,1)}, u32[]{:S(2)}) copy-start(bf16[128,128]{1,0:T(8,128)(2,1)} %constant.27.clone.hx_high.hy_high) | copy-start | bytes 98308
  14.1 23.9 %copy-start.7 = (bf16[128,128]{1,0:T(8,128)(2,1)S(1)}, bf16[128,128]{1,0:T(8,128)(2,1)}, u32[]{:S(2)}) copy-start(bf16[128,128]{1,0:T(8,128)(2,1)} %constant.28.clone.hx_low.hy_low) | copy-start | bytes 98308
  14.1 23.9 %copy-start.8 = (bf16[16,128]{1,0:T(8,128)(2,1)S(1)}, bf16[16,128]{1,0:T(8,128)(2,1)}, u32[]{:S(2)}) copy-start(bf16[16,128]{1,0:T(8,128)(2,1)} %constant.29.clone.hf_high) | copy-start | bytes 12292
  14.1 23.9 %copy-start.9 = (bf16[16,128]{1,0:T(8,128)(2,1)S(1)}, bf16[16,128]{1,0:T(8,128)(2,1)}, u32[]{:S(2)}) copy-start(bf16[16,128]{1,0:T(8,128)(2,1)} %constant.30.clone.hf_low) | copy-start | bytes 12292
  14.1 23.9 %copy-start.10 = (f32[256]{0:T(256)S(1)}, f32[256]{0:T(256)}, u32[]{:S(2)}) copy-start(f32[256]{0:T(256)} %constant.25.clone.lap_z) | copy-start | bytes 3076
  15.4 22.5 %all-to-all-start = ((f32[32,8,512]{2,1,0:T(8,128)}), f32[32,8,512]{2,1,0:T(8,128)S(1)}, u32[]{:S(2)}, u32[]{:S(2)}) async-start(f32[32,8,512]{2,1,0:T(8,128)} %bitcast.11), calls=%async_computation | async-start | bytes 1048576 | tf_op jit(solution)/shard_map/all_to_all | solution.py:609
  65.8 1.0 copy-start
  66.8 27.4 %all-to-all-start.3 = ((f32[32,8,896]{2,1,0:T(8,128)}), f32[32,8,896]{2,1,0:T(8,128)S(1)}, u32[]{:S(2)}, u32[]{:S(2)}) async-start(f32[32,8,896]{2,1,0:T(8,128)} %bitcast.42), calls=%async_computation.3 | async-start | bytes 1835008 | tf_op jit(solution)/shard_map/all_to_all | solution.py:609
  94.2 27.4 %all-to-all-start.2 = ((f32[32,8,896]{2,1,0:T(8,128)}), f32[32,8,896]{2,1,0:T(8,128)S(1)}, u32[]{:S(2)}, u32[]{:S(2)}) async-start(f32[32,8,896]{2,1,0:T(8,128)} %bitcast.16), calls=%async_computation.2 | async-start | bytes 1835008 | tf_op jit(solution)/shard_map/all_to_all | solution.py:609
  131.6 7.1 %collective-permute-start.4 = (f32[36,2,256]{2,1,0:T(2,128)S(1)}, f32[36,2,256]{2,1,0:T(2,128)S(1)}, u32[]{:S(2)}, u32[]{:S(2)}) collective-permute-start(f32[36,2,256]{2,1,0:T(2,128)S(1)} %get-tuple-element.39), channel_id=1, source_target_pairs={{0,1},{1,2},{2,3},{3,4},{4,5},{5,6},{6,7},{7,0},{8,9},{9,10},{10,1... | collective-permute-start | bytes 221192 | tf_op jit(solution)/shard_map/ppermute | solution.py:101
  132.4 6.3 %collective-permute-start.5 = (f32[36,2,256]{2,1,0:T(2,128)S(1)}, f32[36,2,256]{2,1,0:T(2,128)S(1)}, u32[]{:S(2)}, u32[]{:S(2)}) collective-permute-start(f32[36,2,256]{2,1,0:T(2,128)S(1)} %get-tuple-element.38), channel_id=1, source_target_pairs={{0,7},{1,0},{2,1},{3,2},{4,3},{5,4},{6,5},{7,6},{8,15},{9,8},{10,9... | collective-permute-start | bytes 221192 | tf_op jit(solution)/shard_map/ppermute | solution.py:101
  138.7 3.4 %collective-permute-start.6 = (f32[2,16,256]{2,1,0:T(8,128)S(1)}, f32[2,16,256]{2,1,0:T(8,128)S(1)}, u32[]{:S(2)}, u32[]{:S(2)}) collective-permute-start(f32[2,16,256]{2,1,0:T(8,128)S(1)} %get-tuple-element.41), channel_id=1, source_target_pairs={{0,8},{8,16},{16,24},{24,0},{1,9},{9,17},{17,25},{25,1},{2,10},{10... | collective-permute-start | bytes 98312 | tf_op jit(solution)/shard_map/ppermute | solution.py:101
  138.8 3.3 %collective-permute-start.7 = (f32[2,16,256]{2,1,0:T(8,128)S(1)}, f32[2,16,256]{2,1,0:T(8,128)S(1)}, u32[]{:S(2)}, u32[]{:S(2)}) collective-permute-start(f32[2,16,256]{2,1,0:T(8,128)S(1)} %get-tuple-element.40), channel_id=1, source_target_pairs={{0,24},{8,0},{16,8},{24,16},{1,25},{9,1},{17,9},{25,17},{2,26},{10... | collective-permute-start | bytes 98312 | tf_op jit(solution)/shard_map/ppermute | solution.py:101

commit v5 on v4

--- a/solution.py
+++ b/solution.py
@@ -70,14 +70,6 @@
     return np.asarray(high), np.asarray(low)
 
 
-def seeds_of(length, step):
-    along = np.arange(length)
-    coarse = (np.arange(length // step)[:, None] * step * along[None, :] % length) * (2.0 * math.pi / length)
-    fine = (np.arange(step)[:, None] * along[None, :] % length) * (2.0 * math.pi / length)
-    rows = [np.cos(coarse), np.sin(coarse), np.cos(fine) + np.sin(fine), np.cos(fine) - np.sin(fine)]
-    return np.concatenate(rows).astype(np.float32)
-
-
 def laplace_of(length):
     return (2.0 * np.cos(np.arange(length) * (2.0 * math.pi / length)) - 2.0).astype(np.float32)
 
@@ -148,15 +140,23 @@
         y_first[x : x + 1, :] = core[x, 0:1, :]
 
 
-def source_kernel(step, core, y_faces, seeds, high, low, table_high, table_low, pad):
-    coarse = seeds.shape[1] // step
-    fine = seeds[2 * coarse : 2 * coarse + step, :]
-    turned = seeds[2 * coarse + step : 2 * coarse + 2 * step, :]
+def source_kernel(step, core, y_faces, high, low, table_high, table_low, pad):
+    rows_x, rows_y, cells_z = core.shape
+    coarse = cells_z // step
+
+    def turns(count, stride):
+        row = lax.broadcasted_iota(jnp.int32, (count, cells_z), 0) * stride
+        col = lax.broadcasted_iota(jnp.int32, (count, cells_z), 1)
+        angle = (row * col % cells_z).astype(F32) * (2.0 * math.pi / cells_z)
+        return jnp.cos(angle), jnp.sin(angle)
+
+    wide_cos, wide_sin = turns(coarse, step)
+    fine_cos, fine_sin = turns(step, 1)
+    fine, turned = fine_cos + fine_sin, fine_cos - fine_sin
     for k in range(coarse):
         rows = slice(k * step, (k + 1) * step)
-        value = seeds[k : k + 1, :] * fine + seeds[coarse + k : coarse + k + 1, :] * turned
+        value = wide_cos[k : k + 1] * fine + wide_sin[k : k + 1] * turned
         table_high[rows, :], table_low[rows, :] = split(value, 2)
-    rows_x, rows_y, cells_z = core.shape
     pad[:, 8 : rows_y + 8, :] = core[...]
     for x in range(rows_x):
         pad[x, 7:8, :] = y_faces[0, x : x + 1, :]
@@ -202,7 +202,7 @@
 def solve_kernel(
     tiles_x, tiles_y, rows_x, rows_y, scale,
     first, lap_z, slab, labels, lap_xy, hx_high, hx_low, hy_high, hy_low, hf_high, hf_low,
-    out, planes, solved_planes, faces,
+    out, planes, solved_planes, lines, faces,
 ):
     grid_x, grid_y = tiles_x * rows_x, tiles_y * rows_y
     count = slab.shape[1]
@@ -222,24 +222,19 @@
 
     along_y = stacked((hy_high[...], hy_low[...]))
     along_x = jnp.concatenate([hx_high[...], hx_low[...]], 1)
-    high, low = hf_high[...], hf_low[...]
-    along_f = jnp.concatenate(
-        [jnp.concatenate([high, high], 1), jnp.concatenate([low, jnp.zeros_like(low)], 1)], 0
-    )
-
     def times_y(value):
         return joined(dot(jnp.concatenate(split(value, 2), 1), along_y))
 
     for i in range(tiles_x):
         for part in range(rows_x // per):
             lanes = slice(part * LANES, (part + 1) * LANES)
-            lines = [[] for _ in range(per)]
+            found = [[] for _ in range(per)]
             for wide in range(tiles_y // per):
                 rows = [slab[i * tiles_y + wide * per + j, :, lanes] for j in range(per)]
                 for t, row in enumerate(swap_groups(rows, rows_y)):
-                    lines[t].append(row)
+                    found[t].append(row)
             x = (i * rows_x + part * per) * count
-            block = jnp.concatenate([jnp.concatenate(line, 1) for line in lines], 0)
+            block = jnp.concatenate([jnp.concatenate(line, 1) for line in found], 0)
             planes[x : x + per * count, :] = times_y(block)
     for q in range(count):
         rows = pl.ds(q, grid_x, stride=count)
@@ -249,12 +244,20 @@
         solved = jnp.where(anchor, 0.0, scale / jnp.where(anchor, -1.0, eigen)) * modes
         back = joined(dot(along_x, stacked(split(solved, 2))))
         solved_planes[rows, :] = back
-        pieces = jnp.concatenate(split(back, 2), 1)
-        value = dot(along_f, pieces, NT)
-        faces[pl.ds(q, 2 * tiles_y, stride=count), :] = value[: 2 * tiles_y] + value[2 * tiles_y :]
+    sides = 2 * tiles_y
+    along_f = stacked((hf_high[...], hf_low[...]))
     for i in range(tiles_x):
         rows = slice(i * chunk, (i + 1) * chunk)
-        planes[rows, :] = times_y(solved_planes[rows, :])
+        pieces = jnp.concatenate(split(solved_planes[rows, :], 2), 1)
+        planes[rows, :] = joined(dot(pieces, along_y))
+        lines[rows, :] = joined(dot(pieces, along_f))
+    for start in range(0, count, LANES // sides):
+        block = None
+        for q in range(start, start + LANES // sides):
+            item = lines[pl.ds(q, grid_x, stride=count), :]
+            item = pltpu.roll(item, (q - start) * sides, 1) if q > start else item
+            block = item if block is None else block + item
+        faces[start * sides : start * sides + LANES, :] = jnp.transpose(block)
 
     lane = lax.broadcasted_iota(jnp.int32, (count, LANES), 1)
     for i in range(tiles_x):
@@ -278,8 +281,8 @@
                 moved = pltpu.roll(after, (shift + rows_y) % LANES, 1)
                 line = jnp.where(lane < rows_y, line, moved)
                 for side in range(2):
-                    at = (side * tiles_y + j) * count
-                    face = faces[at : at + count, :]
+                    at = side * tiles_y + j
+                    face = faces[pl.ds(at, count, stride=sides), :]
                     start = 2 * rows_y + side * rows_x
                     move = (start - i * rows_x) % LANES
                     face = pltpu.roll(face, move, 1) if move else face
@@ -639,7 +642,7 @@
         functools.partial(source_kernel, step), (halves, halves, table, table),
         [pltpu.VMEM((rows_x, rows_y + 16, cells_z), F32)],
         8, 60 * inner * cells_z, 2 << 20,
-    )(core, y_faces, seeds_of(cells_z, step))
+    )(core, y_faces)
     spectrum = call(
         spectrum_kernel, shape(cells_z, inner),
         [pltpu.VMEM((3, rows_y + 16, cells_z), F32)] + [pltpu.VMEM((inner, cells_z), BF16)] * 2,
@@ -648,13 +651,15 @@
     slab = exchange(spectrum).reshape(tiles, planes, inner)
 
     scale = SECOND_ORDER / (grid_x * grid_y * cells_z)
-    if planes % 8 == 0 and tiles_y % (LANES // rows_y) == 0 and grid_x == LANES:
+    if planes % 8 == 0 and tiles_y % (LANES // rows_y) == 0 and grid_x == LANES and 2 * tiles_y <= LANES and planes % (LANES // (2 * tiles_y)) == 0:
         first = (lax.axis_index(both) * planes).astype(jnp.int32).reshape(1)
         x_table, y_table = table_of(grid_x), table_of(grid_y)
         starts = np.arange(tiles_y) * rows_y
         edge = np.concatenate([(starts - 1) % grid_y, (starts + rows_y) % grid_y])
         lap_xy = laplace_of(grid_x)[:, None] + laplace_of(grid_y)[None, :]
-        tables = pieces_of(x_table) + pieces_of(y_table) + pieces_of(y_table[edge])
+        face_table = np.zeros((grid_y, LANES), np.float32)
+        face_table[:, : 2 * tiles_y] = y_table[edge].T
+        tables = pieces_of(x_table) + pieces_of(y_table) + pieces_of(face_table)
         body = functools.partial(solve_kernel, tiles_x, tiles_y, rows_x, rows_y, scale)
         specs = [SMEM, SMEM] + [VMEM] * 9
         returned = pl.pallas_call(
@@ -665,6 +670,7 @@
             scratch_shapes=[
                 pltpu.VMEM((grid_x * planes, grid_y), F32),
                 pltpu.VMEM((grid_x * planes, grid_y), F32),
+                pltpu.VMEM((grid_x * planes, LANES), F32),
                 pltpu.VMEM((2 * tiles_y * planes, grid_x), F32),
             ],
             compiler_params=pltpu.CompilerParams(vmem_limit_bytes=16 << 20),

time: 144 us -> 142 us (0.986)
  no operation moved by 1% of the time
where the time goes in v5:
time: 142 us; the launch traced here: 141 us
  waiting for transfers between devices  57.6 us (41%)
  Pallas kernels  33.3 us (23%)
  starting transfers between devices  26.1 us (18%)
  blocking collectives  21.2 us (15%)
  local copies, waits for them, and re-layouts  2.19 us (2%)
    all_to_all x3, waiting for transfers between devices, exchange(): return lax.all_to_all(x, both, split_axis=0, concat_axis=0, tiled=True)  51.9 us
    all_to_all x1, blocking collectives, exchange(): return lax.all_to_all(x, both, split_axis=0, concat_axis=0, tiled=True)  21.2 us
    ppermute x8, starting transfers between devices, send(): return lax.ppermute(x, axis, [(i, (i + step) % size) for i in range(size)])  14.5 us
    all_to_all x3, starting transfers between devices, exchange(): return lax.all_to_all(x, both, split_axis=0, concat_axis=0, tiled=True)  11.6 us
    pallas_call x1, Pallas kernels, per_device(): call(functools.partial(deposit_kernel, *sizes, True), (shape(rows_x, rows...  9.99 us
    pallas_call x1, Pallas kernels, per_device(): call(functools.partial(deposit_kernel, *sizes, False), shape(*tile_shape)...  9.86 us
    ppermute x8, waiting for transfers between devices, send(): return lax.ppermute(x, axis, [(i, (i + step) % size) for i in range(size)])  5.76 us
    pallas_call x1, Pallas kernels, per_device(): pl.pallas_call(body, out_shape=shape(tiles, planes, used), in_specs=specs...  2.88 us
  transfers between devices with their start and end apart: 11, of which 6 were waited for; matrix products, arithmetic and copies ran while one was open for 0% of the time, Pallas kernels for 11%

profile of v5, /device:TPU:0, one launch (start us, length us, event | category | flops | bytes accessed | tf_op | source)
XLA Modules:
  0.0 141.4 jit_solution(7165299496411196261)
XLA Ops:
  0.6 0.0 copy-start.1
  0.6 1.0 copy-done.1
  1.7 0.1 shard_map.122
  1.8 3.0 %collective-permute-start = (f32[32,256]{1,0:T(8,128)S(1)}, f32[32,256]{1,0:T(8,128)S(1)}, u32[]{:S(2)}, u32[]{:S(2)}) collective-permute-start(f32[32,256]{1,0:T(8,128)S(1)} %get-tuple-element.20), channel_id=1, source_target_pairs={{0,1},{1,2},{2,3},{3,4},{4,5},{5,6},{6,7},{7,0},{8,9},{9,10},{10,1... | collective-permute-start | bytes 98312 | tf_op jit(solution)/shard_map/ppermute | solution.py:93
  4.8 3.1 %collective-permute-start.1 = (f32[32,256]{1,0:T(8,128)S(1)}, f32[32,256]{1,0:T(8,128)S(1)}, u32[]{:S(2)}, u32[]{:S(2)}) collective-permute-start(f32[32,256]{1,0:T(8,128)S(1)} %get-tuple-element.21), channel_id=1, source_target_pairs={{0,7},{1,0},{2,1},{3,2},{4,3},{5,4},{6,5},{7,6},{8,15},{9,8},{10,9... | collective-permute-start | bytes 98312 | tf_op jit(solution)/shard_map/ppermute | solution.py:93
  7.9 1.8 %collective-permute-done = f32[32,256]{1,0:T(8,128)S(1)} collective-permute-done((f32[32,256]{1,0:T(8,128)S(1)}, f32[32,256]{1,0:T(8,128)S(1)}, u32[]{:S(2)}, u32[]{:S(2)}) %collective-permute-start) | collective-permute-done | bytes 32800 | tf_op jit(solution)/shard_map/ppermute | solution.py:93
  9.7 0.0 collective-permute-done.1
  9.7 0.1 collective-permute-start.2
  9.8 1.7 %collective-permute-start.3 = (f32[18,256]{1,0:T(8,128)S(1)}, f32[18,256]{1,0:T(8,128)S(1)}, u32[]{:S(2)}, u32[]{:S(2)}) collective-permute-start(f32[18,256]{1,0:T(8,128)S(1)} %pad_maximum_fusion.3), channel_id=1, source_target_pairs={{0,24},{8,0},{16,8},{24,16},{1,25},{9,1},{17,9},{25,17},{2,26},{10... | collective-permute-start | bytes 55304 | tf_op jit(solution)/shard_map/ppermute | solution.py:93
  11.6 1.8 %shard_map.123 = (bf16[512,256]{1,0:T(8,128)(2,1)S(1)}, bf16[512,256]{1,0:T(8,128)(2,1)S(1)}, bf16[256,256]{1,0:T(8,128)(2,1)S(1)}, bf16[256,256]{1,0:T(8,128)(2,1)S(1)}) custom-call(f32[32,16,256]{2,1,0:T(8,128)S(1)} %get-tuple-element.19.core, f32[2,32,256]{2,1,0:T(8,128)S(1)} %pad_maximum_fusion.y_faces), custom_call_target="tpu_custom_call" | custom-call | flops 7864320 | bytes 2097152 | tf_op jit(solution)/shard_map/pallas_call | solution.py:641
  13.3 0.0 copy-start.2
  13.3 0.0 collective-permute-done.2
  13.4 0.0 collective-permute-done.3
  13.4 0.0 copy-start.3
  13.4 0.0 copy-start.4
  13.4 0.0 copy-start.5
  13.4 0.0 copy-start.6
  13.4 0.0 copy-start.7
  13.4 0.0 copy-start.8
  13.5 0.0 copy-start.9
  13.5 1.3 shard_map.124
  14.8 6.2 %all-to-all-start = ((f32[32,8,512]{2,1,0:T(8,128)}), f32[32,8,512]{2,1,0:T(8,128)S(1)}, u32[]{:S(2)}, u32[]{:S(2)}) async-start(f32[32,8,512]{2,1,0:T(8,128)} %bitcast.11), calls=%async_computation | async-start | bytes 1048576 | tf_op jit(solution)/shard_map/all_to_all | solution.py:612
  20.9 0.0 copy-done.2
  20.9 0.1 copy.13.owner_col
  21.1 0.0 copy-done.3
  21.1 0.2 shard_map.125
  21.3 15.9 %all-to-all-done.slab = f32[32,8,512]{2,1,0:T(8,128)S(1)} async-done(((f32[32,8,512]{2,1,0:T(8,128)}), f32[32,8,512]{2,1,0:T(8,128)S(1)}, u32[]{:S(2)}, u32[]{:S(2)}) %all-to-all-start) | async-done | bytes 524320 | tf_op jit(solution)/shard_map/all_to_all | solution.py:612
  37.3 0.0 copy-done.4
  37.3 0.0 copy-done.5
  37.3 0.0 copy-done.6
  37.3 0.0 copy-done.7
  37.3 0.0 copy-done.8
  37.3 0.0 copy-done.9
  37.3 2.9 %shard_map.126 = f32[32,8,640]{2,1,0:T(8,128)S(1)} custom-call(s32[1]{0:T(128)} %bitcast.10.first, f32[256]{0:T(256)S(1)} %copy-done.9, f32[32,8,512]{2,1,0:T(8,128)S(1)} %all-to-all-done.slab, f32[32,128]{1,0:T(8,128)S(1)} %get-tuple-element.26.labels, f32[128,128]{1,0:T(8,128)S(1)} %copy-done.4, bf16[128,128]{1,0:T(8,128)(2,1)S(1)} %copy-done.5, ...), custom_call_target="tpu_custom_call" | custom-call | flops 402653184 | bytes 2097152 | tf_op jit(solution)/shard_map/pallas_call | solution.py:665
  40.2 21.2 %all_to_all.39 = f32[32,8,640]{2,1,0:T(8,128)S(1)} all-to-all(f32[32,8,640]{2,1,0:T(8,128)S(1)} %shard_map.126), channel_id=1, replica_groups=mesh['px'=4,'py'=8] {'px','py'}, dimensions={0} | all-to-all | bytes 1310720 | tf_op jit(solution)/shard_map/all_to_all | solution.py:612
  61.5 2.7 %shard_map.127 = (f32[256,896]{1,0:T(8,128)S(1)}, f32[896,256]{1,0:T(8,128)S(1)}, s32[2,1,256]{2,1,0:T(1,128)S(1)}) custom-call(f32[32,16,256]{2,1,0:T(8,128)S(1)} %get-tuple-element.19.core, f32[2,18,256]{2,1,0:T(8,128)S(1)} %pad_maximum_fusion.1.x_faces, f32[2,32,256]{2,1,0:T(8,128)S(1)} %pad_maximum_fusion.y_faces, f32[256,640]{1,0:T(8,128)S(1)} %bitcast.40, ...), custom_call_target="tpu_custom_call" | custom-call | flops 838860800 | bytes 6291456 | tf_op jit(solution)/shard_map/pallas_call | solution.py:689
  64.1 0.0 copy-start
  64.1 0.9 copy-done
  65.1 2.6 %all-to-all-start.3 = ((f32[32,8,896]{2,1,0:T(8,128)}), f32[32,8,896]{2,1,0:T(8,128)S(1)}, u32[]{:S(2)}, u32[]{:S(2)}) async-start(f32[32,8,896]{2,1,0:T(8,128)} %bitcast.42), calls=%async_computation.3 | async-start | bytes 1835008 | tf_op jit(solution)/shard_map/all_to_all | solution.py:612
  67.7 2.0 %shard_map.129 = f32[3,32,16,256]{3,2,1,0:T(8,128)} custom-call(f32[32,16,256]{2,1,0:T(8,128)S(1)} %get-tuple-element.19.core, f32[2,18,256]{2,1,0:T(8,128)S(1)} %pad_maximum_fusion.1.x_faces, f32[2,32,256]{2,1,0:T(8,128)S(1)} %pad_maximum_fusion.y_faces, f32[256,640]{1,0:T(8,128)S(1)} %bitcast.41, bf16[256,256]{1,0:T(8,128)(2,1)S(1)} %get-tuple-element.24.high, ...), custom_call_target="tpu_custom_call" | custom-call | flops 251658240 | bytes 4194304 | tf_op jit(solution)/shard_map/pallas_call | solution.py:697
  69.7 1.6 %shard_map.128 = f32[256,896]{1,0:T(8,128)} custom-call(f32[896,256]{1,0:T(8,128)S(1)} %get-tuple-element.28.values, s32[1,256]{1,0:T(1,128)S(1)} %get-tuple-element.27.slots), custom_call_target="tpu_custom_call" | custom-call | flops 352321536 | bytes 4194304 | tf_op jit(solution)/shard_map/pallas_call | solution.py:696
  71.3 21.2 %all-to-all-done.3 = f32[32,8,896]{2,1,0:T(8,128)S(1)} async-done(((f32[32,8,896]{2,1,0:T(8,128)}), f32[32,8,896]{2,1,0:T(8,128)S(1)}, u32[]{:S(2)}, u32[]{:S(2)}) %all-to-all-start.3) | async-done | bytes 917536 | tf_op jit(solution)/shard_map/all_to_all | solution.py:612
  92.5 2.8 %all-to-all-start.2 = ((f32[32,8,896]{2,1,0:T(8,128)}), f32[32,8,896]{2,1,0:T(8,128)S(1)}, u32[]{:S(2)}, u32[]{:S(2)}) async-start(f32[32,8,896]{2,1,0:T(8,128)} %bitcast.16), calls=%async_computation.2 | async-start | bytes 1835008 | tf_op jit(solution)/shard_map/all_to_all | solution.py:612
  95.3 9.9 %shard_map.130.refs_0_ = f32[36,24,256]{2,1,0:T(8,128)S(1)} custom-call(f32[256,896]{1,0:T(8,128)S(1)} %bitcast.38, s32[1,256]{1,0:T(1,128)S(1)} %get-tuple-element.46.labels), custom_call_target="tpu_custom_call" | custom-call | flops 39321600 | bytes 4194304 | tf_op jit(solution)/shard_map/pallas_call | solution.py:715
  105.2 14.7 %all-to-all-done.2 = f32[32,8,896]{2,1,0:T(8,128)S(1)} async-done(((f32[32,8,896]{2,1,0:T(8,128)}), f32[32,8,896]{2,1,0:T(8,128)S(1)}, u32[]{:S(2)}, u32[]{:S(2)}) %all-to-all-start.2) | async-done | bytes 917536 | tf_op jit(solution)/shard_map/all_to_all | solution.py:612
  119.9 10.0 %shard_map.131 = (f32[32,16,256]{2,1,0:T(8,128)S(1)}, f32[2,2,16,256]{3,2,1,0:T(8,128)S(1)}, f32[2,36,2,256]{3,2,1,0:T(2,128)S(1)}) custom-call(f32[256,896]{1,0:T(8,128)S(1)} %bitcast.39, s32[1,256]{1,0:T(1,128)S(1)} %get-tuple-element.47.labels, f32[36,24,256]{2,1,0:T(8,128)S(1)} %shard_map.130.refs_0_), custom_call_target="tpu_custom_call" | custom-call | flops 39321600 | bytes 4194304 | tf_op jit(solution)/shard_map/pallas_call | solution.py:718
  129.9 0.8 collective-permute-start.4
  130.7 4.0 %collective-permute-start.5 = (f32[36,2,256]{2,1,0:T(2,128)S(1)}, f32[36,2,256]{2,1,0:T(2,128)S(1)}, u32[]{:S(2)}, u32[]{:S(2)}) collective-permute-start(f32[36,2,256]{2,1,0:T(2,128)S(1)} %get-tuple-element.38), channel_id=1, source_target_pairs={{0,7},{1,0},{2,1},{3,2},{4,3},{5,4},{6,5},{7,6},{8,15},{9,8},{10,9... | collective-permute-start | bytes 221192 | tf_op jit(solution)/shard_map/ppermute | solution.py:93
  134.7 2.3 %collective-permute-done.4.y_low = f32[36,2,256]{2,1,0:T(2,128)S(1)} collective-permute-done((f32[36,2,256]{2,1,0:T(2,128)S(1)}, f32[36,2,256]{2,1,0:T(2,128)S(1)}, u32[]{:S(2)}, u32[]{:S(2)}) %collective-permute-start.4) | collective-permute-done | bytes 73760 | tf_op jit(solution)/shard_map/ppermute | solution.py:93
  137.0 0.0 collective-permute-done.5.y_top
  137.1 0.1 collective-permute-start.6
  137.1 1.7 %collective-permute-start.7 = (f32[2,16,256]{2,1,0:T(8,128)S(1)}, f32[2,16,256]{2,1,0:T(8,128)S(1)}, u32[]{:S(2)}, u32[]{:S(2)}) collective-permute-start(f32[2,16,256]{2,1,0:T(8,128)S(1)} %get-tuple-element.40), channel_id=1, source_target_pairs={{0,24},{8,0},{16,8},{24,16},{1,25},{9,1},{17,9},{25,17},{2,26},{10... | collective-permute-start | bytes 98312 | tf_op jit(solution)/shard_map/ppermute | solution.py:93
  138.9 1.6 %collective-permute-done.6.x_low = f32[2,16,256]{2,1,0:T(8,128)S(1)} collective-permute-done((f32[2,16,256]{2,1,0:T(8,128)S(1)}, f32[2,16,256]{2,1,0:T(8,128)S(1)}, u32[]{:S(2)}, u32[]{:S(2)}) %collective-permute-start.6) | collective-permute-done | bytes 32800 | tf_op jit(solution)/shard_map/ppermute | solution.py:93
  140.5 0.0 collective-permute-done.7.x_top
  140.5 0.9 shard_map.133
  (11 shorter events, 0.1 us)
Async XLA Ops:
  0.6 1.0 copy-start.1
  1.8 8.0 %collective-permute-start = (f32[32,256]{1,0:T(8,128)S(1)}, f32[32,256]{1,0:T(8,128)S(1)}, u32[]{:S(2)}, u32[]{:S(2)}) collective-permute-start(f32[32,256]{1,0:T(8,128)S(1)} %get-tuple-element.20), channel_id=1, source_target_pairs={{0,1},{1,2},{2,3},{3,4},{4,5},{5,6},{6,7},{7,0},{8,9},{9,10},{10,1... | collective-permute-start | bytes 98312 | tf_op jit(solution)/shard_map/ppermute | solution.py:93
  4.8 4.9 %collective-permute-start.1 = (f32[32,256]{1,0:T(8,128)S(1)}, f32[32,256]{1,0:T(8,128)S(1)}, u32[]{:S(2)}, u32[]{:S(2)}) collective-permute-start(f32[32,256]{1,0:T(8,128)S(1)} %get-tuple-element.21), channel_id=1, source_target_pairs={{0,7},{1,0},{2,1},{3,2},{4,3},{5,4},{6,5},{7,6},{8,15},{9,8},{10,9... | collective-permute-start | bytes 98312 | tf_op jit(solution)/shard_map/ppermute | solution.py:93
  9.7 3.6 %collective-permute-start.2 = (f32[18,256]{1,0:T(8,128)S(1)}, f32[18,256]{1,0:T(8,128)S(1)}, u32[]{:S(2)}, u32[]{:S(2)}) collective-permute-start(f32[18,256]{1,0:T(8,128)S(1)} %pad_maximum_fusion.2), channel_id=1, source_target_pairs={{0,8},{8,16},{16,24},{24,0},{1,9},{9,17},{17,25},{25,1},{2,10},{10... | collective-permute-start | bytes 55304 | tf_op jit(solution)/shard_map/ppermute | solution.py:93
  9.8 3.5 %collective-permute-start.3 = (f32[18,256]{1,0:T(8,128)S(1)}, f32[18,256]{1,0:T(8,128)S(1)}, u32[]{:S(2)}, u32[]{:S(2)}) collective-permute-start(f32[18,256]{1,0:T(8,128)S(1)} %pad_maximum_fusion.3), channel_id=1, source_target_pairs={{0,24},{8,0},{16,8},{24,16},{1,25},{9,1},{17,9},{25,17},{2,26},{10... | collective-permute-start | bytes 55304 | tf_op jit(solution)/shard_map/ppermute | solution.py:93
  13.3 7.6 %copy-start.2 = (s32[1,1,256,1]{2,3,1,0:T(1,128)S(1)}, s32[1,1,256,1]{2,3,1,0:T(1,128)}, u32[]{:S(2)}) copy-start(s32[1,1,256,1]{2,3,1,0:T(1,128)} %param.12) | copy-start | bytes 3076
  13.4 7.7 %copy-start.3 = (s32[1,1,256]{2,1,0:T(1,128)S(1)}, s32[1,1,256]{2,1,0:T(1,128)}, u32[]{:S(2)}) copy-start(s32[1,1,256]{2,1,0:T(1,128)} %param.13) | copy-start | bytes 3076
  13.4 23.9 %copy-start.4 = (f32[128,128]{1,0:T(8,128)S(1)}, f32[128,128]{1,0:T(8,128)}, u32[]{:S(2)}) copy-start(f32[128,128]{1,0:T(8,128)} %constant.23.clone.lap_xy) | copy-start | bytes 196612
  13.4 23.9 %copy-start.5 = (bf16[128,128]{1,0:T(8,128)(2,1)S(1)}, bf16[128,128]{1,0:T(8,128)(2,1)}, u32[]{:S(2)}) copy-start(bf16[128,128]{1,0:T(8,128)(2,1)} %constant.24.clone.hx_high.hy_high) | copy-start | bytes 98308
  13.4 23.9 %copy-start.6 = (bf16[128,128]{1,0:T(8,128)(2,1)S(1)}, bf16[128,128]{1,0:T(8,128)(2,1)}, u32[]{:S(2)}) copy-start(bf16[128,128]{1,0:T(8,128)(2,1)} %constant.25.clone.hx_low.hy_low) | copy-start | bytes 98308
  13.4 23.9 %copy-start.7 = (bf16[128,128]{1,0:T(8,128)(2,1)S(1)}, bf16[128,128]{1,0:T(8,128)(2,1)}, u32[]{:S(2)}) copy-start(bf16[128,128]{1,0:T(8,128)(2,1)} %constant.26.clone.hf_high) | copy-start | bytes 98308
  13.4 23.9 %copy-start.8 = (bf16[128,128]{1,0:T(8,128)(2,1)S(1)}, bf16[128,128]{1,0:T(8,128)(2,1)}, u32[]{:S(2)}) copy-start(bf16[128,128]{1,0:T(8,128)(2,1)} %constant.27.clone.hf_low) | copy-start | bytes 98308
  13.5 23.9 %copy-start.9 = (f32[256]{0:T(256)S(1)}, f32[256]{0:T(256)}, u32[]{:S(2)}) copy-start(f32[256]{0:T(256)} %constant.22.clone.lap_z) | copy-start | bytes 3076
  14.8 22.5 %all-to-all-start = ((f32[32,8,512]{2,1,0:T(8,128)}), f32[32,8,512]{2,1,0:T(8,128)S(1)}, u32[]{:S(2)}, u32[]{:S(2)}) async-start(f32[32,8,512]{2,1,0:T(8,128)} %bitcast.11), calls=%async_computation | async-start | bytes 1048576 | tf_op jit(solution)/shard_map/all_to_all | solution.py:612
  64.1 0.9 copy-start
  65.1 27.4 %all-to-all-start.3 = ((f32[32,8,896]{2,1,0:T(8,128)}), f32[32,8,896]{2,1,0:T(8,128)S(1)}, u32[]{:S(2)}, u32[]{:S(2)}) async-start(f32[32,8,896]{2,1,0:T(8,128)} %bitcast.42), calls=%async_computation.3 | async-start | bytes 1835008 | tf_op jit(solution)/shard_map/all_to_all | solution.py:612
  92.5 27.4 %all-to-all-start.2 = ((f32[32,8,896]{2,1,0:T(8,128)}), f32[32,8,896]{2,1,0:T(8,128)S(1)}, u32[]{:S(2)}, u32[]{:S(2)}) async-start(f32[32,8,896]{2,1,0:T(8,128)} %bitcast.16), calls=%async_computation.2 | async-start | bytes 1835008 | tf_op jit(solution)/shard_map/all_to_all | solution.py:612
  129.9 7.1 %collective-permute-start.4 = (f32[36,2,256]{2,1,0:T(2,128)S(1)}, f32[36,2,256]{2,1,0:T(2,128)S(1)}, u32[]{:S(2)}, u32[]{:S(2)}) collective-permute-start(f32[36,2,256]{2,1,0:T(2,128)S(1)} %get-tuple-element.39), channel_id=1, source_target_pairs={{0,1},{1,2},{2,3},{3,4},{4,5},{5,6},{6,7},{7,0},{8,9},{9,10},{10,1... | collective-permute-start | bytes 221192 | tf_op jit(solution)/shard_map/ppermute | solution.py:93
  130.7 6.3 %collective-permute-start.5 = (f32[36,2,256]{2,1,0:T(2,128)S(1)}, f32[36,2,256]{2,1,0:T(2,128)S(1)}, u32[]{:S(2)}, u32[]{:S(2)}) collective-permute-start(f32[36,2,256]{2,1,0:T(2,128)S(1)} %get-tuple-element.38), channel_id=1, source_target_pairs={{0,7},{1,0},{2,1},{3,2},{4,3},{5,4},{6,5},{7,6},{8,15},{9,8},{10,9... | collective-permute-start | bytes 221192 | tf_op jit(solution)/shard_map/ppermute | solution.py:93
  137.1 3.4 %collective-permute-start.6 = (f32[2,16,256]{2,1,0:T(8,128)S(1)}, f32[2,16,256]{2,1,0:T(8,128)S(1)}, u32[]{:S(2)}, u32[]{:S(2)}) collective-permute-start(f32[2,16,256]{2,1,0:T(8,128)S(1)} %get-tuple-element.41), channel_id=1, source_target_pairs={{0,8},{8,16},{16,24},{24,0},{1,9},{9,17},{17,25},{25,1},{2,10},{10... | collective-permute-start | bytes 98312 | tf_op jit(solution)/shard_map/ppermute | solution.py:93
  137.1 3.3 %collective-permute-start.7 = (f32[2,16,256]{2,1,0:T(8,128)S(1)}, f32[2,16,256]{2,1,0:T(8,128)S(1)}, u32[]{:S(2)}, u32[]{:S(2)}) collective-permute-start(f32[2,16,256]{2,1,0:T(8,128)S(1)} %get-tuple-element.40), channel_id=1, source_target_pairs={{0,24},{8,0},{16,8},{24,16},{1,25},{9,1},{17,9},{25,17},{2,26},{10... | collective-permute-start | bytes 98312 | tf_op jit(solution)/shard_map/ppermute | solution.py:93

commit v6 on v5

--- a/solution.py
+++ b/solution.py
@@ -74,14 +74,19 @@
     return (2.0 * np.cos(np.arange(length) * (2.0 * math.pi / length)) - 2.0).astype(np.float32)
 
 
-def call(body, outs, scratch, vmem, flops, moved):
-    return pl.pallas_call(
-        body,
-        out_shape=outs,
-        scratch_shapes=scratch,
-        compiler_params=pltpu.CompilerParams(vmem_limit_bytes=vmem << 20),
-        cost_estimate=pl.CostEstimate(flops=flops, bytes_accessed=moved, transcendentals=0),
-    )
+def call(body, outs, scratch, vmem, flops, moved, scalars=0):
+    def run(*operands):
+        return pl.pallas_call(
+            body,
+            out_shape=outs,
+            in_specs=[SMEM] * scalars + [VMEM] * (len(operands) - scalars),
+            out_specs=jax.tree.map(lambda _: VMEM, outs),
+            scratch_shapes=scratch,
+            compiler_params=pltpu.CompilerParams(vmem_limit_bytes=vmem << 20),
+            cost_estimate=pl.CostEstimate(flops=flops, bytes_accessed=moved, transcendentals=0),
+        )(*operands)
+
+    return run
 
 
 def shape(*dims, dtype=F32):
@@ -199,97 +204,191 @@
     spectrum[...] = dot3((high[...], low[...]), (source_high[...], source_low[...]), NT)
 
 
-def solve_kernel(
-    tiles_x, tiles_y, rows_x, rows_y, scale,
-    first, lap_z, slab, labels, lap_xy, hx_high, hx_low, hy_high, hy_low, hf_high, hf_low,
-    out, planes, solved_planes, lines, faces,
+def stacked(pieces):
+    high, low = pieces
+    return jnp.concatenate(
+        [jnp.concatenate([high, low], 1), jnp.concatenate([high, jnp.zeros_like(high)], 1)], 0
+    )
+
+
+def joined(value):
+    width = value.shape[1] // 2
+    return value[:, :width] + value[:, width:]
+
+
+def placed(pieces, choose):
+    return dot(pieces[0], choose) + dot(pieces[1], choose) + dot(pieces[2], choose)
+
+
+def iota(dims, axis):
+    return lax.broadcasted_iota(jnp.int32, dims, axis)
+
+
+def decay(w, length):
+    grow = w + jnp.sqrt(w * (w + 2.0))
+    rate = jnp.log(1.0 + grow)
+    ratio = 1.0 / (1.0 + grow)
+    both = (1.0 + grow) + jnp.exp(-rate * (length - 1.0))
+    flat = w <= 0.0
+    return rate, 2.0 * (1.0 + ratio) * both, 2.0 * jnp.where(flat, 1.0, grow * ratio * both), flat
+
+
+def decay_kernel(length, first, lap_z, lap_x, even, odd, edge_even, edge_odd, spread):
+    count = even.shape[0]
+    dims = even.shape[1:]
+    lane = iota(dims, 1)
+    group = lane // length
+    y = (lane % length).astype(F32)
+    start = first[0]
+    for q in range(count):
+        along_z = jnp.where(group == 0, lap_z[start + q], lap_z[start + count + q])
+        rate, plus, minus, flat = decay(-0.5 * (lap_x[...] + along_z), length)
+        rise, fall = jnp.exp(-rate * y), jnp.exp(-rate * (length - 1.0 - y))
+        even[q] = (rise + fall) / plus
+        odd[q] = jnp.where(flat, 0.25 * (length - 1.0) - 0.5 * y, (rise - fall) / minus)
+    along_z = jnp.zeros(dims, F32)
+    for q in range(count):
+        for g in range(2):
+            along_z = jnp.where(lane // 2 == 2 * q + g, lap_z[start + g * count + q], along_z)
+    rate, plus, minus, flat = decay(-0.5 * (lap_x[...] + along_z), length)
+    last = jnp.exp(-rate * (length - 1.0))
+    edge_even[...] = (1.0 + last) / plus
+    edge_odd[...] = jnp.where(flat, 0.25 * (length - 1.0), (1.0 - last) / minus)
+    dims = spread.shape
+    col = iota(dims, 1)
+    row = iota(dims, 0)
+    hit = row // 2 == 2 * (col // (2 * LANES)) + col % LANES // length
+    sign = jnp.where((col // LANES % 2 == 1) & (row % 2 == 0), -1.0, 1.0)
+    spread[...] = jnp.where(hit, sign, 0.0).astype(BF16)
+
+
+def half_kernel(
+    tiles_x, tiles_y, rows_x, rows_y, scale, mark,
+    first, lap_z, slab, labels, lap_xy, hx_high, hx_low, hy_high, hy_low,
+    found, ends, planes,
 ):
-    grid_x, grid_y = tiles_x * rows_x, tiles_y * rows_y
-    count = slab.shape[1]
+    grid_x = tiles_x * rows_x
+    count = slab.shape[1] // 2
+    length = tiles_y * rows_y
     per = LANES // rows_y
-    chunk = rows_x * count
-
-    def stacked(pieces):
-        high, low = pieces
-        zero = jnp.zeros_like(high)
-        return jnp.concatenate(
-            [jnp.concatenate([high, low], 1), jnp.concatenate([high, zero], 1)], 0
-        )
-
-    def joined(value):
-        width = value.shape[1] // 2
-        return value[:, :width] + value[:, width:]
-
     along_y = stacked((hy_high[...], hy_low[...]))
     along_x = jnp.concatenate([hx_high[...], hx_low[...]], 1)
+
     def times_y(value):
         return joined(dot(jnp.concatenate(split(value, 2), 1), along_y))
 
     for i in range(tiles_x):
         for part in range(rows_x // per):
             lanes = slice(part * LANES, (part + 1) * LANES)
-            found = [[] for _ in range(per)]
-            for wide in range(tiles_y // per):
-                rows = [slab[i * tiles_y + wide * per + j, :, lanes] for j in range(per)]
-                for t, row in enumerate(swap_groups(rows, rows_y)):
-                    found[t].append(row)
+            rows = [
+                slab[i * tiles_y + j, g * count : (g + 1) * count, lanes]
+                for g in range(2)
+                for j in range(tiles_y)
+            ]
             x = (i * rows_x + part * per) * count
-            block = jnp.concatenate([jnp.concatenate(line, 1) for line in found], 0)
-            planes[x : x + per * count, :] = times_y(block)
+            planes[x : x + per * count, :] = times_y(jnp.concatenate(swap_groups(rows, rows_y), 0))
+    dims = (grid_x, LANES)
+    lane, row = iota(dims, 1), iota(dims, 0)
+    block = jnp.zeros(dims, F32)
     for q in range(count):
-        rows = pl.ds(q, grid_x, stride=count)
-        modes = joined(dot(along_x, stacked(split(planes[rows, :], 2))))
-        eigen = lap_xy[...] + lap_z[first[0] + q]
+        modes = joined(dot(along_x, stacked(split(planes[pl.ds(q, grid_x, stride=count), :], 2))))
+        eigen = lap_xy[...] + jnp.where(lane < length, lap_z[first[0] + q], lap_z[first[0] + count + q])
         anchor = eigen == 0.0
-        solved = jnp.where(anchor, 0.0, scale / jnp.where(anchor, -1.0, eigen)) * modes
-        back = joined(dot(along_x, stacked(split(solved, 2))))
-        solved_planes[rows, :] = back
-    sides = 2 * tiles_y
-    along_f = stacked((hf_high[...], hf_low[...]))
+        value = times_y(jnp.where(anchor, 0.0, scale / jnp.where(anchor, -1.0, eigen)) * modes)
+        found[q] = value
+        source = lane - 4 * q
+        source = source // 2 * length + source % 2 * (length - 1)
+        choose = (row == source) & (lane >= 4 * q) & (lane < 4 * q + 4)
+        block = block + placed(split(value, 3), choose.astype(BF16))
+        if q == 0:
+            mean = pltpu.roll(modes * scale, 4 * count, 1)
+            block = block + jnp.where((row == 0) & (lane == 4 * count), mean, 0.0)
+    ends[...] = block
+    tiles = labels.shape[0]
+    ends[0:tiles, :] = jnp.where(lane[0:tiles] < mark, block[0:tiles], labels[...])
+
+
+def join_kernel(
+    tiles_x, tiles_y, rows_x, rows_y, places,
+    first, half, found, ends, arrived, labels, even, odd, edge_even, edge_odd, spread, hx_high, hx_low,
+    out, planes, faces,
+):
+    grid_x = tiles_x * rows_x
+    count = found.shape[0]
+    length = tiles_y * rows_y
+    per = LANES // rows_y
+    along_x = jnp.concatenate([hx_high[...], hx_low[...]], 1)
+
+    def times_x(value):
+        return joined(dot(along_x, stacked(split(value, 2))))
+
+    dims = (grid_x, LANES)
+    lane, row = iota(dims, 1), iota(dims, 0)
+    jump = jnp.where(lane < 4 * count + 1, arrived[...] - ends[...], 0.0)
+    pieces = split(jump, 2)
+    wide = dot(pieces[0], spread[...]) + dot(pieces[1], spread[...])
+    mean = jnp.where(first[0] == 0, -0.5 * jump[0:1, 4 * count : 4 * count + 1], 0.0)
+    y = lane.astype(F32)
+    bend = jnp.where(
+        (row == 0) & (lane < length),
+        mean * (0.5 * y * y - 0.5 * (length - 1.0) * y - 0.25 * length),
+        0.0,
+    )
+    target = iota((LANES, LANES), 1)
+    source = iota((LANES, LANES), 0)
+    side, j, group = target // 8 % 2, target // 2 % tiles_y, target % 2
+    inside = ((side == 0) & (j > 0)) | ((side == 1) & (j < tiles_y - 1))
+    wanted = group * length + jnp.where(side == 0, j * rows_y - 1, (j + 1) * rows_y)
+    lines = jnp.zeros(dims, F32)
+    for q in range(count):
+        at = 2 * q * LANES
+        value = found[q] + (wide[:, at : at + LANES] * even[q] + wide[:, at + LANES : at + 2 * LANES] * odd[q])
+        if q == 0:
+            value = value + bend
+        choose = inside & (source == wanted) & (target // 16 == q)
+        lines = lines + placed(split(value, 3), choose.astype(BF16))
+        planes[pl.ds(q, grid_x, stride=count), :] = times_x(value)
+    low = lane % 2 == 0
+    other = jnp.where(low, pltpu.roll(jump, LANES - 1, 1), pltpu.roll(jump, 1, 1))
+    change = (jump + other) * edge_even[...] + (other - jump) * edge_odd[...]
+    change = change + jnp.where((row == 0) & (lane < 2), -0.25 * length * mean, 0.0)
+    beyond = jnp.where(lane < 4 * count, arrived[...] - change, 0.0)
+    first_side = source % 2 == 1
+    goal = source // 4 * 16 + source // 2 % 2 + jnp.where(first_side, 0, 8 + 2 * (tiles_y - 1))
+    choose = (target == goal) & (source < 4 * count)
+    lines = lines + placed(split(beyond, 3), choose.astype(BF16))
+    faces[...] = jnp.transpose(times_x(lines))
+
+    def row_of(x):
+        x = x % grid_x
+        return planes[x * count : (x + 1) * count, :]
+
+    lane = iota((count, LANES), 1)
     for i in range(tiles_x):
-        rows = slice(i * chunk, (i + 1) * chunk)
-        pieces = jnp.concatenate(split(solved_planes[rows, :], 2), 1)
-        planes[rows, :] = joined(dot(pieces, along_y))
-        lines[rows, :] = joined(dot(pieces, along_f))
-    for start in range(0, count, LANES // sides):
-        block = None
-        for q in range(start, start + LANES // sides):
-            item = lines[pl.ds(q, grid_x, stride=count), :]
-            item = pltpu.roll(item, (q - start) * sides, 1) if q > start else item
-            block = item if block is None else block + item
-        faces[start * sides : start * sides + LANES, :] = jnp.transpose(block)
-
-    lane = lax.broadcasted_iota(jnp.int32, (count, LANES), 1)
-    for i in range(tiles_x):
-        for wide in range(tiles_y // per):
-            cols = slice(wide * LANES, (wide + 1) * LANES)
-
-            def row_of(x):
-                x = x % grid_x
-                return planes[x * count : (x + 1) * count, cols]
-
-            for part in range(rows_x // per):
-                lanes = slice(part * LANES, (part + 1) * LANES)
-                rows = [row_of(i * rows_x + part * per + t) for t in range(per)]
-                for j, row in enumerate(swap_groups(rows, rows_y)):
-                    out[i * tiles_y + wide * per + j, :, lanes] = row
-            before, after = row_of(i * rows_x - 1), row_of((i + 1) * rows_x)
-            for k in range(per):
-                j = wide * per + k
-                shift = (LANES - k * rows_y) % LANES
-                line = pltpu.roll(before, shift, 1) if shift else before
-                moved = pltpu.roll(after, (shift + rows_y) % LANES, 1)
-                line = jnp.where(lane < rows_y, line, moved)
-                for side in range(2):
-                    at = side * tiles_y + j
-                    face = faces[pl.ds(at, count, stride=sides), :]
-                    start = 2 * rows_y + side * rows_x
-                    move = (start - i * rows_x) % LANES
-                    face = pltpu.roll(face, move, 1) if move else face
-                    line = jnp.where(lane < start, line, face)
-                at = i * tiles_y + j
-                line = jnp.where(lane < 2 * (rows_x + rows_y), line, labels[at : at + 1, :])
-                out[i * tiles_y + j, :, rows_x * rows_y : rows_x * rows_y + LANES] = line
+        for part in range(rows_x // per):
+            lanes = slice(part * LANES, (part + 1) * LANES)
+            rows = [row_of(i * rows_x + part * per + t) for t in range(per)]
+            for k, item in enumerate(swap_groups(rows, rows_y)):
+                g, j = k // tiles_y, k % tiles_y
+                out[i * tiles_y + j, g * count : (g + 1) * count, lanes] = item
+        before, after = row_of(i * rows_x - 1), row_of((i + 1) * rows_x)
+        for k in range(per):
+            g, j = k // tiles_y, k % tiles_y
+            shift = (LANES - k * rows_y) % LANES
+            line = pltpu.roll(before, shift, 1) if shift else before
+            moved = pltpu.roll(after, (shift + rows_y) % LANES, 1)
+            line = jnp.where(lane < rows_y, line, moved)
+            for side in range(2):
+                face = faces[pl.ds(side * 8 + j * 2 + g, count, stride=16), :]
+                start = 2 * rows_y + side * rows_x
+                move = (start - i * rows_x) % LANES
+                face = pltpu.roll(face, move, 1) if move else face
+                line = jnp.where(lane < start, line, face)
+            start = 2 * (rows_x + rows_y)
+            tile = (2 * i + half[0]) * tiles_y + j
+            own, partner = labels[pl.ds(tile, 1), :], pltpu.roll(arrived[pl.ds(tile, 1), :], places, 1)
+            line = jnp.where(lane < start, line, jnp.where(lane < start + places, own, partner))
+            out[i * tiles_y + j, g * count : (g + 1) * count, rows_x * rows_y : rows_x * rows_y + LANES] = line
 
 
 def solve_plain(slab, labels, rows_x, rows_y, cells_z, tiles_x, tiles_y, scale):
@@ -365,7 +464,7 @@
 
 
 def block_kernel(
-    planes, half, core, x_faces, y_faces, spectrum, high, low, slots,
+    planes, half, tiles_y, span, own, core, x_faces, y_faces, spectrum, high, low, slots,
     out, values, labels,
     cells, spread,
 ):
@@ -425,10 +524,15 @@
     named = spectrum[:, inner : inner + LANES].astype(BF16)
     row = lax.broadcasted_iota(jnp.int32, (cells_z, count), 0)
     slot = lax.broadcasted_iota(jnp.int32, (cells_z, count), 1)
-    source = (row % planes == 0) & (row // planes == slot // half)
+    tile = slot // half
+    member = tile // tiles_y * span + tile % span
+    source = (row % planes == 0) & (row // planes == member)
     by_lane = dot(named, source.astype(BF16), TN)
-    lane = lax.broadcasted_iota(jnp.int32, (LANES, count), 0) - 2 * (rows_x + rows_y)
-    place = lax.broadcasted_iota(jnp.int32, (LANES, count), 1) % half
+    dims = (LANES, count)
+    slot = iota(dims, 1)
+    moved = jnp.where(slot // half % tiles_y // span == own[0], 0, 2 * half)
+    lane = iota(dims, 0) - 2 * (rows_x + rows_y) - moved
+    place = slot % half
     for part in range(2):
         label = jnp.sum(jnp.where(lane == place + part * half, by_lane, 0.0), axis=0, keepdims=True)
         labels[part] = label.astype(jnp.int32)
@@ -648,50 +752,70 @@
         [pltpu.VMEM((3, rows_y + 16, cells_z), F32)] + [pltpu.VMEM((inner, cells_z), BF16)] * 2,
         12, 6 * inner * cells_z**2, 2 << 20,
     )(core, y_faces, x_faces, *source, z_high, z_low)
-    slab = exchange(spectrum).reshape(tiles, planes, inner)
-
-    scale = SECOND_ORDER / (grid_x * grid_y * cells_z)
-    if planes % 8 == 0 and tiles_y % (LANES // rows_y) == 0 and grid_x == LANES and 2 * tiles_y <= LANES and planes % (LANES // (2 * tiles_y)) == 0:
-        first = (lax.axis_index(both) * planes).astype(jnp.int32).reshape(1)
-        x_table, y_table = table_of(grid_x), table_of(grid_y)
-        starts = np.arange(tiles_y) * rows_y
-        edge = np.concatenate([(starts - 1) % grid_y, (starts + rows_y) % grid_y])
-        lap_xy = laplace_of(grid_x)[:, None] + laplace_of(grid_y)[None, :]
-        face_table = np.zeros((grid_y, LANES), np.float32)
-        face_table[:, : 2 * tiles_y] = y_table[edge].T
-        tables = pieces_of(x_table) + pieces_of(y_table) + pieces_of(face_table)
-        body = functools.partial(solve_kernel, tiles_x, tiles_y, rows_x, rows_y, scale)
-        specs = [SMEM, SMEM] + [VMEM] * 9
-        returned = pl.pallas_call(
-            body,
-            out_shape=shape(tiles, planes, used),
-            in_specs=specs,
-            out_specs=VMEM,
-            scratch_shapes=[
-                pltpu.VMEM((grid_x * planes, grid_y), F32),
-                pltpu.VMEM((grid_x * planes, grid_y), F32),
-                pltpu.VMEM((grid_x * planes, LANES), F32),
-                pltpu.VMEM((2 * tiles_y * planes, grid_x), F32),
-            ],
-            compiler_params=pltpu.CompilerParams(vmem_limit_bytes=16 << 20),
-            cost_estimate=pl.CostEstimate(
-                flops=24 * planes * grid_x**2 * grid_y, bytes_accessed=2 << 20, transcendentals=0
+    span = tiles_y // 2
+    length = span * rows_y
+    halved = (
+        2 * length == LANES and grid_x == LANES and planes == 8 and tiles_y == 8
+        and 2 * (rows_x + rows_y) + 4 * half <= LANES
+    )
+    if halved:
+        groups = [
+            [i * tiles_y + g * span + j for i in range(tiles_x) for j in range(span)] for g in range(2)
+        ]
+
+        def exchange_half(x):
+            return lax.all_to_all(x, both, 0, 0, axis_index_groups=groups, tiled=True)
+
+        place_x, place_y = lax.axis_index("px"), lax.axis_index("py")
+        own = (place_y // span).astype(jnp.int32).reshape(1)
+        first = ((place_x * span + place_y % span) * 2 * planes).astype(jnp.int32).reshape(1)
+        lap_z = laplace_of(cells_z)
+        lap_x = np.broadcast_to(laplace_of(grid_x)[:, None], (grid_x, LANES))
+        lap_xy = lap_x + np.tile(laplace_of(length), 2)[None, :]
+        x_table = pieces_of(table_of(grid_x))
+        y_table = pieces_of(np.kron(np.eye(2, dtype=np.float32), table_of(length)))
+        square = shape(grid_x, LANES)
+        cube = shape(planes, grid_x, LANES)
+        slab = exchange_half(spectrum).reshape(tiles // 2, 2 * planes, inner)
+        tables = call(
+            functools.partial(decay_kernel, length),
+            (cube, cube, square, square, shape(LANES, 2 * planes * LANES, dtype=BF16)),
+            [], 16, 100 * planes * grid_x * LANES, 2 << 20, 2,
+        )(first, lap_z, lap_x)
+        found, ends = call(
+            functools.partial(
+                half_kernel, tiles_x, span, rows_x, rows_y,
+                SECOND_ORDER / (grid_x * length * cells_z), 2 * (rows_x + rows_y),
             ),
-        )(first, laplace_of(cells_z), slab, labels, lap_xy, *tables)
+            (cube, square), [pltpu.VMEM((grid_x * planes, LANES), F32)],
+            16, 12 * planes * grid_x**2 * LANES, 2 << 20, 2,
+        )(first, lap_z, slab, labels, lap_xy, *x_table, *y_table)
+        arrived_ends = lax.ppermute(ends, "py", [(j, (j + span) % tiles_y) for j in range(tiles_y)])
+        returned = call(
+            functools.partial(join_kernel, tiles_x, span, rows_x, rows_y, 2 * half),
+            shape(tiles // 2, 2 * planes, used),
+            [pltpu.VMEM((grid_x * planes, LANES), F32), pltpu.VMEM((LANES, grid_x), F32)],
+            24, 12 * planes * grid_x**2 * LANES, 2 << 20, 2,
+        )(first, own, found, ends, arrived_ends, labels, *tables, *x_table)
+        modes = exchange_half(returned.reshape(cells_z, used))
     else:
+        span = tiles_y
+        own = jnp.zeros((1,), jnp.int32)
+        slab = exchange(spectrum).reshape(tiles, planes, inner)
+        scale = SECOND_ORDER / (grid_x * grid_y * cells_z)
         returned = solve_plain(slab, labels, rows_x, rows_y, cells_z, tiles_x, tiles_y, scale)
-    modes = exchange(returned.reshape(cells_z, used))
+        modes = exchange(returned.reshape(cells_z, used))
 
     width = -(-10 * blocks_z // LANES) * LANES
     cells = pltpu.VMEM((used, cells_z), F32)
     tile_args = (core, x_faces, y_faces, modes, z_high, z_low)
     half_out = shape(blocks, ROWS)
     sent, values, arrived_labels = call(
-        functools.partial(block_kernel, planes, half),
+        functools.partial(block_kernel, cells_z // (tiles_x * span), half, tiles_y, span),
         (half_out, shape(ROWS, blocks), shape(2, 1, blocks, dtype=jnp.int32)),
         [cells, pltpu.VMEM((width // LANES, used, LANES), F32)],
-        40, 20 * used * cells_z**2, 6 << 20,
-    )(*tile_args, slots)
+        40, 20 * used * cells_z**2, 6 << 20, 1,
+    )(own, *tile_args, slots)
     first = exchange(sent)
     later = call(functools.partial(fill_slots, 1), half_out, [], 16, 6 * ROWS * blocks**2, 4 << 20)(values, slots)
     displacement = call(

time: 142 us -> 137 us (0.965)
  blocking collectives: 21.2 us -> 14.3 us
  waiting for transfers between devices: 57.6 us -> 53.6 us
  Pallas kernels: 33.3 us -> 36.2 us
  starting transfers between devices: 26.1 us -> 28.7 us
    all_to_all x3 -> x2, waiting for transfers between devices: 51.9 us -> 36 us  [exchange(): return lax.all_to_all(x, both, split_axis=0, concat_axis=0, tiled=True)]
    all_to_all x0 -> x1, waiting for transfers between devices: none -> 9.56 us  [exchange_half(): return lax.all_to_all(x, both, 0, 0, axis_index_groups=groups, tiled=True)]
    all_to_all x1, blocking collectives: 21.2 us -> 14.3 us  [exchange_half(): return lax.all_to_all(x, both, 0, 0, axis_index_groups=groups, tiled=True)]
    all_to_all x3 -> x2, starting transfers between devices: 11.6 us -> 6.39 us  [exchange(): return lax.all_to_all(x, both, split_axis=0, concat_axis=0, tiled=True)]
    all_to_all x0 -> x1, starting transfers between devices: none -> 4.71 us  [exchange_half(): return lax.all_to_all(x, both, 0, 0, axis_index_groups=groups, tiled=True)]
    ppermute x0 -> x1, starting transfers between devices: none -> 3.1 us  [per_device(): lax.ppermute(ends, 'py', [(j, (j + span) % tiles_y) for j in range(tiles_...]
    pallas_call x11 -> x13, Pallas kernels: 33.2 us -> 36.1 us  [run(): pl.pallas_call(body, out_shape=outs, in_specs=[SMEM] * scalars + [VMEM] *...]
    ppermute x0 -> x1, waiting for transfers between devices: none -> 2.31 us  [per_device(): lax.ppermute(ends, 'py', [(j, (j + span) % tiles_y) for j in range(tiles_...]
  transfers between devices with their start and end apart: 11 -> 12, of which waited for: 6 -> 7; matrix products, arithmetic and copies ran while one was open for 0% -> 0% of each run, Pallas kernels for 11% -> 12%
where the time goes in v6:
time: 137 us; the launch traced here: 136 us
  waiting for transfers between devices  53.6 us (39%)
  Pallas kernels  36.2 us (26%)
  starting transfers between devices  28.7 us (21%)
  blocking collectives  14.3 us (10%)
  local copies, waits for them, and re-layouts  2.26 us (2%)
    pallas_call x13, Pallas kernels, run(): pl.pallas_call(body, out_shape=outs, in_specs=[SMEM] * scalars + [VMEM] *...  36.1 us
    all_to_all x2, waiting for transfers between devices, exchange(): return lax.all_to_all(x, both, split_axis=0, concat_axis=0, tiled=True)  36 us
    ppermute x8, starting transfers between devices, send(): return lax.ppermute(x, axis, [(i, (i + step) % size) for i in range(size)])  14.5 us
    all_to_all x1, blocking collectives, exchange_half(): return lax.all_to_all(x, both, 0, 0, axis_index_groups=groups, tiled=True)  14.3 us
    all_to_all x1, waiting for transfers between devices, exchange_half(): return lax.all_to_all(x, both, 0, 0, axis_index_groups=groups, tiled=True)  9.56 us
    all_to_all x2, starting transfers between devices, exchange(): return lax.all_to_all(x, both, split_axis=0, concat_axis=0, tiled=True)  6.39 us
    ppermute x8, waiting for transfers between devices, send(): return lax.ppermute(x, axis, [(i, (i + step) % size) for i in range(size)])  5.76 us
    all_to_all x1, starting transfers between devices, exchange_half(): return lax.all_to_all(x, both, 0, 0, axis_index_groups=groups, tiled=True)  4.71 us
  transfers between devices with their start and end apart: 12, of which 7 were waited for; matrix products, arithmetic and copies ran while one was open for 0% of the time, Pallas kernels for 12%

profile of v6, /device:TPU:0, one launch (start us, length us, event | category | flops | bytes accessed | tf_op | source)
XLA Modules:
  0.0 136.0 jit_solution(2198164270988006726)
XLA Ops:
  0.6 0.0 copy-start.1
  0.6 1.0 copy-done.1
  1.7 0.1 shard_map.113
  1.8 3.0 %collective-permute-start = (f32[32,256]{1,0:T(8,128)S(1)}, f32[32,256]{1,0:T(8,128)S(1)}, u32[]{:S(2)}, u32[]{:S(2)}) collective-permute-start(f32[32,256]{1,0:T(8,128)S(1)} %get-tuple-element.27), channel_id=1, source_target_pairs={{0,1},{1,2},{2,3},{3,4},{4,5},{5,6},{6,7},{7,0},{8,9},{9,10},{10,1... | collective-permute-start | bytes 98312 | tf_op jit(solution)/shard_map/ppermute | solution.py:98
  4.8 3.1 %collective-permute-start.1 = (f32[32,256]{1,0:T(8,128)S(1)}, f32[32,256]{1,0:T(8,128)S(1)}, u32[]{:S(2)}, u32[]{:S(2)}) collective-permute-start(f32[32,256]{1,0:T(8,128)S(1)} %get-tuple-element.28), channel_id=1, source_target_pairs={{0,7},{1,0},{2,1},{3,2},{4,3},{5,4},{6,5},{7,6},{8,15},{9,8},{10,9... | collective-permute-start | bytes 98312 | tf_op jit(solution)/shard_map/ppermute | solution.py:98
  7.9 1.8 %collective-permute-done = f32[32,256]{1,0:T(8,128)S(1)} collective-permute-done((f32[32,256]{1,0:T(8,128)S(1)}, f32[32,256]{1,0:T(8,128)S(1)}, u32[]{:S(2)}, u32[]{:S(2)}) %collective-permute-start) | collective-permute-done | bytes 32800 | tf_op jit(solution)/shard_map/ppermute | solution.py:98
  9.7 0.0 collective-permute-done.1
  9.7 0.1 collective-permute-start.2
  9.8 1.7 %collective-permute-start.3 = (f32[18,256]{1,0:T(8,128)S(1)}, f32[18,256]{1,0:T(8,128)S(1)}, u32[]{:S(2)}, u32[]{:S(2)}) collective-permute-start(f32[18,256]{1,0:T(8,128)S(1)} %pad_maximum_fusion.3), channel_id=1, source_target_pairs={{0,24},{8,0},{16,8},{24,16},{1,25},{9,1},{17,9},{25,17},{2,26},{10... | collective-permute-start | bytes 55304 | tf_op jit(solution)/shard_map/ppermute | solution.py:98
  11.6 1.8 %shard_map.114 = (bf16[512,256]{1,0:T(8,128)(2,1)S(1)}, bf16[512,256]{1,0:T(8,128)(2,1)S(1)}, bf16[256,256]{1,0:T(8,128)(2,1)S(1)}, bf16[256,256]{1,0:T(8,128)(2,1)S(1)}) custom-call(f32[32,16,256]{2,1,0:T(8,128)S(1)} %get-tuple-element.26.core, f32[2,32,256]{2,1,0:T(8,128)S(1)} %pad_maximum_fusion.y_faces), custom_call_target="tpu_custom_call" | custom-call | flops 7864320 | bytes 2097152 | tf_op jit(solution)/shard_map/pallas_call | solution.py:79
  13.3 0.0 copy-start.4
  13.3 0.0 collective-permute-done.2
  13.4 0.0 collective-permute-done.3
  13.4 0.0 copy-start.5
  13.4 0.0 copy-start.2
  13.4 0.0 copy-start.3
  13.4 0.0 copy-start.6
  13.4 0.0 copy-start.7
  13.4 0.0 copy-start.8
  13.5 0.0 copy-start.9
  13.5 0.0 copy-start.10
  13.5 1.3 shard_map.115
  14.8 4.7 %all-to-all-start = ((f32[16,16,512]{2,1,0:T(8,128)}), f32[16,16,512]{2,1,0:T(8,128)S(1)}, u32[]{:S(2)}, u32[]{:S(2)}) async-start(f32[16,16,512]{2,1,0:T(8,128)} %bitcast.12), calls=%async_computation | async-start | bytes 1048576 | tf_op jit(solution)/shard_map/all_to_all | solution.py:767
  19.5 0.0 copy-done.4
  19.5 0.1 copy.12.owner_col
  19.7 0.0 copy-done.5
  19.7 0.2 shard_map.116
  19.9 9.6 %all-to-all-done.slab = f32[16,16,512]{2,1,0:T(8,128)S(1)} async-done(((f32[16,16,512]{2,1,0:T(8,128)}), f32[16,16,512]{2,1,0:T(8,128)S(1)}, u32[]{:S(2)}, u32[]{:S(2)}) %all-to-all-start) | async-done | bytes 524320 | tf_op jit(solution)/shard_map/all_to_all | solution.py:767
  29.5 0.0 copy-done.2
  29.5 0.0 copy-done.3
  29.5 0.0 copy-done.6
  29.5 0.0 copy-done.7
  29.5 0.0 copy-done.8
  29.5 0.0 copy-done.9
  29.5 2.8 %shard_map.117 = (f32[8,128,128]{2,1,0:T(8,128)S(1)}, f32[128,128]{1,0:T(8,128)S(1)}) custom-call(s32[1]{0:T(128)} %bitcast.11.first, f32[256]{0:T(256)S(1)} %copy-done.6, f32[16,16,512]{2,1,0:T(8,128)S(1)} %all-to-all-done.slab, f32[32,128]{1,0:T(8,128)S(1)} %get-tuple-element.33.labels, f32[128,128]{1,0:T(8,128)S(1)} %copy-done.7, ...), custom_call_target="tpu_custom_call" | custom-call | flops 201326592 | bytes 2097152 | tf_op jit(solution)/shard_map/pallas_call | solution.py:79
  32.4 3.1 %collective-permute-start.4 = (f32[128,128]{1,0:T(8,128)S(1)}, f32[128,128]{1,0:T(8,128)S(1)}, u32[]{:S(2)}, u32[]{:S(2)}) collective-permute-start(f32[128,128]{1,0:T(8,128)S(1)} %get-tuple-element.35.ends), channel_id=1, source_target_pairs={{0,4},{1,5},{2,6},{3,7},{4,0},{5,1},{6,2},{7,3},{8,12},{9,13},{10,... | collective-permute-start | bytes 196616 | tf_op jit(solution)/shard_map/ppermute | solution.py:793
  35.5 0.0 copy-done.10
  35.5 0.1 jit_solution_.3.lap_x
  35.5 1.6 %shard_map.118 = (f32[8,128,128]{2,1,0:T(8,128)S(1)}, f32[8,128,128]{2,1,0:T(8,128)S(1)}, f32[128,128]{1,0:T(8,128)S(1)}, f32[128,128]{1,0:T(8,128)S(1)}, bf16[128,2048]{1,0:T(8,128)(2,1)S(1)}) custom-call(s32[1]{0:T(128)} %bitcast.11.first, f32[256]{0:T(256)S(1)} %copy-done.6, f32[128,128]{1,0:T(8,128)S(1)} %jit_solution_.3.lap_x), custom_call_target="tpu_custom_call" | custom-call | flops 13107200 | bytes 2097152 | tf_op jit(solution)/shard_map/pallas_call | solution.py:79
  37.1 2.3 %collective-permute-done.4.arrived = f32[128,128]{1,0:T(8,128)S(1)} collective-permute-done((f32[128,128]{1,0:T(8,128)S(1)}, f32[128,128]{1,0:T(8,128)S(1)}, u32[]{:S(2)}, u32[]{:S(2)}) %collective-permute-start.4) | collective-permute-done | bytes 65568 | tf_op jit(solution)/shard_map/ppermute | solution.py:793
  39.4 1.4 %shard_map.119 = f32[16,16,640]{2,1,0:T(8,128)S(1)} custom-call(s32[1]{0:T(128)} %bitcast.11.first, s32[1]{0:T(128)} %bitcast.half.own, f32[8,128,128]{2,1,0:T(8,128)S(1)} %get-tuple-element.34.found, f32[128,128]{1,0:T(8,128)S(1)} %get-tuple-element.35.ends, f32[128,128]{1,0:T(8,128)S(1)} %collective-permute-done.4.arrived, ...), custom_call_target="tpu_custom_call" | custom-call | flops 201326592 | bytes 2097152 | tf_op jit(solution)/shard_map/pallas_call | solution.py:79
  40.9 14.3 %all_to_all.39 = f32[16,16,640]{2,1,0:T(8,128)S(1)} all-to-all(f32[16,16,640]{2,1,0:T(8,128)S(1)} %shard_map.119), channel_id=1, replica_groups={{0,1,2,3,8,9,10,11,16,17,18,19,24,25,26,27},{4,5,6,7,12,13,14,15,20,21,..., dimensions={0} | all-to-all | bytes 1310720 | tf_op jit(solution)/shard_map/all_to_all | solution.py:767
  55.1 2.7 %shard_map.120 = (f32[256,896]{1,0:T(8,128)S(1)}, f32[896,256]{1,0:T(8,128)S(1)}, s32[2,1,256]{2,1,0:T(1,128)S(1)}) custom-call(s32[1]{0:T(128)} %bitcast.half.own, f32[32,16,256]{2,1,0:T(8,128)S(1)} %get-tuple-element.26.core, f32[2,18,256]{2,1,0:T(8,128)S(1)} %pad_maximum_fusion.1.x_faces, f32[2,32,256]{2,1,0:T(8,128)S(1)} %pad_maximum_fusion.y_faces, ...), custom_call_target="tpu_custom_call" | custom-call | flops 838860800 | bytes 6291456 | tf_op jit(solution)/shard_map/pallas_call | solution.py:79
  57.8 0.0 copy-start
  57.8 0.9 copy-done
  58.7 3.6 %all-to-all-start.3 = ((f32[32,8,896]{2,1,0:T(8,128)}), f32[32,8,896]{2,1,0:T(8,128)S(1)}, u32[]{:S(2)}, u32[]{:S(2)}) async-start(f32[32,8,896]{2,1,0:T(8,128)} %bitcast.43), calls=%async_computation.3 | async-start | bytes 1835008 | tf_op jit(solution)/shard_map/all_to_all | solution.py:716
  62.3 2.0 %shard_map.122 = f32[3,32,16,256]{3,2,1,0:T(8,128)} custom-call(f32[32,16,256]{2,1,0:T(8,128)S(1)} %get-tuple-element.26.core, f32[2,18,256]{2,1,0:T(8,128)S(1)} %pad_maximum_fusion.1.x_faces, f32[2,32,256]{2,1,0:T(8,128)S(1)} %pad_maximum_fusion.y_faces, f32[256,640]{1,0:T(8,128)S(1)} %bitcast.42, bf16[256,256]{1,0:T(8,128)(2,1)S(1)} %get-tuple-element.31.high, ...), custom_call_target="tpu_custom_call" | custom-call | flops 251658240 | bytes 4194304 | tf_op jit(solution)/shard_map/pallas_call | solution.py:79
  64.3 1.6 %shard_map.121 = f32[256,896]{1,0:T(8,128)} custom-call(f32[896,256]{1,0:T(8,128)S(1)} %get-tuple-element.42.values, s32[1,256]{1,0:T(1,128)S(1)} %get-tuple-element.41.slots), custom_call_target="tpu_custom_call" | custom-call | flops 352321536 | bytes 4194304 | tf_op jit(solution)/shard_map/pallas_call | solution.py:79
  65.8 21.2 %all-to-all-done.3 = f32[32,8,896]{2,1,0:T(8,128)S(1)} async-done(((f32[32,8,896]{2,1,0:T(8,128)}), f32[32,8,896]{2,1,0:T(8,128)S(1)}, u32[]{:S(2)}, u32[]{:S(2)}) %all-to-all-start.3) | async-done | bytes 917536 | tf_op jit(solution)/shard_map/all_to_all | solution.py:716
  87.1 2.8 %all-to-all-start.2 = ((f32[32,8,896]{2,1,0:T(8,128)}), f32[32,8,896]{2,1,0:T(8,128)S(1)}, u32[]{:S(2)}, u32[]{:S(2)}) async-start(f32[32,8,896]{2,1,0:T(8,128)} %bitcast.17), calls=%async_computation.2 | async-start | bytes 1835008 | tf_op jit(solution)/shard_map/all_to_all | solution.py:716
  89.9 9.9 %shard_map.123.refs_0_ = f32[36,24,256]{2,1,0:T(8,128)S(1)} custom-call(f32[256,896]{1,0:T(8,128)S(1)} %bitcast.39, s32[1,256]{1,0:T(1,128)S(1)} %get-tuple-element.60.labels), custom_call_target="tpu_custom_call" | custom-call | flops 39321600 | bytes 4194304 | tf_op jit(solution)/shard_map/pallas_call | solution.py:79
  99.8 14.7 %all-to-all-done.2 = f32[32,8,896]{2,1,0:T(8,128)S(1)} async-done(((f32[32,8,896]{2,1,0:T(8,128)}), f32[32,8,896]{2,1,0:T(8,128)S(1)}, u32[]{:S(2)}, u32[]{:S(2)}) %all-to-all-start.2) | async-done | bytes 917536 | tf_op jit(solution)/shard_map/all_to_all | solution.py:716
  114.5 10.0 %shard_map.124 = (f32[32,16,256]{2,1,0:T(8,128)S(1)}, f32[2,2,16,256]{3,2,1,0:T(8,128)S(1)}, f32[2,36,2,256]{3,2,1,0:T(2,128)S(1)}) custom-call(f32[256,896]{1,0:T(8,128)S(1)} %bitcast.40, s32[1,256]{1,0:T(1,128)S(1)} %get-tuple-element.61.labels, f32[36,24,256]{2,1,0:T(8,128)S(1)} %shard_map.123.refs_0_), custom_call_target="tpu_custom_call" | custom-call | flops 39321600 | bytes 4194304 | tf_op jit(solution)/shard_map/pallas_call | solution.py:79
  124.5 0.7 collective-permute-start.5
  125.3 4.0 %collective-permute-start.6 = (f32[36,2,256]{2,1,0:T(2,128)S(1)}, f32[36,2,256]{2,1,0:T(2,128)S(1)}, u32[]{:S(2)}, u32[]{:S(2)}) collective-permute-start(f32[36,2,256]{2,1,0:T(2,128)S(1)} %get-tuple-element.52), channel_id=1, source_target_pairs={{0,7},{1,0},{2,1},{3,2},{4,3},{5,4},{6,5},{7,6},{8,15},{9,8},{10,9... | collective-permute-start | bytes 221192 | tf_op jit(solution)/shard_map/ppermute | solution.py:98
  129.3 2.3 %collective-permute-done.5.y_low = f32[36,2,256]{2,1,0:T(2,128)S(1)} collective-permute-done((f32[36,2,256]{2,1,0:T(2,128)S(1)}, f32[36,2,256]{2,1,0:T(2,128)S(1)}, u32[]{:S(2)}, u32[]{:S(2)}) %collective-permute-start.5) | collective-permute-done | bytes 73760 | tf_op jit(solution)/shard_map/ppermute | solution.py:98
  131.6 0.0 collective-permute-done.6.y_top
  131.7 0.1 collective-permute-start.7
  131.7 1.7 %collective-permute-start.8 = (f32[2,16,256]{2,1,0:T(8,128)S(1)}, f32[2,16,256]{2,1,0:T(8,128)S(1)}, u32[]{:S(2)}, u32[]{:S(2)}) collective-permute-start(f32[2,16,256]{2,1,0:T(8,128)S(1)} %get-tuple-element.54), channel_id=1, source_target_pairs={{0,24},{8,0},{16,8},{24,16},{1,25},{9,1},{17,9},{25,17},{2,26},{10... | collective-permute-start | bytes 98312 | tf_op jit(solution)/shard_map/ppermute | solution.py:98
  133.5 1.6 %collective-permute-done.7.x_low = f32[2,16,256]{2,1,0:T(8,128)S(1)} collective-permute-done((f32[2,16,256]{2,1,0:T(8,128)S(1)}, f32[2,16,256]{2,1,0:T(8,128)S(1)}, u32[]{:S(2)}, u32[]{:S(2)}) %collective-permute-start.7) | collective-permute-done | bytes 32800 | tf_op jit(solution)/shard_map/ppermute | solution.py:98
  135.1 0.0 collective-permute-done.8.x_top
  135.1 0.9 shard_map.126
  (11 shorter events, 0.1 us)
Async XLA Ops:
  0.6 1.0 copy-start.1
  1.8 8.0 %collective-permute-start = (f32[32,256]{1,0:T(8,128)S(1)}, f32[32,256]{1,0:T(8,128)S(1)}, u32[]{:S(2)}, u32[]{:S(2)}) collective-permute-start(f32[32,256]{1,0:T(8,128)S(1)} %get-tuple-element.27), channel_id=1, source_target_pairs={{0,1},{1,2},{2,3},{3,4},{4,5},{5,6},{6,7},{7,0},{8,9},{9,10},{10,1... | collective-permute-start | bytes 98312 | tf_op jit(solution)/shard_map/ppermute | solution.py:98
  4.8 4.9 %collective-permute-start.1 = (f32[32,256]{1,0:T(8,128)S(1)}, f32[32,256]{1,0:T(8,128)S(1)}, u32[]{:S(2)}, u32[]{:S(2)}) collective-permute-start(f32[32,256]{1,0:T(8,128)S(1)} %get-tuple-element.28), channel_id=1, source_target_pairs={{0,7},{1,0},{2,1},{3,2},{4,3},{5,4},{6,5},{7,6},{8,15},{9,8},{10,9... | collective-permute-start | bytes 98312 | tf_op jit(solution)/shard_map/ppermute | solution.py:98
  9.7 3.6 %collective-permute-start.2 = (f32[18,256]{1,0:T(8,128)S(1)}, f32[18,256]{1,0:T(8,128)S(1)}, u32[]{:S(2)}, u32[]{:S(2)}) collective-permute-start(f32[18,256]{1,0:T(8,128)S(1)} %pad_maximum_fusion.2), channel_id=1, source_target_pairs={{0,8},{8,16},{16,24},{24,0},{1,9},{9,17},{17,25},{25,1},{2,10},{10... | collective-permute-start | bytes 55304 | tf_op jit(solution)/shard_map/ppermute | solution.py:98
  9.8 3.5 %collective-permute-start.3 = (f32[18,256]{1,0:T(8,128)S(1)}, f32[18,256]{1,0:T(8,128)S(1)}, u32[]{:S(2)}, u32[]{:S(2)}) collective-permute-start(f32[18,256]{1,0:T(8,128)S(1)} %pad_maximum_fusion.3), channel_id=1, source_target_pairs={{0,24},{8,0},{16,8},{24,16},{1,25},{9,1},{17,9},{25,17},{2,26},{10... | collective-permute-start | bytes 55304 | tf_op jit(solution)/shard_map/ppermute | solution.py:98
  13.3 6.2 %copy-start.4 = (s32[1,1,256,1]{2,3,1,0:T(1,128)S(1)}, s32[1,1,256,1]{2,3,1,0:T(1,128)}, u32[]{:S(2)}) copy-start(s32[1,1,256,1]{2,3,1,0:T(1,128)} %param.11) | copy-start | bytes 3076
  13.4 6.3 %copy-start.5 = (s32[1,1,256]{2,1,0:T(1,128)S(1)}, s32[1,1,256]{2,1,0:T(1,128)}, u32[]{:S(2)}) copy-start(s32[1,1,256]{2,1,0:T(1,128)} %param.12) | copy-start | bytes 3076
  13.4 16.1 %copy-start.2 = (bf16[128,128]{1,0:T(8,128)(2,1)S(1)}, bf16[128,128]{1,0:T(8,128)(2,1)}, u32[]{:S(2)}) copy-start(bf16[128,128]{1,0:T(8,128)(2,1)} %constant.55.clone.hx_high) | copy-start | bytes 98308
  13.4 16.1 %copy-start.3 = (bf16[128,128]{1,0:T(8,128)(2,1)S(1)}, bf16[128,128]{1,0:T(8,128)(2,1)}, u32[]{:S(2)}) copy-start(bf16[128,128]{1,0:T(8,128)(2,1)} %constant.56.clone.hx_low) | copy-start | bytes 98308
  13.4 16.1 %copy-start.6 = (f32[256]{0:T(256)S(1)}, f32[256]{0:T(256)}, u32[]{:S(2)}) copy-start(f32[256]{0:T(256)} %constant.52.clone.lap_z) | copy-start | bytes 3076
  13.4 16.1 %copy-start.7 = (f32[128,128]{1,0:T(8,128)S(1)}, f32[128,128]{1,0:T(8,128)}, u32[]{:S(2)}) copy-start(f32[128,128]{1,0:T(8,128)} %constant.54.clone.lap_xy) | copy-start | bytes 196612
  13.4 16.1 %copy-start.8 = (bf16[128,128]{1,0:T(8,128)(2,1)S(1)}, bf16[128,128]{1,0:T(8,128)(2,1)}, u32[]{:S(2)}) copy-start(bf16[128,128]{1,0:T(8,128)(2,1)} %constant.57.clone.hy_high) | copy-start | bytes 98308
  13.5 16.1 %copy-start.9 = (bf16[128,128]{1,0:T(8,128)(2,1)S(1)}, bf16[128,128]{1,0:T(8,128)(2,1)}, u32[]{:S(2)}) copy-start(bf16[128,128]{1,0:T(8,128)(2,1)} %constant.58.clone.hy_low) | copy-start | bytes 98308
  13.5 22.0 %copy-start.10 = (f32[128]{0:T(128)S(1)}, f32[128]{0:T(128)}, u32[]{:S(2)}) copy-start(f32[128]{0:T(128)} %constant.53.clone) | copy-start | bytes 1540
  14.8 14.7 %all-to-all-start = ((f32[16,16,512]{2,1,0:T(8,128)}), f32[16,16,512]{2,1,0:T(8,128)S(1)}, u32[]{:S(2)}, u32[]{:S(2)}) async-start(f32[16,16,512]{2,1,0:T(8,128)} %bitcast.12), calls=%async_computation | async-start | bytes 1048576 | tf_op jit(solution)/shard_map/all_to_all | solution.py:767
  32.4 7.0 %collective-permute-start.4 = (f32[128,128]{1,0:T(8,128)S(1)}, f32[128,128]{1,0:T(8,128)S(1)}, u32[]{:S(2)}, u32[]{:S(2)}) collective-permute-start(f32[128,128]{1,0:T(8,128)S(1)} %get-tuple-element.35.ends), channel_id=1, source_target_pairs={{0,4},{1,5},{2,6},{3,7},{4,0},{5,1},{6,2},{7,3},{8,12},{9,13},{10,... | collective-permute-start | bytes 196616 | tf_op jit(solution)/shard_map/ppermute | solution.py:793
  57.8 0.9 copy-start
  58.7 28.4 %all-to-all-start.3 = ((f32[32,8,896]{2,1,0:T(8,128)}), f32[32,8,896]{2,1,0:T(8,128)S(1)}, u32[]{:S(2)}, u32[]{:S(2)}) async-start(f32[32,8,896]{2,1,0:T(8,128)} %bitcast.43), calls=%async_computation.3 | async-start | bytes 1835008 | tf_op jit(solution)/shard_map/all_to_all | solution.py:716
  87.1 27.4 %all-to-all-start.2 = ((f32[32,8,896]{2,1,0:T(8,128)}), f32[32,8,896]{2,1,0:T(8,128)S(1)}, u32[]{:S(2)}, u32[]{:S(2)}) async-start(f32[32,8,896]{2,1,0:T(8,128)} %bitcast.17), calls=%async_computation.2 | async-start | bytes 1835008 | tf_op jit(solution)/shard_map/all_to_all | solution.py:716
  124.5 7.1 %collective-permute-start.5 = (f32[36,2,256]{2,1,0:T(2,128)S(1)}, f32[36,2,256]{2,1,0:T(2,128)S(1)}, u32[]{:S(2)}, u32[]{:S(2)}) collective-permute-start(f32[36,2,256]{2,1,0:T(2,128)S(1)} %get-tuple-element.53), channel_id=1, source_target_pairs={{0,1},{1,2},{2,3},{3,4},{4,5},{5,6},{6,7},{7,0},{8,9},{9,10},{10,1... | collective-permute-start | bytes 221192 | tf_op jit(solution)/shard_map/ppermute | solution.py:98
  125.3 6.4 %collective-permute-start.6 = (f32[36,2,256]{2,1,0:T(2,128)S(1)}, f32[36,2,256]{2,1,0:T(2,128)S(1)}, u32[]{:S(2)}, u32[]{:S(2)}) collective-permute-start(f32[36,2,256]{2,1,0:T(2,128)S(1)} %get-tuple-element.52), channel_id=1, source_target_pairs={{0,7},{1,0},{2,1},{3,2},{4,3},{5,4},{6,5},{7,6},{8,15},{9,8},{10,9... | collective-permute-start | bytes 221192 | tf_op jit(solution)/shard_map/ppermute | solution.py:98
  131.7 3.4 %collective-permute-start.7 = (f32[2,16,256]{2,1,0:T(8,128)S(1)}, f32[2,16,256]{2,1,0:T(8,128)S(1)}, u32[]{:S(2)}, u32[]{:S(2)}) collective-permute-start(f32[2,16,256]{2,1,0:T(8,128)S(1)} %get-tuple-element.55), channel_id=1, source_target_pairs={{0,8},{8,16},{16,24},{24,0},{1,9},{9,17},{17,25},{25,1},{2,10},{10... | collective-permute-start | bytes 98312 | tf_op jit(solution)/shard_map/ppermute | solution.py:98
  131.7 3.3 %collective-permute-start.8 = (f32[2,16,256]{2,1,0:T(8,128)S(1)}, f32[2,16,256]{2,1,0:T(8,128)S(1)}, u32[]{:S(2)}, u32[]{:S(2)}) collective-permute-start(f32[2,16,256]{2,1,0:T(8,128)S(1)} %get-tuple-element.54), channel_id=1, source_target_pairs={{0,24},{8,0},{16,8},{24,16},{1,25},{9,1},{17,9},{25,17},{2,26},{10... | collective-permute-start | bytes 98312 | tf_op jit(solution)/shard_map/ppermute | solution.py:98

commit v7 on v6

--- a/solution.py
+++ b/solution.py
@@ -436,9 +436,7 @@
             rows = slice(start, start + length)
             cells[rows, :] = cells[rows, :] + faces[side, skip : skip + length, :]
             start += length
-    x_edge = [inner, inner + rows_y]
-    y_edge = [inner + 2 * rows_y, inner + 2 * rows_y + rows_x]
-    return x_edge, y_edge
+    return edges_of(rows_x, rows_y)
 
 
 def displacement_kernel(core, x_faces, y_faces, spectrum, high, low, displacement, pad, cells):
@@ -463,18 +461,23 @@
         displacement[2, x] = (pltpu.roll(here, 1, 1) - pltpu.roll(here, cells_z - 1, 1)) * 0.5
 
 
-def block_kernel(
-    planes, half, tiles_y, span, own, core, x_faces, y_faces, spectrum, high, low, slots,
-    out, values, labels,
-    cells, spread,
-):
+def edges_of(rows_x, rows_y):
+    inner = rows_x * rows_y
+    return [inner, inner + rows_y], [inner + 2 * rows_y, inner + 2 * rows_y + rows_x]
+
+
+def sort_kernel(core, x_faces, y_faces, high, low, spread, sorted_high, sorted_low, cells):
     rows_x, rows_y, cells_z = core.shape
+    blocks_z = cells_z // 8
     inner = rows_x * rows_y
-    blocks_x, blocks_y, blocks_z = rows_x // 8, rows_y // 8, cells_z // 8
-    per = LANES // blocks_z
-    x_edge, y_edge = combine(core, x_faces, y_faces, spectrum, high, low, cells)
-
-    width = spread.shape[0] * LANES
+    x_edge, y_edge = edges_of(rows_x, rows_y)
+    cells[0:inner, :] = core[...].reshape(inner, cells_z)
+    for side in range(2):
+        cells[x_edge[side] : x_edge[side] + rows_y, :] = x_faces[side, 1 : rows_y + 1, :]
+        cells[y_edge[side] : y_edge[side] + rows_x, :] = y_faces[side]
+    used = y_edge[1] + rows_x
+    cells[used:, :] = jnp.zeros((cells.shape[0] - used, cells_z), F32)
+    width = sorted_high.shape[1]
     col = lax.broadcasted_iota(jnp.int32, (cells_z, width), 1)
     wanted = (8 * (col % blocks_z) + col // blocks_z + cells_z - 1) % cells_z
     choose = (wanted == lax.broadcasted_iota(jnp.int32, (cells_z, width), 0)).astype(BF16)
@@ -482,6 +485,24 @@
     moved = dot(pieces[0], choose) + dot(pieces[1], choose) + dot(pieces[2], choose)
     for quad in range(spread.shape[0]):
         spread[quad] = moved[:, quad * LANES : (quad + 1) * LANES]
+    sorted_high[...] = dot(high[...], choose).astype(BF16)
+    sorted_low[...] = dot(low[...], choose).astype(BF16)
+
+
+def block_kernel(
+    rows_x, rows_y, planes, half, tiles_y, span, own, potential, spectrum, high, low, slots,
+    out, values, labels,
+    spread,
+):
+    cells_z = spectrum.shape[0]
+    inner = rows_x * rows_y
+    blocks_x, blocks_y, blocks_z = rows_x // 8, rows_y // 8, cells_z // 8
+    per = LANES // blocks_z
+    x_edge, y_edge = edges_of(rows_x, rows_y)
+    width = high.shape[1]
+    second = dot3(split(spectrum[...], 2), (high[...], low[...]), TN)
+    for quad in range(width // LANES):
+        spread[quad] = potential[quad] + second[:, quad * LANES : (quad + 1) * LANES]
 
     def put(row, tiles):
         for quad in range(width // LANES):
@@ -601,58 +622,56 @@
                 for axis, diff in enumerate((x_diff, y_low - y_top, z_low - z_top)):
                     for k, weight in enumerate(spline(jnp.clip(diff * 0.5, -1.0, 1.0))):
                         if (axis, k) != (1, 2):
-                            weights[axis * 5 + k, a * 8 + e] = weight
-
-        top_lanes = pl.ds(pl.multiple_of(g * LANES, LANES), LANES)
-        rest_lanes = pl.ds(pl.multiple_of(slots + g * LANES, LANES), LANES)
-
-        def cell_row(s, depths):
-            sums = {}
-            for a in range(8):
-                for k in depths:
-                    at = a * 8 + (s - k)
-                    w_z = weights[10 + k, at]
-                    w_y = [weights[5 + j, at] if j != 2 else None for j in range(5)]
-                    for i in range(5):
-                        plane = weights[i, at] * w_z
-                        for j in range(5):
-                            key = (a + i, j)
-                            term = plane * w_y[j] if j != 2 else plane
-                            sums[key] = sums[key] + term if key in sums else term
-                for u in [a] if a < 7 else range(7, 12):
-                    rows = [sums[u, j] for j in range(5)]
-                    rows[2] = rows[2] - ((rows[0] + rows[1]) + (rows[3] + rows[4]))
-                    moved = [pltpu.roll(rows[j], j, 0) for j in range(1, 5)]
-                    every = rows[0] + ((moved[0] + moved[1]) + (moved[2] + moved[3]))
-                    past = [jnp.where(sub < j + 1, moved[j], 0.0) for j in range(4)]
-                    tail = (past[0] + past[1]) + (past[2] + past[3])
-                    top, rest = split(jnp.concatenate([every - tail, tail], 0), 2)
-                    out = pl.ds(pl.multiple_of((s * 12 + u) * 16, 16), 16)
-                    pieces[out, top_lanes] = top
-                    pieces[out, rest_lanes] = rest
-
-        for s in (0, 1, 2, 3, 8, 9, 10, 11):
-            cell_row(s, [k for k in range(5) if 0 <= s - k < 8])
-
-        @pl.loop(4, 8)
-        def _(s):
-            cell_row(s, range(5))
+                            weights[g, axis * 5 + k, a * 8 + e] = weight
+
+    def cell_row(g, s, depths):
+        top_lanes = slice(g * LANES, (g + 1) * LANES)
+        rest_lanes = slice(slots + g * LANES, slots + (g + 1) * LANES)
+        sums = {}
+        for a in range(8):
+            for k in depths:
+                at = a * 8 + (s - k)
+                w_z = weights[g, 10 + k, at]
+                w_y = [weights[g, 5 + j, at] if j != 2 else None for j in range(5)]
+                for i in range(5):
+                    plane = weights[g, i, at] * w_z
+                    for j in range(5):
+                        key = (a + i, j)
+                        term = plane * w_y[j] if j != 2 else plane
+                        sums[key] = sums[key] + term if key in sums else term
+            for u in [a] if a < 7 else range(7, 12):
+                rows = [sums[u, j] for j in range(5)]
+                rows[2] = rows[2] - ((rows[0] + rows[1]) + (rows[3] + rows[4]))
+                moved = [pltpu.roll(rows[j], j, 0) for j in range(1, 5)]
+                every = rows[0] + ((moved[0] + moved[1]) + (moved[2] + moved[3]))
+                past = [jnp.where(sub < j + 1, moved[j], 0.0) for j in range(4)]
+                tail = (past[0] + past[1]) + (past[2] + past[3])
+                top, rest = split(jnp.concatenate([every - tail, tail], 0), 2)
+                out = slice((s * 12 + u) * 16, (s * 12 + u + 1) * 16)
+                pieces[out, top_lanes] = top
+                pieces[out, rest_lanes] = rest
 
     named = (labels[...] == lax.broadcasted_iota(jnp.int32, (windows, slots), 0)).astype(F32)
     named = jnp.transpose(named).astype(BF16)
     area = 12 * 16
     named = jnp.concatenate([named, named], 0)
 
-    @pl.loop(0, 12 // per)
-    def _(quad):
-        rows = pl.ds(pl.multiple_of(quad * per * area, 16), per * area)
-        summed = dot(pieces[rows, :], named)
+    def gather(quad):
+        summed = dot(pieces[quad * per * area : (quad + 1) * per * area, :], named)
         for wide in range(windows // LANES):
             lanes = slice(wide * LANES, (wide + 1) * LANES)
             part = [summed[k * area : (k + 1) * area, lanes] for k in range(per)]
             for t, item in enumerate(swap_groups(part, blocks_z)):
                 rows = slice((wide * per + t) * area, (wide * per + t + 1) * area)
                 grouped[0, quad, rows, :], grouped[1, quad, rows, :] = split(item, 2)
+
+    for quad in range(12 // per):
+        for s in range(quad * per, (quad + 1) * per):
+            for g in range(slots // LANES):
+                cell_row(g, s, [k for k in range(5) if 0 <= s - k < 8])
+        if quad > 0:
+            gather(quad - 1)
+    gather(12 // per - 1)
 
     depth = 12 * blocks_z
     row = lax.broadcasted_iota(jnp.int32, (depth, cells_z), 0)
@@ -752,6 +771,15 @@
         [pltpu.VMEM((3, rows_y + 16, cells_z), F32)] + [pltpu.VMEM((inner, cells_z), BF16)] * 2,
         12, 6 * inner * cells_z**2, 2 << 20,
     )(core, y_faces, x_faces, *source, z_high, z_low)
+    cells = pltpu.VMEM((used, cells_z), F32)
+    width = -(-10 * blocks_z // LANES) * LANES
+    sorted_table = shape(cells_z, width, dtype=BF16)
+    *sorted_args, high, low = call(
+        sort_kernel, (shape(width // LANES, used, LANES), sorted_table, sorted_table), [cells],
+        10, 12 * used * cells_z**2, 2 << 20,
+    )(core, x_faces, y_faces, z_high, z_low)
+    sorted_tables = (high, low)
+
     span = tiles_y // 2
     length = span * rows_y
     halved = (
@@ -777,6 +805,8 @@
         square = shape(grid_x, LANES)
         cube = shape(planes, grid_x, LANES)
         slab = exchange_half(spectrum).reshape(tiles // 2, 2 * planes, inner)
+        slab, *sorted_args, high, low = lax.optimization_barrier((slab, *sorted_args, high, low))
+        sorted_tables = (high, low)
         tables = call(
             functools.partial(decay_kernel, length),
             (cube, cube, square, square, shape(LANES, 2 * planes * LANES, dtype=BF16)),
@@ -788,14 +818,14 @@
                 SECOND_ORDER / (grid_x * length * cells_z), 2 * (rows_x + rows_y),
             ),
             (cube, square), [pltpu.VMEM((grid_x * planes, LANES), F32)],
-            16, 12 * planes * grid_x**2 * LANES, 2 << 20, 2,
+            12, 12 * planes * grid_x**2 * LANES, 2 << 20, 2,
         )(first, lap_z, slab, labels, lap_xy, *x_table, *y_table)
         arrived_ends = lax.ppermute(ends, "py", [(j, (j + span) % tiles_y) for j in range(tiles_y)])
         returned = call(
             functools.partial(join_kernel, tiles_x, span, rows_x, rows_y, 2 * half),
             shape(tiles // 2, 2 * planes, used),
             [pltpu.VMEM((grid_x * planes, LANES), F32), pltpu.VMEM((LANES, grid_x), F32)],
-            24, 12 * planes * grid_x**2 * LANES, 2 << 20, 2,
+            12, 12 * planes * grid_x**2 * LANES, 2 << 20, 2,
         )(first, own, found, ends, arrived_ends, labels, *tables, *x_table)
         modes = exchange_half(returned.reshape(cells_z, used))
     else:
@@ -806,18 +836,15 @@
         returned = solve_plain(slab, labels, rows_x, rows_y, cells_z, tiles_x, tiles_y, scale)
         modes = exchange(returned.reshape(cells_z, used))
 
-    width = -(-10 * blocks_z // LANES) * LANES
-    cells = pltpu.VMEM((used, cells_z), F32)
     tile_args = (core, x_faces, y_faces, modes, z_high, z_low)
-    half_out = shape(blocks, ROWS)
     sent, values, arrived_labels = call(
-        functools.partial(block_kernel, cells_z // (tiles_x * span), half, tiles_y, span),
-        (half_out, shape(ROWS, blocks), shape(2, 1, blocks, dtype=jnp.int32)),
-        [cells, pltpu.VMEM((width // LANES, used, LANES), F32)],
-        40, 20 * used * cells_z**2, 6 << 20, 1,
-    )(own, *tile_args, slots)
+        functools.partial(block_kernel, rows_x, rows_y, cells_z // (tiles_x * span), half, tiles_y, span),
+        (shape(blocks, ROWS), shape(ROWS, blocks), shape(2, 1, blocks, dtype=jnp.int32)),
+        [pltpu.VMEM((width // LANES, used, LANES), F32)],
+        12, 20 * used * cells_z**2, 6 << 20, 1,
+    )(own, *sorted_args, modes, *sorted_tables, slots)
     first = exchange(sent)
-    later = call(functools.partial(fill_slots, 1), half_out, [], 16, 6 * ROWS * blocks**2, 4 << 20)(values, slots)
+    later = call(functools.partial(fill_slots, 1), shape(blocks, ROWS), [], 16, 6 * ROWS * blocks**2, 4 << 20)(values, slots)
     displacement = call(
         displacement_kernel, shape(3, rows_x, rows_y, cells_z),
         [pltpu.VMEM((rows_x, rows_y + 16, cells_z), F32), cells],
@@ -829,7 +856,7 @@
     tile_shape = (rows_x + 4, rows_y + 8, cells_z)
     scratch = [
         pltpu.VMEM((blocks // LANES, ROWS, LANES), F32),
-        pltpu.VMEM((15, 64, 8, LANES), F32),
+        pltpu.VMEM((blocks // LANES, 15, 64, 8, LANES), F32),
         pltpu.VMEM((12 * 12 * 16, 2 * blocks), BF16),
         pltpu.VMEM((2, 12 * blocks_z // LANES, blocks_x * blocks_y * 12 * 16, LANES), BF16),
         pltpu.VMEM(tile_shape, F32),

time: 137 us -> 136 us (level)
  starting transfers between devices: 28.7 us -> 23.3 us
  waiting for transfers between devices: 53.6 us -> 57.9 us
  local copies, waits for them, and re-layouts: 2.26 us -> 4.54 us
  Pallas kernels: 36.2 us -> 34.8 us
    ppermute x8, waiting for transfers between devices: 5.76 us -> 12.5 us  [send(): return lax.ppermute(x, axis, [(i, (i + step) % size) for i in range(size)])]
    ppermute x8, starting transfers between devices: 14.5 us -> 9.32 us  [send(): return lax.ppermute(x, axis, [(i, (i + step) % size) for i in range(size)])]
    all_to_all x1, waiting for transfers between devices: 9.56 us -> 6.38 us  [exchange_half(): return lax.all_to_all(x, both, 0, 0, axis_index_groups=groups, tiled=True)]
    unnamed x22 -> x34, local copies, waits for them, and re-layouts: 2.02 us -> 4.3 us
    pallas_call x13 -> x14, Pallas kernels: 36.1 us -> 34.7 us  [run(): pl.pallas_call(body, out_shape=outs, in_specs=[SMEM] * scalars + [VMEM] *...]
  transfers between devices with their start and end apart: 12 -> 12, of which waited for: 7 -> 10; matrix products, arithmetic and copies ran while one was open for 0% -> 0% of each run, Pallas kernels for 12% -> 13%
where the time goes in v7:
time: 136 us
  waiting for transfers between devices  57.9 us (43%)
  Pallas kernels  34.8 us (26%)
  starting transfers between devices  23.3 us (17%)
  blocking collectives  14.3 us (11%)
  local copies, waits for them, and re-layouts  4.54 us (3%)
    all_to_all x2, waiting for transfers between devices, exchange(): return lax.all_to_all(x, both, split_axis=0, concat_axis=0, tiled=True)  36.7 us
    pallas_call x14, Pallas kernels, run(): pl.pallas_call(body, out_shape=outs, in_specs=[SMEM] * scalars + [VMEM] *...  34.7 us
    all_to_all x1, blocking collectives, exchange_half(): return lax.all_to_all(x, both, 0, 0, axis_index_groups=groups, tiled=True)  14.3 us
    ppermute x8, waiting for transfers between devices, send(): return lax.ppermute(x, axis, [(i, (i + step) % size) for i in range(size)])  12.5 us
    ppermute x8, starting transfers between devices, send(): return lax.ppermute(x, axis, [(i, (i + step) % size) for i in range(size)])  9.32 us
    all_to_all x2, starting transfers between devices, exchange(): return lax.all_to_all(x, both, split_axis=0, concat_axis=0, tiled=True)  6.42 us
    all_to_all x1, waiting for transfers between devices, exchange_half(): return lax.all_to_all(x, both, 0, 0, axis_index_groups=groups, tiled=True)  6.38 us
    all_to_all x1, starting transfers between devices, exchange_half(): return lax.all_to_all(x, both, 0, 0, axis_index_groups=groups, tiled=True)  4.51 us
  transfers between devices with their start and end apart: 12, of which 10 were waited for; matrix products, arithmetic and copies ran while one was open for 0% of the time, Pallas kernels for 13%

profile of v7, /device:TPU:0, one launch (start us, length us, event | category | flops | bytes accessed | tf_op | source)
XLA Modules:
  0.0 135.8 jit_solution(11695273743331225869)
XLA Ops:
  0.6 0.0 copy-start.1
  0.6 1.0 copy-done.1
  1.7 0.1 shard_map.113
  1.8 3.0 %collective-permute-start = (f32[32,256]{1,0:T(8,128)S(1)}, f32[32,256]{1,0:T(8,128)S(1)}, u32[]{:S(2)}, u32[]{:S(2)}) collective-permute-start(f32[32,256]{1,0:T(8,128)S(1)} %get-tuple-element.34), channel_id=1, source_target_pairs={{0,1},{1,2},{2,3},{3,4},{4,5},{5,6},{6,7},{7,0},{8,9},{9,10},{10,1... | collective-permute-start | bytes 98312 | tf_op jit(solution)/shard_map/ppermute | solution.py:98
  4.8 3.1 %collective-permute-start.1 = (f32[32,256]{1,0:T(8,128)S(1)}, f32[32,256]{1,0:T(8,128)S(1)}, u32[]{:S(2)}, u32[]{:S(2)}) collective-permute-start(f32[32,256]{1,0:T(8,128)S(1)} %get-tuple-element.35), channel_id=1, source_target_pairs={{0,7},{1,0},{2,1},{3,2},{4,3},{5,4},{6,5},{7,6},{8,15},{9,8},{10,9... | collective-permute-start | bytes 98312 | tf_op jit(solution)/shard_map/ppermute | solution.py:98
  7.9 1.8 %collective-permute-done = f32[32,256]{1,0:T(8,128)S(1)} collective-permute-done((f32[32,256]{1,0:T(8,128)S(1)}, f32[32,256]{1,0:T(8,128)S(1)}, u32[]{:S(2)}, u32[]{:S(2)}) %collective-permute-start) | collective-permute-done | bytes 32800 | tf_op jit(solution)/shard_map/ppermute | solution.py:98
  9.7 0.0 collective-permute-done.1
  9.7 0.2 collective-permute-start.3
  10.0 0.3 collective-permute-start.2
  10.3 1.8 %shard_map.114 = (bf16[512,256]{1,0:T(8,128)(2,1)S(1)}, bf16[512,256]{1,0:T(8,128)(2,1)S(1)}, bf16[256,256]{1,0:T(8,128)(2,1)S(1)}, bf16[256,256]{1,0:T(8,128)(2,1)S(1)}) custom-call(f32[32,16,256]{2,1,0:T(8,128)S(1)} %get-tuple-element.33.core, f32[2,32,256]{2,1,0:T(8,128)S(1)} %pad_maximum_fusion.y_faces), custom_call_target="tpu_custom_call" | custom-call | flops 7864320 | bytes 2097152 | tf_op jit(solution)/shard_map/pallas_call | solution.py:79
  12.1 0.0 copy-start.4
  12.1 0.0 collective-permute-done.3
  12.1 1.3 collective-permute-done.2
  13.5 1.3 shard_map.115
  14.8 0.0 copy-start.8
  14.8 0.0 copy-start.9
  14.8 4.5 %all-to-all-start = ((f32[16,16,512]{2,1,0:T(8,128)}), f32[16,16,512]{2,1,0:T(8,128)S(1)}, u32[]{:S(2)}, u32[]{:S(2)}) async-start(f32[16,16,512]{2,1,0:T(8,128)} %bitcast.11), calls=%async_computation | async-start | bytes 1048576 | tf_op jit(solution)/shard_map/all_to_all | solution.py:795
  19.3 0.0 copy-start.16
  19.3 0.0 copy-done.4
  19.4 0.1 copy.12.owner_col
  19.5 0.0 copy-done.5
  19.5 0.2 shard_map.117
  19.8 0.9 shard_map.116
  20.6 0.0 copy-start.10
  20.6 0.9 copy-done.10
  21.6 0.7 copy-done.12
  22.3 0.7 copy-done.14
  22.9 6.4 %all-to-all-done.slab = f32[16,16,512]{2,1,0:T(8,128)S(1)} async-done(((f32[16,16,512]{2,1,0:T(8,128)}), f32[16,16,512]{2,1,0:T(8,128)S(1)}, u32[]{:S(2)}, u32[]{:S(2)}) %all-to-all-start) | async-done | bytes 524320 | tf_op jit(solution)/shard_map/all_to_all | solution.py:795
  29.3 0.0 copy-done.2
  29.3 0.0 copy-done.3
  29.3 0.0 copy-done.6
  29.3 0.0 copy-done.7
  29.3 0.0 copy-done.8
  29.3 0.0 copy-done.9
  29.4 2.8 %shard_map.118 = (f32[8,128,128]{2,1,0:T(8,128)S(1)}, f32[128,128]{1,0:T(8,128)S(1)}) custom-call(s32[1]{0:T(128)} %bitcast.12.first, f32[256]{0:T(256)S(1)} %copy-done.6, f32[16,16,512]{2,1,0:T(8,128)S(1)} %all-to-all-done.slab, f32[32,128]{1,0:T(8,128)S(1)} %get-tuple-element.45.labels, f32[128,128]{1,0:T(8,128)S(1)} %copy-done.7, ...), custom_call_target="tpu_custom_call" | custom-call | flops 201326592 | bytes 2097152 | tf_op jit(solution)/shard_map/pallas_call | solution.py:79
  32.2 3.1 %collective-permute-start.4 = (f32[128,128]{1,0:T(8,128)S(1)}, f32[128,128]{1,0:T(8,128)S(1)}, u32[]{:S(2)}, u32[]{:S(2)}) collective-permute-start(f32[128,128]{1,0:T(8,128)S(1)} %get-tuple-element.47.ends), channel_id=1, source_target_pairs={{0,4},{1,5},{2,6},{3,7},{4,0},{5,1},{6,2},{7,3},{8,12},{9,13},{10,... | collective-permute-start | bytes 196616 | tf_op jit(solution)/shard_map/ppermute | solution.py:823
  35.3 0.0 copy-done.16
  35.3 0.1 jit_solution_.3.lap_x
  35.4 1.6 %shard_map.119 = (f32[8,128,128]{2,1,0:T(8,128)S(1)}, f32[8,128,128]{2,1,0:T(8,128)S(1)}, f32[128,128]{1,0:T(8,128)S(1)}, f32[128,128]{1,0:T(8,128)S(1)}, bf16[128,2048]{1,0:T(8,128)(2,1)S(1)}) custom-call(s32[1]{0:T(128)} %bitcast.12.first, f32[256]{0:T(256)S(1)} %copy-done.6, f32[128,128]{1,0:T(8,128)S(1)} %jit_solution_.3.lap_x), custom_call_target="tpu_custom_call" | custom-call | flops 13107200 | bytes 2097152 | tf_op jit(solution)/shard_map/pallas_call | solution.py:79
  36.9 2.3 %collective-permute-done.4.arrived = f32[128,128]{1,0:T(8,128)S(1)} collective-permute-done((f32[128,128]{1,0:T(8,128)S(1)}, f32[128,128]{1,0:T(8,128)S(1)}, u32[]{:S(2)}, u32[]{:S(2)}) %collective-permute-start.4) | collective-permute-done | bytes 65568 | tf_op jit(solution)/shard_map/ppermute | solution.py:823
  39.2 1.4 %shard_map.120 = f32[16,16,640]{2,1,0:T(8,128)S(1)} custom-call(s32[1]{0:T(128)} %bitcast.12.first, s32[1]{0:T(128)} %bitcast.half.own, f32[8,128,128]{2,1,0:T(8,128)S(1)} %get-tuple-element.46.found, f32[128,128]{1,0:T(8,128)S(1)} %get-tuple-element.47.ends, f32[128,128]{1,0:T(8,128)S(1)} %collective-permute-done.4.arrived, ...), custom_call_target="tpu_custom_call" | custom-call | flops 201326592 | bytes 2097152 | tf_op jit(solution)/shard_map/pallas_call | solution.py:79
  40.7 14.3 %all_to_all.39 = f32[16,16,640]{2,1,0:T(8,128)S(1)} all-to-all(f32[16,16,640]{2,1,0:T(8,128)S(1)} %shard_map.120), channel_id=1, replica_groups={{0,1,2,3,8,9,10,11,16,17,18,19,24,25,26,27},{4,5,6,7,12,13,14,15,20,21,..., dimensions={0} | all-to-all | bytes 1310720 | tf_op jit(solution)/shard_map/all_to_all | solution.py:795
  55.0 0.0 copy-done.11
  55.0 0.0 copy-done.13
  55.0 0.0 copy-done.15
  55.0 1.7 %shard_map.121 = (f32[256,896]{1,0:T(8,128)S(1)}, f32[896,256]{1,0:T(8,128)S(1)}, s32[2,1,256]{2,1,0:T(1,128)S(1)}) custom-call(s32[1]{0:T(128)} %bitcast.half.own, f32[3,640,128]{2,1,0:T(8,128)S(1)} %copy-done.11, f32[256,640]{1,0:T(8,128)S(1)} %bitcast.41, bf16[256,384]{1,0:T(8,128)(2,1)S(1)} %copy-done.13, bf16[256,384]{1,0:T(8,128)(2,1)S(1)} %copy-done.15, ...), custom_call_target="tpu_custom_call" | custom-call | flops 838860800 | bytes 6291456 | tf_op jit(solution)/shard_map/pallas_call | solution.py:79
  56.7 0.9 copy-done
  57.6 3.6 %all-to-all-start.3 = ((f32[32,8,896]{2,1,0:T(8,128)}), f32[32,8,896]{2,1,0:T(8,128)S(1)}, u32[]{:S(2)}, u32[]{:S(2)}) async-start(f32[32,8,896]{2,1,0:T(8,128)} %bitcast.43), calls=%async_computation.3 | async-start | bytes 1835008 | tf_op jit(solution)/shard_map/all_to_all | solution.py:735
  61.2 2.0 %shard_map.123 = f32[3,32,16,256]{3,2,1,0:T(8,128)} custom-call(f32[32,16,256]{2,1,0:T(8,128)S(1)} %get-tuple-element.33.core, f32[2,18,256]{2,1,0:T(8,128)S(1)} %pad_maximum_fusion.1.x_faces, f32[2,32,256]{2,1,0:T(8,128)S(1)} %pad_maximum_fusion.y_faces, f32[256,640]{1,0:T(8,128)S(1)} %bitcast.42, bf16[256,256]{1,0:T(8,128)(2,1)S(1)} %get-tuple-element.38.high, ...), custom_call_target="tpu_custom_call" | custom-call | flops 251658240 | bytes 4194304 | tf_op jit(solution)/shard_map/pallas_call | solution.py:79
  63.2 1.6 %shard_map.122 = f32[256,896]{1,0:T(8,128)} custom-call(f32[896,256]{1,0:T(8,128)S(1)} %get-tuple-element.56.values, s32[1,256]{1,0:T(1,128)S(1)} %get-tuple-element.55.slots), custom_call_target="tpu_custom_call" | custom-call | flops 352321536 | bytes 4194304 | tf_op jit(solution)/shard_map/pallas_call | solution.py:79
  64.7 21.2 %all-to-all-done.3 = f32[32,8,896]{2,1,0:T(8,128)S(1)} async-done(((f32[32,8,896]{2,1,0:T(8,128)}), f32[32,8,896]{2,1,0:T(8,128)S(1)}, u32[]{:S(2)}, u32[]{:S(2)}) %all-to-all-start.3) | async-done | bytes 917536 | tf_op jit(solution)/shard_map/all_to_all | solution.py:735
  86.0 2.8 %all-to-all-start.2 = ((f32[32,8,896]{2,1,0:T(8,128)}), f32[32,8,896]{2,1,0:T(8,128)S(1)}, u32[]{:S(2)}, u32[]{:S(2)}) async-start(f32[32,8,896]{2,1,0:T(8,128)} %bitcast.17), calls=%async_computation.2 | async-start | bytes 1835008 | tf_op jit(solution)/shard_map/all_to_all | solution.py:735
  88.8 9.1 %shard_map.124.refs_0_ = f32[36,24,256]{2,1,0:T(8,128)S(1)} custom-call(f32[256,896]{1,0:T(8,128)S(1)} %bitcast.39, s32[1,256]{1,0:T(1,128)S(1)} %get-tuple-element.74.labels), custom_call_target="tpu_custom_call" | custom-call | flops 39321600 | bytes 4194304 | tf_op jit(solution)/shard_map/pallas_call | solution.py:79
  98.0 15.4 %all-to-all-done.2 = f32[32,8,896]{2,1,0:T(8,128)S(1)} async-done(((f32[32,8,896]{2,1,0:T(8,128)}), f32[32,8,896]{2,1,0:T(8,128)S(1)}, u32[]{:S(2)}, u32[]{:S(2)}) %all-to-all-start.2) | async-done | bytes 917536 | tf_op jit(solution)/shard_map/all_to_all | solution.py:735
  113.4 9.5 %shard_map.125 = (f32[32,16,256]{2,1,0:T(8,128)S(1)}, f32[2,2,16,256]{3,2,1,0:T(8,128)S(1)}, f32[2,36,2,256]{3,2,1,0:T(2,128)S(1)}) custom-call(f32[256,896]{1,0:T(8,128)S(1)} %bitcast.40, s32[1,256]{1,0:T(1,128)S(1)} %get-tuple-element.75.labels, f32[36,24,256]{2,1,0:T(8,128)S(1)} %shard_map.124.refs_0_), custom_call_target="tpu_custom_call" | custom-call | flops 39321600 | bytes 4194304 | tf_op jit(solution)/shard_map/pallas_call | solution.py:79
  122.9 1.4 %collective-permute-start.6 = (f32[36,2,256]{2,1,0:T(2,128)S(1)}, f32[36,2,256]{2,1,0:T(2,128)S(1)}, u32[]{:S(2)}, u32[]{:S(2)}) collective-permute-start(f32[36,2,256]{2,1,0:T(2,128)S(1)} %get-tuple-element.66), channel_id=1, source_target_pairs={{0,7},{1,0},{2,1},{3,2},{4,3},{5,4},{6,5},{7,6},{8,15},{9,8},{10,9... | collective-permute-start | bytes 221192 | tf_op jit(solution)/shard_map/ppermute | solution.py:98
  124.3 0.6 collective-permute-start.5
  125.0 2.3 %collective-permute-done.6.y_top = f32[36,2,256]{2,1,0:T(2,128)S(1)} collective-permute-done((f32[36,2,256]{2,1,0:T(2,128)S(1)}, f32[36,2,256]{2,1,0:T(2,128)S(1)}, u32[]{:S(2)}, u32[]{:S(2)}) %collective-permute-start.6) | collective-permute-done | bytes 73760 | tf_op jit(solution)/shard_map/ppermute | solution.py:98
  127.3 4.1 %collective-permute-done.5.y_low = f32[36,2,256]{2,1,0:T(2,128)S(1)} collective-permute-done((f32[36,2,256]{2,1,0:T(2,128)S(1)}, f32[36,2,256]{2,1,0:T(2,128)S(1)}, u32[]{:S(2)}, u32[]{:S(2)}) %collective-permute-start.5) | collective-permute-done | bytes 73760 | tf_op jit(solution)/shard_map/ppermute | solution.py:98
  131.4 0.1 collective-permute-start.8
  131.5 0.5 collective-permute-start.7
  132.0 1.2 collective-permute-done.8.x_top
  133.2 1.7 %collective-permute-done.7.x_low = f32[2,16,256]{2,1,0:T(8,128)S(1)} collective-permute-done((f32[2,16,256]{2,1,0:T(8,128)S(1)}, f32[2,16,256]{2,1,0:T(8,128)S(1)}, u32[]{:S(2)}, u32[]{:S(2)}) %collective-permute-start.7) | collective-permute-done | bytes 32800 | tf_op jit(solution)/shard_map/ppermute | solution.py:98
  134.9 0.9 shard_map.127
  (22 shorter events, 0.1 us)
Async XLA Ops:
  0.6 1.0 copy-start.1
  1.8 8.0 %collective-permute-start = (f32[32,256]{1,0:T(8,128)S(1)}, f32[32,256]{1,0:T(8,128)S(1)}, u32[]{:S(2)}, u32[]{:S(2)}) collective-permute-start(f32[32,256]{1,0:T(8,128)S(1)} %get-tuple-element.34), channel_id=1, source_target_pairs={{0,1},{1,2},{2,3},{3,4},{4,5},{5,6},{6,7},{7,0},{8,9},{9,10},{10,1... | collective-permute-start | bytes 98312 | tf_op jit(solution)/shard_map/ppermute | solution.py:98
  4.8 4.9 %collective-permute-start.1 = (f32[32,256]{1,0:T(8,128)S(1)}, f32[32,256]{1,0:T(8,128)S(1)}, u32[]{:S(2)}, u32[]{:S(2)}) collective-permute-start(f32[32,256]{1,0:T(8,128)S(1)} %get-tuple-element.35), channel_id=1, source_target_pairs={{0,7},{1,0},{2,1},{3,2},{4,3},{5,4},{6,5},{7,6},{8,15},{9,8},{10,9... | collective-permute-start | bytes 98312 | tf_op jit(solution)/shard_map/ppermute | solution.py:98
  9.7 2.4 %collective-permute-start.3 = (f32[18,256]{1,0:T(8,128)S(1)}, f32[18,256]{1,0:T(8,128)S(1)}, u32[]{:S(2)}, u32[]{:S(2)}) collective-permute-start(f32[18,256]{1,0:T(8,128)S(1)} %pad_maximum_fusion.3), channel_id=1, source_target_pairs={{0,24},{8,0},{16,8},{24,16},{1,25},{9,1},{17,9},{25,17},{2,26},{10... | collective-permute-start | bytes 55304 | tf_op jit(solution)/shard_map/ppermute | solution.py:98
  10.0 3.5 %collective-permute-start.2 = (f32[18,256]{1,0:T(8,128)S(1)}, f32[18,256]{1,0:T(8,128)S(1)}, u32[]{:S(2)}, u32[]{:S(2)}) collective-permute-start(f32[18,256]{1,0:T(8,128)S(1)} %pad_maximum_fusion.2), channel_id=1, source_target_pairs={{0,8},{8,16},{16,24},{24,0},{1,9},{9,17},{17,25},{25,1},{2,10},{10... | collective-permute-start | bytes 55304 | tf_op jit(solution)/shard_map/ppermute | solution.py:98
  12.1 7.2 %copy-start.4 = (s32[1,1,256,1]{2,3,1,0:T(1,128)S(1)}, s32[1,1,256,1]{2,3,1,0:T(1,128)}, u32[]{:S(2)}) copy-start(s32[1,1,256,1]{2,3,1,0:T(1,128)} %param.11) | copy-start | bytes 3076
  13.5 6.0 %copy-start.5 = (s32[1,1,256]{2,1,0:T(1,128)S(1)}, s32[1,1,256]{2,1,0:T(1,128)}, u32[]{:S(2)}) copy-start(s32[1,1,256]{2,1,0:T(1,128)} %param.12) | copy-start | bytes 3076
  14.8 14.6 %copy-start.2 = (bf16[128,128]{1,0:T(8,128)(2,1)S(1)}, bf16[128,128]{1,0:T(8,128)(2,1)}, u32[]{:S(2)}) copy-start(bf16[128,128]{1,0:T(8,128)(2,1)} %constant.56.clone.hx_low) | copy-start | bytes 98308
  14.8 14.6 %copy-start.3 = (bf16[128,128]{1,0:T(8,128)(2,1)S(1)}, bf16[128,128]{1,0:T(8,128)(2,1)}, u32[]{:S(2)}) copy-start(bf16[128,128]{1,0:T(8,128)(2,1)} %constant.55.clone.hx_high) | copy-start | bytes 98308
  14.8 14.6 %copy-start.6 = (f32[256]{0:T(256)S(1)}, f32[256]{0:T(256)}, u32[]{:S(2)}) copy-start(f32[256]{0:T(256)} %constant.52.clone.lap_z) | copy-start | bytes 3076
  14.8 14.6 %copy-start.7 = (f32[128,128]{1,0:T(8,128)S(1)}, f32[128,128]{1,0:T(8,128)}, u32[]{:S(2)}) copy-start(f32[128,128]{1,0:T(8,128)} %constant.54.clone.lap_xy) | copy-start | bytes 196612
  14.8 14.6 %copy-start.8 = (bf16[128,128]{1,0:T(8,128)(2,1)S(1)}, bf16[128,128]{1,0:T(8,128)(2,1)}, u32[]{:S(2)}) copy-start(bf16[128,128]{1,0:T(8,128)(2,1)} %constant.58.clone.hy_low) | copy-start | bytes 98308
  14.8 14.6 %copy-start.9 = (bf16[128,128]{1,0:T(8,128)(2,1)S(1)}, bf16[128,128]{1,0:T(8,128)(2,1)}, u32[]{:S(2)}) copy-start(bf16[128,128]{1,0:T(8,128)(2,1)} %constant.57.clone.hy_high) | copy-start | bytes 98308
  14.8 14.5 %all-to-all-start = ((f32[16,16,512]{2,1,0:T(8,128)}), f32[16,16,512]{2,1,0:T(8,128)S(1)}, u32[]{:S(2)}, u32[]{:S(2)}) async-start(f32[16,16,512]{2,1,0:T(8,128)} %bitcast.11), calls=%async_computation | async-start | bytes 1048576 | tf_op jit(solution)/shard_map/all_to_all | solution.py:795
  19.3 16.0 %copy-start.16 = (f32[128]{0:T(128)S(1)}, f32[128]{0:T(128)}, u32[]{:S(2)}) copy-start(f32[128]{0:T(128)} %constant.53.clone) | copy-start | bytes 1540
  20.6 0.9 copy-start.10
  21.6 0.7 copy-start.12
  22.3 0.7 copy-start.14
  32.2 7.0 %collective-permute-start.4 = (f32[128,128]{1,0:T(8,128)S(1)}, f32[128,128]{1,0:T(8,128)S(1)}, u32[]{:S(2)}, u32[]{:S(2)}) collective-permute-start(f32[128,128]{1,0:T(8,128)S(1)} %get-tuple-element.47.ends), channel_id=1, source_target_pairs={{0,4},{1,5},{2,6},{3,7},{4,0},{5,1},{6,2},{7,3},{8,12},{9,13},{10,... | collective-permute-start | bytes 196616 | tf_op jit(solution)/shard_map/ppermute | solution.py:823
  39.2 15.7 %copy-start.11 = (f32[3,640,128]{2,1,0:T(8,128)S(1)}, f32[3,640,128]{2,1,0:T(8,128)}, u32[]{:S(2)}) copy-start(f32[3,640,128]{2,1,0:T(8,128)} %copy-done.10) | copy-start | bytes 2949124
  39.2 15.7 %copy-start.13 = (bf16[256,384]{1,0:T(8,128)(2,1)S(1)}, bf16[256,384]{1,0:T(8,128)(2,1)}, u32[]{:S(2)}) copy-start(bf16[256,384]{1,0:T(8,128)(2,1)} %copy-done.12) | copy-start | bytes 589828
  39.2 15.7 %copy-start.15 = (bf16[256,384]{1,0:T(8,128)(2,1)S(1)}, bf16[256,384]{1,0:T(8,128)(2,1)}, u32[]{:S(2)}) copy-start(bf16[256,384]{1,0:T(8,128)(2,1)} %copy-done.14) | copy-start | bytes 589828
  56.7 0.9 copy-start
  57.6 28.4 %all-to-all-start.3 = ((f32[32,8,896]{2,1,0:T(8,128)}), f32[32,8,896]{2,1,0:T(8,128)S(1)}, u32[]{:S(2)}, u32[]{:S(2)}) async-start(f32[32,8,896]{2,1,0:T(8,128)} %bitcast.43), calls=%async_computation.3 | async-start | bytes 1835008 | tf_op jit(solution)/shard_map/all_to_all | solution.py:735
  86.0 27.4 %all-to-all-start.2 = ((f32[32,8,896]{2,1,0:T(8,128)}), f32[32,8,896]{2,1,0:T(8,128)S(1)}, u32[]{:S(2)}, u32[]{:S(2)}) async-start(f32[32,8,896]{2,1,0:T(8,128)} %bitcast.17), calls=%async_computation.2 | async-start | bytes 1835008 | tf_op jit(solution)/shard_map/all_to_all | solution.py:735
  122.9 4.4 %collective-permute-start.6 = (f32[36,2,256]{2,1,0:T(2,128)S(1)}, f32[36,2,256]{2,1,0:T(2,128)S(1)}, u32[]{:S(2)}, u32[]{:S(2)}) collective-permute-start(f32[36,2,256]{2,1,0:T(2,128)S(1)} %get-tuple-element.66), channel_id=1, source_target_pairs={{0,7},{1,0},{2,1},{3,2},{4,3},{5,4},{6,5},{7,6},{8,15},{9,8},{10,9... | collective-permute-start | bytes 221192 | tf_op jit(solution)/shard_map/ppermute | solution.py:98
  124.3 7.0 %collective-permute-start.5 = (f32[36,2,256]{2,1,0:T(2,128)S(1)}, f32[36,2,256]{2,1,0:T(2,128)S(1)}, u32[]{:S(2)}, u32[]{:S(2)}) collective-permute-start(f32[36,2,256]{2,1,0:T(2,128)S(1)} %get-tuple-element.67), channel_id=1, source_target_pairs={{0,1},{1,2},{2,3},{3,4},{4,5},{5,6},{6,7},{7,0},{8,9},{9,10},{10,1... | collective-permute-start | bytes 221192 | tf_op jit(solution)/shard_map/ppermute | solution.py:98
  131.4 1.7 %collective-permute-start.8 = (f32[2,16,256]{2,1,0:T(8,128)S(1)}, f32[2,16,256]{2,1,0:T(8,128)S(1)}, u32[]{:S(2)}, u32[]{:S(2)}) collective-permute-start(f32[2,16,256]{2,1,0:T(8,128)S(1)} %get-tuple-element.68), channel_id=1, source_target_pairs={{0,24},{8,0},{16,8},{24,16},{1,25},{9,1},{17,9},{25,17},{2,26},{10... | collective-permute-start | bytes 98312 | tf_op jit(solution)/shard_map/ppermute | solution.py:98
  131.5 3.4 %collective-permute-start.7 = (f32[2,16,256]{2,1,0:T(8,128)S(1)}, f32[2,16,256]{2,1,0:T(8,128)S(1)}, u32[]{:S(2)}, u32[]{:S(2)}) collective-permute-start(f32[2,16,256]{2,1,0:T(8,128)S(1)} %get-tuple-element.69), channel_id=1, source_target_pairs={{0,8},{8,16},{16,24},{24,0},{1,9},{9,17},{17,25},{25,1},{2,10},{10... | collective-permute-start | bytes 98312 | tf_op jit(solution)/shard_map/ppermute | solution.py:98

commit v8 on v7

--- a/solution.py
+++ b/solution.py
@@ -265,7 +265,7 @@
 def half_kernel(
     tiles_x, tiles_y, rows_x, rows_y, scale, mark,
     first, lap_z, slab, labels, lap_xy, hx_high, hx_low, hy_high, hy_low,
-    found, ends, planes,
+    found, ends, sent, planes,
 ):
     grid_x = tiles_x * rows_x
     count = slab.shape[1] // 2
@@ -306,12 +306,16 @@
     ends[...] = block
     tiles = labels.shape[0]
     ends[0:tiles, :] = jnp.where(lane[0:tiles] < mark, block[0:tiles], labels[...])
+    turned = jnp.transpose(ends[...])
+    used = 4 * count + 8
+    sent[0:used, :] = turned[0:used]
+    sent[used:, :] = turned[mark : mark + sent.shape[0] - used]
 
 
 def join_kernel(
     tiles_x, tiles_y, rows_x, rows_y, places,
-    first, half, found, ends, arrived, labels, even, odd, edge_even, edge_odd, spread, hx_high, hx_low,
-    out, planes, faces,
+    first, half, found, ends, received, labels, even, odd, edge_even, edge_odd, spread, hx_high, hx_low,
+    out, planes, faces, arrived,
 ):
     grid_x = tiles_x * rows_x
     count = found.shape[0]
@@ -324,6 +328,13 @@
 
     dims = (grid_x, LANES)
     lane, row = iota(dims, 1), iota(dims, 0)
+    used = 4 * count + 8
+    mark = 2 * (rows_x + rows_y)
+    gap = jnp.zeros((mark - used, LANES), F32)
+    rest = jnp.zeros((LANES - mark - received.shape[0] + used, LANES), F32)
+    arrived[...] = jnp.transpose(
+        jnp.concatenate([received[0:used, :], gap, received[used:, :], rest], 0)
+    )
     jump = jnp.where(lane < 4 * count + 1, arrived[...] - ends[...], 0.0)
     pieces = split(jump, 2)
     wide = dot(pieces[0], spread[...]) + dot(pieces[1], spread[...])
@@ -812,19 +823,20 @@
             (cube, cube, square, square, shape(LANES, 2 * planes * LANES, dtype=BF16)),
             [], 16, 100 * planes * grid_x * LANES, 2 << 20, 2,
         )(first, lap_z, lap_x)
-        found, ends = call(
+        found, ends, sent_ends = call(
             functools.partial(
                 half_kernel, tiles_x, span, rows_x, rows_y,
                 SECOND_ORDER / (grid_x * length * cells_z), 2 * (rows_x + rows_y),
             ),
-            (cube, square), [pltpu.VMEM((grid_x * planes, LANES), F32)],
+            (cube, square, shape(4 * planes + 8 + 2 * half, grid_x)),
+            [pltpu.VMEM((grid_x * planes, LANES), F32)],
             12, 12 * planes * grid_x**2 * LANES, 2 << 20, 2,
         )(first, lap_z, slab, labels, lap_xy, *x_table, *y_table)
-        arrived_ends = lax.ppermute(ends, "py", [(j, (j + span) % tiles_y) for j in range(tiles_y)])
+        arrived_ends = lax.ppermute(sent_ends, "py", [(j, (j + span) % tiles_y) for j in range(tiles_y)])
         returned = call(
             functools.partial(join_kernel, tiles_x, span, rows_x, rows_y, 2 * half),
             shape(tiles // 2, 2 * planes, used),
-            [pltpu.VMEM((grid_x * planes, LANES), F32), pltpu.VMEM((LANES, grid_x), F32)],
+            [pltpu.VMEM((grid_x * planes, LANES), F32)] + [pltpu.VMEM((LANES, grid_x), F32)] * 2,
             12, 12 * planes * grid_x**2 * LANES, 2 << 20, 2,
         )(first, own, found, ends, arrived_ends, labels, *tables, *x_table)
         modes = exchange_half(returned.reshape(cells_z, used))

time: 136 us -> 135 us (level)
  waiting for transfers between devices: 57.9 us -> 56.3 us
    ppermute x1, waiting for transfers between devices: 2.31 us -> 0.75 us  [per_device(): lax.ppermute(sent_ends, 'py', [(j, (j + span) % tiles_y) for j in range(t...]
where the time goes in v8:
time: 135 us; the launch traced here: 134 us
  waiting for transfers between devices  56.3 us (42%)
  Pallas kernels  35 us (26%)
  starting transfers between devices  23.1 us (17%)
  blocking collectives  14.3 us (11%)
  local copies, waits for them, and re-layouts  4.54 us (3%)
    all_to_all x2, waiting for transfers between devices, exchange(): return lax.all_to_all(x, both, split_axis=0, concat_axis=0, tiled=True)  36.7 us
    pallas_call x14, Pallas kernels, run(): pl.pallas_call(body, out_shape=outs, in_specs=[SMEM] * scalars + [VMEM] *...  34.9 us
    all_to_all x1, blocking collectives, exchange_half(): return lax.all_to_all(x, both, 0, 0, axis_index_groups=groups, tiled=True)  14.3 us
    ppermute x8, waiting for transfers between devices, send(): return lax.ppermute(x, axis, [(i, (i + step) % size) for i in range(size)])  12.5 us
    ppermute x8, starting transfers between devices, send(): return lax.ppermute(x, axis, [(i, (i + step) % size) for i in range(size)])  9.32 us
    all_to_all x1, waiting for transfers between devices, exchange_half(): return lax.all_to_all(x, both, 0, 0, axis_index_groups=groups, tiled=True)  6.38 us
    all_to_all x2, starting transfers between devices, exchange(): return lax.all_to_all(x, both, split_axis=0, concat_axis=0, tiled=True)  6.13 us
    all_to_all x1, starting transfers between devices, exchange_half(): return lax.all_to_all(x, both, 0, 0, axis_index_groups=groups, tiled=True)  4.51 us
  transfers between devices with their start and end apart: 12, of which 10 were waited for; matrix products, arithmetic and copies ran while one was open for 0% of the time, Pallas kernels for 13%

profile of v8, /device:TPU:0, one launch (start us, length us, event | category | flops | bytes accessed | tf_op | source)
XLA Modules:
  0.0 134.1 jit_solution(1384632733087361340)
XLA Ops:
  0.6 0.0 copy-start.1
  0.6 1.0 copy-done.1
  1.7 0.1 shard_map.113
  1.8 3.0 %collective-permute-start = (f32[32,256]{1,0:T(8,128)S(1)}, f32[32,256]{1,0:T(8,128)S(1)}, u32[]{:S(2)}, u32[]{:S(2)}) collective-permute-start(f32[32,256]{1,0:T(8,128)S(1)} %get-tuple-element.35), channel_id=1, source_target_pairs={{0,1},{1,2},{2,3},{3,4},{4,5},{5,6},{6,7},{7,0},{8,9},{9,10},{10,1... | collective-permute-start | bytes 98312 | tf_op jit(solution)/shard_map/ppermute | solution.py:98
  4.8 3.1 %collective-permute-start.1 = (f32[32,256]{1,0:T(8,128)S(1)}, f32[32,256]{1,0:T(8,128)S(1)}, u32[]{:S(2)}, u32[]{:S(2)}) collective-permute-start(f32[32,256]{1,0:T(8,128)S(1)} %get-tuple-element.36), channel_id=1, source_target_pairs={{0,7},{1,0},{2,1},{3,2},{4,3},{5,4},{6,5},{7,6},{8,15},{9,8},{10,9... | collective-permute-start | bytes 98312 | tf_op jit(solution)/shard_map/ppermute | solution.py:98
  7.9 1.8 %collective-permute-done = f32[32,256]{1,0:T(8,128)S(1)} collective-permute-done((f32[32,256]{1,0:T(8,128)S(1)}, f32[32,256]{1,0:T(8,128)S(1)}, u32[]{:S(2)}, u32[]{:S(2)}) %collective-permute-start) | collective-permute-done | bytes 32800 | tf_op jit(solution)/shard_map/ppermute | solution.py:98
  9.7 0.0 collective-permute-done.1
  9.7 0.2 collective-permute-start.3
  10.0 0.3 collective-permute-start.2
  10.3 1.8 %shard_map.114 = (bf16[512,256]{1,0:T(8,128)(2,1)S(1)}, bf16[512,256]{1,0:T(8,128)(2,1)S(1)}, bf16[256,256]{1,0:T(8,128)(2,1)S(1)}, bf16[256,256]{1,0:T(8,128)(2,1)S(1)}) custom-call(f32[32,16,256]{2,1,0:T(8,128)S(1)} %get-tuple-element.34.core, f32[2,32,256]{2,1,0:T(8,128)S(1)} %pad_maximum_fusion.y_faces), custom_call_target="tpu_custom_call" | custom-call | flops 7864320 | bytes 2097152 | tf_op jit(solution)/shard_map/pallas_call | solution.py:79
  12.1 0.0 copy-start.4
  12.1 0.0 collective-permute-done.3
  12.1 1.3 %collective-permute-done.2 = f32[18,256]{1,0:T(8,128)S(1)} collective-permute-done((f32[18,256]{1,0:T(8,128)S(1)}, f32[18,256]{1,0:T(8,128)S(1)}, u32[]{:S(2)}, u32[]{:S(2)}) %collective-permute-start.2) | collective-permute-done | bytes 18464 | tf_op jit(solution)/shard_map/ppermute | solution.py:98
  13.5 1.3 shard_map.115
  14.8 0.0 copy-start.8
  14.8 0.0 copy-start.9
  14.8 4.5 %all-to-all-start = ((f32[16,16,512]{2,1,0:T(8,128)}), f32[16,16,512]{2,1,0:T(8,128)S(1)}, u32[]{:S(2)}, u32[]{:S(2)}) async-start(f32[16,16,512]{2,1,0:T(8,128)} %bitcast.11), calls=%async_computation | async-start | bytes 1048576 | tf_op jit(solution)/shard_map/all_to_all | solution.py:806
  19.3 0.0 copy-start.16
  19.3 0.0 copy-done.4
  19.4 0.1 copy.12.owner_col
  19.5 0.0 copy-done.5
  19.5 0.2 shard_map.117
  19.8 0.9 shard_map.116
  20.6 0.0 copy-start.10
  20.6 0.9 copy-done.10
  21.6 0.7 copy-done.12
  22.3 0.7 copy-done.14
  22.9 6.4 %all-to-all-done.slab = f32[16,16,512]{2,1,0:T(8,128)S(1)} async-done(((f32[16,16,512]{2,1,0:T(8,128)}), f32[16,16,512]{2,1,0:T(8,128)S(1)}, u32[]{:S(2)}, u32[]{:S(2)}) %all-to-all-start) | async-done | bytes 524320 | tf_op jit(solution)/shard_map/all_to_all | solution.py:806
  29.3 0.0 copy-done.2
  29.3 0.0 copy-done.3
  29.3 0.0 copy-done.6
  29.3 0.0 copy-done.7
  29.3 0.0 copy-done.8
  29.3 0.0 copy-done.9
  29.4 2.9 %shard_map.118 = (f32[8,128,128]{2,1,0:T(8,128)S(1)}, f32[128,128]{1,0:T(8,128)S(1)}, f32[56,128]{1,0:T(8,128)S(1)}) custom-call(s32[1]{0:T(128)} %bitcast.12.first, f32[256]{0:T(256)S(1)} %copy-done.6, f32[16,16,512]{2,1,0:T(8,128)S(1)} %all-to-all-done.slab, f32[32,128]{1,0:T(8,128)S(1)} %get-tuple-element.46.labels, f32[128,128]{1,0:T(8,128)S(1)} %copy-done.7, ...), custom_call_target="tpu_custom_call" | custom-call | flops 201326592 | bytes 2097152 | tf_op jit(solution)/shard_map/pallas_call | solution.py:79
  32.2 3.1 %collective-permute-start.4 = (f32[56,128]{1,0:T(8,128)S(1)}, f32[56,128]{1,0:T(8,128)S(1)}, u32[]{:S(2)}, u32[]{:S(2)}) collective-permute-start(f32[56,128]{1,0:T(8,128)S(1)} %get-tuple-element.49), channel_id=1, source_target_pairs={{0,4},{1,5},{2,6},{3,7},{4,0},{5,1},{6,2},{7,3},{8,12},{9,13},{10,... | collective-permute-start | bytes 86024 | tf_op jit(solution)/shard_map/ppermute | solution.py:835
  35.4 0.0 copy-done.16
  35.4 0.1 jit_solution_.3.lap_x
  35.4 1.6 %shard_map.119 = (f32[8,128,128]{2,1,0:T(8,128)S(1)}, f32[8,128,128]{2,1,0:T(8,128)S(1)}, f32[128,128]{1,0:T(8,128)S(1)}, f32[128,128]{1,0:T(8,128)S(1)}, bf16[128,2048]{1,0:T(8,128)(2,1)S(1)}) custom-call(s32[1]{0:T(128)} %bitcast.12.first, f32[256]{0:T(256)S(1)} %copy-done.6, f32[128,128]{1,0:T(8,128)S(1)} %jit_solution_.3.lap_x), custom_call_target="tpu_custom_call" | custom-call | flops 13107200 | bytes 2097152 | tf_op jit(solution)/shard_map/pallas_call | solution.py:79
  37.0 0.8 collective-permute-done.4.received
  37.8 1.5 %shard_map.120 = f32[16,16,640]{2,1,0:T(8,128)S(1)} custom-call(s32[1]{0:T(128)} %bitcast.12.first, s32[1]{0:T(128)} %bitcast.half.own, f32[8,128,128]{2,1,0:T(8,128)S(1)} %get-tuple-element.47.found, f32[128,128]{1,0:T(8,128)S(1)} %get-tuple-element.48.ends, f32[56,128]{1,0:T(8,128)S(1)} %collective-permute-done.4.received, ...), custom_call_target="tpu_custom_call" | custom-call | flops 201326592 | bytes 2097152 | tf_op jit(solution)/shard_map/pallas_call | solution.py:79
  39.3 14.3 %all_to_all.39 = f32[16,16,640]{2,1,0:T(8,128)S(1)} all-to-all(f32[16,16,640]{2,1,0:T(8,128)S(1)} %shard_map.120), channel_id=1, replica_groups={{0,1,2,3,8,9,10,11,16,17,18,19,24,25,26,27},{4,5,6,7,12,13,14,15,20,21,..., dimensions={0} | all-to-all | bytes 1310720 | tf_op jit(solution)/shard_map/all_to_all | solution.py:806
  53.5 0.0 copy-done.11
  53.5 0.0 copy-done.15
  53.5 1.7 %shard_map.121 = (f32[256,896]{1,0:T(8,128)S(1)}, f32[896,256]{1,0:T(8,128)S(1)}, s32[2,1,256]{2,1,0:T(1,128)S(1)}) custom-call(s32[1]{0:T(128)} %bitcast.half.own, f32[3,640,128]{2,1,0:T(8,128)S(1)} %copy-done.11, f32[256,640]{1,0:T(8,128)S(1)} %bitcast.41, bf16[256,384]{1,0:T(8,128)(2,1)S(1)} %copy-done.13, bf16[256,384]{1,0:T(8,128)(2,1)S(1)} %copy-done.15, ...), custom_call_target="tpu_custom_call" | custom-call | flops 838860800 | bytes 6291456 | tf_op jit(solution)/shard_map/pallas_call | solution.py:79
  55.3 0.0 copy-start
  55.3 0.9 copy-done
  56.2 3.3 %all-to-all-start.3 = ((f32[32,8,896]{2,1,0:T(8,128)}), f32[32,8,896]{2,1,0:T(8,128)S(1)}, u32[]{:S(2)}, u32[]{:S(2)}) async-start(f32[32,8,896]{2,1,0:T(8,128)} %bitcast.43), calls=%async_computation.3 | async-start | bytes 1835008 | tf_op jit(solution)/shard_map/all_to_all | solution.py:746
  59.5 2.0 %shard_map.123 = f32[3,32,16,256]{3,2,1,0:T(8,128)} custom-call(f32[32,16,256]{2,1,0:T(8,128)S(1)} %get-tuple-element.34.core, f32[2,18,256]{2,1,0:T(8,128)S(1)} %pad_maximum_fusion.1.x_faces, f32[2,32,256]{2,1,0:T(8,128)S(1)} %pad_maximum_fusion.y_faces, f32[256,640]{1,0:T(8,128)S(1)} %bitcast.42, bf16[256,256]{1,0:T(8,128)(2,1)S(1)} %get-tuple-element.39.high, ...), custom_call_target="tpu_custom_call" | custom-call | flops 251658240 | bytes 4194304 | tf_op jit(solution)/shard_map/pallas_call | solution.py:79
  61.5 1.6 %shard_map.122 = f32[256,896]{1,0:T(8,128)} custom-call(f32[896,256]{1,0:T(8,128)S(1)} %get-tuple-element.58.values, s32[1,256]{1,0:T(1,128)S(1)} %get-tuple-element.57.slots), custom_call_target="tpu_custom_call" | custom-call | flops 352321536 | bytes 4194304 | tf_op jit(solution)/shard_map/pallas_call | solution.py:79
  63.0 21.2 %all-to-all-done.3 = f32[32,8,896]{2,1,0:T(8,128)S(1)} async-done(((f32[32,8,896]{2,1,0:T(8,128)}), f32[32,8,896]{2,1,0:T(8,128)S(1)}, u32[]{:S(2)}, u32[]{:S(2)}) %all-to-all-start.3) | async-done | bytes 917536 | tf_op jit(solution)/shard_map/all_to_all | solution.py:746
  84.3 2.8 %all-to-all-start.2 = ((f32[32,8,896]{2,1,0:T(8,128)}), f32[32,8,896]{2,1,0:T(8,128)S(1)}, u32[]{:S(2)}, u32[]{:S(2)}) async-start(f32[32,8,896]{2,1,0:T(8,128)} %bitcast.17), calls=%async_computation.2 | async-start | bytes 1835008 | tf_op jit(solution)/shard_map/all_to_all | solution.py:746
  87.1 9.1 %shard_map.124.refs_0_ = f32[36,24,256]{2,1,0:T(8,128)S(1)} custom-call(f32[256,896]{1,0:T(8,128)S(1)} %bitcast.39, s32[1,256]{1,0:T(1,128)S(1)} %get-tuple-element.76.labels), custom_call_target="tpu_custom_call" | custom-call | flops 39321600 | bytes 4194304 | tf_op jit(solution)/shard_map/pallas_call | solution.py:79
  96.3 15.4 %all-to-all-done.2 = f32[32,8,896]{2,1,0:T(8,128)S(1)} async-done(((f32[32,8,896]{2,1,0:T(8,128)}), f32[32,8,896]{2,1,0:T(8,128)S(1)}, u32[]{:S(2)}, u32[]{:S(2)}) %all-to-all-start.2) | async-done | bytes 917536 | tf_op jit(solution)/shard_map/all_to_all | solution.py:746
  111.7 9.5 %shard_map.125 = (f32[32,16,256]{2,1,0:T(8,128)S(1)}, f32[2,2,16,256]{3,2,1,0:T(8,128)S(1)}, f32[2,36,2,256]{3,2,1,0:T(2,128)S(1)}) custom-call(f32[256,896]{1,0:T(8,128)S(1)} %bitcast.40, s32[1,256]{1,0:T(1,128)S(1)} %get-tuple-element.77.labels, f32[36,24,256]{2,1,0:T(8,128)S(1)} %shard_map.124.refs_0_), custom_call_target="tpu_custom_call" | custom-call | flops 39321600 | bytes 4194304 | tf_op jit(solution)/shard_map/pallas_call | solution.py:79
  121.2 1.4 %collective-permute-start.6 = (f32[36,2,256]{2,1,0:T(2,128)S(1)}, f32[36,2,256]{2,1,0:T(2,128)S(1)}, u32[]{:S(2)}, u32[]{:S(2)}) collective-permute-start(f32[36,2,256]{2,1,0:T(2,128)S(1)} %get-tuple-element.68), channel_id=1, source_target_pairs={{0,7},{1,0},{2,1},{3,2},{4,3},{5,4},{6,5},{7,6},{8,15},{9,8},{10,9... | collective-permute-start | bytes 221192 | tf_op jit(solution)/shard_map/ppermute | solution.py:98
  122.6 0.6 collective-permute-start.5
  123.3 2.3 %collective-permute-done.6.y_top = f32[36,2,256]{2,1,0:T(2,128)S(1)} collective-permute-done((f32[36,2,256]{2,1,0:T(2,128)S(1)}, f32[36,2,256]{2,1,0:T(2,128)S(1)}, u32[]{:S(2)}, u32[]{:S(2)}) %collective-permute-start.6) | collective-permute-done | bytes 73760 | tf_op jit(solution)/shard_map/ppermute | solution.py:98
  125.6 4.1 %collective-permute-done.5.y_low = f32[36,2,256]{2,1,0:T(2,128)S(1)} collective-permute-done((f32[36,2,256]{2,1,0:T(2,128)S(1)}, f32[36,2,256]{2,1,0:T(2,128)S(1)}, u32[]{:S(2)}, u32[]{:S(2)}) %collective-permute-start.5) | collective-permute-done | bytes 73760 | tf_op jit(solution)/shard_map/ppermute | solution.py:98
  129.7 0.1 collective-permute-start.8
  129.8 0.5 collective-permute-start.7
  130.3 1.2 collective-permute-done.8.x_top
  131.5 1.7 %collective-permute-done.7.x_low = f32[2,16,256]{2,1,0:T(8,128)S(1)} collective-permute-done((f32[2,16,256]{2,1,0:T(8,128)S(1)}, f32[2,16,256]{2,1,0:T(8,128)S(1)}, u32[]{:S(2)}, u32[]{:S(2)}) %collective-permute-start.7) | collective-permute-done | bytes 32800 | tf_op jit(solution)/shard_map/ppermute | solution.py:98
  133.2 0.9 shard_map.127
  (22 shorter events, 0.1 us)
Async XLA Ops:
  0.6 1.0 copy-start.1
  1.8 8.0 %collective-permute-start = (f32[32,256]{1,0:T(8,128)S(1)}, f32[32,256]{1,0:T(8,128)S(1)}, u32[]{:S(2)}, u32[]{:S(2)}) collective-permute-start(f32[32,256]{1,0:T(8,128)S(1)} %get-tuple-element.35), channel_id=1, source_target_pairs={{0,1},{1,2},{2,3},{3,4},{4,5},{5,6},{6,7},{7,0},{8,9},{9,10},{10,1... | collective-permute-start | bytes 98312 | tf_op jit(solution)/shard_map/ppermute | solution.py:98
  4.8 4.9 %collective-permute-start.1 = (f32[32,256]{1,0:T(8,128)S(1)}, f32[32,256]{1,0:T(8,128)S(1)}, u32[]{:S(2)}, u32[]{:S(2)}) collective-permute-start(f32[32,256]{1,0:T(8,128)S(1)} %get-tuple-element.36), channel_id=1, source_target_pairs={{0,7},{1,0},{2,1},{3,2},{4,3},{5,4},{6,5},{7,6},{8,15},{9,8},{10,9... | collective-permute-start | bytes 98312 | tf_op jit(solution)/shard_map/ppermute | solution.py:98
  9.7 2.4 %collective-permute-start.3 = (f32[18,256]{1,0:T(8,128)S(1)}, f32[18,256]{1,0:T(8,128)S(1)}, u32[]{:S(2)}, u32[]{:S(2)}) collective-permute-start(f32[18,256]{1,0:T(8,128)S(1)} %pad_maximum_fusion.3), channel_id=1, source_target_pairs={{0,24},{8,0},{16,8},{24,16},{1,25},{9,1},{17,9},{25,17},{2,26},{10... | collective-permute-start | bytes 55304 | tf_op jit(solution)/shard_map/ppermute | solution.py:98
  10.0 3.5 %collective-permute-start.2 = (f32[18,256]{1,0:T(8,128)S(1)}, f32[18,256]{1,0:T(8,128)S(1)}, u32[]{:S(2)}, u32[]{:S(2)}) collective-permute-start(f32[18,256]{1,0:T(8,128)S(1)} %pad_maximum_fusion.2), channel_id=1, source_target_pairs={{0,8},{8,16},{16,24},{24,0},{1,9},{9,17},{17,25},{25,1},{2,10},{10... | collective-permute-start | bytes 55304 | tf_op jit(solution)/shard_map/ppermute | solution.py:98
  12.1 7.2 %copy-start.4 = (s32[1,1,256,1]{2,3,1,0:T(1,128)S(1)}, s32[1,1,256,1]{2,3,1,0:T(1,128)}, u32[]{:S(2)}) copy-start(s32[1,1,256,1]{2,3,1,0:T(1,128)} %param.11) | copy-start | bytes 3076
  13.5 6.0 %copy-start.5 = (s32[1,1,256]{2,1,0:T(1,128)S(1)}, s32[1,1,256]{2,1,0:T(1,128)}, u32[]{:S(2)}) copy-start(s32[1,1,256]{2,1,0:T(1,128)} %param.12) | copy-start | bytes 3076
  14.8 14.6 %copy-start.2 = (bf16[128,128]{1,0:T(8,128)(2,1)S(1)}, bf16[128,128]{1,0:T(8,128)(2,1)}, u32[]{:S(2)}) copy-start(bf16[128,128]{1,0:T(8,128)(2,1)} %constant.56.clone.hx_low) | copy-start | bytes 98308
  14.8 14.6 %copy-start.3 = (bf16[128,128]{1,0:T(8,128)(2,1)S(1)}, bf16[128,128]{1,0:T(8,128)(2,1)}, u32[]{:S(2)}) copy-start(bf16[128,128]{1,0:T(8,128)(2,1)} %constant.55.clone.hx_high) | copy-start | bytes 98308
  14.8 14.6 %copy-start.6 = (f32[256]{0:T(256)S(1)}, f32[256]{0:T(256)}, u32[]{:S(2)}) copy-start(f32[256]{0:T(256)} %constant.52.clone.lap_z) | copy-start | bytes 3076
  14.8 14.6 %copy-start.7 = (f32[128,128]{1,0:T(8,128)S(1)}, f32[128,128]{1,0:T(8,128)}, u32[]{:S(2)}) copy-start(f32[128,128]{1,0:T(8,128)} %constant.54.clone.lap_xy) | copy-start | bytes 196612
  14.8 14.6 %copy-start.8 = (bf16[128,128]{1,0:T(8,128)(2,1)S(1)}, bf16[128,128]{1,0:T(8,128)(2,1)}, u32[]{:S(2)}) copy-start(bf16[128,128]{1,0:T(8,128)(2,1)} %constant.58.clone.hy_low) | copy-start | bytes 98308
  14.8 14.6 %copy-start.9 = (bf16[128,128]{1,0:T(8,128)(2,1)S(1)}, bf16[128,128]{1,0:T(8,128)(2,1)}, u32[]{:S(2)}) copy-start(bf16[128,128]{1,0:T(8,128)(2,1)} %constant.57.clone.hy_high) | copy-start | bytes 98308
  14.8 14.5 %all-to-all-start = ((f32[16,16,512]{2,1,0:T(8,128)}), f32[16,16,512]{2,1,0:T(8,128)S(1)}, u32[]{:S(2)}, u32[]{:S(2)}) async-start(f32[16,16,512]{2,1,0:T(8,128)} %bitcast.11), calls=%async_computation | async-start | bytes 1048576 | tf_op jit(solution)/shard_map/all_to_all | solution.py:806
  19.3 16.0 %copy-start.16 = (f32[128]{0:T(128)S(1)}, f32[128]{0:T(128)}, u32[]{:S(2)}) copy-start(f32[128]{0:T(128)} %constant.53.clone) | copy-start | bytes 1540
  20.6 0.9 copy-start.10
  21.6 0.7 copy-start.12
  22.3 0.7 copy-start.14
  32.2 5.5 %collective-permute-start.4 = (f32[56,128]{1,0:T(8,128)S(1)}, f32[56,128]{1,0:T(8,128)S(1)}, u32[]{:S(2)}, u32[]{:S(2)}) collective-permute-start(f32[56,128]{1,0:T(8,128)S(1)} %get-tuple-element.49), channel_id=1, source_target_pairs={{0,4},{1,5},{2,6},{3,7},{4,0},{5,1},{6,2},{7,3},{8,12},{9,13},{10,... | collective-permute-start | bytes 86024 | tf_op jit(solution)/shard_map/ppermute | solution.py:835
  37.7 15.8 %copy-start.11 = (f32[3,640,128]{2,1,0:T(8,128)S(1)}, f32[3,640,128]{2,1,0:T(8,128)}, u32[]{:S(2)}) copy-start(f32[3,640,128]{2,1,0:T(8,128)} %copy-done.10) | copy-start | bytes 2949124
  37.7 15.8 %copy-start.13 = (bf16[256,384]{1,0:T(8,128)(2,1)S(1)}, bf16[256,384]{1,0:T(8,128)(2,1)}, u32[]{:S(2)}) copy-start(bf16[256,384]{1,0:T(8,128)(2,1)} %copy-done.12) | copy-start | bytes 589828
  37.8 15.8 %copy-start.15 = (bf16[256,384]{1,0:T(8,128)(2,1)S(1)}, bf16[256,384]{1,0:T(8,128)(2,1)}, u32[]{:S(2)}) copy-start(bf16[256,384]{1,0:T(8,128)(2,1)} %copy-done.14) | copy-start | bytes 589828
  55.3 0.9 copy-start
  56.2 28.1 %all-to-all-start.3 = ((f32[32,8,896]{2,1,0:T(8,128)}), f32[32,8,896]{2,1,0:T(8,128)S(1)}, u32[]{:S(2)}, u32[]{:S(2)}) async-start(f32[32,8,896]{2,1,0:T(8,128)} %bitcast.43), calls=%async_computation.3 | async-start | bytes 1835008 | tf_op jit(solution)/shard_map/all_to_all | solution.py:746
  84.3 27.4 %all-to-all-start.2 = ((f32[32,8,896]{2,1,0:T(8,128)}), f32[32,8,896]{2,1,0:T(8,128)S(1)}, u32[]{:S(2)}, u32[]{:S(2)}) async-start(f32[32,8,896]{2,1,0:T(8,128)} %bitcast.17), calls=%async_computation.2 | async-start | bytes 1835008 | tf_op jit(solution)/shard_map/all_to_all | solution.py:746
  121.2 4.4 %collective-permute-start.6 = (f32[36,2,256]{2,1,0:T(2,128)S(1)}, f32[36,2,256]{2,1,0:T(2,128)S(1)}, u32[]{:S(2)}, u32[]{:S(2)}) collective-permute-start(f32[36,2,256]{2,1,0:T(2,128)S(1)} %get-tuple-element.68), channel_id=1, source_target_pairs={{0,7},{1,0},{2,1},{3,2},{4,3},{5,4},{6,5},{7,6},{8,15},{9,8},{10,9... | collective-permute-start | bytes 221192 | tf_op jit(solution)/shard_map/ppermute | solution.py:98
  122.6 7.0 %collective-permute-start.5 = (f32[36,2,256]{2,1,0:T(2,128)S(1)}, f32[36,2,256]{2,1,0:T(2,128)S(1)}, u32[]{:S(2)}, u32[]{:S(2)}) collective-permute-start(f32[36,2,256]{2,1,0:T(2,128)S(1)} %get-tuple-element.69), channel_id=1, source_target_pairs={{0,1},{1,2},{2,3},{3,4},{4,5},{5,6},{6,7},{7,0},{8,9},{9,10},{10,1... | collective-permute-start | bytes 221192 | tf_op jit(solution)/shard_map/ppermute | solution.py:98
  129.7 1.7 %collective-permute-start.8 = (f32[2,16,256]{2,1,0:T(8,128)S(1)}, f32[2,16,256]{2,1,0:T(8,128)S(1)}, u32[]{:S(2)}, u32[]{:S(2)}) collective-permute-start(f32[2,16,256]{2,1,0:T(8,128)S(1)} %get-tuple-element.70), channel_id=1, source_target_pairs={{0,24},{8,0},{16,8},{24,16},{1,25},{9,1},{17,9},{25,17},{2,26},{10... | collective-permute-start | bytes 98312 | tf_op jit(solution)/shard_map/ppermute | solution.py:98
  129.8 3.4 %collective-permute-start.7 = (f32[2,16,256]{2,1,0:T(8,128)S(1)}, f32[2,16,256]{2,1,0:T(8,128)S(1)}, u32[]{:S(2)}, u32[]{:S(2)}) collective-permute-start(f32[2,16,256]{2,1,0:T(8,128)S(1)} %get-tuple-element.71), channel_id=1, source_target_pairs={{0,8},{8,16},{16,24},{24,0},{1,9},{9,17},{17,25},{25,1},{2,10},{10... | collective-permute-start | bytes 98312 | tf_op jit(solution)/shard_map/ppermute | solution.py:98

commit v9 on v8

--- a/solution.py
+++ b/solution.py
@@ -218,6 +218,17 @@
 
 def placed(pieces, choose):
     return dot(pieces[0], choose) + dot(pieces[1], choose) + dot(pieces[2], choose)
+
+
+def gathered(planes, choose, step):
+    count, rows, _ = planes.shape
+    pieces = jnp.concatenate(split(planes[...].reshape(count * rows, LANES), 3), 1)
+    choose = choose.astype(BF16)
+    picked = dot(pieces, jnp.concatenate([choose] * 3, 0))
+    total = picked[0:rows]
+    for q in range(1, count):
+        total = total + pltpu.roll(picked[q * rows : (q + 1) * rows], step * q, 1)
+    return total
 
 
 def iota(dims, axis):
@@ -296,13 +307,11 @@
         anchor = eigen == 0.0
         value = times_y(jnp.where(anchor, 0.0, scale / jnp.where(anchor, -1.0, eigen)) * modes)
         found[q] = value
-        source = lane - 4 * q
-        source = source // 2 * length + source % 2 * (length - 1)
-        choose = (row == source) & (lane >= 4 * q) & (lane < 4 * q + 4)
-        block = block + placed(split(value, 3), choose.astype(BF16))
         if q == 0:
             mean = pltpu.roll(modes * scale, 4 * count, 1)
             block = block + jnp.where((row == 0) & (lane == 4 * count), mean, 0.0)
+    choose = (row == lane // 2 * length + lane % 2 * (length - 1)) & (lane < 4)
+    block = block + gathered(found, choose, 4)
     ends[...] = block
     tiles = labels.shape[0]
     ends[0:tiles, :] = jnp.where(lane[0:tiles] < mark, block[0:tiles], labels[...])

time: 135 us -> 134 us (level)
  no operation moved by 1% of the time
where the time goes in v9:
time: 134 us; the launch traced here: 133 us
  waiting for transfers between devices  56.3 us (42%)
  Pallas kernels  34.4 us (26%)
  starting transfers between devices  23.1 us (17%)
  blocking collectives  14.3 us (11%)
  local copies, waits for them, and re-layouts  4.54 us (3%)
    all_to_all x2, waiting for transfers between devices, exchange(): return lax.all_to_all(x, both, split_axis=0, concat_axis=0, tiled=True)  36.7 us
    pallas_call x14, Pallas kernels, run(): pl.pallas_call(body, out_shape=outs, in_specs=[SMEM] * scalars + [VMEM] *...  34.3 us
    all_to_all x1, blocking collectives, exchange_half(): return lax.all_to_all(x, both, 0, 0, axis_index_groups=groups, tiled=True)  14.3 us
    ppermute x8, waiting for transfers between devices, send(): return lax.ppermute(x, axis, [(i, (i + step) % size) for i in range(size)])  12.5 us
    ppermute x8, starting transfers between devices, send(): return lax.ppermute(x, axis, [(i, (i + step) % size) for i in range(size)])  9.32 us
    all_to_all x1, waiting for transfers between devices, exchange_half(): return lax.all_to_all(x, both, 0, 0, axis_index_groups=groups, tiled=True)  6.38 us
    all_to_all x2, starting transfers between devices, exchange(): return lax.all_to_all(x, both, split_axis=0, concat_axis=0, tiled=True)  6.13 us
    all_to_all x1, starting transfers between devices, exchange_half(): return lax.all_to_all(x, both, 0, 0, axis_index_groups=groups, tiled=True)  4.51 us
  transfers between devices with their start and end apart: 12, of which 10 were waited for; matrix products, arithmetic and copies ran while one was open for 0% of the time, Pallas kernels for 13%

profile of v9, /device:TPU:0, one launch (start us, length us, event | category | flops | bytes accessed | tf_op | source)
XLA Modules:
  0.0 133.5 jit_solution(18143022700855312785)
XLA Ops:
  0.6 0.0 copy-start.1
  0.6 1.0 copy-done.1
  1.7 0.1 shard_map.113
  1.8 3.0 %collective-permute-start = (f32[32,256]{1,0:T(8,128)S(1)}, f32[32,256]{1,0:T(8,128)S(1)}, u32[]{:S(2)}, u32[]{:S(2)}) collective-permute-start(f32[32,256]{1,0:T(8,128)S(1)} %get-tuple-element.35), channel_id=1, source_target_pairs={{0,1},{1,2},{2,3},{3,4},{4,5},{5,6},{6,7},{7,0},{8,9},{9,10},{10,1... | collective-permute-start | bytes 98312 | tf_op jit(solution)/shard_map/ppermute | solution.py:98
  4.8 3.1 %collective-permute-start.1 = (f32[32,256]{1,0:T(8,128)S(1)}, f32[32,256]{1,0:T(8,128)S(1)}, u32[]{:S(2)}, u32[]{:S(2)}) collective-permute-start(f32[32,256]{1,0:T(8,128)S(1)} %get-tuple-element.36), channel_id=1, source_target_pairs={{0,7},{1,0},{2,1},{3,2},{4,3},{5,4},{6,5},{7,6},{8,15},{9,8},{10,9... | collective-permute-start | bytes 98312 | tf_op jit(solution)/shard_map/ppermute | solution.py:98
  7.9 1.8 %collective-permute-done = f32[32,256]{1,0:T(8,128)S(1)} collective-permute-done((f32[32,256]{1,0:T(8,128)S(1)}, f32[32,256]{1,0:T(8,128)S(1)}, u32[]{:S(2)}, u32[]{:S(2)}) %collective-permute-start) | collective-permute-done | bytes 32800 | tf_op jit(solution)/shard_map/ppermute | solution.py:98
  9.7 0.0 collective-permute-done.1
  9.7 0.2 collective-permute-start.3
  10.0 0.3 collective-permute-start.2
  10.3 1.8 %shard_map.114 = (bf16[512,256]{1,0:T(8,128)(2,1)S(1)}, bf16[512,256]{1,0:T(8,128)(2,1)S(1)}, bf16[256,256]{1,0:T(8,128)(2,1)S(1)}, bf16[256,256]{1,0:T(8,128)(2,1)S(1)}) custom-call(f32[32,16,256]{2,1,0:T(8,128)S(1)} %get-tuple-element.34.core, f32[2,32,256]{2,1,0:T(8,128)S(1)} %pad_maximum_fusion.y_faces), custom_call_target="tpu_custom_call" | custom-call | flops 7864320 | bytes 2097152 | tf_op jit(solution)/shard_map/pallas_call | solution.py:79
  12.1 0.0 copy-start.4
  12.1 0.0 collective-permute-done.3
  12.1 1.3 %collective-permute-done.2 = f32[18,256]{1,0:T(8,128)S(1)} collective-permute-done((f32[18,256]{1,0:T(8,128)S(1)}, f32[18,256]{1,0:T(8,128)S(1)}, u32[]{:S(2)}, u32[]{:S(2)}) %collective-permute-start.2) | collective-permute-done | bytes 18464 | tf_op jit(solution)/shard_map/ppermute | solution.py:98
  13.5 1.3 shard_map.115
  14.8 0.0 copy-start.8
  14.8 0.0 copy-start.9
  14.8 4.5 %all-to-all-start = ((f32[16,16,512]{2,1,0:T(8,128)}), f32[16,16,512]{2,1,0:T(8,128)S(1)}, u32[]{:S(2)}, u32[]{:S(2)}) async-start(f32[16,16,512]{2,1,0:T(8,128)} %bitcast.11), calls=%async_computation | async-start | bytes 1048576 | tf_op jit(solution)/shard_map/all_to_all | solution.py:815
  19.3 0.0 copy-start.16
  19.3 0.0 copy-done.4
  19.4 0.1 copy.12.owner_col
  19.5 0.0 copy-done.5
  19.5 0.2 shard_map.117
  19.8 0.9 shard_map.116
  20.6 0.0 copy-start.10
  20.6 0.9 copy-done.10
  21.6 0.7 copy-done.12
  22.3 0.7 copy-done.14
  22.9 6.4 %all-to-all-done.slab = f32[16,16,512]{2,1,0:T(8,128)S(1)} async-done(((f32[16,16,512]{2,1,0:T(8,128)}), f32[16,16,512]{2,1,0:T(8,128)S(1)}, u32[]{:S(2)}, u32[]{:S(2)}) %all-to-all-start) | async-done | bytes 524320 | tf_op jit(solution)/shard_map/all_to_all | solution.py:815
  29.3 0.0 copy-done.2
  29.3 0.0 copy-done.3
  29.3 0.0 copy-done.6
  29.3 0.0 copy-done.7
  29.3 0.0 copy-done.8
  29.3 0.0 copy-done.9
  29.4 2.3 %shard_map.118 = (f32[8,128,128]{2,1,0:T(8,128)S(1)}, f32[128,128]{1,0:T(8,128)S(1)}, f32[56,128]{1,0:T(8,128)S(1)}) custom-call(s32[1]{0:T(128)} %bitcast.12.first, f32[256]{0:T(256)S(1)} %copy-done.6, f32[16,16,512]{2,1,0:T(8,128)S(1)} %all-to-all-done.slab, f32[32,128]{1,0:T(8,128)S(1)} %get-tuple-element.46.labels, f32[128,128]{1,0:T(8,128)S(1)} %copy-done.7, ...), custom_call_target="tpu_custom_call" | custom-call | flops 201326592 | bytes 2097152 | tf_op jit(solution)/shard_map/pallas_call | solution.py:79
  31.6 3.1 %collective-permute-start.4 = (f32[56,128]{1,0:T(8,128)S(1)}, f32[56,128]{1,0:T(8,128)S(1)}, u32[]{:S(2)}, u32[]{:S(2)}) collective-permute-start(f32[56,128]{1,0:T(8,128)S(1)} %get-tuple-element.49), channel_id=1, source_target_pairs={{0,4},{1,5},{2,6},{3,7},{4,0},{5,1},{6,2},{7,3},{8,12},{9,13},{10,... | collective-permute-start | bytes 86024 | tf_op jit(solution)/shard_map/ppermute | solution.py:844
  34.8 0.0 copy-done.16
  34.8 0.1 jit_solution_.3.lap_x
  34.8 1.6 %shard_map.119 = (f32[8,128,128]{2,1,0:T(8,128)S(1)}, f32[8,128,128]{2,1,0:T(8,128)S(1)}, f32[128,128]{1,0:T(8,128)S(1)}, f32[128,128]{1,0:T(8,128)S(1)}, bf16[128,2048]{1,0:T(8,128)(2,1)S(1)}) custom-call(s32[1]{0:T(128)} %bitcast.12.first, f32[256]{0:T(256)S(1)} %copy-done.6, f32[128,128]{1,0:T(8,128)S(1)} %jit_solution_.3.lap_x), custom_call_target="tpu_custom_call" | custom-call | flops 13107200 | bytes 2097152 | tf_op jit(solution)/shard_map/pallas_call | solution.py:79
  36.4 0.8 collective-permute-done.4.received
  37.2 1.5 %shard_map.120 = f32[16,16,640]{2,1,0:T(8,128)S(1)} custom-call(s32[1]{0:T(128)} %bitcast.12.first, s32[1]{0:T(128)} %bitcast.half.own, f32[8,128,128]{2,1,0:T(8,128)S(1)} %get-tuple-element.47.found, f32[128,128]{1,0:T(8,128)S(1)} %get-tuple-element.48.ends, f32[56,128]{1,0:T(8,128)S(1)} %collective-permute-done.4.received, ...), custom_call_target="tpu_custom_call" | custom-call | flops 201326592 | bytes 2097152 | tf_op jit(solution)/shard_map/pallas_call | solution.py:79
  38.7 14.3 %all_to_all.39 = f32[16,16,640]{2,1,0:T(8,128)S(1)} all-to-all(f32[16,16,640]{2,1,0:T(8,128)S(1)} %shard_map.120), channel_id=1, replica_groups={{0,1,2,3,8,9,10,11,16,17,18,19,24,25,26,27},{4,5,6,7,12,13,14,15,20,21,..., dimensions={0} | all-to-all | bytes 1310720 | tf_op jit(solution)/shard_map/all_to_all | solution.py:815
  52.9 0.0 copy-done.11
  52.9 0.0 copy-done.15
  52.9 1.7 %shard_map.121 = (f32[256,896]{1,0:T(8,128)S(1)}, f32[896,256]{1,0:T(8,128)S(1)}, s32[2,1,256]{2,1,0:T(1,128)S(1)}) custom-call(s32[1]{0:T(128)} %bitcast.half.own, f32[3,640,128]{2,1,0:T(8,128)S(1)} %copy-done.11, f32[256,640]{1,0:T(8,128)S(1)} %bitcast.41, bf16[256,384]{1,0:T(8,128)(2,1)S(1)} %copy-done.13, bf16[256,384]{1,0:T(8,128)(2,1)S(1)} %copy-done.15, ...), custom_call_target="tpu_custom_call" | custom-call | flops 838860800 | bytes 6291456 | tf_op jit(solution)/shard_map/pallas_call | solution.py:79
  54.7 0.0 copy-start
  54.7 0.9 copy-done
  55.6 3.3 %all-to-all-start.3 = ((f32[32,8,896]{2,1,0:T(8,128)}), f32[32,8,896]{2,1,0:T(8,128)S(1)}, u32[]{:S(2)}, u32[]{:S(2)}) async-start(f32[32,8,896]{2,1,0:T(8,128)} %bitcast.43), calls=%async_computation.3 | async-start | bytes 1835008 | tf_op jit(solution)/shard_map/all_to_all | solution.py:755
  58.9 2.0 %shard_map.123 = f32[3,32,16,256]{3,2,1,0:T(8,128)} custom-call(f32[32,16,256]{2,1,0:T(8,128)S(1)} %get-tuple-element.34.core, f32[2,18,256]{2,1,0:T(8,128)S(1)} %pad_maximum_fusion.1.x_faces, f32[2,32,256]{2,1,0:T(8,128)S(1)} %pad_maximum_fusion.y_faces, f32[256,640]{1,0:T(8,128)S(1)} %bitcast.42, bf16[256,256]{1,0:T(8,128)(2,1)S(1)} %get-tuple-element.39.high, ...), custom_call_target="tpu_custom_call" | custom-call | flops 251658240 | bytes 4194304 | tf_op jit(solution)/shard_map/pallas_call | solution.py:79
  60.9 1.6 %shard_map.122 = f32[256,896]{1,0:T(8,128)} custom-call(f32[896,256]{1,0:T(8,128)S(1)} %get-tuple-element.58.values, s32[1,256]{1,0:T(1,128)S(1)} %get-tuple-element.57.slots), custom_call_target="tpu_custom_call" | custom-call | flops 352321536 | bytes 4194304 | tf_op jit(solution)/shard_map/pallas_call | solution.py:79
  62.4 21.2 %all-to-all-done.3 = f32[32,8,896]{2,1,0:T(8,128)S(1)} async-done(((f32[32,8,896]{2,1,0:T(8,128)}), f32[32,8,896]{2,1,0:T(8,128)S(1)}, u32[]{:S(2)}, u32[]{:S(2)}) %all-to-all-start.3) | async-done | bytes 917536 | tf_op jit(solution)/shard_map/all_to_all | solution.py:755
  83.7 2.8 %all-to-all-start.2 = ((f32[32,8,896]{2,1,0:T(8,128)}), f32[32,8,896]{2,1,0:T(8,128)S(1)}, u32[]{:S(2)}, u32[]{:S(2)}) async-start(f32[32,8,896]{2,1,0:T(8,128)} %bitcast.17), calls=%async_computation.2 | async-start | bytes 1835008 | tf_op jit(solution)/shard_map/all_to_all | solution.py:755
  86.5 9.1 %shard_map.124.refs_0_ = f32[36,24,256]{2,1,0:T(8,128)S(1)} custom-call(f32[256,896]{1,0:T(8,128)S(1)} %bitcast.39, s32[1,256]{1,0:T(1,128)S(1)} %get-tuple-element.76.labels), custom_call_target="tpu_custom_call" | custom-call | flops 39321600 | bytes 4194304 | tf_op jit(solution)/shard_map/pallas_call | solution.py:79
  95.7 15.4 %all-to-all-done.2 = f32[32,8,896]{2,1,0:T(8,128)S(1)} async-done(((f32[32,8,896]{2,1,0:T(8,128)}), f32[32,8,896]{2,1,0:T(8,128)S(1)}, u32[]{:S(2)}, u32[]{:S(2)}) %all-to-all-start.2) | async-done | bytes 917536 | tf_op jit(solution)/shard_map/all_to_all | solution.py:755
  111.1 9.5 %shard_map.125 = (f32[32,16,256]{2,1,0:T(8,128)S(1)}, f32[2,2,16,256]{3,2,1,0:T(8,128)S(1)}, f32[2,36,2,256]{3,2,1,0:T(2,128)S(1)}) custom-call(f32[256,896]{1,0:T(8,128)S(1)} %bitcast.40, s32[1,256]{1,0:T(1,128)S(1)} %get-tuple-element.77.labels, f32[36,24,256]{2,1,0:T(8,128)S(1)} %shard_map.124.refs_0_), custom_call_target="tpu_custom_call" | custom-call | flops 39321600 | bytes 4194304 | tf_op jit(solution)/shard_map/pallas_call | solution.py:79
  120.6 1.4 %collective-permute-start.6 = (f32[36,2,256]{2,1,0:T(2,128)S(1)}, f32[36,2,256]{2,1,0:T(2,128)S(1)}, u32[]{:S(2)}, u32[]{:S(2)}) collective-permute-start(f32[36,2,256]{2,1,0:T(2,128)S(1)} %get-tuple-element.68), channel_id=1, source_target_pairs={{0,7},{1,0},{2,1},{3,2},{4,3},{5,4},{6,5},{7,6},{8,15},{9,8},{10,9... | collective-permute-start | bytes 221192 | tf_op jit(solution)/shard_map/ppermute | solution.py:98
  122.0 0.6 collective-permute-start.5
  122.7 2.3 %collective-permute-done.6.y_top = f32[36,2,256]{2,1,0:T(2,128)S(1)} collective-permute-done((f32[36,2,256]{2,1,0:T(2,128)S(1)}, f32[36,2,256]{2,1,0:T(2,128)S(1)}, u32[]{:S(2)}, u32[]{:S(2)}) %collective-permute-start.6) | collective-permute-done | bytes 73760 | tf_op jit(solution)/shard_map/ppermute | solution.py:98
  125.0 4.1 %collective-permute-done.5.y_low = f32[36,2,256]{2,1,0:T(2,128)S(1)} collective-permute-done((f32[36,2,256]{2,1,0:T(2,128)S(1)}, f32[36,2,256]{2,1,0:T(2,128)S(1)}, u32[]{:S(2)}, u32[]{:S(2)}) %collective-permute-start.5) | collective-permute-done | bytes 73760 | tf_op jit(solution)/shard_map/ppermute | solution.py:98
  129.1 0.1 collective-permute-start.8
  129.2 0.5 collective-permute-start.7
  129.7 1.2 collective-permute-done.8.x_top
  130.9 1.7 %collective-permute-done.7.x_low = f32[2,16,256]{2,1,0:T(8,128)S(1)} collective-permute-done((f32[2,16,256]{2,1,0:T(8,128)S(1)}, f32[2,16,256]{2,1,0:T(8,128)S(1)}, u32[]{:S(2)}, u32[]{:S(2)}) %collective-permute-start.7) | collective-permute-done | bytes 32800 | tf_op jit(solution)/shard_map/ppermute | solution.py:98
  132.6 0.9 shard_map.127
  (22 shorter events, 0.1 us)
Async XLA Ops:
  0.6 1.0 copy-start.1
  1.8 8.0 %collective-permute-start = (f32[32,256]{1,0:T(8,128)S(1)}, f32[32,256]{1,0:T(8,128)S(1)}, u32[]{:S(2)}, u32[]{:S(2)}) collective-permute-start(f32[32,256]{1,0:T(8,128)S(1)} %get-tuple-element.35), channel_id=1, source_target_pairs={{0,1},{1,2},{2,3},{3,4},{4,5},{5,6},{6,7},{7,0},{8,9},{9,10},{10,1... | collective-permute-start | bytes 98312 | tf_op jit(solution)/shard_map/ppermute | solution.py:98
  4.8 4.9 %collective-permute-start.1 = (f32[32,256]{1,0:T(8,128)S(1)}, f32[32,256]{1,0:T(8,128)S(1)}, u32[]{:S(2)}, u32[]{:S(2)}) collective-permute-start(f32[32,256]{1,0:T(8,128)S(1)} %get-tuple-element.36), channel_id=1, source_target_pairs={{0,7},{1,0},{2,1},{3,2},{4,3},{5,4},{6,5},{7,6},{8,15},{9,8},{10,9... | collective-permute-start | bytes 98312 | tf_op jit(solution)/shard_map/ppermute | solution.py:98
  9.7 2.4 %collective-permute-start.3 = (f32[18,256]{1,0:T(8,128)S(1)}, f32[18,256]{1,0:T(8,128)S(1)}, u32[]{:S(2)}, u32[]{:S(2)}) collective-permute-start(f32[18,256]{1,0:T(8,128)S(1)} %pad_maximum_fusion.3), channel_id=1, source_target_pairs={{0,24},{8,0},{16,8},{24,16},{1,25},{9,1},{17,9},{25,17},{2,26},{10... | collective-permute-start | bytes 55304 | tf_op jit(solution)/shard_map/ppermute | solution.py:98
  10.0 3.5 %collective-permute-start.2 = (f32[18,256]{1,0:T(8,128)S(1)}, f32[18,256]{1,0:T(8,128)S(1)}, u32[]{:S(2)}, u32[]{:S(2)}) collective-permute-start(f32[18,256]{1,0:T(8,128)S(1)} %pad_maximum_fusion.2), channel_id=1, source_target_pairs={{0,8},{8,16},{16,24},{24,0},{1,9},{9,17},{17,25},{25,1},{2,10},{10... | collective-permute-start | bytes 55304 | tf_op jit(solution)/shard_map/ppermute | solution.py:98
  12.1 7.2 %copy-start.4 = (s32[1,1,256,1]{2,3,1,0:T(1,128)S(1)}, s32[1,1,256,1]{2,3,1,0:T(1,128)}, u32[]{:S(2)}) copy-start(s32[1,1,256,1]{2,3,1,0:T(1,128)} %param.11) | copy-start | bytes 3076
  13.5 6.0 %copy-start.5 = (s32[1,1,256]{2,1,0:T(1,128)S(1)}, s32[1,1,256]{2,1,0:T(1,128)}, u32[]{:S(2)}) copy-start(s32[1,1,256]{2,1,0:T(1,128)} %param.12) | copy-start | bytes 3076
  14.8 14.6 %copy-start.2 = (bf16[128,128]{1,0:T(8,128)(2,1)S(1)}, bf16[128,128]{1,0:T(8,128)(2,1)}, u32[]{:S(2)}) copy-start(bf16[128,128]{1,0:T(8,128)(2,1)} %constant.56.clone.hx_low) | copy-start | bytes 98308
  14.8 14.6 %copy-start.3 = (bf16[128,128]{1,0:T(8,128)(2,1)S(1)}, bf16[128,128]{1,0:T(8,128)(2,1)}, u32[]{:S(2)}) copy-start(bf16[128,128]{1,0:T(8,128)(2,1)} %constant.55.clone.hx_high) | copy-start | bytes 98308
  14.8 14.6 %copy-start.6 = (f32[256]{0:T(256)S(1)}, f32[256]{0:T(256)}, u32[]{:S(2)}) copy-start(f32[256]{0:T(256)} %constant.52.clone.lap_z) | copy-start | bytes 3076
  14.8 14.6 %copy-start.7 = (f32[128,128]{1,0:T(8,128)S(1)}, f32[128,128]{1,0:T(8,128)}, u32[]{:S(2)}) copy-start(f32[128,128]{1,0:T(8,128)} %constant.54.clone.lap_xy) | copy-start | bytes 196612
  14.8 14.6 %copy-start.8 = (bf16[128,128]{1,0:T(8,128)(2,1)S(1)}, bf16[128,128]{1,0:T(8,128)(2,1)}, u32[]{:S(2)}) copy-start(bf16[128,128]{1,0:T(8,128)(2,1)} %constant.58.clone.hy_low) | copy-start | bytes 98308
  14.8 14.6 %copy-start.9 = (bf16[128,128]{1,0:T(8,128)(2,1)S(1)}, bf16[128,128]{1,0:T(8,128)(2,1)}, u32[]{:S(2)}) copy-start(bf16[128,128]{1,0:T(8,128)(2,1)} %constant.57.clone.hy_high) | copy-start | bytes 98308
  14.8 14.5 %all-to-all-start = ((f32[16,16,512]{2,1,0:T(8,128)}), f32[16,16,512]{2,1,0:T(8,128)S(1)}, u32[]{:S(2)}, u32[]{:S(2)}) async-start(f32[16,16,512]{2,1,0:T(8,128)} %bitcast.11), calls=%async_computation | async-start | bytes 1048576 | tf_op jit(solution)/shard_map/all_to_all | solution.py:815
  19.3 15.4 %copy-start.16 = (f32[128]{0:T(128)S(1)}, f32[128]{0:T(128)}, u32[]{:S(2)}) copy-start(f32[128]{0:T(128)} %constant.53.clone) | copy-start | bytes 1540
  20.6 0.9 copy-start.10
  21.6 0.7 copy-start.12
  22.3 0.7 copy-start.14
  31.6 5.5 %collective-permute-start.4 = (f32[56,128]{1,0:T(8,128)S(1)}, f32[56,128]{1,0:T(8,128)S(1)}, u32[]{:S(2)}, u32[]{:S(2)}) collective-permute-start(f32[56,128]{1,0:T(8,128)S(1)} %get-tuple-element.49), channel_id=1, source_target_pairs={{0,4},{1,5},{2,6},{3,7},{4,0},{5,1},{6,2},{7,3},{8,12},{9,13},{10,... | collective-permute-start | bytes 86024 | tf_op jit(solution)/shard_map/ppermute | solution.py:844
  37.1 15.8 %copy-start.11 = (f32[3,640,128]{2,1,0:T(8,128)S(1)}, f32[3,640,128]{2,1,0:T(8,128)}, u32[]{:S(2)}) copy-start(f32[3,640,128]{2,1,0:T(8,128)} %copy-done.10) | copy-start | bytes 2949124
  37.1 15.8 %copy-start.13 = (bf16[256,384]{1,0:T(8,128)(2,1)S(1)}, bf16[256,384]{1,0:T(8,128)(2,1)}, u32[]{:S(2)}) copy-start(bf16[256,384]{1,0:T(8,128)(2,1)} %copy-done.12) | copy-start | bytes 589828
  37.2 15.8 %copy-start.15 = (bf16[256,384]{1,0:T(8,128)(2,1)S(1)}, bf16[256,384]{1,0:T(8,128)(2,1)}, u32[]{:S(2)}) copy-start(bf16[256,384]{1,0:T(8,128)(2,1)} %copy-done.14) | copy-start | bytes 589828
  54.7 0.9 copy-start
  55.6 28.1 %all-to-all-start.3 = ((f32[32,8,896]{2,1,0:T(8,128)}), f32[32,8,896]{2,1,0:T(8,128)S(1)}, u32[]{:S(2)}, u32[]{:S(2)}) async-start(f32[32,8,896]{2,1,0:T(8,128)} %bitcast.43), calls=%async_computation.3 | async-start | bytes 1835008 | tf_op jit(solution)/shard_map/all_to_all | solution.py:755
  83.7 27.4 %all-to-all-start.2 = ((f32[32,8,896]{2,1,0:T(8,128)}), f32[32,8,896]{2,1,0:T(8,128)S(1)}, u32[]{:S(2)}, u32[]{:S(2)}) async-start(f32[32,8,896]{2,1,0:T(8,128)} %bitcast.17), calls=%async_computation.2 | async-start | bytes 1835008 | tf_op jit(solution)/shard_map/all_to_all | solution.py:755
  120.6 4.4 %collective-permute-start.6 = (f32[36,2,256]{2,1,0:T(2,128)S(1)}, f32[36,2,256]{2,1,0:T(2,128)S(1)}, u32[]{:S(2)}, u32[]{:S(2)}) collective-permute-start(f32[36,2,256]{2,1,0:T(2,128)S(1)} %get-tuple-element.68), channel_id=1, source_target_pairs={{0,7},{1,0},{2,1},{3,2},{4,3},{5,4},{6,5},{7,6},{8,15},{9,8},{10,9... | collective-permute-start | bytes 221192 | tf_op jit(solution)/shard_map/ppermute | solution.py:98
  122.0 7.0 %collective-permute-start.5 = (f32[36,2,256]{2,1,0:T(2,128)S(1)}, f32[36,2,256]{2,1,0:T(2,128)S(1)}, u32[]{:S(2)}, u32[]{:S(2)}) collective-permute-start(f32[36,2,256]{2,1,0:T(2,128)S(1)} %get-tuple-element.69), channel_id=1, source_target_pairs={{0,1},{1,2},{2,3},{3,4},{4,5},{5,6},{6,7},{7,0},{8,9},{9,10},{10,1... | collective-permute-start | bytes 221192 | tf_op jit(solution)/shard_map/ppermute | solution.py:98
  129.1 1.8 %collective-permute-start.8 = (f32[2,16,256]{2,1,0:T(8,128)S(1)}, f32[2,16,256]{2,1,0:T(8,128)S(1)}, u32[]{:S(2)}, u32[]{:S(2)}) collective-permute-start(f32[2,16,256]{2,1,0:T(8,128)S(1)} %get-tuple-element.70), channel_id=1, source_target_pairs={{0,24},{8,0},{16,8},{24,16},{1,25},{9,1},{17,9},{25,17},{2,26},{10... | collective-permute-start | bytes 98312 | tf_op jit(solution)/shard_map/ppermute | solution.py:98
  129.2 3.4 %collective-permute-start.7 = (f32[2,16,256]{2,1,0:T(8,128)S(1)}, f32[2,16,256]{2,1,0:T(8,128)S(1)}, u32[]{:S(2)}, u32[]{:S(2)}) collective-permute-start(f32[2,16,256]{2,1,0:T(8,128)S(1)} %get-tuple-element.71), channel_id=1, source_target_pairs={{0,8},{8,16},{16,24},{24,0},{1,9},{9,17},{17,25},{25,1},{2,10},{10... | collective-permute-start | bytes 98312 | tf_op jit(solution)/shard_map/ppermute | solution.py:98
